TPU v7x, 256 devices: a whole 4x4x8 slice. The times are simulated.
256 devices in a mesh: row: 16 (over y, z_lo), col: 16 (over z_hi, x, core).
Axes of the slice: x: 4, y: 4, z: 8 (z_hi: 2, z_lo: 4; z = z_hi * 4 + z_lo), core: 2. Of those that a mesh axis runs over, the one named last changes fastest.
Arguments:
- student: bfloat16 [8192, 2048], P(('row', 'col')), may hold values from -0.125 to 0.125
- teacher: bfloat16 [8192, 4096], P(('row', 'col')), may hold values from -0.09375 to 0.09375
Outputs:
- distance: float32 [], replicated
- student_grad: float32 [8192, 2048], P(('row', 'col'))
All inputs are finite; a program needn't handle non-finite values.
Results may differ from a plain program's by a relative error of at most 0.0015.
Values may be sent and summed in bfloat16 or wider, within the bound.
No kernel may reach another device: no remote copies, remote signals or barrier semaphores. Data moves between devices by JAX's collectives and lax.ppermute only.
A program may use at most 64 MiB of HBM per device.

v0:
```python
import jax
import jax.numpy as jnp
from jax import lax
from jax.sharding import PartitionSpec as P


def shards(student, teacher):
    rows_s, rows_t = (
        lax.all_gather(student, "col", axis=0, tiled=True),
        lax.all_gather(teacher, "col", axis=0, tiled=True),
    )
    cols_s, cols_t = (
        lax.all_gather(student, "row", axis=0, tiled=True),
        lax.all_gather(teacher, "row", axis=0, tiled=True),
    )
    contract = (((1,), (1,)), ((), ()))
    gram_s = lax.dot_general(rows_s, cols_s, contract, preferred_element_type=jnp.float32)
    gram_t = lax.dot_general(rows_t, cols_t, contract, preferred_element_type=jnp.float32)
    excess = gram_s - gram_t
    squares = jnp.sum(excess * excess)
    rounded = excess.astype(jnp.bfloat16)
    partial_term = jnp.dot(rounded, cols_s, preferred_element_type=jnp.float32)
    pulled = lax.psum_scatter(partial_term, "col", scatter_dimension=0, tiled=True)
    summed = lax.psum(squares, ("row", "col"))
    texts = student.shape[0] * lax.axis_size("row") * lax.axis_size("col")
    distance = summed / jnp.float32(texts)
    return (distance, pulled)


def solution(mesh):
    in_specs = (P(("row", "col"), None), P(("row", "col"), None))
    out_specs = (P(), P(("row", "col"), None))
    return jax.shard_map(shards, mesh=mesh, in_specs=in_specs, out_specs=out_specs, check_vma=False)
```

profile of v0, /device:TPU:2, one launch (start us, length us, event | category | flops | bytes accessed | tf_op | source)
XLA Modules:
  0.0 459.3 jit_solution(6883434457836587965)
XLA Ops:
  7.2 0.0 all-gather.5.cloned.1.call-start
  7.2 0.7 all-gather.5.cloned.1.call-update
  7.9 0.0 all-gather.7.cloned.1.call-start
  7.9 0.7 all-gather.7.cloned.1.call-update
  8.6 0.0 all-gather.9.cloned.1.call-start
  8.7 0.7 all-gather.9.cloned.1.call-update
  9.4 0.0 all-gather.11.cloned.1.call-start
  9.4 0.5 all-gather.11.cloned.1.call-update
  10.0 0.0 reduce-scatter.2.cloned.1.call-start
  10.0 66.3 %all-gather.5.cloned.1.call-done = bf16[512,2048]{1,0:T(8,128)(2,1)} async-done(((bf16[32,2048]{1,0:T(8,128)(2,1)}), bf16[512,2048]{1,0:T(8,128)(2,1)}) %all-gather.5.cloned.1.call-update) | async-done | bytes 2097168 | tf_op jit(solution)/shard_map/all_gather | solution.py:9
  76.3 84.8 %all-gather.7.cloned.1.call-done = bf16[512,2048]{1,0:T(8,128)(2,1)} async-done(((bf16[32,2048]{1,0:T(8,128)(2,1)}), bf16[512,2048]{1,0:T(8,128)(2,1)}) %all-gather.7.cloned.1.call-update) | async-done | bytes 2097168 | tf_op jit(solution)/shard_map/all_gather | solution.py:13
  161.1 3.5 fusion.2
  164.6 0.0 copy-start
  164.6 75.6 %all-gather.9.cloned.1.call-done = bf16[512,4096]{1,0:T(8,128)(2,1)} async-done(((bf16[32,4096]{1,0:T(8,128)(2,1)}), bf16[512,4096]{1,0:T(8,128)(2,1)}) %all-gather.9.cloned.1.call-update) | async-done | bytes 4194320 | tf_op jit(solution)/shard_map/all_gather | solution.py:10
  240.2 99.5 %all-gather.11.cloned.1.call-done = bf16[512,4096]{1,0:T(8,128)(2,1)} async-done(((bf16[32,4096]{1,0:T(8,128)(2,1)}), bf16[512,4096]{1,0:T(8,128)(2,1)}) %all-gather.11.cloned.1.call-update) | async-done | bytes 4194320 | tf_op jit(solution)/shard_map/all_gather | solution.py:14
  339.7 6.6 %multiply_reduce_fusion = (f32[]{:T(128)}, bf16[512,512]{1,0:T(8,128)(2,1)S(1)}) fusion(f32[512,512]{1,0:T(8,128)S(1)} %fusion.2, bf16[512,4096]{1,0:T(8,128)(2,1)} %all-gather.9.cloned.1.call-done, bf16[512,4096]{1,0:T(8,128)(2,1)} %all-gather.11.cloned.1.call-done), kind=kOutput, calls=%fused_computation.1 | convolution fusion | flops 2148532224 | bytes 9961476 | tf_op jit(solution)/shard_map/dot_general | solution.py:18
  346.3 0.0 copy-done
  346.3 3.2 fusion
  349.6 0.0 reduce-scatter.2.cloned.1.call-update
  349.6 86.9 %psum.7 = f32[]{:T(128)} all-reduce(f32[]{:T(128)} %get-tuple-element.2), channel_id=1, replica_groups=mesh['row'=16,'col'=16] {'row','col'}, use_global_device_ids=true, to_apply=%region_1.0 | all-reduce | flops 1 | bytes 8 | tf_op jit(solution)/shard_map/psum | solution.py:24
  437.1 14.5 %reduce-scatter.2.cloned.1.call-done = f32[32,2048]{1,0:T(8,128)} async-done(((f32[512,2048]{1,0:T(8,128)}), f32[32,2048]{1,0:T(8,128)}) %reduce-scatter.2.cloned.1.call-update) | async-done | bytes 262160 | tf_op jit(solution)/shard_map/reduce_scatter | solution.py:23
Async XLA Ops:
  7.2 69.1 %all-gather.5.cloned.1.call-start = ((), (), s32[]{:S(2)}) async-start(), calls=%async_computation.1 | async-start | bytes 2228224 | tf_op jit(solution)/shard_map/all_gather | solution.py:9
  7.9 153.2 %all-gather.7.cloned.1.call-start = ((), (), s32[]{:S(2)}) async-start(), calls=%async_computation.2 | async-start | bytes 2228224 | tf_op jit(solution)/shard_map/all_gather | solution.py:13
  8.6 231.6 %all-gather.9.cloned.1.call-start = ((), (), s32[]{:S(2)}) async-start(), calls=%async_computation.3 | async-start | bytes 4456448 | tf_op jit(solution)/shard_map/all_gather | solution.py:10
  9.4 330.4 %all-gather.11.cloned.1.call-start = ((), (), s32[]{:S(2)}) async-start(), calls=%async_computation.4 | async-start | bytes 4456448 | tf_op jit(solution)/shard_map/all_gather | solution.py:14
  10.0 441.7 %reduce-scatter.2.cloned.1.call-start = ((), (), s32[]{:S(2)}) async-start(), calls=%async_computation.5 | async-start | bytes 4456448 | tf_op jit(solution)/shard_map/reduce_scatter | solution.py:23
  164.6 181.7 %copy-start = (bf16[512,2048]{1,0:T(8,128)(2,1)S(1)}, bf16[512,2048]{1,0:T(8,128)(2,1)}, u32[]{:S(2)}) copy-start(bf16[512,2048]{1,0:T(8,128)(2,1)} %all-gather.7.cloned.1.call-done) | copy-start | bytes 6291460
Sparse Core Ops, SparseCore 0:
  10.7 65.5 all-gather.4
  78.1 82.9 all-gather.6
  163.8 76.3 all-gather.8
  241.9 97.8 all-gather.10
  349.7 101.9 reduce-scatter.1
where the time goes:
time: 460 us; the launch traced here: 459 us
  waiting for transfers between devices  343 us (75%)
  blocking collectives  86.9 us (19%)
  between operations  15.6 us (3%)
  matrix products  13.3 us (3%)
    all_gather x1, waiting for transfers between devices, shards(): lax.all_gather(teacher, 'row', axis=0, tiled=True)  99.5 us
    psum x1, blocking collectives, shards(): summed = lax.psum(squares, ('row', 'col'))  86.9 us
    all_gather x1, waiting for transfers between devices, shards(): lax.all_gather(student, 'row', axis=0, tiled=True)  84.8 us
    all_gather x1, waiting for transfers between devices, shards(): lax.all_gather(teacher, 'col', axis=0, tiled=True)  75.6 us
    all_gather x1, waiting for transfers between devices, shards(): lax.all_gather(student, 'col', axis=0, tiled=True)  66.3 us
    reduce_scatter x1, waiting for transfers between devices, shards(): lax.psum_scatter(partial_term, 'col', scatter_dimension=0, tiled=True)  14.5 us
  transfers between devices with their start and end apart: 5, of which 5 were waited for; matrix products, arithmetic and copies ran while one was open for 1% of the time, Pallas kernels for 0%

commit v1 on v0

v1 whole, which is shorter than its diff:
```python
import jax
import jax.numpy as jnp
from jax import lax
from jax.sharding import Mesh, PartitionSpec as P

AXES = ("y", "zl", "zh", "x", "core")
SIZES = (4, 4, 2, 4, 2)
STRIDES = (64, 16, 8, 2, 1)


def shift(value, **steps):
    pairs = []
    for target in range(256):
        source = 0
        for axis, size, stride in zip(AXES, SIZES, STRIDES):
            source += (target // stride + steps.get(axis, 0)) % size * stride
        pairs.append((source, target))
    return lax.ppermute(value, AXES, pairs)


def shards(student, teacher):
    texts, width = student.shape
    rows = lax.all_gather(
        jnp.concatenate([student, -teacher], axis=1), ("zh", "zl", "core"), axis=0, tiled=True
    )
    both = jnp.concatenate([student, teacher], axis=1)
    half = texts // 2
    upper, lower = both[:half], both[half:]
    upper = jnp.concatenate([upper] + [shift(upper, x=k) for k in (1, 3, 2)])
    lower = jnp.concatenate([lower] + [shift(lower, y=k) for k in (1, 3, 2)])
    cols = jnp.concatenate(
        [upper, lower]
        + [f for k in (1, 3, 2) for f in (shift(upper, y=k), shift(lower, x=k))]
    )
    excess = lax.dot_general(
        rows, cols, (((1,), (1,)), ((), ())), preferred_element_type=jnp.float32
    )
    squares = jnp.sum(excess * excess)
    rounded = excess.astype(jnp.bfloat16).reshape(8, 2, texts, -1)
    cols_s = cols[:, :width]
    core = lax.axis_index("core")

    def pull(which):
        picked = lax.dynamic_index_in_dim(rounded, which, 1, keepdims=False)
        return jnp.dot(
            picked.reshape(8 * texts, -1), cols_s, preferred_element_type=jnp.float32
        )

    other = shift(pull(1 - core), core=1)
    partial_term = pull(core) + other
    pulled = lax.psum_scatter(partial_term, ("zh", "zl"), scatter_dimension=0, tiled=True)

    plane = lax.all_to_all(
        jnp.broadcast_to(squares, (32, 8, 128)), ("y", "x", "core"), 0, 0
    )
    plane = jnp.sum(plane[:, 0, 0])
    line = lax.all_to_all(jnp.broadcast_to(plane, (8, 8, 128)), ("zh", "zl"), 0, 0)
    distance = jnp.sum(line[:, 0, 0]) / jnp.float32(texts * 256)
    return distance, pulled


def solution(mesh):
    fine = Mesh(mesh.devices.reshape(SIZES), AXES)
    spec = P(AXES, None)
    return jax.shard_map(
        shards, mesh=fine, in_specs=(spec, spec), out_specs=(P(), spec), check_vma=False
    )
```

time: 460 us -> 152 us (0.33)
  waiting for transfers between devices: 343 us -> 50.9 us
  blocking collectives: 86.9 us -> 36.5 us
  starting transfers between devices: 0.19 us -> 17.9 us
  local copies, waits for them, and re-layouts: 0.01 us -> 13.7 us
    all_gather x4 -> x1, waiting for transfers between devices: 326 us -> 0.01 us  [shards(): lax.all_gather(jnp.concatenate([student, -teacher], axis=1), ('zh', 'zl',...]
    psum x1 -> x0, blocking collectives: 86.9 us -> none  [shards(): summed = lax.psum(squares, ('row', 'col'))]
    ppermute x0 -> x13, waiting for transfers between devices: none -> 39.7 us  [shift(): return lax.ppermute(value, AXES, pairs)]
    all_to_all x0 -> x2, blocking collectives: none -> 36.5 us  [the longest x1 19.7 us: shards(): lax.all_to_all(jnp.broadcast_to(squares, (32, 8, 128)), ('y', 'x', 'core'...]
    ppermute x0 -> x13, starting transfers between devices: none -> 17.8 us  [shift(): return lax.ppermute(value, AXES, pairs)]
    unnamed x2 -> x15, local copies, waits for them, and re-layouts: 0.01 us -> 10.7 us
  transfers between devices with their start and end apart: 5 -> 15, of which waited for: 5 -> 8; matrix products, arithmetic and copies ran while one was open for 1% -> 9% of each run, Pallas kernels for 0% -> 0%
where the time goes in v1:
time: 152 us; the launch traced here: 151 us
  waiting for transfers between devices  50.9 us (33%)
  blocking collectives  36.5 us (24%)
  starting transfers between devices  17.9 us (12%)
  between operations  15.9 us (10%)
  local copies, waits for them, and re-layouts  13.7 us (9%)
  matrix products  11.7 us (8%)
  other arithmetic  4.12 us (3%)
    ppermute x13, waiting for transfers between devices, shift(): return lax.ppermute(value, AXES, pairs)  39.7 us
    all_to_all x1, blocking collectives, shards(): lax.all_to_all(jnp.broadcast_to(squares, (32, 8, 128)), ('y', 'x', 'core'...  19.7 us
    ppermute x13, starting transfers between devices, shift(): return lax.ppermute(value, AXES, pairs)  17.8 us
    all_to_all x1, blocking collectives, shards(): lax.all_to_all(jnp.broadcast_to(plane, (8, 8, 128)), ('zh', 'zl'), 0, 0)  16.8 us
    reduce_scatter x1, waiting for transfers between devices, shards(): lax.psum_scatter(partial_term, ('zh', 'zl'), scatter_dimension=0, tiled=T...  11.2 us
    unnamed x15, local copies, waits for them, and re-layouts  10.7 us
    dot_general x1, matrix products, shards(): lax.dot_general(rows, cols, (((1,), (1,)), ((), ())), preferred_element_t...  8.94 us
  transfers between devices with their start and end apart: 15, of which 8 were waited for; matrix products, arithmetic and copies ran while one was open for 9% of the time, Pallas kernels for 0%

profile of v1, /device:TPU:2, one launch (start us, length us, event | category | flops | bytes accessed | tf_op | source)
XLA Modules:
  0.0 150.8 jit_solution(8877082053254961179)
XLA Ops:
  7.2 0.0 all-gather.2.cloned.1.call-start
  7.2 0.9 constant_dynamic-update-slice_fusion.1
  8.1 1.1 constant_dynamic-update-slice_fusion
  9.2 1.7 %pad_maximum_fusion.2 = bf16[32,6144]{1,0:T(8,128)(2,1)} fusion(bf16[32,4096]{1,0:T(8,128)(2,1)S(1)} %get-tuple-element.10, bf16[32,2048]{1,0:T(8,128)(2,1)} %param.2), kind=kLoop, calls=%fused_computation.7 | loop fusion | flops 786432 | bytes 786432 | tf_op jit(solution)/shard_map/concatenate | solution.py:24
  10.9 0.0 all-gather.2.cloned.1.call-update
  10.9 0.0 reduce-scatter.2.cloned.1.call-start
  11.0 0.7 fusion.4
  11.7 2.3 %collective-permute-start = (bf16[16,6144]{1,0:T(8,128)(2,1)S(1)}, bf16[16,6144]{1,0:T(8,128)(2,1)S(1)}, u32[]{:S(2)}, u32[]{:S(2)}) collective-permute-start(bf16[16,6144]{1,0:T(8,128)(2,1)S(1)} %get-tuple-element.8), channel_id=1, source_target_pairs={{2,0},{3,1},{4,2},{5,3},{6,4},{7,5},{0,6},{1,7},{10,8},{11,9},{12,... | collective-permute-start | bytes 589832 | tf_op jit(solution)/shard_map/ppermute | solution.py:18
  14.0 3.1 %collective-permute-start.2 = (bf16[16,6144]{1,0:T(8,128)(2,1)S(1)}, bf16[16,6144]{1,0:T(8,128)(2,1)S(1)}, u32[]{:S(2)}, u32[]{:S(2)}) collective-permute-start(bf16[16,6144]{1,0:T(8,128)(2,1)S(1)} %get-tuple-element.8), channel_id=1, source_target_pairs={{4,0},{5,1},{6,2},{7,3},{0,4},{1,5},{2,6},{3,7},{12,8},{13,9},{14,... | collective-permute-start | bytes 589832 | tf_op jit(solution)/shard_map/ppermute | solution.py:18
  17.1 3.0 %collective-permute-start.3 = (bf16[16,6144]{1,0:T(8,128)(2,1)S(1)}, bf16[16,6144]{1,0:T(8,128)(2,1)S(1)}, u32[]{:S(2)}, u32[]{:S(2)}) collective-permute-start(bf16[16,6144]{1,0:T(8,128)(2,1)S(1)} %get-tuple-element.6), channel_id=1, source_target_pairs={{64,0},{65,1},{66,2},{67,3},{68,4},{69,5},{70,6},{71,7},{72,8},{73... | collective-permute-start | bytes 589832 | tf_op jit(solution)/shard_map/ppermute | solution.py:18
  20.1 2.2 %collective-permute-start.5 = (bf16[16,6144]{1,0:T(8,128)(2,1)S(1)}, bf16[16,6144]{1,0:T(8,128)(2,1)S(1)}, u32[]{:S(2)}, u32[]{:S(2)}) collective-permute-start(bf16[16,6144]{1,0:T(8,128)(2,1)S(1)} %get-tuple-element.6), channel_id=1, source_target_pairs={{128,0},{129,1},{130,2},{131,3},{132,4},{133,5},{134,6},{135,7},{1... | collective-permute-start | bytes 589832 | tf_op jit(solution)/shard_map/ppermute | solution.py:18
  22.3 1.2 collective-permute-done.2
  23.5 0.1 pad_maximum_fusion
  23.5 3.1 %collective-permute-start.6 = (bf16[64,6144]{1,0:T(8,128)(2,1)S(1)}, bf16[64,6144]{1,0:T(8,128)(2,1)S(1)}, u32[]{:S(2)}, u32[]{:S(2)}) collective-permute-start(bf16[64,6144]{1,0:T(8,128)(2,1)S(1)} %pad_maximum_fusion), channel_id=1, source_target_pairs={{64,0},{65,1},{66,2},{67,3},{68,4},{69,5},{70,6},{71,7},{72,8},{73... | collective-permute-start | bytes 2359304 | tf_op jit(solution)/shard_map/ppermute | solution.py:18
  26.6 4.5 %collective-permute-done.4 = bf16[16,6144]{1,0:T(8,128)(2,1)S(1)} collective-permute-done((bf16[16,6144]{1,0:T(8,128)(2,1)S(1)}, bf16[16,6144]{1,0:T(8,128)(2,1)S(1)}, u32[]{:S(2)}, u32[]{:S(2)}) %collective-permute-start.4) | collective-permute-done | bytes 196640 | tf_op jit(solution)/shard_map/ppermute | solution.py:18
  31.2 0.7 collective-permute-done.5
  31.8 0.1 pad_maximum_fusion.1
  31.9 0.1 collective-permute-start.7
  32.0 2.0 %collective-permute-start.9 = (bf16[64,6144]{1,0:T(8,128)(2,1)S(1)}, bf16[64,6144]{1,0:T(8,128)(2,1)S(1)}, u32[]{:S(2)}, u32[]{:S(2)}) collective-permute-start(bf16[64,6144]{1,0:T(8,128)(2,1)S(1)} %pad_maximum_fusion.1), channel_id=1, source_target_pairs={{6,0},{7,1},{0,2},{1,3},{2,4},{3,5},{4,6},{5,7},{14,8},{15,9},{8,1... | collective-permute-start | bytes 2359304 | tf_op jit(solution)/shard_map/ppermute | solution.py:18
  34.0 1.9 %collective-permute-start.10 = (bf16[64,6144]{1,0:T(8,128)(2,1)S(1)}, bf16[64,6144]{1,0:T(8,128)(2,1)S(1)}, u32[]{:S(2)}, u32[]{:S(2)}) collective-permute-start(bf16[64,6144]{1,0:T(8,128)(2,1)S(1)} %pad_maximum_fusion), channel_id=1, source_target_pairs={{128,0},{129,1},{130,2},{131,3},{132,4},{133,5},{134,6},{135,7},{1... | collective-permute-start | bytes 2359304 | tf_op jit(solution)/shard_map/ppermute | solution.py:18
  35.9 0.7 constant_dynamic-update-slice_fusion.14
  36.6 0.7 constant_dynamic-update-slice_fusion.13
  37.3 0.7 constant_dynamic-update-slice_fusion.12
  38.0 0.7 constant_dynamic-update-slice_fusion.11
  38.7 0.7 constant_dynamic-update-slice_fusion.10
  39.4 0.7 constant_dynamic-update-slice_fusion.9
  40.1 0.7 constant_dynamic-update-slice_fusion.8
  40.8 20.6 %collective-permute-done.6 = bf16[64,6144]{1,0:T(8,128)(2,1)S(1)} collective-permute-done((bf16[64,6144]{1,0:T(8,128)(2,1)S(1)}, bf16[64,6144]{1,0:T(8,128)(2,1)S(1)}, u32[]{:S(2)}, u32[]{:S(2)}) %collective-permute-start.6) | collective-permute-done | bytes 786464 | tf_op jit(solution)/shard_map/ppermute | solution.py:18
  61.3 1.0 constant_dynamic-update-slice_fusion.7
  62.4 1.0 constant_dynamic-update-slice_fusion.6
  63.4 1.3 collective-permute-done.8
  64.7 0.9 constant_dynamic-update-slice_fusion.5
  65.7 0.9 constant_dynamic-update-slice_fusion.4
  66.6 0.9 constant_dynamic-update-slice_fusion.3
  67.5 7.3 %collective-permute-done.11 = bf16[64,6144]{1,0:T(8,128)(2,1)S(1)} collective-permute-done((bf16[64,6144]{1,0:T(8,128)(2,1)S(1)}, bf16[64,6144]{1,0:T(8,128)(2,1)S(1)}, u32[]{:S(2)}, u32[]{:S(2)}) %collective-permute-start.11) | collective-permute-done | bytes 786464 | tf_op jit(solution)/shard_map/ppermute | solution.py:18
  74.8 0.9 constant_dynamic-update-slice_fusion.2
  75.8 8.9 %fusion.3 = (bf16[512,512]{1,0:T(8,128)(2,1)S(1)}, f32[]{:T(128)}) fusion(bf16[512,6144]{1,0:T(8,128)(2,1)} %all-gather.2.cloned.1.call-done, bf16[512,6144]{1,0:T(8,128)(2,1)} %constant_dynamic-update-slice_fusion.2), kind=kOutput, calls=%fused_computation.28 | convolution fusion | flops 3222011904 | bytes 13107204 | tf_op jit(solution)/shard_map/dot_general | solution.py:35
  84.8 0.7 fusion
  85.5 0.1 collective-permute-start.12
  85.6 4.1 %collective-permute-done.12 = f32[256,2048]{1,0:T(8,128)S(1)} collective-permute-done((f32[256,2048]{1,0:T(8,128)S(1)}, f32[256,2048]{1,0:T(8,128)S(1)}, u32[]{:S(2)}, u32[]{:S(2)}) %collective-permute-start.12) | collective-permute-done | bytes 2097184 | tf_op jit(solution)/shard_map/ppermute | solution.py:18
  89.7 2.1 %convolution_add_fusion = f32[256,2048]{1,0:T(8,128)} fusion(f32[256,2048]{1,0:T(8,128)S(1)} %collective-permute-done.12, bf16[256,512]{1,0:T(8,128)(2,1)S(1)} %bitcast.7, bf16[512,6144]{1,0:T(8,128)(2,1)S(1)} %copy-done), kind=kOutput, calls=%fused_computation | convolution fusion | flops 537395200 | bytes 6553600 | tf_op jit(solution)/shard_map/dot_general | solution.py:45
  91.8 0.7 broadcast_in_dim.6
  92.5 19.7 %all_to_all.10 = f32[32,8,128]{2,1,0:T(8,128)S(1)} all-to-all(f32[32,8,128]{2,1,0:T(8,128)S(1)} %broadcast_in_dim.6), channel_id=1, replica_groups=mesh['y'=4,'zl'=4,'zh'=2,'x'=4,'core'=2] {'y','x','core'}, dimensions={0} | all-to-all | bytes 262144 | tf_op jit(solution)/shard_map/all_to_all | solution.py:53
  112.3 0.6 slice_reduce_fusion
  112.9 0.6 broadcast_in_dim.7
  113.5 16.8 %all_to_all.11 = f32[8,8,128]{2,1,0:T(8,128)S(1)} all-to-all(f32[8,8,128]{2,1,0:T(8,128)S(1)} %broadcast_in_dim.7), channel_id=1, replica_groups=mesh['y'=4,'zl'=4,'zh'=2,'x'=4,'core'=2] {'zh','zl'}, dimensions={0} | all-to-all | bytes 65536 | tf_op jit(solution)/shard_map/all_to_all | solution.py:57
  130.3 0.6 slice_reduce_fusion.1
  131.6 11.2 %reduce-scatter.2.cloned.1.call-done = f32[32,2048]{1,0:T(8,128)} async-done(((f32[256,2048]{1,0:T(8,128)}), f32[32,2048]{1,0:T(8,128)}) %reduce-scatter.2.cloned.1.call-update) | async-done | bytes 262160 | tf_op jit(solution)/shard_map/reduce_scatter | solution.py:51
  (15 shorter events, 0.1 us)
Async XLA Ops:
  7.2 68.6 %all-gather.2.cloned.1.call-start = ((), (), s32[]{:S(2)}) async-start(), calls=%async_computation.3 | async-start | bytes 6684672 | tf_op jit(solution)/shard_map/all_gather | solution.py:23
  10.9 131.9 %reduce-scatter.2.cloned.1.call-start = ((), (), s32[]{:S(2)}) async-start(), calls=%async_computation.4 | async-start | bytes 2359296 | tf_op jit(solution)/shard_map/reduce_scatter | solution.py:51
  11.7 8.4 %collective-permute-start = (bf16[16,6144]{1,0:T(8,128)(2,1)S(1)}, bf16[16,6144]{1,0:T(8,128)(2,1)S(1)}, u32[]{:S(2)}, u32[]{:S(2)}) collective-permute-start(bf16[16,6144]{1,0:T(8,128)(2,1)S(1)} %get-tuple-element.8), channel_id=1, source_target_pairs={{2,0},{3,1},{4,2},{5,3},{6,4},{7,5},{0,6},{1,7},{10,8},{11,9},{12,... | collective-permute-start | bytes 589832 | tf_op jit(solution)/shard_map/ppermute | solution.py:18
  14.0 8.3 %collective-permute-start.1 = (bf16[16,6144]{1,0:T(8,128)(2,1)S(1)}, bf16[16,6144]{1,0:T(8,128)(2,1)S(1)}, u32[]{:S(2)}, u32[]{:S(2)}) collective-permute-start(bf16[16,6144]{1,0:T(8,128)(2,1)S(1)} %get-tuple-element.8), channel_id=1, source_target_pairs={{6,0},{7,1},{0,2},{1,3},{2,4},{3,5},{4,6},{5,7},{14,8},{15,9},{8,1... | collective-permute-start | bytes 589832 | tf_op jit(solution)/shard_map/ppermute | solution.py:18
  14.0 9.5 %collective-permute-start.2 = (bf16[16,6144]{1,0:T(8,128)(2,1)S(1)}, bf16[16,6144]{1,0:T(8,128)(2,1)S(1)}, u32[]{:S(2)}, u32[]{:S(2)}) collective-permute-start(bf16[16,6144]{1,0:T(8,128)(2,1)S(1)} %get-tuple-element.8), channel_id=1, source_target_pairs={{4,0},{5,1},{6,2},{7,3},{0,4},{1,5},{2,6},{3,7},{12,8},{13,9},{14,... | collective-permute-start | bytes 589832 | tf_op jit(solution)/shard_map/ppermute | solution.py:18
  17.1 9.6 %collective-permute-start.3 = (bf16[16,6144]{1,0:T(8,128)(2,1)S(1)}, bf16[16,6144]{1,0:T(8,128)(2,1)S(1)}, u32[]{:S(2)}, u32[]{:S(2)}) collective-permute-start(bf16[16,6144]{1,0:T(8,128)(2,1)S(1)} %get-tuple-element.6), channel_id=1, source_target_pairs={{64,0},{65,1},{66,2},{67,3},{68,4},{69,5},{70,6},{71,7},{72,8},{73... | collective-permute-start | bytes 589832 | tf_op jit(solution)/shard_map/ppermute | solution.py:18
  20.1 11.1 %collective-permute-start.4 = (bf16[16,6144]{1,0:T(8,128)(2,1)S(1)}, bf16[16,6144]{1,0:T(8,128)(2,1)S(1)}, u32[]{:S(2)}, u32[]{:S(2)}) collective-permute-start(bf16[16,6144]{1,0:T(8,128)(2,1)S(1)} %get-tuple-element.6), channel_id=1, source_target_pairs={{192,0},{193,1},{194,2},{195,3},{196,4},{197,5},{198,6},{199,7},{2... | collective-permute-start | bytes 589832 | tf_op jit(solution)/shard_map/ppermute | solution.py:18
  20.1 11.7 %collective-permute-start.5 = (bf16[16,6144]{1,0:T(8,128)(2,1)S(1)}, bf16[16,6144]{1,0:T(8,128)(2,1)S(1)}, u32[]{:S(2)}, u32[]{:S(2)}) collective-permute-start(bf16[16,6144]{1,0:T(8,128)(2,1)S(1)} %get-tuple-element.6), channel_id=1, source_target_pairs={{128,0},{129,1},{130,2},{131,3},{132,4},{133,5},{134,6},{135,7},{1... | collective-permute-start | bytes 589832 | tf_op jit(solution)/shard_map/ppermute | solution.py:18
  23.5 37.8 %collective-permute-start.6 = (bf16[64,6144]{1,0:T(8,128)(2,1)S(1)}, bf16[64,6144]{1,0:T(8,128)(2,1)S(1)}, u32[]{:S(2)}, u32[]{:S(2)}) collective-permute-start(bf16[64,6144]{1,0:T(8,128)(2,1)S(1)} %pad_maximum_fusion), channel_id=1, source_target_pairs={{64,0},{65,1},{66,2},{67,3},{68,4},{69,5},{70,6},{71,7},{72,8},{73... | collective-permute-start | bytes 2359304 | tf_op jit(solution)/shard_map/ppermute | solution.py:18
  26.6 38.1 %collective-permute-start.8 = (bf16[64,6144]{1,0:T(8,128)(2,1)S(1)}, bf16[64,6144]{1,0:T(8,128)(2,1)S(1)}, u32[]{:S(2)}, u32[]{:S(2)}) collective-permute-start(bf16[64,6144]{1,0:T(8,128)(2,1)S(1)} %pad_maximum_fusion), channel_id=1, source_target_pairs={{192,0},{193,1},{194,2},{195,3},{196,4},{197,5},{198,6},{199,7},{2... | collective-permute-start | bytes 2359304 | tf_op jit(solution)/shard_map/ppermute | solution.py:18
  31.9 30.5 %collective-permute-start.7 = (bf16[64,6144]{1,0:T(8,128)(2,1)S(1)}, bf16[64,6144]{1,0:T(8,128)(2,1)S(1)}, u32[]{:S(2)}, u32[]{:S(2)}) collective-permute-start(bf16[64,6144]{1,0:T(8,128)(2,1)S(1)} %pad_maximum_fusion.1), channel_id=1, source_target_pairs={{2,0},{3,1},{4,2},{5,3},{6,4},{7,5},{0,6},{1,7},{10,8},{11,9},{12,... | collective-permute-start | bytes 2359304 | tf_op jit(solution)/shard_map/ppermute | solution.py:18
  32.0 33.7 %collective-permute-start.9 = (bf16[64,6144]{1,0:T(8,128)(2,1)S(1)}, bf16[64,6144]{1,0:T(8,128)(2,1)S(1)}, u32[]{:S(2)}, u32[]{:S(2)}) collective-permute-start(bf16[64,6144]{1,0:T(8,128)(2,1)S(1)} %pad_maximum_fusion.1), channel_id=1, source_target_pairs={{6,0},{7,1},{0,2},{1,3},{2,4},{3,5},{4,6},{5,7},{14,8},{15,9},{8,1... | collective-permute-start | bytes 2359304 | tf_op jit(solution)/shard_map/ppermute | solution.py:18
  34.0 32.6 %collective-permute-start.10 = (bf16[64,6144]{1,0:T(8,128)(2,1)S(1)}, bf16[64,6144]{1,0:T(8,128)(2,1)S(1)}, u32[]{:S(2)}, u32[]{:S(2)}) collective-permute-start(bf16[64,6144]{1,0:T(8,128)(2,1)S(1)} %pad_maximum_fusion), channel_id=1, source_target_pairs={{128,0},{129,1},{130,2},{131,3},{132,4},{133,5},{134,6},{135,7},{1... | collective-permute-start | bytes 2359304 | tf_op jit(solution)/shard_map/ppermute | solution.py:18
  61.3 13.5 %collective-permute-start.11 = (bf16[64,6144]{1,0:T(8,128)(2,1)S(1)}, bf16[64,6144]{1,0:T(8,128)(2,1)S(1)}, u32[]{:S(2)}, u32[]{:S(2)}) collective-permute-start(bf16[64,6144]{1,0:T(8,128)(2,1)S(1)} %pad_maximum_fusion.1), channel_id=1, source_target_pairs={{4,0},{5,1},{6,2},{7,3},{0,4},{1,5},{2,6},{3,7},{12,8},{13,9},{14,... | collective-permute-start | bytes 2359304 | tf_op jit(solution)/shard_map/ppermute | solution.py:18
  75.8 9.0 %copy-start = (bf16[512,6144]{1,0:T(8,128)(2,1)S(1)}, bf16[512,6144]{1,0:T(8,128)(2,1)}, u32[]{:S(2)}) copy-start(bf16[512,6144]{1,0:T(8,128)(2,1)} %constant_dynamic-update-slice_fusion.2) | copy-start | bytes 18874372
  85.5 4.2 %collective-permute-start.12 = (f32[256,2048]{1,0:T(8,128)S(1)}, f32[256,2048]{1,0:T(8,128)S(1)}, u32[]{:S(2)}, u32[]{:S(2)}) collective-permute-start(f32[256,2048]{1,0:T(8,128)S(1)} %fusion), channel_id=1, source_target_pairs={{1,0},{0,1},{3,2},{2,3},{5,4},{4,5},{7,6},{6,7},{9,8},{8,9},{11,10... | collective-permute-start | bytes 6291464 | tf_op jit(solution)/shard_map/ppermute | solution.py:18
Sparse Core Ops, SparseCore 0:
  11.1 48.9 all-gather.1
  92.0 50.7 reduce-scatter.1

commit v2 on v1

v2 whole, which is shorter than its diff:
```python
import jax
import jax.numpy as jnp
from jax import lax
from jax.experimental import pallas as pl
from jax.experimental.pallas import tpu as pltpu
from jax.sharding import Mesh, PartitionSpec as P

AXES = ("y", "zl", "zh", "x", "core")
SIZES = (4, 4, 2, 4, 2)
STRIDES = (64, 16, 8, 2, 1)
NEAR = (1, 3, 2)
DEPTH = 1024


def shift(value, **steps):
    pairs = []
    for target in range(256):
        source = 0
        for axis, size, stride in zip(AXES, SIZES, STRIDES):
            source += (target // stride + steps.get(axis, 0)) % size * stride
        pairs.append((source, target))
    return lax.ppermute(value, AXES, pairs)


def join_kernel(student_ref, teacher_ref, both_ref, upper_ref, lower_ref):
    width = student_ref.shape[1]
    half = upper_ref.shape[0]
    for source, place in ((student_ref, slice(0, width)), (teacher_ref, slice(width, None))):
        both_ref[:, place] = source[...]
        upper_ref[:, place] = source[:half]
        lower_ref[:, place] = source[half:]


def join(student, teacher):
    texts, total = student.shape[0], student.shape[1] + teacher.shape[1]
    whole = jax.ShapeDtypeStruct((texts, total), student.dtype)
    part = jax.ShapeDtypeStruct((texts // 2, total), student.dtype)
    return pl.pallas_call(join_kernel, out_shape=(whole, part, part))(student, teacher)


def excess_kernel(student_steps, *refs):
    *pieces, rows_ref, rounded_ref, squares_ref, total = refs
    step = pl.program_id(0)
    cols = jnp.concatenate([piece[...] for piece in pieces])
    product = lax.dot_general(
        cols, rows_ref[...], (((1,), (1,)), ((), ())), preferred_element_type=jnp.float32
    )

    @pl.when(step == 0)
    def _():
        total[...] = product

    @pl.when((step > 0) & (step < student_steps))
    def _():
        total[...] += product

    @pl.when(step >= student_steps)
    def _():
        total[...] -= product

    @pl.when(step == pl.num_programs(0) - 1)
    def _():
        excess = total[...]
        rounded_ref[...] = excess.astype(rounded_ref.dtype)
        squares = jnp.sum(jnp.sum(excess * excess, axis=0, keepdims=True), axis=1, keepdims=True)
        squares_ref[...] = jnp.broadcast_to(squares, squares_ref.shape)


def excess_of(pieces, rows, student_width):
    texts, width = rows.shape
    count = sum(piece.shape[0] for piece in pieces)
    block = lambda height: pl.BlockSpec((height, DEPTH), lambda k: (0, k))
    fixed = lambda *shape: pl.BlockSpec(shape, lambda k: (0,) * len(shape))
    return pl.pallas_call(
        lambda *refs: excess_kernel(student_width // DEPTH, *refs),
        grid=(width // DEPTH,),
        in_specs=[block(piece.shape[0]) for piece in pieces] + [block(texts)],
        out_specs=(fixed(count, texts), fixed(8, 128)),
        out_shape=(
            jax.ShapeDtypeStruct((count, texts), jnp.bfloat16),
            jax.ShapeDtypeStruct((8, 128), jnp.float32),
        ),
        scratch_shapes=[pltpu.VMEM((count, texts), jnp.float32)],
        compiler_params=pltpu.CompilerParams(vmem_limit_bytes=32 * 1024 * 1024),
        cost_estimate=pl.CostEstimate(
            flops=2 * count * texts * width,
            bytes_accessed=2 * (count + texts) * width,
            transcendentals=0,
        ),
    )(*pieces, rows)


def shards(student, teacher):
    texts, width = student.shape
    half = texts // 2
    both, upper, lower = join(student, teacher)
    rows = lax.all_gather(both, ("zh", "zl", "core"), axis=0, tiled=True)
    upper = jnp.concatenate([upper] + [shift(upper, x=k) for k in NEAR])
    lower = jnp.concatenate([lower] + [shift(lower, y=k) for k in NEAR])
    pieces = []
    for k in NEAR:
        pieces += [shift(upper, y=k), shift(lower, x=k)]
    pieces += [upper, lower]
    rounded, squares = excess_of(pieces, rows, width)
    rows_s = rows[:, :width]
    bundle = 4 * half
    pull = lambda start, count: jnp.dot(
        rounded[start * bundle : (start + count) * bundle],
        rows_s,
        preferred_element_type=jnp.float32,
    ).reshape(count, 4, half, width)
    sent = pull(0, 6)
    own = pull(6, 2)
    upper_sum, lower_sum = own[0], own[1]
    for i, k in enumerate(NEAR):
        back = shift(sent[2 * i], y=-k)
        if i == 0:
            back, squares = lax.optimization_barrier((back, squares))
        upper_sum += back
        lower_sum += shift(sent[2 * i + 1], x=-k)
    upper_grad, lower_grad = upper_sum[0], lower_sum[0]
    for i, k in enumerate(NEAR):
        upper_grad += shift(upper_sum[i + 1], x=-k)
        lower_grad += shift(lower_sum[i + 1], y=-k)
    pulled = jnp.concatenate([upper_grad, lower_grad])

    line = lax.all_to_all(
        jnp.broadcast_to(squares[None], (16, 8, 128)), ("zh", "zl", "core"), 0, 0
    )
    total = jnp.sum(line, axis=0)
    for axis in ("x", "y"):
        near = [shift(total, **{axis: k}) for k in (1, 2, 3)]
        total = (total + near[1]) + (near[0] + near[2])
    distance = total[0, 0] / jnp.float32(texts * 256)
    return distance, pulled


def solution(mesh):
    fine = Mesh(mesh.devices.reshape(SIZES), AXES)
    spec = P(AXES, None)
    return jax.shard_map(
        shards, mesh=fine, in_specs=(spec, spec), out_specs=(P(), spec), check_vma=False
    )
```

time: 152 us -> 161 us (1.059)
  blocking collectives: 36.5 us -> 0 us
  starting transfers between devices: 17.9 us -> 53 us
  waiting for transfers between devices: 50.9 us -> 63 us
  matrix products: 11.7 us -> 1.42 us
  Pallas kernels: 0 us -> 8.19 us
  local copies, waits for them, and re-layouts: 13.7 us -> 15.5 us
    all_to_all x2 -> x0, blocking collectives: 36.5 us -> none  [the longest x1 19.7 us: shards(): lax.all_to_all(jnp.broadcast_to(squares, (32, 8, 128)), ('y', 'x', 'core'...]
    ppermute x13 -> x30, starting transfers between devices: 17.8 us -> 44.2 us  [shift(): return lax.ppermute(value, AXES, pairs)]
    ppermute x13 -> x30, waiting for transfers between devices: 39.7 us -> 60.5 us  [shift(): return lax.ppermute(value, AXES, pairs)]
    reduce_scatter x1 -> x0, waiting for transfers between devices: 11.2 us -> none  [shards(): lax.psum_scatter(partial_term, ('zh', 'zl'), scatter_dimension=0, tiled=T...]
    dot_general x3 -> x2, matrix products: 11.7 us -> 1.42 us  [shards(): jnp.dot(rounded[start * bundle:(start + count) * bundle], rows_s, preferr...]
    all_to_all x0 -> x1, starting transfers between devices: none -> 8.79 us  [shards(): lax.all_to_all(jnp.broadcast_to(squares[None], (16, 8, 128)), ('zh', 'zl'...]
    pallas_call x0 -> x2, Pallas kernels: none -> 8.19 us  [the longest x1 6.26 us: excess_of(): pl.pallas_call(lambda *refs: excess_kernel(student_width // DEPTH, *refs)...]
    add x0 -> x6, other arithmetic: none -> 2.83 us  [the longest x1 1.46 us: shards(): lower_sum += shift(sent[2 * i + 1], x=-k)]
  transfers between devices with their start and end apart: 15 -> 32, of which waited for: 8 -> 12; matrix products, arithmetic and copies ran while one was open for 9% -> 4% of each run, Pallas kernels for 0% -> 0%
where the time goes in v2:
time: 161 us
  waiting for transfers between devices  63 us (39%)
  starting transfers between devices  53 us (33%)
  between operations  16 us (10%)
  local copies, waits for them, and re-layouts  15.5 us (10%)
  Pallas kernels  8.19 us (5%)
  other arithmetic  3.57 us (2%)
    ppermute x30, waiting for transfers between devices, shift(): return lax.ppermute(value, AXES, pairs)  60.5 us
    ppermute x30, starting transfers between devices, shift(): return lax.ppermute(value, AXES, pairs)  44.2 us
    unnamed x26, local copies, waits for them, and re-layouts  13 us
    all_to_all x1, starting transfers between devices, shards(): lax.all_to_all(jnp.broadcast_to(squares[None], (16, 8, 128)), ('zh', 'zl'...  8.79 us
    pallas_call x1, Pallas kernels, excess_of(): pl.pallas_call(lambda *refs: excess_kernel(student_width // DEPTH, *refs)...  6.26 us
  transfers between devices with their start and end apart: 32, of which 12 were waited for; matrix products, arithmetic and copies ran while one was open for 4% of the time, Pallas kernels for 0%

profile of v2, /device:TPU:2, one launch (start us, length us, event | category | flops | bytes accessed | tf_op | source)
XLA Modules:
  0.0 160.7 jit_solution(18401508478311430001)
XLA Ops:
  7.2 1.9 %shard_map.41 = (bf16[32,6144]{1,0:T(8,128)(2,1)}, bf16[16,6144]{1,0:T(8,128)(2,1)}, bf16[16,6144]{1,0:T(8,128)(2,1)}) custom-call(bf16[32,2048]{1,0:T(8,128)(2,1)} %student_ref.1, bf16[32,4096]{1,0:T(8,128)(2,1)} %teacher_ref.1), custom_call_target="tpu_custom_call" | custom-call | tf_op jit(solution)/shard_map/pallas_call | solution.py:38
  9.2 2.2 %collective-permute-start.2 = (bf16[16,6144]{1,0:T(8,128)(2,1)}, bf16[16,6144]{1,0:T(8,128)(2,1)S(1)}, u32[]{:S(2)}, u32[]{:S(2)}) collective-permute-start(bf16[16,6144]{1,0:T(8,128)(2,1)} %get-tuple-element.9), channel_id=1, source_target_pairs={{4,0},{5,1},{6,2},{7,3},{0,4},{1,5},{2,6},{3,7},{12,8},{13,9},{14,... | collective-permute-start | bytes 589832 | tf_op jit(solution)/shard_map/ppermute | solution.py:22
  11.4 1.6 %collective-permute-start.1 = (bf16[16,6144]{1,0:T(8,128)(2,1)}, bf16[16,6144]{1,0:T(8,128)(2,1)S(1)}, u32[]{:S(2)}, u32[]{:S(2)}) collective-permute-start(bf16[16,6144]{1,0:T(8,128)(2,1)} %get-tuple-element.9), channel_id=1, source_target_pairs={{6,0},{7,1},{0,2},{1,3},{2,4},{3,5},{4,6},{5,7},{14,8},{15,9},{8,1... | collective-permute-start | bytes 589832 | tf_op jit(solution)/shard_map/ppermute | solution.py:22
  13.4 3.2 %collective-permute-start.6 = (bf16[16,6144]{1,0:T(8,128)(2,1)}, bf16[16,6144]{1,0:T(8,128)(2,1)S(1)}, u32[]{:S(2)}, u32[]{:S(2)}) collective-permute-start(bf16[16,6144]{1,0:T(8,128)(2,1)} %get-tuple-element.10), channel_id=1, source_target_pairs={{128,0},{129,1},{130,2},{131,3},{132,4},{133,5},{134,6},{135,7},{1... | collective-permute-start | bytes 589832 | tf_op jit(solution)/shard_map/ppermute | solution.py:22
  16.6 1.1 collective-permute-start.4
  17.7 0.9 constant_dynamic-update-slice_fusion.3
  18.6 0.9 constant_dynamic-update-slice_fusion.7
  19.5 5.9 %collective-permute-done.4 = bf16[16,6144]{1,0:T(8,128)(2,1)S(1)} collective-permute-done((bf16[16,6144]{1,0:T(8,128)(2,1)}, bf16[16,6144]{1,0:T(8,128)(2,1)S(1)}, u32[]{:S(2)}, u32[]{:S(2)}) %collective-permute-start.4) | collective-permute-done | bytes 196640 | tf_op jit(solution)/shard_map/ppermute | solution.py:22
  25.5 1.2 collective-permute-start.5
  26.7 6.4 %collective-permute-done.5 = bf16[16,6144]{1,0:T(8,128)(2,1)S(1)} collective-permute-done((bf16[16,6144]{1,0:T(8,128)(2,1)}, bf16[16,6144]{1,0:T(8,128)(2,1)S(1)}, u32[]{:S(2)}, u32[]{:S(2)}) %collective-permute-start.5) | collective-permute-done | bytes 196640 | tf_op jit(solution)/shard_map/ppermute | solution.py:22
  33.1 2.2 %collective-permute-start.11 = (bf16[64,6144]{1,0:T(8,128)(2,1)S(1)}, bf16[64,6144]{1,0:T(8,128)(2,1)S(1)}, u32[]{:S(2)}, u32[]{:S(2)}) collective-permute-start(bf16[64,6144]{1,0:T(8,128)(2,1)S(1)} %constant_dynamic-update-slice_fusion.4.refs_7_), channel_id=1, source_target_pairs={{4,0},{5,1},{6,2},{7,3},{0,4},{1,5},{2,6},{3,7},{12,8},{13,9},{14,... | collective-permute-start | bytes 2359304 | tf_op jit(solution)/shard_map/ppermute | solution.py:22
  35.3 2.0 %collective-permute-start.9 = (bf16[64,6144]{1,0:T(8,128)(2,1)S(1)}, bf16[64,6144]{1,0:T(8,128)(2,1)S(1)}, u32[]{:S(2)}, u32[]{:S(2)}) collective-permute-start(bf16[64,6144]{1,0:T(8,128)(2,1)S(1)} %constant_dynamic-update-slice_fusion.4.refs_7_), channel_id=1, source_target_pairs={{6,0},{7,1},{0,2},{1,3},{2,4},{3,5},{4,6},{5,7},{14,8},{15,9},{8,1... | collective-permute-start | bytes 2359304 | tf_op jit(solution)/shard_map/ppermute | solution.py:22
  37.4 0.9 collective-permute-start.10
  38.4 1.7 %collective-permute-start.8 = (bf16[64,6144]{1,0:T(8,128)(2,1)S(1)}, bf16[64,6144]{1,0:T(8,128)(2,1)S(1)}, u32[]{:S(2)}, u32[]{:S(2)}) collective-permute-start(bf16[64,6144]{1,0:T(8,128)(2,1)S(1)} %constant_dynamic-update-slice_fusion.refs_6_), channel_id=1, source_target_pairs={{192,0},{193,1},{194,2},{195,3},{196,4},{197,5},{198,6},{199,7},{2... | collective-permute-start | bytes 2359304 | tf_op jit(solution)/shard_map/ppermute | solution.py:22
  40.1 15.1 %collective-permute-done.11.refs_5_ = bf16[64,6144]{1,0:T(8,128)(2,1)S(1)} collective-permute-done((bf16[64,6144]{1,0:T(8,128)(2,1)S(1)}, bf16[64,6144]{1,0:T(8,128)(2,1)S(1)}, u32[]{:S(2)}, u32[]{:S(2)}) %collective-permute-start.11) | collective-permute-done | bytes 786464 | tf_op jit(solution)/shard_map/ppermute | solution.py:22
  55.3 1.7 %collective-permute-start.3 = (bf16[64,6144]{1,0:T(8,128)(2,1)S(1)}, bf16[64,6144]{1,0:T(8,128)(2,1)S(1)}, u32[]{:S(2)}, u32[]{:S(2)}) collective-permute-start(bf16[64,6144]{1,0:T(8,128)(2,1)S(1)} %constant_dynamic-update-slice_fusion.refs_6_), channel_id=1, source_target_pairs={{64,0},{65,1},{66,2},{67,3},{68,4},{69,5},{70,6},{71,7},{72,8},{73... | collective-permute-start | bytes 2359304 | tf_op jit(solution)/shard_map/ppermute | solution.py:22
  57.0 12.1 %collective-permute-done.9.refs_3_ = bf16[64,6144]{1,0:T(8,128)(2,1)S(1)} collective-permute-done((bf16[64,6144]{1,0:T(8,128)(2,1)S(1)}, bf16[64,6144]{1,0:T(8,128)(2,1)S(1)}, u32[]{:S(2)}, u32[]{:S(2)}) %collective-permute-start.9) | collective-permute-done | bytes 786464 | tf_op jit(solution)/shard_map/ppermute | solution.py:22
  69.6 1.0 copy-done.1
  70.6 0.9 copy-done.3
  71.5 1.9 %collective-permute-done.8.refs_2_ = bf16[64,6144]{1,0:T(8,128)(2,1)S(1)} collective-permute-done((bf16[64,6144]{1,0:T(8,128)(2,1)S(1)}, bf16[64,6144]{1,0:T(8,128)(2,1)S(1)}, u32[]{:S(2)}, u32[]{:S(2)}) %collective-permute-start.8) | collective-permute-done | bytes 786464 | tf_op jit(solution)/shard_map/ppermute | solution.py:22
  73.4 1.0 copy-done.5
  75.3 2.8 %copy-done = bf16[512,6144]{1,0:T(8,128)(2,1)S(1)} copy-done((bf16[512,6144]{1,0:T(8,128)(2,1)S(1)}, bf16[512,6144]{1,0:T(8,128)(2,1)}, u32[]{:S(2)}) %copy-start) | copy-done | bytes 6291480
  78.0 1.1 copy-done.2
  79.2 1.1 copy-done.4
  80.3 1.1 copy-done.6
  81.4 1.1 copy-done.8
  82.6 6.3 %shard_map.42 = (bf16[512,512]{1,0:T(8,128)(2,1)S(1)}, f32[8,128]{1,0:T(8,128)S(1)}) custom-call(bf16[64,6144]{1,0:T(8,128)(2,1)S(1)} %copy-done.8, bf16[64,6144]{1,0:T(8,128)(2,1)S(1)} %copy-done.2, bf16[64,6144]{1,0:T(8,128)(2,1)S(1)} %copy-done.6, bf16[64,6144]{1,0:T(8,128)(2,1)S(1)} %collective-permute-done.9.refs_3_, bf16[64,6144]{1,0:T(8,128)(2,1)S(1)} %copy-done.4, ...), custom_call_target="tpu_custom_call" | custom-call | flops 3221225472 | bytes 12582912 | tf_op jit(solution)/shard_map/pallas_call | solution.py:74
  88.8 1.0 fusion.2
  89.8 1.2 fusion.12
  91.0 1.4 collective-permute-start.26
  92.4 1.5 collective-permute-start.19
  94.0 2.3 %collective-permute-start.25 = (f32[4,16,2048]{2,1,0:T(8,128)}, f32[4,16,2048]{2,1,0:T(8,128)}, u32[]{:S(2)}, u32[]{:S(2)}) collective-permute-start(f32[4,16,2048]{2,1,0:T(8,128)} %bitcast.11), channel_id=1, source_target_pairs={{2,0},{3,1},{4,2},{5,3},{6,4},{7,5},{0,6},{1,7},{10,8},{11,9},{12,... | collective-permute-start | bytes 1572872 | tf_op jit(solution)/shard_map/ppermute | solution.py:22
  97.3 12.2 %collective-permute-done.12 = f32[4,16,2048]{2,1,0:T(8,128)S(1)} collective-permute-done((f32[4,16,2048]{2,1,0:T(8,128)S(1)}, f32[4,16,2048]{2,1,0:T(8,128)S(1)}, u32[]{:S(2)}, u32[]{:S(2)}) %collective-permute-start.12) | collective-permute-done | bytes 524320 | tf_op jit(solution)/shard_map/ppermute | solution.py:22
  110.8 8.8 %all-to-all-start = ((f32[16,8,128]{2,1,0:T(8,128)}), f32[16,8,128]{2,1,0:T(8,128)S(1)}, u32[]{:S(2)}, u32[]{:S(2)}) async-start(f32[16,8,128]{2,1,0:T(8,128)} %broadcast_in_dim.2), calls=%async_computation | async-start | bytes 131072 | tf_op jit(solution)/shard_map/all_to_all | solution.py:127
  119.6 1.5 add_add_fusion
  121.3 3.7 %collective-permute-start.29 = (f32[16,2048]{1,0:T(8,128)S(1)}, f32[16,2048]{1,0:T(8,128)S(1)}, u32[]{:S(2)}, u32[]{:S(2)}) collective-permute-start(f32[16,2048]{1,0:T(8,128)S(1)} %get-tuple-element.28), channel_id=1, source_target_pairs={{128,0},{129,1},{130,2},{131,3},{132,4},{133,5},{134,6},{135,7},{1... | collective-permute-start | bytes 393224 | tf_op jit(solution)/shard_map/ppermute | solution.py:22
  125.0 2.4 %all-to-all-done = f32[16,8,128]{2,1,0:T(8,128)S(1)} async-done(((f32[16,8,128]{2,1,0:T(8,128)}), f32[16,8,128]{2,1,0:T(8,128)S(1)}, u32[]{:S(2)}, u32[]{:S(2)}) %all-to-all-start) | async-done | bytes 65568 | tf_op jit(solution)/shard_map/all_to_all | solution.py:127
  127.4 1.3 collective-permute-start.15
  129.5 2.8 %collective-permute-start.13 = (f32[8,128]{1,0:T(8,128)S(1)}, f32[8,128]{1,0:T(8,128)S(1)}, u32[]{:S(2)}, u32[]{:S(2)}) collective-permute-start(f32[8,128]{1,0:T(8,128)S(1)} %reduce_sum.9), channel_id=1, source_target_pairs={{4,0},{5,1},{6,2},{7,3},{0,4},{1,5},{2,6},{3,7},{12,8},{13,9},{14,... | collective-permute-start | bytes 12296 | tf_op jit(solution)/shard_map/ppermute | solution.py:22
  132.3 1.3 add_add_fusion.1
  133.6 1.0 collective-permute-done.13
  134.8 3.1 %collective-permute-start.17 = (f32[8,128]{1,0:T(8,128)S(1)}, f32[8,128]{1,0:T(8,128)S(1)}, u32[]{:S(2)}, u32[]{:S(2)}) collective-permute-start(f32[8,128]{1,0:T(8,128)S(1)} %add_add_fusion.3), channel_id=1, source_target_pairs={{64,0},{65,1},{66,2},{67,3},{68,4},{69,5},{70,6},{71,7},{72,8},{73... | collective-permute-start | bytes 12296 | tf_op jit(solution)/shard_map/ppermute | solution.py:22
  137.9 1.8 %collective-permute-start.16 = (f32[8,128]{1,0:T(8,128)S(1)}, f32[8,128]{1,0:T(8,128)S(1)}, u32[]{:S(2)}, u32[]{:S(2)}) collective-permute-start(f32[8,128]{1,0:T(8,128)S(1)} %add_add_fusion.3), channel_id=1, source_target_pairs={{128,0},{129,1},{130,2},{131,3},{132,4},{133,5},{134,6},{135,7},{1... | collective-permute-start | bytes 12296 | tf_op jit(solution)/shard_map/ppermute | solution.py:22
  140.6 1.4 collective-permute-start.21
  142.0 1.0 collective-permute-done.16
  143.0 2.8 %collective-permute-start.23 = (f32[16,2048]{1,0:T(8,128)S(1)}, f32[16,2048]{1,0:T(8,128)S(1)}, u32[]{:S(2)}, u32[]{:S(2)}) collective-permute-start(f32[16,2048]{1,0:T(8,128)S(1)} %get-tuple-element.25), channel_id=1, source_target_pairs={{4,0},{5,1},{6,2},{7,3},{0,4},{1,5},{2,6},{3,7},{12,8},{13,9},{14,... | collective-permute-start | bytes 393224 | tf_op jit(solution)/shard_map/ppermute | solution.py:22
  147.8 2.4 %collective-permute-done.23 = f32[16,2048]{1,0:T(8,128)S(1)} collective-permute-done((f32[16,2048]{1,0:T(8,128)S(1)}, f32[16,2048]{1,0:T(8,128)S(1)}, u32[]{:S(2)}, u32[]{:S(2)}) %collective-permute-start.23) | collective-permute-done | bytes 131104 | tf_op jit(solution)/shard_map/ppermute | solution.py:22
  150.2 1.8 %collective-permute-done.22 = f32[16,2048]{1,0:T(8,128)S(1)} collective-permute-done((f32[16,2048]{1,0:T(8,128)S(1)}, f32[16,2048]{1,0:T(8,128)S(1)}, u32[]{:S(2)}, u32[]{:S(2)}) %collective-permute-start.22) | collective-permute-done | bytes 131104 | tf_op jit(solution)/shard_map/ppermute | solution.py:22
  (63 shorter events, 8.3 us)
Async XLA Ops:
  7.2 68.1 %all-gather.2.cloned.1.call-start = ((), (), s32[]{:S(2)}) async-start(), calls=%async_computation.1 | async-start | bytes 6684672 | tf_op jit(solution)/shard_map/all_gather | solution.py:97
  9.2 28.2 %collective-permute-start.2 = (bf16[16,6144]{1,0:T(8,128)(2,1)}, bf16[16,6144]{1,0:T(8,128)(2,1)S(1)}, u32[]{:S(2)}, u32[]{:S(2)}) collective-permute-start(bf16[16,6144]{1,0:T(8,128)(2,1)} %get-tuple-element.9), channel_id=1, source_target_pairs={{4,0},{5,1},{6,2},{7,3},{0,4},{1,5},{2,6},{3,7},{12,8},{13,9},{14,... | collective-permute-start | bytes 589832 | tf_op jit(solution)/shard_map/ppermute | solution.py:22
  11.4 26.0 %collective-permute-start.1 = (bf16[16,6144]{1,0:T(8,128)(2,1)}, bf16[16,6144]{1,0:T(8,128)(2,1)S(1)}, u32[]{:S(2)}, u32[]{:S(2)}) collective-permute-start(bf16[16,6144]{1,0:T(8,128)(2,1)} %get-tuple-element.9), channel_id=1, source_target_pairs={{6,0},{7,1},{0,2},{1,3},{2,4},{3,5},{4,6},{5,7},{14,8},{15,9},{8,1... | collective-permute-start | bytes 589832 | tf_op jit(solution)/shard_map/ppermute | solution.py:22
  13.0 24.4 %collective-permute-start = (bf16[16,6144]{1,0:T(8,128)(2,1)}, bf16[16,6144]{1,0:T(8,128)(2,1)S(1)}, u32[]{:S(2)}, u32[]{:S(2)}) collective-permute-start(bf16[16,6144]{1,0:T(8,128)(2,1)} %get-tuple-element.9), channel_id=1, source_target_pairs={{2,0},{3,1},{4,2},{5,3},{6,4},{7,5},{0,6},{1,7},{10,8},{11,9},{12,... | collective-permute-start | bytes 589832 | tf_op jit(solution)/shard_map/ppermute | solution.py:22
  13.4 19.7 %collective-permute-start.6 = (bf16[16,6144]{1,0:T(8,128)(2,1)}, bf16[16,6144]{1,0:T(8,128)(2,1)S(1)}, u32[]{:S(2)}, u32[]{:S(2)}) collective-permute-start(bf16[16,6144]{1,0:T(8,128)(2,1)} %get-tuple-element.10), channel_id=1, source_target_pairs={{128,0},{129,1},{130,2},{131,3},{132,4},{133,5},{134,6},{135,7},{1... | collective-permute-start | bytes 589832 | tf_op jit(solution)/shard_map/ppermute | solution.py:22
  16.6 8.9 %collective-permute-start.4 = (bf16[16,6144]{1,0:T(8,128)(2,1)}, bf16[16,6144]{1,0:T(8,128)(2,1)S(1)}, u32[]{:S(2)}, u32[]{:S(2)}) collective-permute-start(bf16[16,6144]{1,0:T(8,128)(2,1)} %get-tuple-element.10), channel_id=1, source_target_pairs={{64,0},{65,1},{66,2},{67,3},{68,4},{69,5},{70,6},{71,7},{72,8},{73... | collective-permute-start | bytes 589832 | tf_op jit(solution)/shard_map/ppermute | solution.py:22
  25.5 7.6 %collective-permute-start.5 = (bf16[16,6144]{1,0:T(8,128)(2,1)}, bf16[16,6144]{1,0:T(8,128)(2,1)S(1)}, u32[]{:S(2)}, u32[]{:S(2)}) collective-permute-start(bf16[16,6144]{1,0:T(8,128)(2,1)} %get-tuple-element.10), channel_id=1, source_target_pairs={{192,0},{193,1},{194,2},{195,3},{196,4},{197,5},{198,6},{199,7},{2... | collective-permute-start | bytes 589832 | tf_op jit(solution)/shard_map/ppermute | solution.py:22
  33.1 22.1 %collective-permute-start.11 = (bf16[64,6144]{1,0:T(8,128)(2,1)S(1)}, bf16[64,6144]{1,0:T(8,128)(2,1)S(1)}, u32[]{:S(2)}, u32[]{:S(2)}) collective-permute-start(bf16[64,6144]{1,0:T(8,128)(2,1)S(1)} %constant_dynamic-update-slice_fusion.4.refs_7_), channel_id=1, source_target_pairs={{4,0},{5,1},{6,2},{7,3},{0,4},{1,5},{2,6},{3,7},{12,8},{13,9},{14,... | collective-permute-start | bytes 2359304 | tf_op jit(solution)/shard_map/ppermute | solution.py:22
  35.3 33.8 %collective-permute-start.9 = (bf16[64,6144]{1,0:T(8,128)(2,1)S(1)}, bf16[64,6144]{1,0:T(8,128)(2,1)S(1)}, u32[]{:S(2)}, u32[]{:S(2)}) collective-permute-start(bf16[64,6144]{1,0:T(8,128)(2,1)S(1)} %constant_dynamic-update-slice_fusion.4.refs_7_), channel_id=1, source_target_pairs={{6,0},{7,1},{0,2},{1,3},{2,4},{3,5},{4,6},{5,7},{14,8},{15,9},{8,1... | collective-permute-start | bytes 2359304 | tf_op jit(solution)/shard_map/ppermute | solution.py:22
  37.3 32.3 %collective-permute-start.7 = (bf16[64,6144]{1,0:T(8,128)(2,1)S(1)}, bf16[64,6144]{1,0:T(8,128)(2,1)S(1)}, u32[]{:S(2)}, u32[]{:S(2)}) collective-permute-start(bf16[64,6144]{1,0:T(8,128)(2,1)S(1)} %constant_dynamic-update-slice_fusion.4.refs_7_), channel_id=1, source_target_pairs={{2,0},{3,1},{4,2},{5,3},{6,4},{7,5},{0,6},{1,7},{10,8},{11,9},{12,... | collective-permute-start | bytes 2359304 | tf_op jit(solution)/shard_map/ppermute | solution.py:22
  37.4 33.1 %collective-permute-start.10 = (bf16[64,6144]{1,0:T(8,128)(2,1)S(1)}, bf16[64,6144]{1,0:T(8,128)(2,1)S(1)}, u32[]{:S(2)}, u32[]{:S(2)}) collective-permute-start(bf16[64,6144]{1,0:T(8,128)(2,1)S(1)} %constant_dynamic-update-slice_fusion.refs_6_), channel_id=1, source_target_pairs={{128,0},{129,1},{130,2},{131,3},{132,4},{133,5},{134,6},{135,7},{1... | collective-permute-start | bytes 2359304 | tf_op jit(solution)/shard_map/ppermute | solution.py:22
  38.4 35.0 %collective-permute-start.8 = (bf16[64,6144]{1,0:T(8,128)(2,1)S(1)}, bf16[64,6144]{1,0:T(8,128)(2,1)S(1)}, u32[]{:S(2)}, u32[]{:S(2)}) collective-permute-start(bf16[64,6144]{1,0:T(8,128)(2,1)S(1)} %constant_dynamic-update-slice_fusion.refs_6_), channel_id=1, source_target_pairs={{192,0},{193,1},{194,2},{195,3},{196,4},{197,5},{198,6},{199,7},{2... | collective-permute-start | bytes 2359304 | tf_op jit(solution)/shard_map/ppermute | solution.py:22
  55.3 19.1 %collective-permute-start.3 = (bf16[64,6144]{1,0:T(8,128)(2,1)S(1)}, bf16[64,6144]{1,0:T(8,128)(2,1)S(1)}, u32[]{:S(2)}, u32[]{:S(2)}) collective-permute-start(bf16[64,6144]{1,0:T(8,128)(2,1)S(1)} %constant_dynamic-update-slice_fusion.refs_6_), channel_id=1, source_target_pairs={{64,0},{65,1},{66,2},{67,3},{68,4},{69,5},{70,6},{71,7},{72,8},{73... | collective-permute-start | bytes 2359304 | tf_op jit(solution)/shard_map/ppermute | solution.py:22
  69.6 1.0 copy-start.1
  70.6 0.9 copy-start.3
  73.4 1.0 copy-start.5
  74.4 0.9 copy-start.7
  75.3 2.8 %copy-start = (bf16[512,6144]{1,0:T(8,128)(2,1)S(1)}, bf16[512,6144]{1,0:T(8,128)(2,1)}, u32[]{:S(2)}) copy-start(bf16[512,6144]{1,0:T(8,128)(2,1)} %all-gather.2.cloned.1.call-done.refs_8_) | copy-start | bytes 18874372
  78.0 1.1 copy-start.2
  79.2 1.1 copy-start.4
  80.3 1.1 copy-start.6
  81.4 1.1 copy-start.8
  91.0 28.5 %collective-permute-start.26 = (f32[4,16,2048]{2,1,0:T(8,128)}, f32[4,16,2048]{2,1,0:T(8,128)}, u32[]{:S(2)}, u32[]{:S(2)}) collective-permute-start(f32[4,16,2048]{2,1,0:T(8,128)} %bitcast.12), channel_id=1, source_target_pairs={{4,0},{5,1},{6,2},{7,3},{0,4},{1,5},{2,6},{3,7},{12,8},{13,9},{14,... | collective-permute-start | bytes 1572872 | tf_op jit(solution)/shard_map/ppermute | solution.py:22
  92.4 36.4 %collective-permute-start.19 = (f32[4,16,2048]{2,1,0:T(8,128)S(1)}, f32[4,16,2048]{2,1,0:T(8,128)S(1)}, u32[]{:S(2)}, u32[]{:S(2)}) collective-permute-start(f32[4,16,2048]{2,1,0:T(8,128)S(1)} %bitcast.40), channel_id=1, source_target_pairs={{64,0},{65,1},{66,2},{67,3},{68,4},{69,5},{70,6},{71,7},{72,8},{73... | collective-permute-start | bytes 1572872 | tf_op jit(solution)/shard_map/ppermute | solution.py:22
  94.0 25.6 %collective-permute-start.25 = (f32[4,16,2048]{2,1,0:T(8,128)}, f32[4,16,2048]{2,1,0:T(8,128)}, u32[]{:S(2)}, u32[]{:S(2)}) collective-permute-start(f32[4,16,2048]{2,1,0:T(8,128)} %bitcast.11), channel_id=1, source_target_pairs={{2,0},{3,1},{4,2},{5,3},{6,4},{7,5},{0,6},{1,7},{10,8},{11,9},{12,... | collective-permute-start | bytes 1572872 | tf_op jit(solution)/shard_map/ppermute | solution.py:22
  96.3 23.3 %collective-permute-start.24 = (f32[4,16,2048]{2,1,0:T(8,128)}, f32[4,16,2048]{2,1,0:T(8,128)}, u32[]{:S(2)}, u32[]{:S(2)}) collective-permute-start(f32[4,16,2048]{2,1,0:T(8,128)} %bitcast.10), channel_id=1, source_target_pairs={{6,0},{7,1},{0,2},{1,3},{2,4},{3,5},{4,6},{5,7},{14,8},{15,9},{8,1... | collective-permute-start | bytes 1572872 | tf_op jit(solution)/shard_map/ppermute | solution.py:22
  96.3 13.3 %collective-permute-start.12 = (f32[4,16,2048]{2,1,0:T(8,128)S(1)}, f32[4,16,2048]{2,1,0:T(8,128)S(1)}, u32[]{:S(2)}, u32[]{:S(2)}) collective-permute-start(f32[4,16,2048]{2,1,0:T(8,128)S(1)} %bitcast.41), channel_id=1, source_target_pairs={{192,0},{193,1},{194,2},{195,3},{196,4},{197,5},{198,6},{199,7},{2... | collective-permute-start | bytes 1572872 | tf_op jit(solution)/shard_map/ppermute | solution.py:22
  109.6 10.0 %copy-start.9 = (f32[4,16,2048]{2,1,0:T(8,128)}, f32[4,16,2048]{2,1,0:T(8,128)S(1)}, u32[]{:S(2)}) copy-start(f32[4,16,2048]{2,1,0:T(8,128)S(1)} %collective-permute-done.12) | copy-start | bytes 1572868
  109.6 20.0 %collective-permute-start.20 = (f32[4,16,2048]{2,1,0:T(8,128)S(1)}, f32[4,16,2048]{2,1,0:T(8,128)}, u32[]{:S(2)}, u32[]{:S(2)}) collective-permute-start(f32[4,16,2048]{2,1,0:T(8,128)S(1)} %bitcast.39), channel_id=1, source_target_pairs={{128,0},{129,1},{130,2},{131,3},{132,4},{133,5},{134,6},{135,7},{1... | collective-permute-start | bytes 1572872 | tf_op jit(solution)/shard_map/ppermute | solution.py:22
  110.8 16.7 %all-to-all-start = ((f32[16,8,128]{2,1,0:T(8,128)}), f32[16,8,128]{2,1,0:T(8,128)S(1)}, u32[]{:S(2)}, u32[]{:S(2)}) async-start(f32[16,8,128]{2,1,0:T(8,128)} %broadcast_in_dim.2), calls=%async_computation | async-start | bytes 131072 | tf_op jit(solution)/shard_map/all_to_all | solution.py:127
  121.1 25.8 %collective-permute-start.27 = (f32[16,2048]{1,0:T(8,128)S(1)}, f32[16,2048]{1,0:T(8,128)S(1)}, u32[]{:S(2)}, u32[]{:S(2)}) collective-permute-start(f32[16,2048]{1,0:T(8,128)S(1)} %get-tuple-element.27), channel_id=1, source_target_pairs={{192,0},{193,1},{194,2},{195,3},{196,4},{197,5},{198,6},{199,7},{2... | collective-permute-start | bytes 393224 | tf_op jit(solution)/shard_map/ppermute | solution.py:22
  121.3 26.4 %collective-permute-start.29 = (f32[16,2048]{1,0:T(8,128)S(1)}, f32[16,2048]{1,0:T(8,128)S(1)}, u32[]{:S(2)}, u32[]{:S(2)}) collective-permute-start(f32[16,2048]{1,0:T(8,128)S(1)} %get-tuple-element.28), channel_id=1, source_target_pairs={{128,0},{129,1},{130,2},{131,3},{132,4},{133,5},{134,6},{135,7},{1... | collective-permute-start | bytes 393224 | tf_op jit(solution)/shard_map/ppermute | solution.py:22
  127.4 6.2 %collective-permute-start.15 = (f32[8,128]{1,0:T(8,128)S(1)}, f32[8,128]{1,0:T(8,128)S(1)}, u32[]{:S(2)}, u32[]{:S(2)}) collective-permute-start(f32[8,128]{1,0:T(8,128)S(1)} %reduce_sum.9), channel_id=1, source_target_pairs={{6,0},{7,1},{0,2},{1,3},{2,4},{3,5},{4,6},{5,7},{14,8},{15,9},{8,1... | collective-permute-start | bytes 12296 | tf_op jit(solution)/shard_map/ppermute | solution.py:22
  128.8 4.8 %collective-permute-start.14 = (f32[8,128]{1,0:T(8,128)S(1)}, f32[8,128]{1,0:T(8,128)S(1)}, u32[]{:S(2)}, u32[]{:S(2)}) collective-permute-start(f32[8,128]{1,0:T(8,128)S(1)} %reduce_sum.9), channel_id=1, source_target_pairs={{2,0},{3,1},{4,2},{5,3},{6,4},{7,5},{0,6},{1,7},{10,8},{11,9},{12,... | collective-permute-start | bytes 12296 | tf_op jit(solution)/shard_map/ppermute | solution.py:22
  129.5 5.1 %collective-permute-start.13 = (f32[8,128]{1,0:T(8,128)S(1)}, f32[8,128]{1,0:T(8,128)S(1)}, u32[]{:S(2)}, u32[]{:S(2)}) collective-permute-start(f32[8,128]{1,0:T(8,128)S(1)} %reduce_sum.9), channel_id=1, source_target_pairs={{4,0},{5,1},{6,2},{7,3},{0,4},{1,5},{2,6},{3,7},{12,8},{13,9},{14,... | collective-permute-start | bytes 12296 | tf_op jit(solution)/shard_map/ppermute | solution.py:22
  134.7 5.1 %collective-permute-start.18 = (f32[8,128]{1,0:T(8,128)S(1)}, f32[8,128]{1,0:T(8,128)S(1)}, u32[]{:S(2)}, u32[]{:S(2)}) collective-permute-start(f32[8,128]{1,0:T(8,128)S(1)} %add_add_fusion.3), channel_id=1, source_target_pairs={{192,0},{193,1},{194,2},{195,3},{196,4},{197,5},{198,6},{199,7},{2... | collective-permute-start | bytes 12296 | tf_op jit(solution)/shard_map/ppermute | solution.py:22
  134.8 5.8 %collective-permute-start.17 = (f32[8,128]{1,0:T(8,128)S(1)}, f32[8,128]{1,0:T(8,128)S(1)}, u32[]{:S(2)}, u32[]{:S(2)}) collective-permute-start(f32[8,128]{1,0:T(8,128)S(1)} %add_add_fusion.3), channel_id=1, source_target_pairs={{64,0},{65,1},{66,2},{67,3},{68,4},{69,5},{70,6},{71,7},{72,8},{73... | collective-permute-start | bytes 12296 | tf_op jit(solution)/shard_map/ppermute | solution.py:22
  137.9 5.1 %collective-permute-start.16 = (f32[8,128]{1,0:T(8,128)S(1)}, f32[8,128]{1,0:T(8,128)S(1)}, u32[]{:S(2)}, u32[]{:S(2)}) collective-permute-start(f32[8,128]{1,0:T(8,128)S(1)} %add_add_fusion.3), channel_id=1, source_target_pairs={{128,0},{129,1},{130,2},{131,3},{132,4},{133,5},{134,6},{135,7},{1... | collective-permute-start | bytes 12296 | tf_op jit(solution)/shard_map/ppermute | solution.py:22
  139.7 8.0 %collective-permute-start.28 = (f32[16,2048]{1,0:T(8,128)S(1)}, f32[16,2048]{1,0:T(8,128)S(1)}, u32[]{:S(2)}, u32[]{:S(2)}) collective-permute-start(f32[16,2048]{1,0:T(8,128)S(1)} %get-tuple-element.29), channel_id=1, source_target_pairs={{64,0},{65,1},{66,2},{67,3},{68,4},{69,5},{70,6},{71,7},{72,8},{73... | collective-permute-start | bytes 393224 | tf_op jit(solution)/shard_map/ppermute | solution.py:22
  140.6 7.1 %collective-permute-start.21 = (f32[16,2048]{1,0:T(8,128)S(1)}, f32[16,2048]{1,0:T(8,128)S(1)}, u32[]{:S(2)}, u32[]{:S(2)}) collective-permute-start(f32[16,2048]{1,0:T(8,128)S(1)} %get-tuple-element.24), channel_id=1, source_target_pairs={{6,0},{7,1},{0,2},{1,3},{2,4},{3,5},{4,6},{5,7},{14,8},{15,9},{8,1... | collective-permute-start | bytes 393224 | tf_op jit(solution)/shard_map/ppermute | solution.py:22
  143.0 7.2 %collective-permute-start.23 = (f32[16,2048]{1,0:T(8,128)S(1)}, f32[16,2048]{1,0:T(8,128)S(1)}, u32[]{:S(2)}, u32[]{:S(2)}) collective-permute-start(f32[16,2048]{1,0:T(8,128)S(1)} %get-tuple-element.25), channel_id=1, source_target_pairs={{4,0},{5,1},{6,2},{7,3},{0,4},{1,5},{2,6},{3,7},{12,8},{13,9},{14,... | collective-permute-start | bytes 393224 | tf_op jit(solution)/shard_map/ppermute | solution.py:22
  146.9 5.0 %collective-permute-start.22 = (f32[16,2048]{1,0:T(8,128)S(1)}, f32[16,2048]{1,0:T(8,128)S(1)}, u32[]{:S(2)}, u32[]{:S(2)}) collective-permute-start(f32[16,2048]{1,0:T(8,128)S(1)} %get-tuple-element.26), channel_id=1, source_target_pairs={{2,0},{3,1},{4,2},{5,3},{6,4},{7,5},{0,6},{1,7},{10,8},{11,9},{12,... | collective-permute-start | bytes 393224 | tf_op jit(solution)/shard_map/ppermute | solution.py:22
Sparse Core Ops, SparseCore 0:
  9.8 48.9 all-gather.1

commit v3 on v0

v3 whole, which is shorter than its diff:
```python
import jax
import jax.numpy as jnp
from jax import lax
from jax.experimental import pallas as pl
from jax.experimental.pallas import tpu as pltpu
from jax.sharding import Mesh, PartitionSpec as P

AXES = ("y", "zl", "zh", "x", "core")
SIZES = (4, 4, 2, 4, 2)
DEPTH = 1024


def join_kernel(student_ref, teacher_ref, both_ref, upper_ref, lower_ref):
    width = student_ref.shape[1]
    half = upper_ref.shape[1]
    for source, place in ((student_ref, slice(0, width)), (teacher_ref, slice(width, None))):
        both_ref[:, place] = source[...]
        for i in range(4):
            upper_ref[i, :, place] = source[:half]
            lower_ref[i, :, place] = source[half:]


def join(student, teacher):
    texts, total = student.shape[0], student.shape[1] + teacher.shape[1]
    whole = jax.ShapeDtypeStruct((texts, total), student.dtype)
    part = jax.ShapeDtypeStruct((4, texts // 2, total), student.dtype)
    return pl.pallas_call(join_kernel, out_shape=(whole, part, part))(student, teacher)


def excess_kernel(
    upper_ref, lower_ref, rows_ref,
    upper_out, lower_out, squares_ref,
    cols, rows, total, rounded, sems,
):
    count, width = upper_ref.shape[0], upper_out.shape[1]
    steps = rows.shape[0]
    copies = []
    for k in range(steps):
        block = pl.ds(k * DEPTH, DEPTH)
        moves = (
            (upper_ref.at[:, block], cols.at[k, pl.ds(0, count)]),
            (lower_ref.at[:, block], cols.at[k, pl.ds(count, count)]),
            (rows_ref.at[:, block], rows.at[k]),
        )
        copies.append(
            [pltpu.make_async_copy(a, b, sems.at[k, i]) for i, (a, b) in enumerate(moves)]
        )
        for copy in copies[-1]:
            copy.start()
    for k in range(steps):
        for copy in copies[k]:
            copy.wait()
        product = lax.dot_general(
            cols[k], rows[k], (((1,), (1,)), ((), ())), preferred_element_type=jnp.float32
        )
        if k == 0:
            total[...] = product
        elif k * DEPTH < width:
            total[...] += product
        else:
            total[...] -= product
    excess = total[...]
    rounded[...] = excess.astype(rounded.dtype)
    squares = jnp.sum(jnp.sum(excess * excess, axis=0, keepdims=True), axis=1, keepdims=True)
    squares_ref[...] = jnp.broadcast_to(squares[None], squares_ref.shape)
    for k in range(width // DEPTH):
        place = slice(k * DEPTH, (k + 1) * DEPTH)
        for half, out in enumerate((upper_out, lower_out)):
            out[:, place] = jnp.dot(
                rounded[half * count : (half + 1) * count],
                rows[k],
                preferred_element_type=jnp.float32,
            )


def pulls(upper, lower, rows, student_width):
    texts, width = rows.shape
    count = upper.shape[0]
    anywhere = pl.BlockSpec(memory_space=pl.ANY)
    partial_term = jax.ShapeDtypeStruct((count, student_width), jnp.float32)
    return pl.pallas_call(
        excess_kernel,
        in_specs=[anywhere] * 3,
        out_shape=(
            partial_term, partial_term, jax.ShapeDtypeStruct((16, 8, 128), jnp.float32)
        ),
        scratch_shapes=[
            pltpu.VMEM((width // DEPTH, 2 * count, DEPTH), jnp.bfloat16),
            pltpu.VMEM((width // DEPTH, texts, DEPTH), jnp.bfloat16),
            pltpu.VMEM((2 * count, texts), jnp.float32),
            pltpu.VMEM((2 * count, texts), jnp.bfloat16),
            pltpu.SemaphoreType.DMA((width // DEPTH, 3)),
        ],
        compiler_params=pltpu.CompilerParams(vmem_limit_bytes=56 * 1024 * 1024),
        cost_estimate=pl.CostEstimate(
            flops=4 * count * texts * (width + student_width),
            bytes_accessed=2 * (2 * count + texts) * width + 8 * count * student_width,
            transcendentals=0,
        ),
    )(upper, lower, rows)


def swap(value, axes):
    return lax.all_to_all(value, axes, 0, 0)


def shards(student, teacher):
    texts, width = student.shape
    both, upper, lower = join(student, teacher)
    rows = lax.all_gather(both, ("zh", "zl", "core"), axis=0, tiled=True)
    to_all = lambda value: jnp.broadcast_to(value[None], (4,) + value.shape)
    upper, lower = swap(upper, "x"), swap(lower, "y")
    upper, lower = swap(to_all(upper), "y"), swap(to_all(lower), "x")
    flat = lambda value: value.reshape(-1, value.shape[-1])
    upper, lower, squares = pulls(flat(upper), flat(lower), rows, width)
    unflat = lambda value: value.reshape(4, 4, texts // 2, width)
    upper = jnp.sum(swap(unflat(upper), "y"), axis=0)
    lower = jnp.sum(swap(unflat(lower), "x"), axis=0)
    upper = jnp.sum(swap(upper, "x"), axis=0)
    lower = jnp.sum(swap(lower, "y"), axis=0)
    pulled = jnp.concatenate([upper, lower])

    line = jnp.sum(swap(squares, ("zh", "zl", "core")), axis=0)
    plane = swap(jnp.broadcast_to(line[None], (16, 8, 128)), ("y", "x"))
    distance = jnp.sum(plane[:, 0, 0]) / jnp.float32(texts * 256)
    return distance, pulled


def solution(mesh):
    fine = Mesh(mesh.devices.reshape(SIZES), AXES)
    spec = P(AXES, None)
    return jax.shard_map(
        shards, mesh=fine, in_specs=(spec, spec), out_specs=(P(), spec), check_vma=False
    )
```

time: 460 us -> 245 us (0.53)
  waiting for transfers between devices: 343 us -> 33.2 us
  blocking collectives: 86.9 us -> 165 us
  matrix products: 13.3 us -> 0 us
  starting transfers between devices: 0.19 us -> 13.4 us
  Pallas kernels: 0 us -> 11.4 us
  other arithmetic: 0 us -> 4.91 us
    all_gather x4 -> x1, waiting for transfers between devices: 326 us -> 0.01 us  [shards(): rows = lax.all_gather(both, ('zh', 'zl', 'core'), axis=0, tiled=True)]
    all_to_all x0 -> x7, blocking collectives: none -> 165 us  [swap(): return lax.all_to_all(value, axes, 0, 0)]
    psum x1 -> x0, blocking collectives: 86.9 us -> none  [shards(): summed = lax.psum(squares, ('row', 'col'))]
    all_to_all x0 -> x3, waiting for transfers between devices: none -> 33.2 us  [swap(): return lax.all_to_all(value, axes, 0, 0)]
    reduce_scatter x1 -> x0, waiting for transfers between devices: 14.5 us -> none  [shards(): lax.psum_scatter(partial_term, 'col', scatter_dimension=0, tiled=True)]
    all_to_all x0 -> x3, starting transfers between devices: none -> 13.3 us  [swap(): return lax.all_to_all(value, axes, 0, 0)]
    dot_general x3 -> x0, matrix products: 13.3 us -> none  [the longest x1 6.57 us: shards(): lax.dot_general(rows_t, cols_t, contract, preferred_element_type=jnp.floa...]
    pallas_call x0 -> x2, Pallas kernels: none -> 11.4 us  [the longest x1 8.97 us: pulls(): pl.pallas_call(excess_kernel, in_specs=[anywhere] * 3, out_shape=(partial...]
  transfers between devices with their start and end apart: 5 -> 4, of which waited for: 5 -> 3; matrix products, arithmetic and copies ran while one was open for 1% -> 2% of each run, Pallas kernels for 0% -> 0%
where the time goes in v3:
time: 245 us; the launch traced here: 244 us
  blocking collectives  165 us (67%)
  waiting for transfers between devices  33.2 us (14%)
  between operations  15.9 us (6%)
  starting transfers between devices  13.4 us (5%)
  Pallas kernels  11.4 us (5%)
  other arithmetic  4.91 us (2%)
    all_to_all x7, blocking collectives, swap(): return lax.all_to_all(value, axes, 0, 0)  165 us
    all_to_all x3, waiting for transfers between devices, swap(): return lax.all_to_all(value, axes, 0, 0)  33.2 us
    all_to_all x3, starting transfers between devices, swap(): return lax.all_to_all(value, axes, 0, 0)  13.3 us
    pallas_call x1, Pallas kernels, pulls(): pl.pallas_call(excess_kernel, in_specs=[anywhere] * 3, out_shape=(partial...  8.97 us
  transfers between devices with their start and end apart: 4, of which 3 were waited for; matrix products, arithmetic and copies ran while one was open for 2% of the time, Pallas kernels for 0%

profile of v3, /device:TPU:2, one launch (start us, length us, event | category | flops | bytes accessed | tf_op | source)
XLA Modules:
  0.0 244.1 jit_solution(11957332675725379685)
XLA Ops:
  7.2 0.0 all-gather.2.cloned.1.call-start
  7.2 2.4 shard_map.41
  9.6 0.0 all-gather.2.cloned.1.call-update
  9.7 15.7 %all_to_all.50 = bf16[4,16,6144]{2,1,0:T(8,128)(2,1)S(1)} all-to-all(bf16[4,16,6144]{2,1,0:T(8,128)(2,1)} %get-tuple-element.8), channel_id=1, replica_groups=mesh['y'=4,'zl'=4,'zh'=2,'x'=4,'core'=2] {'x'}, dimensions={0} | all-to-all | bytes 1572864 | tf_op jit(solution)/shard_map/all_to_all | solution.py:104
  25.3 15.6 %all_to_all.51 = bf16[4,16,6144]{2,1,0:T(8,128)(2,1)S(1)} all-to-all(bf16[4,16,6144]{2,1,0:T(8,128)(2,1)} %get-tuple-element.9), channel_id=1, replica_groups=mesh['y'=4,'zl'=4,'zh'=2,'x'=4,'core'=2] {'y'}, dimensions={0} | all-to-all | bytes 1572864 | tf_op jit(solution)/shard_map/all_to_all | solution.py:104
  40.9 0.4 broadcast_in_dim.7
  41.3 38.5 %all_to_all.52 = bf16[4,4,16,6144]{3,2,1,0:T(8,128)(2,1)} all-to-all(bf16[4,4,16,6144]{3,2,1,0:T(8,128)(2,1)S(1)} %broadcast_in_dim.7), channel_id=1, replica_groups=mesh['y'=4,'zl'=4,'zh'=2,'x'=4,'core'=2] {'x'}, dimensions={0} | all-to-all | bytes 6291456 | tf_op jit(solution)/shard_map/all_to_all | solution.py:104
  79.8 0.4 broadcast_in_dim.6
  80.2 37.6 %all_to_all.53 = bf16[4,4,16,6144]{3,2,1,0:T(8,128)(2,1)} all-to-all(bf16[4,4,16,6144]{3,2,1,0:T(8,128)(2,1)S(1)} %broadcast_in_dim.6), channel_id=1, replica_groups=mesh['y'=4,'zl'=4,'zh'=2,'x'=4,'core'=2] {'y'}, dimensions={0} | all-to-all | bytes 6291456 | tf_op jit(solution)/shard_map/all_to_all | solution.py:104
  117.8 0.0 all-gather.2.cloned.1.call-done.rows_ref
  117.8 9.0 %shard_map.42 = (f32[256,2048]{1,0:T(8,128)}, f32[256,2048]{1,0:T(8,128)}, f32[16,8,128]{2,1,0:T(8,128)}) custom-call(bf16[256,6144]{1,0:T(8,128)(2,1)} %bitcast.5, bf16[256,6144]{1,0:T(8,128)(2,1)} %bitcast.4, bf16[512,6144]{1,0:T(8,128)(2,1)} %all-gather.2.cloned.1.call-done.rows_ref), custom_call_target="tpu_custom_call" | custom-call | flops 4294967296 | bytes 16777216 | tf_op jit(solution)/shard_map/pallas_call | solution.py:81
  126.8 16.4 %all_to_all.54 = f32[16,8,128]{2,1,0:T(8,128)S(1)} all-to-all(f32[16,8,128]{2,1,0:T(8,128)} %get-tuple-element.11), channel_id=1, replica_groups=mesh['y'=4,'zl'=4,'zh'=2,'x'=4,'core'=2] {'zh','zl','core'}, dimensions={0} | all-to-all | bytes 131072 | tf_op jit(solution)/shard_map/all_to_all | solution.py:104
  143.3 10.6 %all_to_all.55 = f32[16,8,128]{2,1,0:T(8,128)S(1)} all-to-all(f32[16,8,128]{2,1,0:T(8,128)S(1)} %broadcast_in_dim.8), channel_id=1, replica_groups=mesh['y'=4,'zl'=4,'zh'=2,'x'=4,'core'=2] {'y','x'}, dimensions={0} | all-to-all | bytes 131072 | tf_op jit(solution)/shard_map/all_to_all | solution.py:104
  153.9 30.2 %all_to_all.56 = f32[4,4,16,2048]{3,2,1,0:T(8,128)} all-to-all(f32[4,4,16,2048]{3,2,1,0:T(8,128)} %bitcast.7), channel_id=1, replica_groups=mesh['y'=4,'zl'=4,'zh'=2,'x'=4,'core'=2] {'y'}, dimensions={0} | all-to-all | bytes 4194304 | tf_op jit(solution)/shard_map/all_to_all | solution.py:104
  184.1 5.0 %all-to-all-start.8 = ((f32[4,4,16,2048]{3,2,1,0:T(8,128)}), f32[4,4,16,2048]{3,2,1,0:T(8,128)S(1)}, u32[]{:S(2)}, u32[]{:S(2)}) async-start(f32[4,4,16,2048]{3,2,1,0:T(8,128)} %bitcast.6), calls=%async_computation.8 | async-start | bytes 4194304 | tf_op jit(solution)/shard_map/all_to_all | solution.py:104
  189.0 2.6 %reduce_sum.56 = f32[4,16,2048]{2,1,0:T(8,128)} reduce(f32[4,4,16,2048]{3,2,1,0:T(8,128)} %all_to_all.56, f32[]{:T(128)} %constant.1.clone.1), dimensions={0}, to_apply=%region_2.0 | reduce | flops 393216 | bytes 2621444 | tf_op jit(solution)/shard_map/reduce_sum | solution.py:117
  191.6 20.8 %all-to-all-done.8 = f32[4,4,16,2048]{3,2,1,0:T(8,128)S(1)} async-done(((f32[4,4,16,2048]{3,2,1,0:T(8,128)}), f32[4,4,16,2048]{3,2,1,0:T(8,128)S(1)}, u32[]{:S(2)}, u32[]{:S(2)}) %all-to-all-start.8) | async-done | bytes 2097184 | tf_op jit(solution)/shard_map/all_to_all | solution.py:104
  212.4 4.9 %all-to-all-start.7 = ((f32[4,16,2048]{2,1,0:T(8,128)}), f32[4,16,2048]{2,1,0:T(8,128)S(1)}, u32[]{:S(2)}, u32[]{:S(2)}) async-start(f32[4,16,2048]{2,1,0:T(8,128)} %reduce_sum.56), calls=%async_computation.7 | async-start | bytes 1048576 | tf_op jit(solution)/shard_map/all_to_all | solution.py:104
  217.3 0.9 reduce_sum.58
  218.2 5.7 %all-to-all-done.7 = f32[4,16,2048]{2,1,0:T(8,128)S(1)} async-done(((f32[4,16,2048]{2,1,0:T(8,128)}), f32[4,16,2048]{2,1,0:T(8,128)S(1)}, u32[]{:S(2)}, u32[]{:S(2)}) %all-to-all-start.7) | async-done | bytes 524320 | tf_op jit(solution)/shard_map/all_to_all | solution.py:104
  223.9 3.5 %all-to-all-start.9 = ((f32[4,16,2048]{2,1,0:T(8,128)}), f32[4,16,2048]{2,1,0:T(8,128)S(1)}, u32[]{:S(2)}, u32[]{:S(2)}) async-start(f32[4,16,2048]{2,1,0:T(8,128)} %reduce_sum.58), calls=%async_computation.9 | async-start | bytes 1048576 | tf_op jit(solution)/shard_map/all_to_all | solution.py:104
  227.4 0.6 slice_reduce_fusion
  228.7 6.7 %all-to-all-done.9 = f32[4,16,2048]{2,1,0:T(8,128)S(1)} async-done(((f32[4,16,2048]{2,1,0:T(8,128)}), f32[4,16,2048]{2,1,0:T(8,128)S(1)}, u32[]{:S(2)}, u32[]{:S(2)}) %all-to-all-start.9) | async-done | bytes 524320 | tf_op jit(solution)/shard_map/all_to_all | solution.py:104
  235.4 0.7 pad_maximum_fusion
  (4 shorter events, 0.1 us)
Async XLA Ops:
  7.2 110.6 %all-gather.2.cloned.1.call-start = ((), (), s32[]{:S(2)}) async-start(), calls=%async_computation.10 | async-start | bytes 6684672 | tf_op jit(solution)/shard_map/all_gather | solution.py:110
  184.1 28.3 %all-to-all-start.8 = ((f32[4,4,16,2048]{3,2,1,0:T(8,128)}), f32[4,4,16,2048]{3,2,1,0:T(8,128)S(1)}, u32[]{:S(2)}, u32[]{:S(2)}) async-start(f32[4,4,16,2048]{3,2,1,0:T(8,128)} %bitcast.6), calls=%async_computation.8 | async-start | bytes 4194304 | tf_op jit(solution)/shard_map/all_to_all | solution.py:104
  212.4 11.5 %all-to-all-start.7 = ((f32[4,16,2048]{2,1,0:T(8,128)}), f32[4,16,2048]{2,1,0:T(8,128)S(1)}, u32[]{:S(2)}, u32[]{:S(2)}) async-start(f32[4,16,2048]{2,1,0:T(8,128)} %reduce_sum.56), calls=%async_computation.7 | async-start | bytes 1048576 | tf_op jit(solution)/shard_map/all_to_all | solution.py:104
  223.9 11.5 %all-to-all-start.9 = ((f32[4,16,2048]{2,1,0:T(8,128)}), f32[4,16,2048]{2,1,0:T(8,128)S(1)}, u32[]{:S(2)}, u32[]{:S(2)}) async-start(f32[4,16,2048]{2,1,0:T(8,128)} %reduce_sum.58), calls=%async_computation.9 | async-start | bytes 1048576 | tf_op jit(solution)/shard_map/all_to_all | solution.py:104
Sparse Core Ops, SparseCore 0:
  9.8 48.9 all-gather.1

commit v4 on v0

v4 whole, which is shorter than its diff:
```python
import jax
import jax.numpy as jnp
from jax import lax
from jax.experimental import pallas as pl
from jax.experimental.pallas import tpu as pltpu
from jax.sharding import Mesh, PartitionSpec as P

AXES = ("y", "zl", "zh", "x", "core")
SIZES = (4, 4, 2, 4, 2)
STRIDES = dict(zip(AXES, (64, 16, 8, 2, 1)))
NEAR = (2, 1, 3)
DEPTH = 1024


def shift(value, axes, step):
    pairs = []
    for target in range(256):
        stride = STRIDES[axes[target % 2]]
        place = target // stride % 4
        pairs.append((target + ((place + step) % 4 - place) * stride, target))
    return lax.ppermute(value, AXES, pairs)


def join_kernel(student_ref, teacher_ref, both_ref):
    width = student_ref.shape[1]
    both_ref[:, :width] = student_ref[...]
    both_ref[:, width:] = teacher_ref[...]


def join(student, teacher):
    texts, total = student.shape[0], student.shape[1] + teacher.shape[1]
    return pl.pallas_call(
        join_kernel, out_shape=jax.ShapeDtypeStruct((texts, total), student.dtype)
    )(student, teacher)


def excess_kernel(*refs):
    bundles, rows_ref, outs = refs[:4], refs[4], refs[5:9]
    squares_ref, rows, total, rounded, sems = refs[9:]
    count, width = outs[0].shape
    steps = rows.shape[0]
    copies = [
        pltpu.make_async_copy(rows_ref.at[:, pl.ds(k * DEPTH, DEPTH)], rows.at[k], sems.at[k])
        for k in range(steps)
    ]
    for copy in copies:
        copy.start()
    for k in range(steps):
        place = slice(k * DEPTH, (k + 1) * DEPTH)
        cols = jnp.concatenate([bundle[:, place] for bundle in bundles])
        copies[k].wait()
        product = lax.dot_general(
            cols, rows[k], (((1,), (1,)), ((), ())), preferred_element_type=jnp.float32
        )
        if k == 0:
            total[...] = product
        elif k * DEPTH < width:
            total[...] += product
        else:
            total[...] -= product
    excess = total[...]
    rounded[...] = excess.astype(rounded.dtype)
    squares = jnp.sum(jnp.sum(excess * excess, axis=0, keepdims=True), axis=1, keepdims=True)
    squares_ref[...] = jnp.broadcast_to(squares[None], squares_ref.shape)
    for k in range(width // DEPTH):
        place = slice(k * DEPTH, (k + 1) * DEPTH)
        product = jnp.dot(rounded[...], rows[k], preferred_element_type=jnp.float32)
        for i, out in enumerate(outs):
            out[:, place] = product[i * count : (i + 1) * count]


def pulls(bundles, rows, student_width):
    texts, width = rows.shape
    count = bundles[0].shape[0]
    inside = pl.BlockSpec(memory_space=pltpu.VMEM)
    partial_term = jax.ShapeDtypeStruct((count, student_width), jnp.float32)
    return pl.pallas_call(
        excess_kernel,
        in_specs=[inside] * 4 + [pl.BlockSpec(memory_space=pl.ANY)],
        out_specs=(inside,) * 5,
        out_shape=(partial_term,) * 4 + (jax.ShapeDtypeStruct((16, 8, 128), jnp.float32),),
        scratch_shapes=[
            pltpu.VMEM((width // DEPTH, texts, DEPTH), jnp.bfloat16),
            pltpu.VMEM((4 * count, texts), jnp.float32),
            pltpu.VMEM((4 * count, texts), jnp.bfloat16),
            pltpu.SemaphoreType.DMA((width // DEPTH,)),
        ],
        compiler_params=pltpu.CompilerParams(vmem_limit_bytes=40 * 1024 * 1024),
        cost_estimate=pl.CostEstimate(
            flops=8 * count * texts * (width + student_width),
            bytes_accessed=2 * texts * width,
            transcendentals=0,
        ),
    )(*bundles, rows)


def shards(student, teacher):
    texts, width = student.shape
    both = join(student, teacher)
    rows = lax.all_gather(both, ("zh", "zl", "core"), axis=0, tiled=True)
    near, far = ("x", "y"), ("y", "x")
    own = jnp.concatenate([both] + [shift(both, near, k) for k in NEAR])
    bundles = [own] + [shift(own, far, k) for k in NEAR]
    *terms, squares = pulls(bundles, rows, width)
    partial_term = terms[0]
    for i, k in enumerate(NEAR):
        back = shift(terms[i + 1], far, -k)
        if i == 0:
            back, squares = lax.optimization_barrier((back, squares))
        partial_term += back
    blocks = partial_term.reshape(4, texts, width)
    pulled = blocks[0]
    for i, k in enumerate(NEAR):
        pulled += shift(blocks[i + 1], near, -k)

    line = jnp.sum(
        lax.all_to_all(squares, ("zh", "zl", "core"), 0, 0), axis=0, keepdims=True
    )
    plane = lax.all_to_all(jnp.broadcast_to(line, (16, 8, 128)), ("y", "x"), 0, 0)
    distance = jnp.sum(plane[:, 0, 0]) / jnp.float32(texts * 256)
    return distance, pulled


def solution(mesh):
    fine = Mesh(mesh.devices.reshape(SIZES), AXES)
    spec = P(AXES, None)
    return jax.shard_map(
        shards, mesh=fine, in_specs=(spec, spec), out_specs=(P(), spec), check_vma=False
    )
```

time: 460 us -> 138 us (0.30)
  waiting for transfers between devices: 343 us -> 55.9 us
  blocking collectives: 86.9 us -> 11.7 us
  starting transfers between devices: 0.19 us -> 30.3 us
  matrix products: 13.3 us -> 0 us
  Pallas kernels: 0 us -> 10.2 us
  local copies, waits for them, and re-layouts: 0.01 us -> 7.81 us
  other arithmetic: 0 us -> 4.68 us
    all_gather x4 -> x1, waiting for transfers between devices: 326 us -> 0.01 us  [shards(): rows = lax.all_gather(both, ('zh', 'zl', 'core'), axis=0, tiled=True)]
    psum x1 -> x0, blocking collectives: 86.9 us -> none  [shards(): summed = lax.psum(squares, ('row', 'col'))]
    ppermute x0 -> x12, waiting for transfers between devices: none -> 55.9 us  [shift(): return lax.ppermute(value, AXES, pairs)]
    ppermute x0 -> x12, starting transfers between devices: none -> 21.8 us  [shift(): return lax.ppermute(value, AXES, pairs)]
    reduce_scatter x1 -> x0, waiting for transfers between devices: 14.5 us -> none  [shards(): lax.psum_scatter(partial_term, 'col', scatter_dimension=0, tiled=True)]
    dot_general x3 -> x0, matrix products: 13.3 us -> none  [the longest x1 6.57 us: shards(): lax.dot_general(rows_t, cols_t, contract, preferred_element_type=jnp.floa...]
    all_to_all x0 -> x1, blocking collectives: none -> 11.7 us  [shards(): lax.all_to_all(jnp.broadcast_to(line, (16, 8, 128)), ('y', 'x'), 0, 0)]
    pallas_call x0 -> x2, Pallas kernels: none -> 10.2 us  [the longest x1 8.4 us: pulls(): pl.pallas_call(excess_kernel, in_specs=[inside] * 4 + [pl.BlockSpec(memor...]
  transfers between devices with their start and end apart: 5 -> 14, of which waited for: 5 -> 9; matrix products, arithmetic and copies ran while one was open for 1% -> 3% of each run, Pallas kernels for 0% -> 0%
where the time goes in v4:
time: 138 us; the launch traced here: 136 us
  waiting for transfers between devices  55.9 us (41%)
  starting transfers between devices  30.3 us (22%)
  between operations  15.9 us (12%)
  blocking collectives  11.7 us (8%)
  Pallas kernels  10.2 us (7%)
  local copies, waits for them, and re-layouts  7.81 us (6%)
  other arithmetic  4.68 us (3%)
    ppermute x12, waiting for transfers between devices, shift(): return lax.ppermute(value, AXES, pairs)  55.9 us
    ppermute x12, starting transfers between devices, shift(): return lax.ppermute(value, AXES, pairs)  21.8 us
    all_to_all x1, blocking collectives, shards(): lax.all_to_all(jnp.broadcast_to(line, (16, 8, 128)), ('y', 'x'), 0, 0)  11.7 us
    all_to_all x1, starting transfers between devices, shards(): lax.all_to_all(squares, ('zh', 'zl', 'core'), 0, 0)  8.53 us
    pallas_call x1, Pallas kernels, pulls(): pl.pallas_call(excess_kernel, in_specs=[inside] * 4 + [pl.BlockSpec(memor...  8.4 us
    unnamed x12, local copies, waits for them, and re-layouts  7.75 us
  transfers between devices with their start and end apart: 14, of which 9 were waited for; matrix products, arithmetic and copies ran while one was open for 3% of the time, Pallas kernels for 0%

profile of v4, /device:TPU:2, one launch (start us, length us, event | category | flops | bytes accessed | tf_op | source)
XLA Modules:
  0.0 136.5 jit_solution(7660311718272812753)
XLA Ops:
  7.2 0.0 all-gather.2.cloned.1.call-start
  7.2 1.8 %shard_map.41 = bf16[32,6144]{1,0:T(8,128)(2,1)} custom-call(bf16[32,2048]{1,0:T(8,128)(2,1)} %student_ref.1, bf16[32,4096]{1,0:T(8,128)(2,1)} %teacher_ref.1), custom_call_target="tpu_custom_call" | custom-call | tf_op jit(solution)/shard_map/pallas_call | solution.py:32
  9.0 0.0 all-gather.2.cloned.1.call-update
  9.0 1.6 %collective-permute-start.2 = (bf16[32,6144]{1,0:T(8,128)(2,1)}, bf16[32,6144]{1,0:T(8,128)(2,1)S(1)}, u32[]{:S(2)}, u32[]{:S(2)}) collective-permute-start(bf16[32,6144]{1,0:T(8,128)(2,1)} %shard_map.41), channel_id=1, source_target_pairs={{6,0},{193,1},{0,2},{195,3},{2,4},{197,5},{4,6},{199,7},{14,8},{20... | collective-permute-start | bytes 1179656 | tf_op jit(solution)/shard_map/ppermute | solution.py:21
  10.6 0.9 collective-permute-start.1
  11.5 2.0 %collective-permute-start = (bf16[32,6144]{1,0:T(8,128)(2,1)}, bf16[32,6144]{1,0:T(8,128)(2,1)S(1)}, u32[]{:S(2)}, u32[]{:S(2)}) collective-permute-start(bf16[32,6144]{1,0:T(8,128)(2,1)} %shard_map.41), channel_id=1, source_target_pairs={{4,0},{129,1},{6,2},{131,3},{0,4},{133,5},{2,6},{135,7},{12,8},{13... | collective-permute-start | bytes 1179656 | tf_op jit(solution)/shard_map/ppermute | solution.py:21
  13.4 3.9 %collective-permute-done.2 = bf16[32,6144]{1,0:T(8,128)(2,1)S(1)} collective-permute-done((bf16[32,6144]{1,0:T(8,128)(2,1)}, bf16[32,6144]{1,0:T(8,128)(2,1)S(1)}, u32[]{:S(2)}, u32[]{:S(2)}) %collective-permute-start.2) | collective-permute-done | bytes 393248 | tf_op jit(solution)/shard_map/ppermute | solution.py:21
  17.3 1.2 collective-permute-done.1
  18.6 5.1 %collective-permute-done = bf16[32,6144]{1,0:T(8,128)(2,1)S(1)} collective-permute-done((bf16[32,6144]{1,0:T(8,128)(2,1)}, bf16[32,6144]{1,0:T(8,128)(2,1)S(1)}, u32[]{:S(2)}, u32[]{:S(2)}) %collective-permute-start) | collective-permute-done | bytes 393248 | tf_op jit(solution)/shard_map/ppermute | solution.py:21
  23.6 1.2 pad_maximum_fusion.refs_0_
  24.8 1.4 %collective-permute-start.5 = (bf16[128,6144]{1,0:T(8,128)(2,1)S(1)}, bf16[128,6144]{1,0:T(8,128)(2,1)S(1)}, u32[]{:S(2)}, u32[]{:S(2)}) collective-permute-start(bf16[128,6144]{1,0:T(8,128)(2,1)S(1)} %pad_maximum_fusion.refs_0_), channel_id=1, source_target_pairs={{192,0},{7,1},{194,2},{1,3},{196,4},{3,5},{198,6},{5,7},{200,8},{1... | collective-permute-start | bytes 4718600 | tf_op jit(solution)/shard_map/ppermute | solution.py:21
  26.3 1.9 %collective-permute-start.4 = (bf16[128,6144]{1,0:T(8,128)(2,1)S(1)}, bf16[128,6144]{1,0:T(8,128)(2,1)S(1)}, u32[]{:S(2)}, u32[]{:S(2)}) collective-permute-start(bf16[128,6144]{1,0:T(8,128)(2,1)S(1)} %pad_maximum_fusion.refs_0_), channel_id=1, source_target_pairs={{64,0},{3,1},{66,2},{5,3},{68,4},{7,5},{70,6},{1,7},{72,8},{11,9},... | collective-permute-start | bytes 4718600 | tf_op jit(solution)/shard_map/ppermute | solution.py:21
  28.1 1.8 %collective-permute-start.3 = (bf16[128,6144]{1,0:T(8,128)(2,1)S(1)}, bf16[128,6144]{1,0:T(8,128)(2,1)S(1)}, u32[]{:S(2)}, u32[]{:S(2)}) collective-permute-start(bf16[128,6144]{1,0:T(8,128)(2,1)S(1)} %pad_maximum_fusion.refs_0_), channel_id=1, source_target_pairs={{128,0},{5,1},{130,2},{7,3},{132,4},{1,5},{134,6},{3,7},{136,8},{1... | collective-permute-start | bytes 4718600 | tf_op jit(solution)/shard_map/ppermute | solution.py:21
  29.9 16.6 %collective-permute-done.5.refs_3_ = bf16[128,6144]{1,0:T(8,128)(2,1)S(1)} collective-permute-done((bf16[128,6144]{1,0:T(8,128)(2,1)S(1)}, bf16[128,6144]{1,0:T(8,128)(2,1)S(1)}, u32[]{:S(2)}, u32[]{:S(2)}) %collective-permute-start.5) | collective-permute-done | bytes 1572896 | tf_op jit(solution)/shard_map/ppermute | solution.py:21
  46.5 0.0 copy-start
  46.5 1.1 copy-done
  47.7 15.3 %collective-permute-done.4.refs_2_ = bf16[128,6144]{1,0:T(8,128)(2,1)S(1)} collective-permute-done((bf16[128,6144]{1,0:T(8,128)(2,1)S(1)}, bf16[128,6144]{1,0:T(8,128)(2,1)S(1)}, u32[]{:S(2)}, u32[]{:S(2)}) %collective-permute-start.4) | collective-permute-done | bytes 1572896 | tf_op jit(solution)/shard_map/ppermute | solution.py:21
  63.0 0.0 copy-start.2
  63.0 1.2 copy-done.2
  64.2 0.2 collective-permute-done.3.refs_1_
  64.4 0.0 copy-start.4
  64.4 1.1 copy-done.4
  65.5 0.0 copy-start.1
  65.6 1.4 %copy-done.1 = bf16[128,6144]{1,0:T(8,128)(2,1)S(1)} copy-done((bf16[128,6144]{1,0:T(8,128)(2,1)S(1)}, bf16[128,6144]{1,0:T(8,128)(2,1)}, u32[]{:S(2)}) %copy-start.1) | copy-done | bytes 1572888
  67.0 0.0 copy-start.3
  67.0 1.4 %copy-done.3 = bf16[128,6144]{1,0:T(8,128)(2,1)S(1)} copy-done((bf16[128,6144]{1,0:T(8,128)(2,1)S(1)}, bf16[128,6144]{1,0:T(8,128)(2,1)}, u32[]{:S(2)}) %copy-start.3) | copy-done | bytes 1572888
  68.4 0.0 copy-start.5
  68.4 1.4 %copy-done.5 = bf16[128,6144]{1,0:T(8,128)(2,1)S(1)} copy-done((bf16[128,6144]{1,0:T(8,128)(2,1)S(1)}, bf16[128,6144]{1,0:T(8,128)(2,1)}, u32[]{:S(2)}) %copy-start.5) | copy-done | bytes 1572888
  69.8 8.4 %shard_map.42 = (f32[128,2048]{1,0:T(8,128)S(1)}, f32[128,2048]{1,0:T(8,128)S(1)}, f32[128,2048]{1,0:T(8,128)}, f32[128,2048]{1,0:T(8,128)}, f32[16,8,128]{2,1,0:T(8,128)}) custom-call(bf16[128,6144]{1,0:T(8,128)(2,1)S(1)} %pad_maximum_fusion.refs_0_, bf16[128,6144]{1,0:T(8,128)(2,1)S(1)} %copy-done.5, bf16[128,6144]{1,0:T(8,128)(2,1)S(1)} %copy-done.3, ...), custom_call_target="tpu_custom_call" | custom-call | flops 4294967296 | bytes 6291456 | tf_op jit(solution)/shard_map/pallas_call | solution.py:77
  78.2 3.2 %collective-permute-start.6 = (f32[128,2048]{1,0:T(8,128)S(1)}, f32[128,2048]{1,0:T(8,128)}, u32[]{:S(2)}, u32[]{:S(2)}) collective-permute-start(f32[128,2048]{1,0:T(8,128)S(1)} %get-tuple-element.9), channel_id=1, source_target_pairs={{128,0},{5,1},{130,2},{7,3},{132,4},{1,5},{134,6},{3,7},{136,8},{1... | collective-permute-start | bytes 3145736 | tf_op jit(solution)/shard_map/ppermute | solution.py:21
  81.4 1.2 collective-permute-start.7
  82.6 2.0 %collective-permute-start.8 = (f32[128,2048]{1,0:T(8,128)}, f32[128,2048]{1,0:T(8,128)}, u32[]{:S(2)}, u32[]{:S(2)}) collective-permute-start(f32[128,2048]{1,0:T(8,128)} %get-tuple-element.15), channel_id=1, source_target_pairs={{64,0},{3,1},{66,2},{5,3},{68,4},{7,5},{70,6},{1,7},{72,8},{11,9},... | collective-permute-start | bytes 3145736 | tf_op jit(solution)/shard_map/ppermute | solution.py:21
  84.6 10.2 %collective-permute-done.6 = f32[128,2048]{1,0:T(8,128)} collective-permute-done((f32[128,2048]{1,0:T(8,128)S(1)}, f32[128,2048]{1,0:T(8,128)}, u32[]{:S(2)}, u32[]{:S(2)}) %collective-permute-start.6) | collective-permute-done | bytes 1048608 | tf_op jit(solution)/shard_map/ppermute | solution.py:21
  94.8 8.5 %all-to-all-start = ((f32[16,8,128]{2,1,0:T(8,128)}), f32[16,8,128]{2,1,0:T(8,128)S(1)}, u32[]{:S(2)}, u32[]{:S(2)}) async-start(f32[16,8,128]{2,1,0:T(8,128)} %get-tuple-element.11), calls=%async_computation | async-start | bytes 131072 | tf_op jit(solution)/shard_map/all_to_all | solution.py:117
  103.3 2.6 %collective-permute-done.7 = f32[128,2048]{1,0:T(8,128)} collective-permute-done((f32[128,2048]{1,0:T(8,128)}, f32[128,2048]{1,0:T(8,128)}, u32[]{:S(2)}, u32[]{:S(2)}) %collective-permute-start.7) | collective-permute-done | bytes 1048608 | tf_op jit(solution)/shard_map/ppermute | solution.py:21
  105.9 0.8 collective-permute-done.8
  106.7 2.1 %add_add_fusion = f32[128,2048]{1,0:T(8,128)S(1)} fusion(f32[128,2048]{1,0:T(8,128)} %collective-permute-done.8, f32[128,2048]{1,0:T(8,128)} %collective-permute-done.7, f32[128,2048]{1,0:T(8,128)S(1)} %get-tuple-element.12, f32[128,2048]{1,0:T(8,128)} %collective-permute-done.6), kind=kLoop, calls=%fused_computation.1 | loop fusion | flops 786432 | bytes 5242880 | tf_op jit(solution)/shard_map/add | solution.py:110
  108.9 0.1 fusion.2
  108.9 3.8 %collective-permute-start.9 = (f32[32,2048]{1,0:T(8,128)S(1)}, f32[32,2048]{1,0:T(8,128)S(1)}, u32[]{:S(2)}, u32[]{:S(2)}) collective-permute-start(f32[32,2048]{1,0:T(8,128)S(1)} %get-tuple-element.16), channel_id=1, source_target_pairs={{4,0},{129,1},{6,2},{131,3},{0,4},{133,5},{2,6},{135,7},{12,8},{13... | collective-permute-start | bytes 786440 | tf_op jit(solution)/shard_map/ppermute | solution.py:21
  112.7 0.0 collective-permute-start.11
  112.7 2.0 %collective-permute-start.10 = (f32[32,2048]{1,0:T(8,128)S(1)}, f32[32,2048]{1,0:T(8,128)S(1)}, u32[]{:S(2)}, u32[]{:S(2)}) collective-permute-start(f32[32,2048]{1,0:T(8,128)S(1)} %get-tuple-element.18), channel_id=1, source_target_pairs={{6,0},{193,1},{0,2},{195,3},{2,4},{197,5},{4,6},{199,7},{14,8},{20... | collective-permute-start | bytes 786440 | tf_op jit(solution)/shard_map/ppermute | solution.py:21
  114.8 0.0 all-to-all-done
  114.8 11.7 %all_to_all.10 = f32[16,8,128]{2,1,0:T(8,128)S(1)} all-to-all(f32[16,8,128]{2,1,0:T(8,128)S(1)} %broadcast_in_dim.2), channel_id=1, replica_groups=mesh['y'=4,'zl'=4,'zh'=2,'x'=4,'core'=2] {'y','x'}, dimensions={0} | all-to-all | bytes 131072 | tf_op jit(solution)/shard_map/all_to_all | solution.py:119
  126.4 0.6 slice_reduce_fusion
  127.7 0.0 collective-permute-done.9
  127.7 0.0 collective-permute-done.11
  127.7 0.0 collective-permute-done.10
  127.7 0.8 fusion.1
  (3 shorter events, 0.0 us)
Async XLA Ops:
  7.2 58.4 %all-gather.2.cloned.1.call-start = ((), (), s32[]{:S(2)}) async-start(), calls=%async_computation.2 | async-start | bytes 6684672 | tf_op jit(solution)/shard_map/all_gather | solution.py:100
  9.0 8.3 %collective-permute-start.2 = (bf16[32,6144]{1,0:T(8,128)(2,1)}, bf16[32,6144]{1,0:T(8,128)(2,1)S(1)}, u32[]{:S(2)}, u32[]{:S(2)}) collective-permute-start(bf16[32,6144]{1,0:T(8,128)(2,1)} %shard_map.41), channel_id=1, source_target_pairs={{6,0},{193,1},{0,2},{195,3},{2,4},{197,5},{4,6},{199,7},{14,8},{20... | collective-permute-start | bytes 1179656 | tf_op jit(solution)/shard_map/ppermute | solution.py:21
  10.6 8.0 %collective-permute-start.1 = (bf16[32,6144]{1,0:T(8,128)(2,1)}, bf16[32,6144]{1,0:T(8,128)(2,1)S(1)}, u32[]{:S(2)}, u32[]{:S(2)}) collective-permute-start(bf16[32,6144]{1,0:T(8,128)(2,1)} %shard_map.41), channel_id=1, source_target_pairs={{2,0},{65,1},{4,2},{67,3},{6,4},{69,5},{0,6},{71,7},{10,8},{73,9},... | collective-permute-start | bytes 1179656 | tf_op jit(solution)/shard_map/ppermute | solution.py:21
  11.5 12.2 %collective-permute-start = (bf16[32,6144]{1,0:T(8,128)(2,1)}, bf16[32,6144]{1,0:T(8,128)(2,1)S(1)}, u32[]{:S(2)}, u32[]{:S(2)}) collective-permute-start(bf16[32,6144]{1,0:T(8,128)(2,1)} %shard_map.41), channel_id=1, source_target_pairs={{4,0},{129,1},{6,2},{131,3},{0,4},{133,5},{2,6},{135,7},{12,8},{13... | collective-permute-start | bytes 1179656 | tf_op jit(solution)/shard_map/ppermute | solution.py:21
  24.8 21.7 %collective-permute-start.5 = (bf16[128,6144]{1,0:T(8,128)(2,1)S(1)}, bf16[128,6144]{1,0:T(8,128)(2,1)S(1)}, u32[]{:S(2)}, u32[]{:S(2)}) collective-permute-start(bf16[128,6144]{1,0:T(8,128)(2,1)S(1)} %pad_maximum_fusion.refs_0_), channel_id=1, source_target_pairs={{192,0},{7,1},{194,2},{1,3},{196,4},{3,5},{198,6},{5,7},{200,8},{1... | collective-permute-start | bytes 4718600 | tf_op jit(solution)/shard_map/ppermute | solution.py:21
  26.3 36.7 %collective-permute-start.4 = (bf16[128,6144]{1,0:T(8,128)(2,1)S(1)}, bf16[128,6144]{1,0:T(8,128)(2,1)S(1)}, u32[]{:S(2)}, u32[]{:S(2)}) collective-permute-start(bf16[128,6144]{1,0:T(8,128)(2,1)S(1)} %pad_maximum_fusion.refs_0_), channel_id=1, source_target_pairs={{64,0},{3,1},{66,2},{5,3},{68,4},{7,5},{70,6},{1,7},{72,8},{11,9},... | collective-permute-start | bytes 4718600 | tf_op jit(solution)/shard_map/ppermute | solution.py:21
  28.1 36.3 %collective-permute-start.3 = (bf16[128,6144]{1,0:T(8,128)(2,1)S(1)}, bf16[128,6144]{1,0:T(8,128)(2,1)S(1)}, u32[]{:S(2)}, u32[]{:S(2)}) collective-permute-start(bf16[128,6144]{1,0:T(8,128)(2,1)S(1)} %pad_maximum_fusion.refs_0_), channel_id=1, source_target_pairs={{128,0},{5,1},{130,2},{7,3},{132,4},{1,5},{134,6},{3,7},{136,8},{1... | collective-permute-start | bytes 4718600 | tf_op jit(solution)/shard_map/ppermute | solution.py:21
  46.5 1.1 copy-start
  63.0 1.2 copy-start.2
  64.4 1.2 copy-start.4
  65.5 1.4 %copy-start.1 = (bf16[128,6144]{1,0:T(8,128)(2,1)S(1)}, bf16[128,6144]{1,0:T(8,128)(2,1)}, u32[]{:S(2)}) copy-start(bf16[128,6144]{1,0:T(8,128)(2,1)} %copy-done) | copy-start | bytes 4718596
  67.0 1.4 %copy-start.3 = (bf16[128,6144]{1,0:T(8,128)(2,1)S(1)}, bf16[128,6144]{1,0:T(8,128)(2,1)}, u32[]{:S(2)}) copy-start(bf16[128,6144]{1,0:T(8,128)(2,1)} %copy-done.2) | copy-start | bytes 4718596
  68.4 1.4 %copy-start.5 = (bf16[128,6144]{1,0:T(8,128)(2,1)S(1)}, bf16[128,6144]{1,0:T(8,128)(2,1)}, u32[]{:S(2)}) copy-start(bf16[128,6144]{1,0:T(8,128)(2,1)} %copy-done.4) | copy-start | bytes 4718596
  78.2 16.6 %collective-permute-start.6 = (f32[128,2048]{1,0:T(8,128)S(1)}, f32[128,2048]{1,0:T(8,128)}, u32[]{:S(2)}, u32[]{:S(2)}) collective-permute-start(f32[128,2048]{1,0:T(8,128)S(1)} %get-tuple-element.9), channel_id=1, source_target_pairs={{128,0},{5,1},{130,2},{7,3},{132,4},{1,5},{134,6},{3,7},{136,8},{1... | collective-permute-start | bytes 3145736 | tf_op jit(solution)/shard_map/ppermute | solution.py:21
  81.4 24.5 %collective-permute-start.7 = (f32[128,2048]{1,0:T(8,128)}, f32[128,2048]{1,0:T(8,128)}, u32[]{:S(2)}, u32[]{:S(2)}) collective-permute-start(f32[128,2048]{1,0:T(8,128)} %get-tuple-element.14), channel_id=1, source_target_pairs={{192,0},{7,1},{194,2},{1,3},{196,4},{3,5},{198,6},{5,7},{200,8},{1... | collective-permute-start | bytes 3145736 | tf_op jit(solution)/shard_map/ppermute | solution.py:21
  82.6 24.2 %collective-permute-start.8 = (f32[128,2048]{1,0:T(8,128)}, f32[128,2048]{1,0:T(8,128)}, u32[]{:S(2)}, u32[]{:S(2)}) collective-permute-start(f32[128,2048]{1,0:T(8,128)} %get-tuple-element.15), channel_id=1, source_target_pairs={{64,0},{3,1},{66,2},{5,3},{68,4},{7,5},{70,6},{1,7},{72,8},{11,9},... | collective-permute-start | bytes 3145736 | tf_op jit(solution)/shard_map/ppermute | solution.py:21
  94.8 20.0 %all-to-all-start = ((f32[16,8,128]{2,1,0:T(8,128)}), f32[16,8,128]{2,1,0:T(8,128)S(1)}, u32[]{:S(2)}, u32[]{:S(2)}) async-start(f32[16,8,128]{2,1,0:T(8,128)} %get-tuple-element.11), calls=%async_computation | async-start | bytes 131072 | tf_op jit(solution)/shard_map/all_to_all | solution.py:117
  108.9 18.8 %collective-permute-start.9 = (f32[32,2048]{1,0:T(8,128)S(1)}, f32[32,2048]{1,0:T(8,128)S(1)}, u32[]{:S(2)}, u32[]{:S(2)}) collective-permute-start(f32[32,2048]{1,0:T(8,128)S(1)} %get-tuple-element.16), channel_id=1, source_target_pairs={{4,0},{129,1},{6,2},{131,3},{0,4},{133,5},{2,6},{135,7},{12,8},{13... | collective-permute-start | bytes 786440 | tf_op jit(solution)/shard_map/ppermute | solution.py:21
  112.7 15.0 %collective-permute-start.11 = (f32[32,2048]{1,0:T(8,128)S(1)}, f32[32,2048]{1,0:T(8,128)S(1)}, u32[]{:S(2)}, u32[]{:S(2)}) collective-permute-start(f32[32,2048]{1,0:T(8,128)S(1)} %get-tuple-element.17), channel_id=1, source_target_pairs={{2,0},{65,1},{4,2},{67,3},{6,4},{69,5},{0,6},{71,7},{10,8},{73,9},... | collective-permute-start | bytes 786440 | tf_op jit(solution)/shard_map/ppermute | solution.py:21
  112.7 15.0 %collective-permute-start.10 = (f32[32,2048]{1,0:T(8,128)S(1)}, f32[32,2048]{1,0:T(8,128)S(1)}, u32[]{:S(2)}, u32[]{:S(2)}) collective-permute-start(f32[32,2048]{1,0:T(8,128)S(1)} %get-tuple-element.18), channel_id=1, source_target_pairs={{6,0},{193,1},{0,2},{195,3},{2,4},{197,5},{4,6},{199,7},{14,8},{20... | collective-permute-start | bytes 786440 | tf_op jit(solution)/shard_map/ppermute | solution.py:21
Sparse Core Ops, SparseCore 0:
  9.8 48.9 all-gather.1

commit v5 on v4

v5 whole, which is shorter than its diff:
```python
import jax
import jax.numpy as jnp
from jax import lax
from jax.experimental import pallas as pl
from jax.experimental.pallas import tpu as pltpu
from jax.sharding import Mesh, PartitionSpec as P

AXES = ("y", "zl", "zh", "x", "core")
SIZES = (4, 4, 2, 4, 2)
STRIDES = dict(zip(AXES, (64, 16, 8, 2, 1)))
DEPTH = 1024
EXTRA = 16


def shift(value, axes, step):
    pairs = []
    for target in range(256):
        stride = STRIDES[axes[target % 2]]
        place = target // stride % 4
        pairs.append((target + ((place + step) % 4 - place) * stride, target))
    return lax.ppermute(value, AXES, pairs)


def join_kernel(student_ref, teacher_ref, both_ref):
    width = student_ref.shape[1]
    both_ref[:, :width] = student_ref[...]
    both_ref[:, width:] = teacher_ref[...]


def join(student, teacher):
    texts, total = student.shape[0], student.shape[1] + teacher.shape[1]
    return pl.pallas_call(
        join_kernel, out_shape=jax.ShapeDtypeStruct((texts, total), student.dtype)
    )(student, teacher)


def excess_kernel(*refs):
    pieces, rows_ref, outs = refs[:8], refs[8], refs[9:12]
    own_ref, squares_ref, cols, rows, total, rounded, sems = refs[12:]
    height = pieces[0].shape[0]
    count = own_ref.shape[0]
    width = outs[0].shape[1]
    steps = rows.shape[0]
    copies = []
    for k in range(steps):
        block = pl.ds(k * DEPTH, DEPTH)
        moves = [(rows_ref.at[:, block], rows.at[k])]
        for i, piece in enumerate(pieces):
            moves.append((piece.at[:, block], cols.at[k, pl.ds(i * height, height)]))
        copies.append(
            [pltpu.make_async_copy(a, b, sems.at[k, i]) for i, (a, b) in enumerate(moves)]
        )
        for copy in copies[-1]:
            copy.start()
    for k in range(steps):
        for copy in copies[k]:
            copy.wait()
        product = lax.dot_general(
            cols[k], rows[k], (((1,), (1,)), ((), ())), preferred_element_type=jnp.float32
        )
        if k == 0:
            total[...] = product
        elif k * DEPTH < width:
            total[...] += product
        else:
            total[...] -= product
    excess = total[...]
    rounded[...] = excess.astype(rounded.dtype)
    squares = jnp.sum(jnp.sum(excess * excess, axis=0, keepdims=True), axis=1, keepdims=True)
    squares_ref[...] = jnp.broadcast_to(squares[None], squares_ref.shape)
    own_ref[...] = rounded[3 * count :]
    largest = [jnp.full((1, 1), 1e-36, jnp.float32)] * 3
    for k in range(width // DEPTH):
        place = slice(k * DEPTH, (k + 1) * DEPTH)
        product = jnp.dot(rounded[: 3 * count], rows[k], preferred_element_type=jnp.float32)
        for i, out in enumerate(outs):
            part = product[i * count : (i + 1) * count]
            out[:count, place] = part
            most = jnp.max(jnp.max(jnp.abs(part), axis=0, keepdims=True), axis=1, keepdims=True)
            largest[i] = jnp.maximum(largest[i], most)
    for most, out in zip(largest, outs):
        power = jnp.minimum(jnp.floor(14.0 - jnp.log2(most)), 120.0)
        out[:count] = out[:count] * jnp.exp2(power)
        out[count:] = jnp.broadcast_to(power, (EXTRA, width))


def pulls(pieces, rows, student_width):
    texts, width = rows.shape
    count = 2 * pieces[0].shape[0]
    inside = pl.BlockSpec(memory_space=pltpu.VMEM)
    scaled = jax.ShapeDtypeStruct((count + EXTRA, student_width), jnp.float32)
    return pl.pallas_call(
        excess_kernel,
        in_specs=[pl.BlockSpec(memory_space=pltpu.HBM)] * 9,
        out_specs=(inside,) * 5,
        out_shape=(scaled,) * 3
        + (
            jax.ShapeDtypeStruct((count, texts), jnp.bfloat16),
            jax.ShapeDtypeStruct((16, 8, 128), jnp.float32),
        ),
        scratch_shapes=[
            pltpu.VMEM((width // DEPTH, 4 * count, DEPTH), jnp.bfloat16),
            pltpu.VMEM((width // DEPTH, texts, DEPTH), jnp.bfloat16),
            pltpu.VMEM((4 * count, texts), jnp.float32),
            pltpu.VMEM((4 * count, texts), jnp.bfloat16),
            pltpu.SemaphoreType.DMA((width // DEPTH, 9)),
        ],
        compiler_params=pltpu.CompilerParams(vmem_limit_bytes=VMEM_LIMIT),
        cost_estimate=pl.CostEstimate(
            flops=8 * count * texts * (width + student_width),
            bytes_accessed=2 * (4 * count + texts) * width,
            transcendentals=0,
        ),
    )(*pieces, rows)


VMEM_LIMIT = 56 * 1024 * 1024


def shards(student, teacher):
    texts, width = student.shape
    both = join(student, teacher)
    rows = lax.all_gather(both, ("zh", "zl", "core"), axis=0, tiled=True)
    near, far = ("x", "y"), ("y", "x")
    first = jnp.concatenate([both, shift(both, near, 1)])
    second = jnp.concatenate([shift(both, near, 3), shift(both, near, 2)])
    first_up, first_down = shift(first, far, 1), shift(first, far, 3)
    second_down, second_up = shift(second, far, 3), shift(second, far, 1)
    pieces = (shift(first_up, far, 1), shift(second_down, far, 3))
    pieces += (first_up, second_up, first_down, second_down, first, second)
    *scaled, own, squares = pulls(pieces, rows, width)
    *sent, own, squares = lax.optimization_barrier(
        [term.astype(jnp.float16) for term in scaled] + [own, squares]
    )
    returned = [shift(term, far, -k) for term, k in zip(sent, (2, 1, 3))]
    returned[1], squares = lax.optimization_barrier((returned[1], squares))
    partial_term = jnp.dot(own, rows[:, :width], preferred_element_type=jnp.float32)
    count = own.shape[0]
    for term in returned:
        scale = jnp.exp2(-term[count : count + 1].astype(jnp.float32))
        partial_term += term[:count].astype(jnp.float32) * scale
    blocks = partial_term.reshape(4, texts, width)
    pulled = blocks[0]
    for i, k in ((3, 2), (1, 1), (2, 3)):
        pulled += shift(blocks[i], near, -k)

    line = jnp.sum(
        lax.all_to_all(squares, ("zh", "zl", "core"), 0, 0), axis=0, keepdims=True
    )
    plane = lax.all_to_all(jnp.broadcast_to(line, (16, 8, 128)), ("y", "x"), 0, 0)
    distance = jnp.sum(plane[:, 0, 0]) / jnp.float32(texts * 256)
    return distance, pulled


def solution(mesh):
    fine = Mesh(mesh.devices.reshape(SIZES), AXES)
    spec = P(AXES, None)
    return jax.shard_map(
        shards, mesh=fine, in_specs=(spec, spec), out_specs=(P(), spec), check_vma=False
    )
```

time: 138 us -> 124 us (0.90)
  waiting for transfers between devices: 55.9 us -> 38.7 us
  starting transfers between devices: 30.3 us -> 37.8 us
  local copies, waits for them, and re-layouts: 7.81 us -> 1.44 us
  matrix products: 0 us -> 2.33 us
    ppermute x12 -> x15, waiting for transfers between devices: 55.9 us -> 33.6 us  [shift(): return lax.ppermute(value, AXES, pairs)]
    ppermute x12 -> x15, starting transfers between devices: 21.8 us -> 33.3 us  [shift(): return lax.ppermute(value, AXES, pairs)]
    unnamed x12 -> x19, local copies, waits for them, and re-layouts: 7.75 us -> 1.35 us
    all_gather x1, waiting for transfers between devices: 0.01 us -> 5.09 us  [shards(): rows = lax.all_gather(both, ('zh', 'zl', 'core'), axis=0, tiled=True)]
    all_to_all x1, starting transfers between devices: 8.53 us -> 4.47 us  [shards(): lax.all_to_all(squares, ('zh', 'zl', 'core'), 0, 0)]
    dot_general x0 -> x1, matrix products: none -> 2.33 us  [shards(): jnp.dot(own, rows[:, :width], preferred_element_type=jnp.float32)]
    add x2 -> x1, other arithmetic: 2.88 us -> 0.76 us  [shards(): pulled += shift(blocks[i], near, -k)]
    convert_element_type x0 -> x3, other arithmetic: none -> 1.63 us  [shards(): term.astype(jnp.float16)]
  transfers between devices with their start and end apart: 14 -> 17, of which waited for: 9 -> 10; matrix products, arithmetic and copies ran while one was open for 3% -> 3% of each run, Pallas kernels for 0% -> 0%
where the time goes in v5:
time: 124 us; the launch traced here: 123 us
  waiting for transfers between devices  38.7 us (31%)
  starting transfers between devices  37.8 us (30%)
  between operations  16 us (13%)
  blocking collectives  11.8 us (10%)
  Pallas kernels  11 us (9%)
  other arithmetic  4.13 us (3%)
  matrix products  2.33 us (2%)
  local copies, waits for them, and re-layouts  1.44 us (1%)
    ppermute x15, waiting for transfers between devices, shift(): return lax.ppermute(value, AXES, pairs)  33.6 us
    ppermute x15, starting transfers between devices, shift(): return lax.ppermute(value, AXES, pairs)  33.3 us
    all_to_all x1, blocking collectives, shards(): lax.all_to_all(jnp.broadcast_to(line, (16, 8, 128)), ('y', 'x'), 0, 0)  11.8 us
    pallas_call x1, Pallas kernels, pulls(): pl.pallas_call(excess_kernel, in_specs=[pl.BlockSpec(memory_space=pltpu.H...  9.22 us
    all_gather x1, waiting for transfers between devices, shards(): rows = lax.all_gather(both, ('zh', 'zl', 'core'), axis=0, tiled=True)  5.09 us
    all_to_all x1, starting transfers between devices, shards(): lax.all_to_all(squares, ('zh', 'zl', 'core'), 0, 0)  4.47 us
  transfers between devices with their start and end apart: 17, of which 10 were waited for; matrix products, arithmetic and copies ran while one was open for 3% of the time, Pallas kernels for 0%

profile of v5, /device:TPU:2, one launch (start us, length us, event | category | flops | bytes accessed | tf_op | source)
XLA Modules:
  0.0 123.2 jit_solution(6517564753320459700)
XLA Ops:
  7.2 0.0 all-gather.2.cloned.1.call-start
  7.2 1.8 %shard_map.41 = bf16[32,6144]{1,0:T(8,128)(2,1)} custom-call(bf16[32,2048]{1,0:T(8,128)(2,1)} %student_ref.1, bf16[32,4096]{1,0:T(8,128)(2,1)} %teacher_ref.1), custom_call_target="tpu_custom_call" | custom-call | tf_op jit(solution)/shard_map/pallas_call | solution.py:32
  9.0 0.0 all-gather.2.cloned.1.call-update
  9.0 2.3 %collective-permute-start = (bf16[32,6144]{1,0:T(8,128)(2,1)}, bf16[32,6144]{1,0:T(8,128)(2,1)S(1)}, u32[]{:S(2)}, u32[]{:S(2)}) collective-permute-start(bf16[32,6144]{1,0:T(8,128)(2,1)} %shard_map.41), channel_id=1, source_target_pairs={{2,0},{65,1},{4,2},{67,3},{6,4},{69,5},{0,6},{71,7},{10,8},{73,9},... | collective-permute-start | bytes 1179656 | tf_op jit(solution)/shard_map/ppermute | solution.py:21
  11.4 0.7 collective-permute-start.4
  12.1 1.8 %collective-permute-start.3 = (bf16[32,6144]{1,0:T(8,128)(2,1)}, bf16[32,6144]{1,0:T(8,128)(2,1)S(1)}, u32[]{:S(2)}, u32[]{:S(2)}) collective-permute-start(bf16[32,6144]{1,0:T(8,128)(2,1)} %shard_map.41), channel_id=1, source_target_pairs={{6,0},{193,1},{0,2},{195,3},{2,4},{197,5},{4,6},{199,7},{14,8},{20... | collective-permute-start | bytes 1179656 | tf_op jit(solution)/shard_map/ppermute | solution.py:21
  13.9 3.2 %collective-permute-done = bf16[32,6144]{1,0:T(8,128)(2,1)S(1)} collective-permute-done((bf16[32,6144]{1,0:T(8,128)(2,1)}, bf16[32,6144]{1,0:T(8,128)(2,1)S(1)}, u32[]{:S(2)}, u32[]{:S(2)}) %collective-permute-start) | collective-permute-done | bytes 393248 | tf_op jit(solution)/shard_map/ppermute | solution.py:21
  17.1 1.0 pad_maximum_fusion.refs_6_
  18.2 3.1 %collective-permute-start.1 = (bf16[64,6144]{1,0:T(8,128)(2,1)S(1)}, bf16[64,6144]{1,0:T(8,128)(2,1)S(1)}, u32[]{:S(2)}, u32[]{:S(2)}) collective-permute-start(bf16[64,6144]{1,0:T(8,128)(2,1)S(1)} %pad_maximum_fusion.refs_6_), channel_id=1, source_target_pairs={{64,0},{3,1},{66,2},{5,3},{68,4},{7,5},{70,6},{1,7},{72,8},{11,9},... | collective-permute-start | bytes 2359304 | tf_op jit(solution)/shard_map/ppermute | solution.py:21
  21.3 2.2 %collective-permute-done.3 = bf16[32,6144]{1,0:T(8,128)(2,1)S(1)} collective-permute-done((bf16[32,6144]{1,0:T(8,128)(2,1)}, bf16[32,6144]{1,0:T(8,128)(2,1)S(1)}, u32[]{:S(2)}, u32[]{:S(2)}) %collective-permute-start.3) | collective-permute-done | bytes 393248 | tf_op jit(solution)/shard_map/ppermute | solution.py:21
  23.5 0.0 collective-permute-done.4
  23.5 1.9 %collective-permute-start.5 = (bf16[64,6144]{1,0:T(8,128)(2,1)S(1)}, bf16[64,6144]{1,0:T(8,128)(2,1)S(1)}, u32[]{:S(2)}, u32[]{:S(2)}) collective-permute-start(bf16[64,6144]{1,0:T(8,128)(2,1)S(1)} %constant_dynamic-update-slice_fusion.refs_7_), channel_id=1, source_target_pairs={{192,0},{7,1},{194,2},{1,3},{196,4},{3,5},{198,6},{5,7},{200,8},{1... | collective-permute-start | bytes 2359304 | tf_op jit(solution)/shard_map/ppermute | solution.py:21
  25.4 1.6 %collective-permute-start.8 = (bf16[64,6144]{1,0:T(8,128)(2,1)S(1)}, bf16[64,6144]{1,0:T(8,128)(2,1)S(1)}, u32[]{:S(2)}, u32[]{:S(2)}) collective-permute-start(bf16[64,6144]{1,0:T(8,128)(2,1)S(1)} %pad_maximum_fusion.refs_6_), channel_id=1, source_target_pairs={{192,0},{7,1},{194,2},{1,3},{196,4},{3,5},{198,6},{5,7},{200,8},{1... | collective-permute-start | bytes 2359304 | tf_op jit(solution)/shard_map/ppermute | solution.py:21
  27.0 1.7 %collective-permute-start.7 = (bf16[64,6144]{1,0:T(8,128)(2,1)S(1)}, bf16[64,6144]{1,0:T(8,128)(2,1)S(1)}, u32[]{:S(2)}, u32[]{:S(2)}) collective-permute-start(bf16[64,6144]{1,0:T(8,128)(2,1)S(1)} %constant_dynamic-update-slice_fusion.refs_7_), channel_id=1, source_target_pairs={{64,0},{3,1},{66,2},{5,3},{68,4},{7,5},{70,6},{1,7},{72,8},{11,9},... | collective-permute-start | bytes 2359304 | tf_op jit(solution)/shard_map/ppermute | solution.py:21
  28.6 2.2 %collective-permute-done.1.refs_2_ = bf16[64,6144]{1,0:T(8,128)(2,1)S(1)} collective-permute-done((bf16[64,6144]{1,0:T(8,128)(2,1)S(1)}, bf16[64,6144]{1,0:T(8,128)(2,1)S(1)}, u32[]{:S(2)}, u32[]{:S(2)}) %collective-permute-start.1) | collective-permute-done | bytes 786464 | tf_op jit(solution)/shard_map/ppermute | solution.py:21
  30.8 3.7 %collective-permute-start.2 = (bf16[64,6144]{1,0:T(8,128)(2,1)S(1)}, bf16[64,6144]{1,0:T(8,128)(2,1)S(1)}, u32[]{:S(2)}, u32[]{:S(2)}) collective-permute-start(bf16[64,6144]{1,0:T(8,128)(2,1)S(1)} %collective-permute-done.1.refs_2_), channel_id=1, source_target_pairs={{64,0},{3,1},{66,2},{5,3},{68,4},{7,5},{70,6},{1,7},{72,8},{11,9},... | collective-permute-start | bytes 2359304 | tf_op jit(solution)/shard_map/ppermute | solution.py:21
  34.5 2.3 %collective-permute-done.5.refs_5_ = bf16[64,6144]{1,0:T(8,128)(2,1)S(1)} collective-permute-done((bf16[64,6144]{1,0:T(8,128)(2,1)S(1)}, bf16[64,6144]{1,0:T(8,128)(2,1)S(1)}, u32[]{:S(2)}, u32[]{:S(2)}) %collective-permute-start.5) | collective-permute-done | bytes 786464 | tf_op jit(solution)/shard_map/ppermute | solution.py:21
  36.8 0.6 collective-permute-start.6
  37.4 7.9 %collective-permute-done.8.refs_4_ = bf16[64,6144]{1,0:T(8,128)(2,1)S(1)} collective-permute-done((bf16[64,6144]{1,0:T(8,128)(2,1)S(1)}, bf16[64,6144]{1,0:T(8,128)(2,1)S(1)}, u32[]{:S(2)}, u32[]{:S(2)}) %collective-permute-start.8) | collective-permute-done | bytes 786464 | tf_op jit(solution)/shard_map/ppermute | solution.py:21
  45.2 0.0 collective-permute-done.7.refs_3_
  45.2 2.4 %collective-permute-done.2.refs_0_ = bf16[64,6144]{1,0:T(8,128)(2,1)S(1)} collective-permute-done((bf16[64,6144]{1,0:T(8,128)(2,1)S(1)}, bf16[64,6144]{1,0:T(8,128)(2,1)S(1)}, u32[]{:S(2)}, u32[]{:S(2)}) %collective-permute-start.2) | collective-permute-done | bytes 786464 | tf_op jit(solution)/shard_map/ppermute | solution.py:21
  47.6 0.9 copy-done.8
  48.5 5.2 %collective-permute-done.6.refs_1_ = bf16[64,6144]{1,0:T(8,128)(2,1)} collective-permute-done((bf16[64,6144]{1,0:T(8,128)(2,1)S(1)}, bf16[64,6144]{1,0:T(8,128)(2,1)}, u32[]{:S(2)}, u32[]{:S(2)}) %collective-permute-start.6) | collective-permute-done | bytes 786464 | tf_op jit(solution)/shard_map/ppermute | solution.py:21
  53.8 5.1 %all-gather.2.cloned.1.call-done.refs_8_ = bf16[512,6144]{1,0:T(8,128)(2,1)} async-done(((bf16[32,6144]{1,0:T(8,128)(2,1)}), bf16[512,6144]{1,0:T(8,128)(2,1)}) %all-gather.2.cloned.1.call-update) | async-done | bytes 6291472 | tf_op jit(solution)/shard_map/all_gather | solution.py:123
  58.9 9.2 %shard_map.42 = (f32[144,2048]{1,0:T(8,128)}, f32[144,2048]{1,0:T(8,128)}, f32[144,2048]{1,0:T(8,128)}, bf16[128,512]{1,0:T(8,128)(2,1)}, f32[16,8,128]{2,1,0:T(8,128)}) custom-call(bf16[64,6144]{1,0:T(8,128)(2,1)} %copy-done.8, bf16[64,6144]{1,0:T(8,128)(2,1)} %collective-permute-done.6.refs_1_, bf16[64,6144]{1,0:T(8,128)(2,1)} %copy-done.4, ...), custom_call_target="tpu_custom_call" | custom-call | flops 4294967296 | bytes 12582912 | tf_op jit(solution)/shard_map/pallas_call | solution.py:92
  68.1 1.5 %convert_element_type.27 = f16[144,2048]{1,0:T(8,128)(2,1)S(1)} convert(f32[144,2048]{1,0:T(8,128)} %get-tuple-element.14) | non-fusion elementwise | flops 294912 | bytes 1769472 | tf_op jit(solution)/shard_map/convert_element_type | solution.py:133
  69.6 0.1 copy-done.1
  69.7 0.1 convert_element_type.28
  69.8 0.3 copy-done
  70.1 0.1 convert_element_type.29
  70.2 1.8 %collective-permute-start.9 = (f16[144,2048]{1,0:T(8,128)(2,1)S(1)}, f16[144,2048]{1,0:T(8,128)(2,1)S(1)}, u32[]{:S(2)}, u32[]{:S(2)}) collective-permute-start(f16[144,2048]{1,0:T(8,128)(2,1)S(1)} %convert_element_type.28), channel_id=1, source_target_pairs={{192,0},{7,1},{194,2},{1,3},{196,4},{3,5},{198,6},{5,7},{200,8},{1... | collective-permute-start | bytes 1769480 | tf_op jit(solution)/shard_map/ppermute | solution.py:21
  71.9 2.7 %collective-permute-start.10 = (f16[144,2048]{1,0:T(8,128)(2,1)S(1)}, f16[144,2048]{1,0:T(8,128)(2,1)S(1)}, u32[]{:S(2)}, u32[]{:S(2)}) collective-permute-start(f16[144,2048]{1,0:T(8,128)(2,1)S(1)} %convert_element_type.27), channel_id=1, source_target_pairs={{128,0},{5,1},{130,2},{7,3},{132,4},{1,5},{134,6},{3,7},{136,8},{1... | collective-permute-start | bytes 1769480 | tf_op jit(solution)/shard_map/ppermute | solution.py:21
  74.6 1.4 %collective-permute-start.11 = (f16[144,2048]{1,0:T(8,128)(2,1)S(1)}, f16[144,2048]{1,0:T(8,128)(2,1)S(1)}, u32[]{:S(2)}, u32[]{:S(2)}) collective-permute-start(f16[144,2048]{1,0:T(8,128)(2,1)S(1)} %convert_element_type.29), channel_id=1, source_target_pairs={{64,0},{3,1},{66,2},{5,3},{68,4},{7,5},{70,6},{1,7},{72,8},{11,9},... | collective-permute-start | bytes 1769480 | tf_op jit(solution)/shard_map/ppermute | solution.py:21
  76.1 5.4 %collective-permute-done.9 = f16[144,2048]{1,0:T(8,128)(2,1)S(1)} collective-permute-done((f16[144,2048]{1,0:T(8,128)(2,1)S(1)}, f16[144,2048]{1,0:T(8,128)(2,1)S(1)}, u32[]{:S(2)}, u32[]{:S(2)}) %collective-permute-start.9) | collective-permute-done | bytes 589856 | tf_op jit(solution)/shard_map/ppermute | solution.py:21
  81.5 4.5 %all-to-all-start = ((f32[16,8,128]{2,1,0:T(8,128)}), f32[16,8,128]{2,1,0:T(8,128)S(1)}, u32[]{:S(2)}, u32[]{:S(2)}) async-start(f32[16,8,128]{2,1,0:T(8,128)} %get-tuple-element.21), calls=%async_computation | async-start | bytes 131072 | tf_op jit(solution)/shard_map/all_to_all | solution.py:148
  86.0 2.8 %collective-permute-done.10 = f16[144,2048]{1,0:T(8,128)(2,1)S(1)} collective-permute-done((f16[144,2048]{1,0:T(8,128)(2,1)S(1)}, f16[144,2048]{1,0:T(8,128)(2,1)S(1)}, u32[]{:S(2)}, u32[]{:S(2)}) %collective-permute-start.10) | collective-permute-done | bytes 589856 | tf_op jit(solution)/shard_map/ppermute | solution.py:21
  88.8 0.0 collective-permute-done.11
  88.9 2.3 %multiply_add_fusion = f32[128,2048]{1,0:T(8,128)S(1)} fusion(f16[144,2048]{1,0:T(8,128)(2,1)S(1)} %collective-permute-done.11, f16[144,2048]{1,0:T(8,128)(2,1)S(1)} %collective-permute-done.10, f32[2048]{0:T(1024)S(1)} %bitcast.6, f32[2048]{0:T(1024)S(1)} %bitcast.4, f16[144,2048]{1,0:T(8,128)(2,1)S(1)} %collective-permute-done.9, f32[2048]{0:T(1024)S(1)} %bitcast.5, ...), kind=kOutput, calls=%fused_computation.2 | convolution fusion | flops 270794752 | bytes 4874240 | tf_op jit(solution)/shard_map/dot_general | solution.py:137
  91.2 0.1 fusion.10
  91.2 8.0 %collective-permute-start.12 = (f32[32,2048]{1,0:T(8,128)S(1)}, f32[32,2048]{1,0:T(8,128)S(1)}, u32[]{:S(2)}, u32[]{:S(2)}) collective-permute-start(f32[32,2048]{1,0:T(8,128)S(1)} %get-tuple-element.26), channel_id=1, source_target_pairs={{4,0},{129,1},{6,2},{131,3},{0,4},{133,5},{2,6},{135,7},{12,8},{13... | collective-permute-start | bytes 786440 | tf_op jit(solution)/shard_map/ppermute | solution.py:21
  99.3 0.0 collective-permute-start.14
  99.3 2.0 %collective-permute-start.13 = (f32[32,2048]{1,0:T(8,128)S(1)}, f32[32,2048]{1,0:T(8,128)S(1)}, u32[]{:S(2)}, u32[]{:S(2)}) collective-permute-start(f32[32,2048]{1,0:T(8,128)S(1)} %get-tuple-element.28), channel_id=1, source_target_pairs={{6,0},{193,1},{0,2},{195,3},{2,4},{197,5},{4,6},{199,7},{14,8},{20... | collective-permute-start | bytes 786440 | tf_op jit(solution)/shard_map/ppermute | solution.py:21
  101.3 0.0 all-to-all-done
  101.4 11.8 %all_to_all.10 = f32[16,8,128]{2,1,0:T(8,128)S(1)} all-to-all(f32[16,8,128]{2,1,0:T(8,128)S(1)} %broadcast_in_dim.2), channel_id=1, replica_groups=mesh['y'=4,'zl'=4,'zh'=2,'x'=4,'core'=2] {'y','x'}, dimensions={0} | all-to-all | bytes 131072 | tf_op jit(solution)/shard_map/all_to_all | solution.py:150
  113.2 0.6 slice_reduce_fusion
  114.5 0.0 collective-permute-done.12
  114.5 0.0 collective-permute-done.13
  114.5 0.8 fusion.3
  (23 shorter events, 0.2 us)
Async XLA Ops:
  7.2 51.7 %all-gather.2.cloned.1.call-start = ((), (), s32[]{:S(2)}) async-start(), calls=%async_computation.2 | async-start | bytes 6684672 | tf_op jit(solution)/shard_map/all_gather | solution.py:123
  9.0 8.1 %collective-permute-start = (bf16[32,6144]{1,0:T(8,128)(2,1)}, bf16[32,6144]{1,0:T(8,128)(2,1)S(1)}, u32[]{:S(2)}, u32[]{:S(2)}) collective-permute-start(bf16[32,6144]{1,0:T(8,128)(2,1)} %shard_map.41), channel_id=1, source_target_pairs={{2,0},{65,1},{4,2},{67,3},{6,4},{69,5},{0,6},{71,7},{10,8},{73,9},... | collective-permute-start | bytes 1179656 | tf_op jit(solution)/shard_map/ppermute | solution.py:21
  11.4 12.1 %collective-permute-start.4 = (bf16[32,6144]{1,0:T(8,128)(2,1)}, bf16[32,6144]{1,0:T(8,128)(2,1)S(1)}, u32[]{:S(2)}, u32[]{:S(2)}) collective-permute-start(bf16[32,6144]{1,0:T(8,128)(2,1)} %shard_map.41), channel_id=1, source_target_pairs={{4,0},{129,1},{6,2},{131,3},{0,4},{133,5},{2,6},{135,7},{12,8},{13... | collective-permute-start | bytes 1179656 | tf_op jit(solution)/shard_map/ppermute | solution.py:21
  12.1 11.4 %collective-permute-start.3 = (bf16[32,6144]{1,0:T(8,128)(2,1)}, bf16[32,6144]{1,0:T(8,128)(2,1)S(1)}, u32[]{:S(2)}, u32[]{:S(2)}) collective-permute-start(bf16[32,6144]{1,0:T(8,128)(2,1)} %shard_map.41), channel_id=1, source_target_pairs={{6,0},{193,1},{0,2},{195,3},{2,4},{197,5},{4,6},{199,7},{14,8},{20... | collective-permute-start | bytes 1179656 | tf_op jit(solution)/shard_map/ppermute | solution.py:21
  18.2 40.7 %copy-start.2 = (bf16[64,6144]{1,0:T(8,128)(2,1)}, bf16[64,6144]{1,0:T(8,128)(2,1)S(1)}, u32[]{:S(2)}) copy-start(bf16[64,6144]{1,0:T(8,128)(2,1)S(1)} %pad_maximum_fusion.refs_6_) | copy-start | bytes 2359300
  18.2 12.6 %collective-permute-start.1 = (bf16[64,6144]{1,0:T(8,128)(2,1)S(1)}, bf16[64,6144]{1,0:T(8,128)(2,1)S(1)}, u32[]{:S(2)}, u32[]{:S(2)}) collective-permute-start(bf16[64,6144]{1,0:T(8,128)(2,1)S(1)} %pad_maximum_fusion.refs_6_), channel_id=1, source_target_pairs={{64,0},{3,1},{66,2},{5,3},{68,4},{7,5},{70,6},{1,7},{72,8},{11,9},... | collective-permute-start | bytes 2359304 | tf_op jit(solution)/shard_map/ppermute | solution.py:21
  23.5 35.3 %copy-start.3 = (bf16[64,6144]{1,0:T(8,128)(2,1)}, bf16[64,6144]{1,0:T(8,128)(2,1)S(1)}, u32[]{:S(2)}) copy-start(bf16[64,6144]{1,0:T(8,128)(2,1)S(1)} %constant_dynamic-update-slice_fusion.refs_7_) | copy-start | bytes 2359300
  23.5 13.3 %collective-permute-start.5 = (bf16[64,6144]{1,0:T(8,128)(2,1)S(1)}, bf16[64,6144]{1,0:T(8,128)(2,1)S(1)}, u32[]{:S(2)}, u32[]{:S(2)}) collective-permute-start(bf16[64,6144]{1,0:T(8,128)(2,1)S(1)} %constant_dynamic-update-slice_fusion.refs_7_), channel_id=1, source_target_pairs={{192,0},{7,1},{194,2},{1,3},{196,4},{3,5},{198,6},{5,7},{200,8},{1... | collective-permute-start | bytes 2359304 | tf_op jit(solution)/shard_map/ppermute | solution.py:21
  25.4 19.8 %collective-permute-start.8 = (bf16[64,6144]{1,0:T(8,128)(2,1)S(1)}, bf16[64,6144]{1,0:T(8,128)(2,1)S(1)}, u32[]{:S(2)}, u32[]{:S(2)}) collective-permute-start(bf16[64,6144]{1,0:T(8,128)(2,1)S(1)} %pad_maximum_fusion.refs_6_), channel_id=1, source_target_pairs={{192,0},{7,1},{194,2},{1,3},{196,4},{3,5},{198,6},{5,7},{200,8},{1... | collective-permute-start | bytes 2359304 | tf_op jit(solution)/shard_map/ppermute | solution.py:21
  27.0 18.3 %collective-permute-start.7 = (bf16[64,6144]{1,0:T(8,128)(2,1)S(1)}, bf16[64,6144]{1,0:T(8,128)(2,1)S(1)}, u32[]{:S(2)}, u32[]{:S(2)}) collective-permute-start(bf16[64,6144]{1,0:T(8,128)(2,1)S(1)} %constant_dynamic-update-slice_fusion.refs_7_), channel_id=1, source_target_pairs={{64,0},{3,1},{66,2},{5,3},{68,4},{7,5},{70,6},{1,7},{72,8},{11,9},... | collective-permute-start | bytes 2359304 | tf_op jit(solution)/shard_map/ppermute | solution.py:21
  30.8 28.1 %copy-start.4 = (bf16[64,6144]{1,0:T(8,128)(2,1)}, bf16[64,6144]{1,0:T(8,128)(2,1)S(1)}, u32[]{:S(2)}) copy-start(bf16[64,6144]{1,0:T(8,128)(2,1)S(1)} %collective-permute-done.1.refs_2_) | copy-start | bytes 2359300
  30.8 16.9 %collective-permute-start.2 = (bf16[64,6144]{1,0:T(8,128)(2,1)S(1)}, bf16[64,6144]{1,0:T(8,128)(2,1)S(1)}, u32[]{:S(2)}, u32[]{:S(2)}) collective-permute-start(bf16[64,6144]{1,0:T(8,128)(2,1)S(1)} %collective-permute-done.1.refs_2_), channel_id=1, source_target_pairs={{64,0},{3,1},{66,2},{5,3},{68,4},{7,5},{70,6},{1,7},{72,8},{11,9},... | collective-permute-start | bytes 2359304 | tf_op jit(solution)/shard_map/ppermute | solution.py:21
  36.8 22.1 %copy-start.5 = (bf16[64,6144]{1,0:T(8,128)(2,1)}, bf16[64,6144]{1,0:T(8,128)(2,1)S(1)}, u32[]{:S(2)}) copy-start(bf16[64,6144]{1,0:T(8,128)(2,1)S(1)} %collective-permute-done.5.refs_5_) | copy-start | bytes 2359300
  36.8 17.0 %collective-permute-start.6 = (bf16[64,6144]{1,0:T(8,128)(2,1)S(1)}, bf16[64,6144]{1,0:T(8,128)(2,1)}, u32[]{:S(2)}, u32[]{:S(2)}) collective-permute-start(bf16[64,6144]{1,0:T(8,128)(2,1)S(1)} %collective-permute-done.5.refs_5_), channel_id=1, source_target_pairs={{192,0},{7,1},{194,2},{1,3},{196,4},{3,5},{198,6},{5,7},{200,8},{1... | collective-permute-start | bytes 2359304 | tf_op jit(solution)/shard_map/ppermute | solution.py:21
  45.2 2.4 %copy-start.6 = (bf16[64,6144]{1,0:T(8,128)(2,1)}, bf16[64,6144]{1,0:T(8,128)(2,1)S(1)}, u32[]{:S(2)}) copy-start(bf16[64,6144]{1,0:T(8,128)(2,1)S(1)} %collective-permute-done.8.refs_4_) | copy-start | bytes 2359300
  45.2 2.4 %copy-start.7 = (bf16[64,6144]{1,0:T(8,128)(2,1)}, bf16[64,6144]{1,0:T(8,128)(2,1)S(1)}, u32[]{:S(2)}) copy-start(bf16[64,6144]{1,0:T(8,128)(2,1)S(1)} %collective-permute-done.7.refs_3_) | copy-start | bytes 2359300
  47.6 0.9 copy-start.8
  68.1 1.6 %copy-start.1 = (f32[144,2048]{1,0:T(8,128)S(1)}, f32[144,2048]{1,0:T(8,128)}, u32[]{:S(2)}) copy-start(f32[144,2048]{1,0:T(8,128)} %get-tuple-element.15) | copy-start | bytes 3538948
  68.1 2.0 %copy-start = (f32[144,2048]{1,0:T(8,128)S(1)}, f32[144,2048]{1,0:T(8,128)}, u32[]{:S(2)}) copy-start(f32[144,2048]{1,0:T(8,128)} %get-tuple-element.16) | copy-start | bytes 3538948
  70.2 11.4 %collective-permute-start.9 = (f16[144,2048]{1,0:T(8,128)(2,1)S(1)}, f16[144,2048]{1,0:T(8,128)(2,1)S(1)}, u32[]{:S(2)}, u32[]{:S(2)}) collective-permute-start(f16[144,2048]{1,0:T(8,128)(2,1)S(1)} %convert_element_type.28), channel_id=1, source_target_pairs={{192,0},{7,1},{194,2},{1,3},{196,4},{3,5},{198,6},{5,7},{200,8},{1... | collective-permute-start | bytes 1769480 | tf_op jit(solution)/shard_map/ppermute | solution.py:21
  71.9 16.9 %collective-permute-start.10 = (f16[144,2048]{1,0:T(8,128)(2,1)S(1)}, f16[144,2048]{1,0:T(8,128)(2,1)S(1)}, u32[]{:S(2)}, u32[]{:S(2)}) collective-permute-start(f16[144,2048]{1,0:T(8,128)(2,1)S(1)} %convert_element_type.27), channel_id=1, source_target_pairs={{128,0},{5,1},{130,2},{7,3},{132,4},{1,5},{134,6},{3,7},{136,8},{1... | collective-permute-start | bytes 1769480 | tf_op jit(solution)/shard_map/ppermute | solution.py:21
  74.6 14.2 %collective-permute-start.11 = (f16[144,2048]{1,0:T(8,128)(2,1)S(1)}, f16[144,2048]{1,0:T(8,128)(2,1)S(1)}, u32[]{:S(2)}, u32[]{:S(2)}) collective-permute-start(f16[144,2048]{1,0:T(8,128)(2,1)S(1)} %convert_element_type.29), channel_id=1, source_target_pairs={{64,0},{3,1},{66,2},{5,3},{68,4},{7,5},{70,6},{1,7},{72,8},{11,9},... | collective-permute-start | bytes 1769480 | tf_op jit(solution)/shard_map/ppermute | solution.py:21
  81.5 19.8 %all-to-all-start = ((f32[16,8,128]{2,1,0:T(8,128)}), f32[16,8,128]{2,1,0:T(8,128)S(1)}, u32[]{:S(2)}, u32[]{:S(2)}) async-start(f32[16,8,128]{2,1,0:T(8,128)} %get-tuple-element.21), calls=%async_computation | async-start | bytes 131072 | tf_op jit(solution)/shard_map/all_to_all | solution.py:148
  91.2 23.2 %collective-permute-start.12 = (f32[32,2048]{1,0:T(8,128)S(1)}, f32[32,2048]{1,0:T(8,128)S(1)}, u32[]{:S(2)}, u32[]{:S(2)}) collective-permute-start(f32[32,2048]{1,0:T(8,128)S(1)} %get-tuple-element.26), channel_id=1, source_target_pairs={{4,0},{129,1},{6,2},{131,3},{0,4},{133,5},{2,6},{135,7},{12,8},{13... | collective-permute-start | bytes 786440 | tf_op jit(solution)/shard_map/ppermute | solution.py:21
  99.3 15.2 %collective-permute-start.14 = (f32[32,2048]{1,0:T(8,128)S(1)}, f32[32,2048]{1,0:T(8,128)S(1)}, u32[]{:S(2)}, u32[]{:S(2)}) collective-permute-start(f32[32,2048]{1,0:T(8,128)S(1)} %get-tuple-element.27), channel_id=1, source_target_pairs={{2,0},{65,1},{4,2},{67,3},{6,4},{69,5},{0,6},{71,7},{10,8},{73,9},... | collective-permute-start | bytes 786440 | tf_op jit(solution)/shard_map/ppermute | solution.py:21
  99.3 15.2 %collective-permute-start.13 = (f32[32,2048]{1,0:T(8,128)S(1)}, f32[32,2048]{1,0:T(8,128)S(1)}, u32[]{:S(2)}, u32[]{:S(2)}) collective-permute-start(f32[32,2048]{1,0:T(8,128)S(1)} %get-tuple-element.28), channel_id=1, source_target_pairs={{6,0},{193,1},{0,2},{195,3},{2,4},{197,5},{4,6},{199,7},{14,8},{20... | collective-permute-start | bytes 786440 | tf_op jit(solution)/shard_map/ppermute | solution.py:21
Sparse Core Ops, SparseCore 0:
  9.8 48.9 all-gather.1

commit v6 on v5

v6 whole, which is shorter than its diff:
```python
import jax
import jax.numpy as jnp
from jax import lax
from jax.experimental import pallas as pl
from jax.experimental.pallas import tpu as pltpu
from jax.sharding import Mesh, PartitionSpec as P

AXES = ("y", "zl", "zh", "x", "core")
SIZES = (4, 4, 2, 4, 2)
STRIDES = dict(zip(AXES, (64, 16, 8, 2, 1)))
DEPTH = 1024
EXTRA = 16


def shift(value, axes, step):
    pairs = []
    for target in range(256):
        stride = STRIDES[axes[target % 2]]
        place = target // stride % 4
        pairs.append((target + ((place + step) % 4 - place) * stride, target))
    return lax.ppermute(value, AXES, pairs)


def round_z(value):
    pairs = []
    for target in range(256):
        z = target // 16 % 4 + target // 8 % 2 * 4
        source = (z - 1 + target % 2 * 2) % 8
        pairs.append((target + (source % 4 - z % 4) * 16 + (source // 4 - z // 4) * 8, target))
    return lax.ppermute(value, AXES, pairs)


def other_core(value):
    return lax.ppermute(value, "core", [(0, 1), (1, 0)])


def join_kernel(student_ref, teacher_ref, both_ref):
    width = student_ref.shape[1]
    both_ref[:, :width] = student_ref[...]
    both_ref[:, width:] = teacher_ref[...]


def join(student, teacher):
    texts, total = student.shape[0], student.shape[1] + teacher.shape[1]
    return pl.pallas_call(
        join_kernel, out_shape=jax.ShapeDtypeStruct((texts, total), student.dtype)
    )(student, teacher)


def excess_kernel(*refs):
    pieces, lines, outs = refs[:8], refs[8:17], refs[17:20]
    own_ref, squares_ref, rows, total, rounded = refs[20:]
    count = own_ref.shape[0]
    width = outs[0].shape[1]
    for k in range(pieces[0].shape[1] // DEPTH):
        place = slice(k * DEPTH, (k + 1) * DEPTH)
        cols = jnp.concatenate([piece[:, place] for piece in pieces])
        line = jnp.concatenate([piece[:, place] for piece in lines])
        product = lax.dot_general(
            cols, line, (((1,), (1,)), ((), ())), preferred_element_type=jnp.float32
        )
        if k * DEPTH < width:
            rows[k] = line
        if k == 0:
            total[...] = product
        elif k * DEPTH < width:
            total[...] += product
        else:
            total[...] -= product
    excess = total[...]
    rounded[...] = excess.astype(rounded.dtype)
    squares = jnp.sum(jnp.sum(excess * excess, axis=0, keepdims=True), axis=1, keepdims=True)
    squares_ref[...] = jnp.broadcast_to(squares, squares_ref.shape)
    own_ref[...] = rounded[3 * count :]
    largest = [jnp.full((1, 1), 1e-36, jnp.float32)] * 3
    for k in range(width // DEPTH):
        place = slice(k * DEPTH, (k + 1) * DEPTH)
        product = jnp.dot(rounded[: 3 * count], rows[k], preferred_element_type=jnp.float32)
        for i, out in enumerate(outs):
            part = product[i * count : (i + 1) * count]
            out[:count, place] = part
            most = jnp.max(jnp.max(jnp.abs(part), axis=0, keepdims=True), axis=1, keepdims=True)
            largest[i] = jnp.maximum(largest[i], most)
    for most, out in zip(largest, outs):
        power = jnp.minimum(jnp.floor(14.0 - jnp.log2(most)), 120.0)
        out[:count] = out[:count] * jnp.exp2(power)
        out[count:] = jnp.broadcast_to(power, (EXTRA, width))


def own_kernel(own_ref, squares_ref, *refs):
    lines, out_ref, spread_ref = refs[:9], refs[9], refs[10]
    line = jnp.concatenate([piece[...] for piece in lines])
    out_ref[...] = jnp.dot(own_ref[...], line, preferred_element_type=jnp.float32)
    spread_ref[...] = jnp.broadcast_to(squares_ref[...][None], spread_ref.shape)


def pulls(pieces, lines, student_width):
    width = lines[0].shape[1]
    texts = sum(line.shape[0] for line in lines)
    count = 2 * pieces[0].shape[0]
    inside = pl.BlockSpec(memory_space=pltpu.VMEM)
    scaled = jax.ShapeDtypeStruct((count + EXTRA, student_width), jnp.float32)
    return pl.pallas_call(
        excess_kernel,
        in_specs=[inside] * 17,
        out_specs=(inside,) * 5,
        out_shape=(scaled,) * 3
        + (
            jax.ShapeDtypeStruct((count, texts), jnp.bfloat16),
            jax.ShapeDtypeStruct((8, 128), jnp.float32),
        ),
        scratch_shapes=[
            pltpu.VMEM((student_width // DEPTH, texts, DEPTH), jnp.bfloat16),
            pltpu.VMEM((4 * count, texts), jnp.float32),
            pltpu.VMEM((4 * count, texts), jnp.bfloat16),
        ],
        compiler_params=pltpu.CompilerParams(vmem_limit_bytes=VMEM_LIMIT),
        cost_estimate=pl.CostEstimate(
            flops=8 * count * texts * (width + student_width),
            bytes_accessed=2 * (4 * count + texts) * width,
            transcendentals=0,
        ),
    )(*pieces, *lines)


def own_pull(own, squares, lines, student_width):
    count, texts = own.shape
    whole = lambda shape: pl.BlockSpec(shape, lambda i: (0,) * len(shape))
    return pl.pallas_call(
        own_kernel,
        grid=(1,),
        in_specs=[whole(own.shape), whole(squares.shape)]
        + [whole((line.shape[0], student_width)) for line in lines],
        out_specs=(whole((count, student_width)), whole((64,) + squares.shape)),
        out_shape=(
            jax.ShapeDtypeStruct((count, student_width), jnp.float32),
            jax.ShapeDtypeStruct((64,) + squares.shape, jnp.float32),
        ),
        compiler_params=pltpu.CompilerParams(vmem_limit_bytes=VMEM_LIMIT),
        cost_estimate=pl.CostEstimate(
            flops=2 * count * texts * student_width,
            bytes_accessed=2 * texts * student_width,
            transcendentals=0,
        ),
    )(own, squares, *lines)


VMEM_LIMIT = 24 * 1024 * 1024


def shards(student, teacher):
    texts, width = student.shape
    both = join(student, teacher)
    pair = jnp.concatenate([both, other_core(both)])
    lines = [pair]
    for step in range(4):
        arrived = round_z(lines[max(2 * step - 1, 0)][: pair.shape[0] if step < 3 else texts])
        lines += [arrived, other_core(arrived)]
    near, far = ("x", "y"), ("y", "x")
    first = jnp.concatenate([both, shift(both, near, 1)])
    second = jnp.concatenate([shift(both, near, 3), shift(both, near, 2)])
    first_up, first_down = shift(first, far, 1), shift(first, far, 3)
    second_down, second_up = shift(second, far, 3), shift(second, far, 1)
    pieces = (shift(first_up, far, 1), shift(second_down, far, 3))
    pieces += (first_up, second_up, first_down, second_down, first, second)
    *scaled, own, squares = pulls(pieces, lines, width)
    sent = [term.astype(jnp.float16) for term in scaled]
    returned = [shift(term, far, -k) for term, k in zip(sent, (2, 1, 3))]
    own, squares = lax.optimization_barrier((own, squares, *sent))[:2]
    partial_term, squares = own_pull(own, squares, lines, width)
    count = own.shape[0]
    for term in returned:
        scale = jnp.exp2(-term[count : count + 1].astype(jnp.float32))
        partial_term += term[:count].astype(jnp.float32) * scale
    blocks = partial_term.reshape(4, texts, width)
    pulled = blocks[0]
    for i, k in ((3, 2), (1, 1), (2, 3)):
        pulled += shift(blocks[i], near, -k)

    total = jnp.sum(lax.all_to_all(squares, ("y", "zh", "zl", "core"), 0, 0), axis=0)
    ring = [shift(total, ("x", "x"), k) for k in (1, 2, 3)]
    total = (total + ring[1]) + (ring[0] + ring[2])
    return total[0, 0] / jnp.float32(texts * 256), pulled


def solution(mesh):
    fine = Mesh(mesh.devices.reshape(SIZES), AXES)
    spec = P(AXES, None)
    return jax.shard_map(
        shards, mesh=fine, in_specs=(spec, spec), out_specs=(P(), spec), check_vma=False
    )
```

time: 124 us -> 115 us (0.927)
  waiting for transfers between devices: 38.7 us -> 53.7 us
  between operations: 16 us -> 2.61 us
  blocking collectives: 11.8 us -> 0 us
  starting transfers between devices: 37.8 us -> 42.7 us
  other arithmetic: 4.13 us -> 7.87 us
  Pallas kernels: 11 us -> 7.44 us
  matrix products: 2.33 us -> 0 us
    ppermute x0 -> x9, waiting for transfers between devices: none -> 34.6 us  [the longest x4 34.6 us: round_z(): return lax.ppermute(value, AXES, pairs)]
    ppermute x15 -> x18, waiting for transfers between devices: 33.6 us -> 19.1 us  [shift(): return lax.ppermute(value, AXES, pairs)]
    all_to_all x1 -> x0, blocking collectives: 11.8 us -> none  [shards(): lax.all_to_all(jnp.broadcast_to(line, (16, 8, 128)), ('y', 'x'), 0, 0)]
    all_to_all x1, starting transfers between devices: 4.47 us -> 9.73 us  [shards(): lax.all_to_all(squares, ('y', 'zh', 'zl', 'core'), 0, 0)]
    all_gather x1 -> x0, waiting for transfers between devices: 5.09 us -> none  [shards(): rows = lax.all_gather(both, ('zh', 'zl', 'core'), axis=0, tiled=True)]
    pallas_call x1 -> x2, Pallas kernels: 9.22 us -> 5.64 us  [the longest x1 4.6 us: pulls(): pl.pallas_call(excess_kernel, in_specs=[inside] * 17, out_specs=(inside,)...]
    ppermute x15 -> x18, starting transfers between devices: 33.3 us -> 30.3 us  [shift(): return lax.ppermute(value, AXES, pairs)]
    ppermute x0 -> x9, starting transfers between devices: none -> 2.67 us  [the longest x4 2.08 us: round_z(): return lax.ppermute(value, AXES, pairs)]
  transfers between devices with their start and end apart: 17 -> 28, of which waited for: 10 -> 9; matrix products, arithmetic and copies ran while one was open for 3% -> 6% of each run, Pallas kernels for 0% -> 1%
where the time goes in v6:
time: 115 us
  waiting for transfers between devices  53.7 us (47%)
  starting transfers between devices  42.7 us (37%)
  other arithmetic  7.87 us (7%)
  Pallas kernels  7.44 us (6%)
  between operations  2.61 us (2%)
    ppermute x4, waiting for transfers between devices, round_z(): return lax.ppermute(value, AXES, pairs)  34.6 us
    ppermute x18, starting transfers between devices, shift(): return lax.ppermute(value, AXES, pairs)  30.3 us
    ppermute x18, waiting for transfers between devices, shift(): return lax.ppermute(value, AXES, pairs)  19.1 us
    all_to_all x1, starting transfers between devices, shards(): lax.all_to_all(squares, ('y', 'zh', 'zl', 'core'), 0, 0)  9.73 us
    pallas_call x1, Pallas kernels, pulls(): pl.pallas_call(excess_kernel, in_specs=[inside] * 17, out_specs=(inside,)...  4.6 us
    exp2 x3, other arithmetic, shards(): scale = jnp.exp2(-term[count:count + 1].astype(jnp.float32))  2.33 us
  transfers between devices with their start and end apart: 28, of which 9 were waited for; matrix products, arithmetic and copies ran while one was open for 6% of the time, Pallas kernels for 1%

profile of v6, /device:TPU:2, one launch (start us, length us, event | category | flops | bytes accessed | tf_op | source)
XLA Modules:
  0.0 115.0 jit_solution(16140162461591889170)
XLA Ops:
  0.6 1.8 %shard_map.41 = bf16[32,6144]{1,0:T(8,128)(2,1)} custom-call(bf16[32,2048]{1,0:T(8,128)(2,1)} %student_ref.1, bf16[32,4096]{1,0:T(8,128)(2,1)} %teacher_ref.1), custom_call_target="tpu_custom_call" | custom-call | tf_op jit(solution)/shard_map/pallas_call | solution.py:45
  2.4 2.3 %collective-permute-start = (bf16[32,6144]{1,0:T(8,128)(2,1)}, bf16[32,6144]{1,0:T(8,128)(2,1)S(1)}, u32[]{:S(2)}, u32[]{:S(2)}) collective-permute-start(bf16[32,6144]{1,0:T(8,128)(2,1)} %shard_map.41), channel_id=1, source_target_pairs={{2,0},{65,1},{4,2},{67,3},{6,4},{69,5},{0,6},{71,7},{10,8},{73,9},... | collective-permute-start | bytes 1179656 | tf_op jit(solution)/shard_map/ppermute | solution.py:21
  4.7 5.7 %collective-permute-done = bf16[32,6144]{1,0:T(8,128)(2,1)S(1)} collective-permute-done((bf16[32,6144]{1,0:T(8,128)(2,1)}, bf16[32,6144]{1,0:T(8,128)(2,1)S(1)}, u32[]{:S(2)}, u32[]{:S(2)}) %collective-permute-start) | collective-permute-done | bytes 393248 | tf_op jit(solution)/shard_map/ppermute | solution.py:21
  10.4 1.1 pad_maximum_fusion
  11.6 2.0 %collective-permute-start.10 = (bf16[64,6144]{1,0:T(8,128)(2,1)S(1)}, bf16[64,6144]{1,0:T(8,128)(2,1)S(1)}, u32[]{:S(2)}, u32[]{:S(2)}) collective-permute-start(bf16[64,6144]{1,0:T(8,128)(2,1)S(1)} %get-tuple-element.23.refs_8_.refs_0_), channel_id=1, source_target_pairs={{56,0},{17,1},{58,2},{19,3},{60,4},{21,5},{62,6},{23,7},{48,8},{25... | collective-permute-start | bytes 2359304 | tf_op jit(solution)/shard_map/ppermute | solution.py:30
  13.6 1.5 %collective-permute-start.3 = (bf16[32,6144]{1,0:T(8,128)(2,1)S(1)}, bf16[32,6144]{1,0:T(8,128)(2,1)S(1)}, u32[]{:S(2)}, u32[]{:S(2)}) collective-permute-start(bf16[32,6144]{1,0:T(8,128)(2,1)S(1)} %copy-done), channel_id=1, source_target_pairs={{6,0},{193,1},{0,2},{195,3},{2,4},{197,5},{4,6},{199,7},{14,8},{20... | collective-permute-start | bytes 1179656 | tf_op jit(solution)/shard_map/ppermute | solution.py:21
  15.1 1.8 %collective-permute-start.4 = (bf16[32,6144]{1,0:T(8,128)(2,1)S(1)}, bf16[32,6144]{1,0:T(8,128)(2,1)S(1)}, u32[]{:S(2)}, u32[]{:S(2)}) collective-permute-start(bf16[32,6144]{1,0:T(8,128)(2,1)S(1)} %copy-done), channel_id=1, source_target_pairs={{4,0},{129,1},{6,2},{131,3},{0,4},{133,5},{2,6},{135,7},{12,8},{13... | collective-permute-start | bytes 1179656 | tf_op jit(solution)/shard_map/ppermute | solution.py:21
  16.9 3.0 %collective-permute-start.1 = (bf16[64,6144]{1,0:T(8,128)(2,1)S(1)}, bf16[64,6144]{1,0:T(8,128)(2,1)S(1)}, u32[]{:S(2)}, u32[]{:S(2)}) collective-permute-start(bf16[64,6144]{1,0:T(8,128)(2,1)S(1)} %get-tuple-element.24.refs_6_), channel_id=1, source_target_pairs={{64,0},{3,1},{66,2},{5,3},{68,4},{7,5},{70,6},{1,7},{72,8},{11,9},... | collective-permute-start | bytes 2359304 | tf_op jit(solution)/shard_map/ppermute | solution.py:21
  19.9 7.6 %collective-permute-done.10.refs_9_.refs_1_ = bf16[64,6144]{1,0:T(8,128)(2,1)S(1)} collective-permute-done((bf16[64,6144]{1,0:T(8,128)(2,1)S(1)}, bf16[64,6144]{1,0:T(8,128)(2,1)S(1)}, u32[]{:S(2)}, u32[]{:S(2)}) %collective-permute-start.10) | collective-permute-done | bytes 786464 | tf_op jit(solution)/shard_map/ppermute | solution.py:30
  27.6 1.7 %collective-permute-start.5 = (bf16[64,6144]{1,0:T(8,128)(2,1)S(1)}, bf16[64,6144]{1,0:T(8,128)(2,1)S(1)}, u32[]{:S(2)}, u32[]{:S(2)}) collective-permute-start(bf16[64,6144]{1,0:T(8,128)(2,1)S(1)} %constant_dynamic-update-slice_fusion.refs_7_), channel_id=1, source_target_pairs={{192,0},{7,1},{194,2},{1,3},{196,4},{3,5},{198,6},{5,7},{200,8},{1... | collective-permute-start | bytes 2359304 | tf_op jit(solution)/shard_map/ppermute | solution.py:21
  29.2 11.5 %collective-permute-done.12.refs_11_.refs_3_ = bf16[64,6144]{1,0:T(8,128)(2,1)S(1)} collective-permute-done((bf16[64,6144]{1,0:T(8,128)(2,1)S(1)}, bf16[64,6144]{1,0:T(8,128)(2,1)S(1)}, u32[]{:S(2)}, u32[]{:S(2)}) %collective-permute-start.12) | collective-permute-done | bytes 786464 | tf_op jit(solution)/shard_map/ppermute | solution.py:30
  40.7 1.6 %collective-permute-start.8 = (bf16[64,6144]{1,0:T(8,128)(2,1)S(1)}, bf16[64,6144]{1,0:T(8,128)(2,1)S(1)}, u32[]{:S(2)}, u32[]{:S(2)}) collective-permute-start(bf16[64,6144]{1,0:T(8,128)(2,1)S(1)} %get-tuple-element.24.refs_6_), channel_id=1, source_target_pairs={{192,0},{7,1},{194,2},{1,3},{196,4},{3,5},{198,6},{5,7},{200,8},{1... | collective-permute-start | bytes 2359304 | tf_op jit(solution)/shard_map/ppermute | solution.py:21
  42.3 1.7 %collective-permute-start.7 = (bf16[64,6144]{1,0:T(8,128)(2,1)S(1)}, bf16[64,6144]{1,0:T(8,128)(2,1)S(1)}, u32[]{:S(2)}, u32[]{:S(2)}) collective-permute-start(bf16[64,6144]{1,0:T(8,128)(2,1)S(1)} %constant_dynamic-update-slice_fusion.refs_7_), channel_id=1, source_target_pairs={{64,0},{3,1},{66,2},{5,3},{68,4},{7,5},{70,6},{1,7},{72,8},{11,9},... | collective-permute-start | bytes 2359304 | tf_op jit(solution)/shard_map/ppermute | solution.py:21
  43.9 2.8 %collective-permute-start.2 = (bf16[64,6144]{1,0:T(8,128)(2,1)S(1)}, bf16[64,6144]{1,0:T(8,128)(2,1)S(1)}, u32[]{:S(2)}, u32[]{:S(2)}) collective-permute-start(bf16[64,6144]{1,0:T(8,128)(2,1)S(1)} %collective-permute-done.1.refs_2_), channel_id=1, source_target_pairs={{64,0},{3,1},{66,2},{5,3},{68,4},{7,5},{70,6},{1,7},{72,8},{11,9},... | collective-permute-start | bytes 2359304 | tf_op jit(solution)/shard_map/ppermute | solution.py:21
  46.7 7.2 %collective-permute-done.14.refs_13_.refs_5_ = bf16[64,6144]{1,0:T(8,128)(2,1)S(1)} collective-permute-done((bf16[64,6144]{1,0:T(8,128)(2,1)S(1)}, bf16[64,6144]{1,0:T(8,128)(2,1)S(1)}, u32[]{:S(2)}, u32[]{:S(2)}) %collective-permute-start.14) | collective-permute-done | bytes 786464 | tf_op jit(solution)/shard_map/ppermute | solution.py:30
  53.9 1.6 %collective-permute-start.6 = (bf16[64,6144]{1,0:T(8,128)(2,1)S(1)}, bf16[64,6144]{1,0:T(8,128)(2,1)S(1)}, u32[]{:S(2)}, u32[]{:S(2)}) collective-permute-start(bf16[64,6144]{1,0:T(8,128)(2,1)S(1)} %collective-permute-done.5.refs_5_), channel_id=1, source_target_pairs={{192,0},{7,1},{194,2},{1,3},{196,4},{3,5},{198,6},{5,7},{200,8},{1... | collective-permute-start | bytes 2359304 | tf_op jit(solution)/shard_map/ppermute | solution.py:21
  55.5 0.1 collective-permute-start.16
  55.6 0.1 collective-permute-start.13
  55.7 0.5 collective-permute-start.15
  56.2 8.4 %collective-permute-done.16.refs_15_.refs_7_ = bf16[32,6144]{1,0:T(8,128)(2,1)S(1)} collective-permute-done((bf16[32,6144]{1,0:T(8,128)(2,1)S(1)}, bf16[32,6144]{1,0:T(8,128)(2,1)S(1)}, u32[]{:S(2)}, u32[]{:S(2)}) %collective-permute-start.16) | collective-permute-done | bytes 393248 | tf_op jit(solution)/shard_map/ppermute | solution.py:30
  64.6 0.0 collective-permute-start.17
  64.6 2.5 %collective-permute-done.6.refs_1_ = bf16[64,6144]{1,0:T(8,128)(2,1)S(1)} collective-permute-done((bf16[64,6144]{1,0:T(8,128)(2,1)S(1)}, bf16[64,6144]{1,0:T(8,128)(2,1)S(1)}, u32[]{:S(2)}, u32[]{:S(2)}) %collective-permute-start.6) | collective-permute-done | bytes 786464 | tf_op jit(solution)/shard_map/ppermute | solution.py:21
  67.1 4.6 %shard_map.42 = (f32[144,2048]{1,0:T(8,128)S(1)}, f32[144,2048]{1,0:T(8,128)S(1)}, f32[144,2048]{1,0:T(8,128)S(1)}, bf16[128,512]{1,0:T(8,128)(2,1)S(1)}, f32[8,128]{1,0:T(8,128)S(1)}) custom-call(bf16[64,6144]{1,0:T(8,128)(2,1)S(1)} %collective-permute-done.2.refs_0_, bf16[64,6144]{1,0:T(8,128)(2,1)S(1)} %collective-permute-done.6.refs_1_, ...), custom_call_target="tpu_custom_call" | custom-call | flops 4294967296 | bytes 12582912 | tf_op jit(solution)/shard_map/pallas_call | solution.py:103
  71.7 0.1 convert_element_type.29
  71.8 1.9 %collective-permute-start.23 = (f16[144,2048]{1,0:T(8,128)(2,1)S(1)}, f16[144,2048]{1,0:T(8,128)(2,1)}, u32[]{:S(2)}, u32[]{:S(2)}) collective-permute-start(f16[144,2048]{1,0:T(8,128)(2,1)S(1)} %convert_element_type.29), channel_id=1, source_target_pairs={{64,0},{3,1},{66,2},{5,3},{68,4},{7,5},{70,6},{1,7},{72,8},{11,9},... | collective-permute-start | bytes 1769480 | tf_op jit(solution)/shard_map/ppermute | solution.py:21
  73.7 0.9 convert_element_type.28
  74.6 0.2 collective-permute-start.22
  74.8 0.9 convert_element_type.27
  75.7 2.1 %collective-permute-start.21 = (f16[144,2048]{1,0:T(8,128)(2,1)}, f16[144,2048]{1,0:T(8,128)(2,1)}, u32[]{:S(2)}, u32[]{:S(2)}) collective-permute-start(f16[144,2048]{1,0:T(8,128)(2,1)} %convert_element_type.27), channel_id=1, source_target_pairs={{128,0},{5,1},{130,2},{7,3},{132,4},{1,5},{134,6},{3,7},{136,8},{1... | collective-permute-start | bytes 1769480 | tf_op jit(solution)/shard_map/ppermute | solution.py:21
  77.8 1.0 shard_map.43
  78.8 9.7 %all-to-all-start = ((f32[64,8,128]{2,1,0:T(8,128)}), f32[64,8,128]{2,1,0:T(8,128)S(1)}, u32[]{:S(2)}, u32[]{:S(2)}) async-start(f32[64,8,128]{2,1,0:T(8,128)} %get-tuple-element.18), calls=%async_computation | async-start | bytes 524288 | tf_op jit(solution)/shard_map/all_to_all | solution.py:180
  88.6 0.8 fusion.4
  89.3 3.0 %collective-permute-done.22 = f16[144,2048]{1,0:T(8,128)(2,1)} collective-permute-done((f16[144,2048]{1,0:T(8,128)(2,1)}, f16[144,2048]{1,0:T(8,128)(2,1)}, u32[]{:S(2)}, u32[]{:S(2)}) %collective-permute-start.22) | collective-permute-done | bytes 589856 | tf_op jit(solution)/shard_map/ppermute | solution.py:21
  92.3 0.8 fusion.7
  93.1 0.8 fusion.10
  93.9 1.7 %multiply_add_fusion = f32[128,2048]{1,0:T(8,128)S(1)} fusion(f32[128,2048]{1,0:T(8,128)S(1)} %get-tuple-element.19, f16[144,2048]{1,0:T(8,128)(2,1)} %collective-permute-done.23, f16[144,2048]{1,0:T(8,128)(2,1)} %collective-permute-done.22, f16[144,2048]{1,0:T(8,128)(2,1)} %collective-permute-done.21, f32[2048]{0:T(1024)S(1)} %bitcast.4, f32[2048]{0:T(1024)S(1)} %bitcast.5, ...), kind=kLoop, calls=%fused_computation | loop fusion | flops 2359296 | bytes 3694592 | tf_op jit(solution)/shard_map/add | solution.py:174
  95.6 0.1 fusion.11
  95.6 3.7 %collective-permute-start.24 = (f32[32,2048]{1,0:T(8,128)S(1)}, f32[32,2048]{1,0:T(8,128)S(1)}, u32[]{:S(2)}, u32[]{:S(2)}) collective-permute-start(f32[32,2048]{1,0:T(8,128)S(1)} %get-tuple-element.20), channel_id=1, source_target_pairs={{4,0},{129,1},{6,2},{131,3},{0,4},{133,5},{2,6},{135,7},{12,8},{13... | collective-permute-start | bytes 786440 | tf_op jit(solution)/shard_map/ppermute | solution.py:21
  99.3 0.2 collective-permute-start.26
  99.6 1.8 %collective-permute-start.25 = (f32[32,2048]{1,0:T(8,128)S(1)}, f32[32,2048]{1,0:T(8,128)S(1)}, u32[]{:S(2)}, u32[]{:S(2)}) collective-permute-start(f32[32,2048]{1,0:T(8,128)S(1)} %get-tuple-element.22), channel_id=1, source_target_pairs={{6,0},{193,1},{0,2},{195,3},{2,4},{197,5},{4,6},{199,7},{14,8},{20... | collective-permute-start | bytes 786440 | tf_op jit(solution)/shard_map/ppermute | solution.py:21
  101.4 0.1 reduce_sum.9
  101.4 0.1 collective-permute-start.20
  101.5 2.0 %collective-permute-start.19 = (f32[8,128]{1,0:T(8,128)S(1)}, f32[8,128]{1,0:T(8,128)S(1)}, u32[]{:S(2)}, u32[]{:S(2)}) collective-permute-start(f32[8,128]{1,0:T(8,128)S(1)} %reduce_sum.9), channel_id=1, source_target_pairs={{2,0},{3,1},{4,2},{5,3},{6,4},{7,5},{0,6},{1,7},{10,8},{11,9},{12,... | collective-permute-start | bytes 12296 | tf_op jit(solution)/shard_map/ppermute | solution.py:21
  103.5 3.3 %collective-permute-done.20 = f32[8,128]{1,0:T(8,128)S(1)} collective-permute-done((f32[8,128]{1,0:T(8,128)S(1)}, f32[8,128]{1,0:T(8,128)S(1)}, u32[]{:S(2)}, u32[]{:S(2)}) %collective-permute-start.20) | collective-permute-done | bytes 4128 | tf_op jit(solution)/shard_map/ppermute | solution.py:21
  106.8 0.5 collective-permute-start.18
  107.3 4.6 %collective-permute-done.18 = f32[8,128]{1,0:T(8,128)S(1)} collective-permute-done((f32[8,128]{1,0:T(8,128)S(1)}, f32[8,128]{1,0:T(8,128)S(1)}, u32[]{:S(2)}, u32[]{:S(2)}) %collective-permute-start.18) | collective-permute-done | bytes 4128 | tf_op jit(solution)/shard_map/ppermute | solution.py:21
  111.9 0.5 slice.41
  113.1 0.8 fusion.1
  (29 shorter events, 0.2 us)
Async XLA Ops:
  2.4 11.1 %copy-start = (bf16[32,6144]{1,0:T(8,128)(2,1)S(1)}, bf16[32,6144]{1,0:T(8,128)(2,1)}, u32[]{:S(2)}) copy-start(bf16[32,6144]{1,0:T(8,128)(2,1)} %shard_map.41) | copy-start | bytes 1179652
  2.4 2.3 %collective-permute-start.9 = (bf16[32,6144]{1,0:T(8,128)(2,1)}, bf16[32,6144]{1,0:T(8,128)(2,1)S(1)}, u32[]{:S(2)}, u32[]{:S(2)}) collective-permute-start(bf16[32,6144]{1,0:T(8,128)(2,1)} %shard_map.41), channel_id=1, source_target_pairs={{0,1},{1,0},{2,3},{3,2},{4,5},{5,4},{6,7},{7,6},{8,9},{9,8},{10,11... | collective-permute-start | bytes 1179656 | tf_op jit(solution)/shard_map/ppermute | solution.py:34
  2.4 8.0 %collective-permute-start = (bf16[32,6144]{1,0:T(8,128)(2,1)}, bf16[32,6144]{1,0:T(8,128)(2,1)S(1)}, u32[]{:S(2)}, u32[]{:S(2)}) collective-permute-start(bf16[32,6144]{1,0:T(8,128)(2,1)} %shard_map.41), channel_id=1, source_target_pairs={{2,0},{65,1},{4,2},{67,3},{6,4},{69,5},{0,6},{71,7},{10,8},{73,9},... | collective-permute-start | bytes 1179656 | tf_op jit(solution)/shard_map/ppermute | solution.py:21
  11.6 15.9 %collective-permute-start.10 = (bf16[64,6144]{1,0:T(8,128)(2,1)S(1)}, bf16[64,6144]{1,0:T(8,128)(2,1)S(1)}, u32[]{:S(2)}, u32[]{:S(2)}) collective-permute-start(bf16[64,6144]{1,0:T(8,128)(2,1)S(1)} %get-tuple-element.23.refs_8_.refs_0_), channel_id=1, source_target_pairs={{56,0},{17,1},{58,2},{19,3},{60,4},{21,5},{62,6},{23,7},{48,8},{25... | collective-permute-start | bytes 2359304 | tf_op jit(solution)/shard_map/ppermute | solution.py:30
  13.6 13.9 %collective-permute-start.3 = (bf16[32,6144]{1,0:T(8,128)(2,1)S(1)}, bf16[32,6144]{1,0:T(8,128)(2,1)S(1)}, u32[]{:S(2)}, u32[]{:S(2)}) collective-permute-start(bf16[32,6144]{1,0:T(8,128)(2,1)S(1)} %copy-done), channel_id=1, source_target_pairs={{6,0},{193,1},{0,2},{195,3},{2,4},{197,5},{4,6},{199,7},{14,8},{20... | collective-permute-start | bytes 1179656 | tf_op jit(solution)/shard_map/ppermute | solution.py:21
  15.1 12.5 %collective-permute-start.4 = (bf16[32,6144]{1,0:T(8,128)(2,1)S(1)}, bf16[32,6144]{1,0:T(8,128)(2,1)S(1)}, u32[]{:S(2)}, u32[]{:S(2)}) collective-permute-start(bf16[32,6144]{1,0:T(8,128)(2,1)S(1)} %copy-done), channel_id=1, source_target_pairs={{4,0},{129,1},{6,2},{131,3},{0,4},{133,5},{2,6},{135,7},{12,8},{13... | collective-permute-start | bytes 1179656 | tf_op jit(solution)/shard_map/ppermute | solution.py:21
  16.9 27.0 %collective-permute-start.1 = (bf16[64,6144]{1,0:T(8,128)(2,1)S(1)}, bf16[64,6144]{1,0:T(8,128)(2,1)S(1)}, u32[]{:S(2)}, u32[]{:S(2)}) collective-permute-start(bf16[64,6144]{1,0:T(8,128)(2,1)S(1)} %get-tuple-element.24.refs_6_), channel_id=1, source_target_pairs={{64,0},{3,1},{66,2},{5,3},{68,4},{7,5},{70,6},{1,7},{72,8},{11,9},... | collective-permute-start | bytes 2359304 | tf_op jit(solution)/shard_map/ppermute | solution.py:21
  27.5 13.2 %collective-permute-start.12 = (bf16[64,6144]{1,0:T(8,128)(2,1)S(1)}, bf16[64,6144]{1,0:T(8,128)(2,1)S(1)}, u32[]{:S(2)}, u32[]{:S(2)}) collective-permute-start(bf16[64,6144]{1,0:T(8,128)(2,1)S(1)} %collective-permute-done.10.refs_9_.refs_1_), channel_id=1, source_target_pairs={{56,0},{17,1},{58,2},{19,3},{60,4},{21,5},{62,6},{23,7},{48,8},{25... | collective-permute-start | bytes 2359304 | tf_op jit(solution)/shard_map/ppermute | solution.py:30
  27.6 16.4 %collective-permute-start.5 = (bf16[64,6144]{1,0:T(8,128)(2,1)S(1)}, bf16[64,6144]{1,0:T(8,128)(2,1)S(1)}, u32[]{:S(2)}, u32[]{:S(2)}) collective-permute-start(bf16[64,6144]{1,0:T(8,128)(2,1)S(1)} %constant_dynamic-update-slice_fusion.refs_7_), channel_id=1, source_target_pairs={{192,0},{7,1},{194,2},{1,3},{196,4},{3,5},{198,6},{5,7},{200,8},{1... | collective-permute-start | bytes 2359304 | tf_op jit(solution)/shard_map/ppermute | solution.py:21
  40.7 13.2 %collective-permute-start.14 = (bf16[64,6144]{1,0:T(8,128)(2,1)S(1)}, bf16[64,6144]{1,0:T(8,128)(2,1)S(1)}, u32[]{:S(2)}, u32[]{:S(2)}) collective-permute-start(bf16[64,6144]{1,0:T(8,128)(2,1)S(1)} %collective-permute-done.12.refs_11_.refs_3_), channel_id=1, source_target_pairs={{56,0},{17,1},{58,2},{19,3},{60,4},{21,5},{62,6},{23,7},{48,8},{25... | collective-permute-start | bytes 2359304 | tf_op jit(solution)/shard_map/ppermute | solution.py:30
  40.7 14.8 %collective-permute-start.8 = (bf16[64,6144]{1,0:T(8,128)(2,1)S(1)}, bf16[64,6144]{1,0:T(8,128)(2,1)S(1)}, u32[]{:S(2)}, u32[]{:S(2)}) collective-permute-start(bf16[64,6144]{1,0:T(8,128)(2,1)S(1)} %get-tuple-element.24.refs_6_), channel_id=1, source_target_pairs={{192,0},{7,1},{194,2},{1,3},{196,4},{3,5},{198,6},{5,7},{200,8},{1... | collective-permute-start | bytes 2359304 | tf_op jit(solution)/shard_map/ppermute | solution.py:21
  42.3 13.3 %collective-permute-start.7 = (bf16[64,6144]{1,0:T(8,128)(2,1)S(1)}, bf16[64,6144]{1,0:T(8,128)(2,1)S(1)}, u32[]{:S(2)}, u32[]{:S(2)}) collective-permute-start(bf16[64,6144]{1,0:T(8,128)(2,1)S(1)} %constant_dynamic-update-slice_fusion.refs_7_), channel_id=1, source_target_pairs={{64,0},{3,1},{66,2},{5,3},{68,4},{7,5},{70,6},{1,7},{72,8},{11,9},... | collective-permute-start | bytes 2359304 | tf_op jit(solution)/shard_map/ppermute | solution.py:21
  43.9 11.8 %collective-permute-start.11 = (bf16[64,6144]{1,0:T(8,128)(2,1)S(1)}, bf16[64,6144]{1,0:T(8,128)(2,1)S(1)}, u32[]{:S(2)}, u32[]{:S(2)}) collective-permute-start(bf16[64,6144]{1,0:T(8,128)(2,1)S(1)} %collective-permute-done.10.refs_9_.refs_1_), channel_id=1, source_target_pairs={{0,1},{1,0},{2,3},{3,2},{4,5},{5,4},{6,7},{7,6},{8,9},{9,8},{10,11... | collective-permute-start | bytes 2359304 | tf_op jit(solution)/shard_map/ppermute | solution.py:34
  43.9 20.6 %collective-permute-start.2 = (bf16[64,6144]{1,0:T(8,128)(2,1)S(1)}, bf16[64,6144]{1,0:T(8,128)(2,1)S(1)}, u32[]{:S(2)}, u32[]{:S(2)}) collective-permute-start(bf16[64,6144]{1,0:T(8,128)(2,1)S(1)} %collective-permute-done.1.refs_2_), channel_id=1, source_target_pairs={{64,0},{3,1},{66,2},{5,3},{68,4},{7,5},{70,6},{1,7},{72,8},{11,9},... | collective-permute-start | bytes 2359304 | tf_op jit(solution)/shard_map/ppermute | solution.py:21
  53.9 13.2 %collective-permute-start.6 = (bf16[64,6144]{1,0:T(8,128)(2,1)S(1)}, bf16[64,6144]{1,0:T(8,128)(2,1)S(1)}, u32[]{:S(2)}, u32[]{:S(2)}) collective-permute-start(bf16[64,6144]{1,0:T(8,128)(2,1)S(1)} %collective-permute-done.5.refs_5_), channel_id=1, source_target_pairs={{192,0},{7,1},{194,2},{1,3},{196,4},{3,5},{198,6},{5,7},{200,8},{1... | collective-permute-start | bytes 2359304 | tf_op jit(solution)/shard_map/ppermute | solution.py:21
  55.5 9.1 %collective-permute-start.16 = (bf16[32,6144]{1,0:T(8,128)(2,1)S(1)}, bf16[32,6144]{1,0:T(8,128)(2,1)S(1)}, u32[]{:S(2)}, u32[]{:S(2)}) collective-permute-start(bf16[32,6144]{1,0:T(8,128)(2,1)S(1)} %slice.52), channel_id=1, source_target_pairs={{56,0},{17,1},{58,2},{19,3},{60,4},{21,5},{62,6},{23,7},{48,8},{25... | collective-permute-start | bytes 1179656 | tf_op jit(solution)/shard_map/ppermute | solution.py:30
  55.6 11.5 %collective-permute-start.13 = (bf16[64,6144]{1,0:T(8,128)(2,1)S(1)}, bf16[64,6144]{1,0:T(8,128)(2,1)S(1)}, u32[]{:S(2)}, u32[]{:S(2)}) collective-permute-start(bf16[64,6144]{1,0:T(8,128)(2,1)S(1)} %collective-permute-done.12.refs_11_.refs_3_), channel_id=1, source_target_pairs={{0,1},{1,0},{2,3},{3,2},{4,5},{5,4},{6,7},{7,6},{8,9},{9,8},{10,11... | collective-permute-start | bytes 2359304 | tf_op jit(solution)/shard_map/ppermute | solution.py:34
  55.7 11.4 %collective-permute-start.15 = (bf16[64,6144]{1,0:T(8,128)(2,1)S(1)}, bf16[64,6144]{1,0:T(8,128)(2,1)S(1)}, u32[]{:S(2)}, u32[]{:S(2)}) collective-permute-start(bf16[64,6144]{1,0:T(8,128)(2,1)S(1)} %collective-permute-done.14.refs_13_.refs_5_), channel_id=1, source_target_pairs={{0,1},{1,0},{2,3},{3,2},{4,5},{5,4},{6,7},{7,6},{8,9},{9,8},{10,11... | collective-permute-start | bytes 2359304 | tf_op jit(solution)/shard_map/ppermute | solution.py:34
  64.6 2.5 %collective-permute-start.17 = (bf16[32,6144]{1,0:T(8,128)(2,1)S(1)}, bf16[32,6144]{1,0:T(8,128)(2,1)S(1)}, u32[]{:S(2)}, u32[]{:S(2)}) collective-permute-start(bf16[32,6144]{1,0:T(8,128)(2,1)S(1)} %collective-permute-done.16.refs_15_.refs_7_), channel_id=1, source_target_pairs={{0,1},{1,0},{2,3},{3,2},{4,5},{5,4},{6,7},{7,6},{8,9},{9,8},{10,11... | collective-permute-start | bytes 1179656 | tf_op jit(solution)/shard_map/ppermute | solution.py:34
  71.8 16.8 %collective-permute-start.23 = (f16[144,2048]{1,0:T(8,128)(2,1)S(1)}, f16[144,2048]{1,0:T(8,128)(2,1)}, u32[]{:S(2)}, u32[]{:S(2)}) collective-permute-start(f16[144,2048]{1,0:T(8,128)(2,1)S(1)} %convert_element_type.29), channel_id=1, source_target_pairs={{64,0},{3,1},{66,2},{5,3},{68,4},{7,5},{70,6},{1,7},{72,8},{11,9},... | collective-permute-start | bytes 1769480 | tf_op jit(solution)/shard_map/ppermute | solution.py:21
  74.6 17.7 %collective-permute-start.22 = (f16[144,2048]{1,0:T(8,128)(2,1)}, f16[144,2048]{1,0:T(8,128)(2,1)}, u32[]{:S(2)}, u32[]{:S(2)}) collective-permute-start(f16[144,2048]{1,0:T(8,128)(2,1)} %convert_element_type.28), channel_id=1, source_target_pairs={{192,0},{7,1},{194,2},{1,3},{196,4},{3,5},{198,6},{5,7},{200,8},{1... | collective-permute-start | bytes 1769480 | tf_op jit(solution)/shard_map/ppermute | solution.py:21
  75.7 17.4 %collective-permute-start.21 = (f16[144,2048]{1,0:T(8,128)(2,1)}, f16[144,2048]{1,0:T(8,128)(2,1)}, u32[]{:S(2)}, u32[]{:S(2)}) collective-permute-start(f16[144,2048]{1,0:T(8,128)(2,1)} %convert_element_type.27), channel_id=1, source_target_pairs={{128,0},{5,1},{130,2},{7,3},{132,4},{1,5},{134,6},{3,7},{136,8},{1... | collective-permute-start | bytes 1769480 | tf_op jit(solution)/shard_map/ppermute | solution.py:21
  78.8 22.6 %all-to-all-start = ((f32[64,8,128]{2,1,0:T(8,128)}), f32[64,8,128]{2,1,0:T(8,128)S(1)}, u32[]{:S(2)}, u32[]{:S(2)}) async-start(f32[64,8,128]{2,1,0:T(8,128)} %get-tuple-element.18), calls=%async_computation | async-start | bytes 524288 | tf_op jit(solution)/shard_map/all_to_all | solution.py:180
  95.6 17.4 %collective-permute-start.24 = (f32[32,2048]{1,0:T(8,128)S(1)}, f32[32,2048]{1,0:T(8,128)S(1)}, u32[]{:S(2)}, u32[]{:S(2)}) collective-permute-start(f32[32,2048]{1,0:T(8,128)S(1)} %get-tuple-element.20), channel_id=1, source_target_pairs={{4,0},{129,1},{6,2},{131,3},{0,4},{133,5},{2,6},{135,7},{12,8},{13... | collective-permute-start | bytes 786440 | tf_op jit(solution)/shard_map/ppermute | solution.py:21
  99.3 13.8 %collective-permute-start.26 = (f32[32,2048]{1,0:T(8,128)S(1)}, f32[32,2048]{1,0:T(8,128)S(1)}, u32[]{:S(2)}, u32[]{:S(2)}) collective-permute-start(f32[32,2048]{1,0:T(8,128)S(1)} %get-tuple-element.21), channel_id=1, source_target_pairs={{2,0},{65,1},{4,2},{67,3},{6,4},{69,5},{0,6},{71,7},{10,8},{73,9},... | collective-permute-start | bytes 786440 | tf_op jit(solution)/shard_map/ppermute | solution.py:21
  99.6 13.6 %collective-permute-start.25 = (f32[32,2048]{1,0:T(8,128)S(1)}, f32[32,2048]{1,0:T(8,128)S(1)}, u32[]{:S(2)}, u32[]{:S(2)}) collective-permute-start(f32[32,2048]{1,0:T(8,128)S(1)} %get-tuple-element.22), channel_id=1, source_target_pairs={{6,0},{193,1},{0,2},{195,3},{2,4},{197,5},{4,6},{199,7},{14,8},{20... | collective-permute-start | bytes 786440 | tf_op jit(solution)/shard_map/ppermute | solution.py:21
  101.4 5.4 %collective-permute-start.20 = (f32[8,128]{1,0:T(8,128)S(1)}, f32[8,128]{1,0:T(8,128)S(1)}, u32[]{:S(2)}, u32[]{:S(2)}) collective-permute-start(f32[8,128]{1,0:T(8,128)S(1)} %reduce_sum.9), channel_id=1, source_target_pairs={{6,0},{7,1},{0,2},{1,3},{2,4},{3,5},{4,6},{5,7},{14,8},{15,9},{8,1... | collective-permute-start | bytes 12296 | tf_op jit(solution)/shard_map/ppermute | solution.py:21
  101.5 5.7 %collective-permute-start.19 = (f32[8,128]{1,0:T(8,128)S(1)}, f32[8,128]{1,0:T(8,128)S(1)}, u32[]{:S(2)}, u32[]{:S(2)}) collective-permute-start(f32[8,128]{1,0:T(8,128)S(1)} %reduce_sum.9), channel_id=1, source_target_pairs={{2,0},{3,1},{4,2},{5,3},{6,4},{7,5},{0,6},{1,7},{10,8},{11,9},{12,... | collective-permute-start | bytes 12296 | tf_op jit(solution)/shard_map/ppermute | solution.py:21
  106.8 5.1 %collective-permute-start.18 = (f32[8,128]{1,0:T(8,128)S(1)}, f32[8,128]{1,0:T(8,128)S(1)}, u32[]{:S(2)}, u32[]{:S(2)}) collective-permute-start(f32[8,128]{1,0:T(8,128)S(1)} %reduce_sum.9), channel_id=1, source_target_pairs={{4,0},{5,1},{6,2},{7,3},{0,4},{1,5},{2,6},{3,7},{12,8},{13,9},{14,... | collective-permute-start | bytes 12296 | tf_op jit(solution)/shard_map/ppermute | solution.py:21

commit v7 on v6

--- a/solution.py
+++ b/solution.py
@@ -48,8 +48,8 @@
 
 
 def excess_kernel(*refs):
-    pieces, lines, outs = refs[:8], refs[8:17], refs[17:20]
-    own_ref, squares_ref, rows, total, rounded = refs[20:]
+    pieces, lines, outs = refs[:8], refs[8:-8], refs[-8:-5]
+    own_ref, squares_ref, rows, total, rounded = refs[-5:]
     count = own_ref.shape[0]
     width = outs[0].shape[1]
     for k in range(pieces[0].shape[1] // DEPTH):
@@ -82,13 +82,13 @@
             most = jnp.max(jnp.max(jnp.abs(part), axis=0, keepdims=True), axis=1, keepdims=True)
             largest[i] = jnp.maximum(largest[i], most)
     for most, out in zip(largest, outs):
-        power = jnp.minimum(jnp.floor(14.0 - jnp.log2(most)), 120.0)
-        out[:count] = out[:count] * jnp.exp2(power)
-        out[count:] = jnp.broadcast_to(power, (EXTRA, width))
+        power = jnp.clip(jnp.floor((14.0 - jnp.log2(most)) / 6.0), 0.0, 14.0)
+        out[:count] = out[:count] * jnp.exp2(6.0 * power)
+        out[count:] = jnp.broadcast_to(jnp.exp2(-power), (EXTRA, width))
 
 
 def own_kernel(own_ref, squares_ref, *refs):
-    lines, out_ref, spread_ref = refs[:9], refs[9], refs[10]
+    *lines, out_ref, spread_ref = refs
     line = jnp.concatenate([piece[...] for piece in lines])
     out_ref[...] = jnp.dot(own_ref[...], line, preferred_element_type=jnp.float32)
     spread_ref[...] = jnp.broadcast_to(squares_ref[...][None], spread_ref.shape)
@@ -102,7 +102,7 @@
     scaled = jax.ShapeDtypeStruct((count + EXTRA, student_width), jnp.float32)
     return pl.pallas_call(
         excess_kernel,
-        in_specs=[inside] * 17,
+        in_specs=[inside] * (len(pieces) + len(lines)),
         out_specs=(inside,) * 5,
         out_shape=(scaled,) * 3
         + (
@@ -151,17 +151,30 @@
 def shards(student, teacher):
     texts, width = student.shape
     both = join(student, teacher)
-    pair = jnp.concatenate([both, other_core(both)])
-    lines = [pair]
-    for step in range(4):
-        arrived = round_z(lines[max(2 * step - 1, 0)][: pair.shape[0] if step < 3 else texts])
-        lines += [arrived, other_core(arrived)]
+    tie = lax.optimization_barrier
     near, far = ("x", "y"), ("y", "x")
-    first = jnp.concatenate([both, shift(both, near, 1)])
-    second = jnp.concatenate([shift(both, near, 3), shift(both, near, 2)])
-    first_up, first_down = shift(first, far, 1), shift(first, far, 3)
-    second_down, second_up = shift(second, far, 3), shift(second, far, 1)
-    pieces = (shift(first_up, far, 1), shift(second_down, far, 3))
+    other = other_core(both)
+    ring = [round_z(both)]
+    both, other = tie((both, other))
+    ring.append(round_z(other))
+    right, left, across = (shift(both, near, k) for k in (1, 3, 2))
+    lines = [both, other]
+    ring = jnp.concatenate(ring)
+    lines += [ring, other_core(ring)]
+    ring, right, left, across = round_z(ring), *tie((right, left, across, ring))[:3]
+    first, second = jnp.concatenate([both, right]), jnp.concatenate([left, across])
+    first_up, second_down = shift(first, far, 1), shift(second, far, 3)
+    ring, first, second = tie((ring, first, second))
+    lines += [ring, other_core(ring)]
+    ring = round_z(ring)
+    first, second, first_up, second_down = tie((first, second, first_up, second_down))
+    first_across, second_across = shift(first_up, far, 1), shift(second_down, far, 3)
+    first_down, second_up = shift(first, far, 3), shift(second, far, 1)
+    ring, first_up, second_down = tie((ring, first_up, second_down))
+    lines += [ring, other_core(ring)]
+    ring = round_z(ring[:texts])
+    lines += [ring, other_core(ring)]
+    pieces = (first_across, second_across)
     pieces += (first_up, second_up, first_down, second_down, first, second)
     *scaled, own, squares = pulls(pieces, lines, width)
     sent = [term.astype(jnp.float16) for term in scaled]
@@ -170,8 +183,9 @@
     partial_term, squares = own_pull(own, squares, lines, width)
     count = own.shape[0]
     for term in returned:
-        scale = jnp.exp2(-term[count : count + 1].astype(jnp.float32))
-        partial_term += term[:count].astype(jnp.float32) * scale
+        root = term[count : count + 1].astype(jnp.float32)
+        root = root * root * root
+        partial_term += term[:count].astype(jnp.float32) * (root * root)
     blocks = partial_term.reshape(4, texts, width)
     pulled = blocks[0]
     for i, k in ((3, 2), (1, 1), (2, 3)):

time: 115 us -> 108 us (0.939); the launches traced: 115 us -> 106 us
  waiting for transfers between devices: 53.7 us -> 47.4 us
  other arithmetic: 7.87 us -> 5.07 us
    ppermute x18, starting transfers between devices: 30.3 us -> 25.7 us  [shift(): return lax.ppermute(value, AXES, pairs)]
    ppermute x18, waiting for transfers between devices: 19.1 us -> 15.3 us  [shift(): return lax.ppermute(value, AXES, pairs)]
    ppermute x5, starting transfers between devices: 0.59 us -> 3.81 us  [other_core(): return lax.ppermute(value, 'core', [(0, 1), (1, 0)])]
    ppermute x4 -> x5, waiting for transfers between devices: 34.6 us -> 32.1 us  [round_z(): return lax.ppermute(value, AXES, pairs)]
    exp2 x3 -> x0, other arithmetic: 2.33 us -> none  [shards(): scale = jnp.exp2(-term[count:count + 1].astype(jnp.float32))]
    mul x0 -> x3, other arithmetic: none -> 2.31 us  [shards(): partial_term += term[:count].astype(jnp.float32) * (root * root)]
    ppermute x4 -> x5, starting transfers between devices: 2.08 us -> 4 us  [round_z(): return lax.ppermute(value, AXES, pairs)]
    convert_element_type x3, other arithmetic: 1.86 us -> 0.22 us  [shards(): sent = [term.astype(jnp.float16) for term in scaled]]
  transfers between devices with their start and end apart: 28 -> 29, of which waited for: 9 -> 13; matrix products, arithmetic and copies ran while one was open for 6% -> 6% of each run, Pallas kernels for 1% -> 1%
where the time goes in v7:
time: 108 us; the launch traced here: 106 us
  waiting for transfers between devices  47.4 us (44%)
  starting transfers between devices  41.7 us (39%)
  Pallas kernels  7.47 us (7%)
  other arithmetic  5.07 us (5%)
  between operations  2.64 us (2%)
  local copies, waits for them, and re-layouts  1.75 us (2%)
    ppermute x5, waiting for transfers between devices, round_z(): return lax.ppermute(value, AXES, pairs)  32.1 us
    ppermute x18, starting transfers between devices, shift(): return lax.ppermute(value, AXES, pairs)  25.7 us
    ppermute x18, waiting for transfers between devices, shift(): return lax.ppermute(value, AXES, pairs)  15.3 us
    all_to_all x1, starting transfers between devices, shards(): lax.all_to_all(squares, ('y', 'zh', 'zl', 'core'), 0, 0)  8.18 us
    pallas_call x1, Pallas kernels, pulls(): pl.pallas_call(excess_kernel, in_specs=[inside] * (len(pieces) + len(line...  4.63 us
    ppermute x5, starting transfers between devices, round_z(): return lax.ppermute(value, AXES, pairs)  4 us
    ppermute x5, starting transfers between devices, other_core(): return lax.ppermute(value, 'core', [(0, 1), (1, 0)])  3.81 us
    mul x3, other arithmetic, shards(): partial_term += term[:count].astype(jnp.float32) * (root * root)  2.31 us
  transfers between devices with their start and end apart: 29, of which 13 were waited for; matrix products, arithmetic and copies ran while one was open for 6% of the time, Pallas kernels for 1%

profile of v7, /device:TPU:2, one launch (start us, length us, event | category | flops | bytes accessed | tf_op | source)
XLA Modules:
  0.0 106.1 jit_solution(10057508057475755679)
XLA Ops:
  0.6 1.8 %shard_map.41.refs_8_.refs_0_ = bf16[32,6144]{1,0:T(8,128)(2,1)} custom-call(bf16[32,2048]{1,0:T(8,128)(2,1)} %student_ref.1, bf16[32,4096]{1,0:T(8,128)(2,1)} %teacher_ref.1), custom_call_target="tpu_custom_call" | custom-call | tf_op jit(solution)/shard_map/pallas_call | solution.py:45
  2.4 1.9 %collective-permute-start = (bf16[32,6144]{1,0:T(8,128)(2,1)}, bf16[32,6144]{1,0:T(8,128)(2,1)S(1)}, u32[]{:S(2)}, u32[]{:S(2)}) collective-permute-start(bf16[32,6144]{1,0:T(8,128)(2,1)} %shard_map.41.refs_8_.refs_0_), channel_id=1, source_target_pairs={{56,0},{17,1},{58,2},{19,3},{60,4},{21,5},{62,6},{23,7},{48,8},{25... | collective-permute-start | bytes 1179656 | tf_op jit(solution)/shard_map/ppermute | solution.py:30
  4.4 2.1 %collective-permute-start.6 = (bf16[32,6144]{1,0:T(8,128)(2,1)}, bf16[32,6144]{1,0:T(8,128)(2,1)S(1)}, u32[]{:S(2)}, u32[]{:S(2)}) collective-permute-start(bf16[32,6144]{1,0:T(8,128)(2,1)} %shard_map.41.refs_8_.refs_0_), channel_id=1, source_target_pairs={{4,0},{129,1},{6,2},{131,3},{0,4},{133,5},{2,6},{135,7},{12,8},{13... | collective-permute-start | bytes 1179656 | tf_op jit(solution)/shard_map/ppermute | solution.py:21
  6.5 1.6 %collective-permute-start.5 = (bf16[32,6144]{1,0:T(8,128)(2,1)}, bf16[32,6144]{1,0:T(8,128)(2,1)S(1)}, u32[]{:S(2)}, u32[]{:S(2)}) collective-permute-start(bf16[32,6144]{1,0:T(8,128)(2,1)} %shard_map.41.refs_8_.refs_0_), channel_id=1, source_target_pairs={{6,0},{193,1},{0,2},{195,3},{2,4},{197,5},{4,6},{199,7},{14,8},{20... | collective-permute-start | bytes 1179656 | tf_op jit(solution)/shard_map/ppermute | solution.py:21
  8.1 0.4 collective-permute-start.4
  8.5 1.9 %collective-permute-start.2 = (bf16[32,6144]{1,0:T(8,128)(2,1)S(1)}, bf16[32,6144]{1,0:T(8,128)(2,1)S(1)}, u32[]{:S(2)}, u32[]{:S(2)}) collective-permute-start(bf16[32,6144]{1,0:T(8,128)(2,1)S(1)} %collective-permute-done.1.refs_9_.refs_1_), channel_id=1, source_target_pairs={{56,0},{17,1},{58,2},{19,3},{60,4},{21,5},{62,6},{23,7},{48,8},{25... | collective-permute-start | bytes 1179656 | tf_op jit(solution)/shard_map/ppermute | solution.py:30
  10.4 1.0 constant_dynamic-update-slice_fusion.3
  11.5 2.8 %collective-permute-done = bf16[32,6144]{1,0:T(8,128)(2,1)S(1)} collective-permute-done((bf16[32,6144]{1,0:T(8,128)(2,1)}, bf16[32,6144]{1,0:T(8,128)(2,1)S(1)}, u32[]{:S(2)}, u32[]{:S(2)}) %collective-permute-start) | collective-permute-done | bytes 393248 | tf_op jit(solution)/shard_map/ppermute | solution.py:30
  14.3 5.8 %collective-permute-done.2 = bf16[32,6144]{1,0:T(8,128)(2,1)S(1)} collective-permute-done((bf16[32,6144]{1,0:T(8,128)(2,1)S(1)}, bf16[32,6144]{1,0:T(8,128)(2,1)S(1)}, u32[]{:S(2)}, u32[]{:S(2)}) %collective-permute-start.2) | collective-permute-done | bytes 393248 | tf_op jit(solution)/shard_map/ppermute | solution.py:30
  20.2 0.1 collective-permute-start.3
  20.4 3.1 %collective-permute-start.7 = (bf16[64,6144]{1,0:T(8,128)(2,1)S(1)}, bf16[64,6144]{1,0:T(8,128)(2,1)S(1)}, u32[]{:S(2)}, u32[]{:S(2)}) collective-permute-start(bf16[64,6144]{1,0:T(8,128)(2,1)S(1)} %constant_dynamic-update-slice_fusion.2.refs_6_), channel_id=1, source_target_pairs={{64,0},{3,1},{66,2},{5,3},{68,4},{7,5},{70,6},{1,7},{72,8},{11,9},... | collective-permute-start | bytes 2359304 | tf_op jit(solution)/shard_map/ppermute | solution.py:21
  23.5 0.1 collective-permute-start.8
  23.6 9.9 %collective-permute-done.3.refs_12_.refs_4_ = bf16[64,6144]{1,0:T(8,128)(2,1)S(1)} collective-permute-done((bf16[64,6144]{1,0:T(8,128)(2,1)S(1)}, bf16[64,6144]{1,0:T(8,128)(2,1)S(1)}, u32[]{:S(2)}, u32[]{:S(2)}) %collective-permute-start.3) | collective-permute-done | bytes 786464 | tf_op jit(solution)/shard_map/ppermute | solution.py:30
  33.4 2.5 %collective-permute-start.14 = (bf16[64,6144]{1,0:T(8,128)(2,1)S(1)}, bf16[64,6144]{1,0:T(8,128)(2,1)S(1)}, u32[]{:S(2)}, u32[]{:S(2)}) collective-permute-start(bf16[64,6144]{1,0:T(8,128)(2,1)S(1)} %constant_dynamic-update-slice_fusion.refs_10_.refs_2_), channel_id=1, source_target_pairs={{0,1},{1,0},{2,3},{3,2},{4,5},{5,4},{6,7},{7,6},{8,9},{9,8},{10,11... | collective-permute-start | bytes 2359304 | tf_op jit(solution)/shard_map/ppermute | solution.py:34
  36.0 0.8 collective-permute-done.8.refs_5_
  36.8 2.0 %collective-permute-start.10 = (bf16[64,6144]{1,0:T(8,128)(2,1)S(1)}, bf16[64,6144]{1,0:T(8,128)(2,1)S(1)}, u32[]{:S(2)}, u32[]{:S(2)}) collective-permute-start(bf16[64,6144]{1,0:T(8,128)(2,1)S(1)} %collective-permute-done.8.refs_5_), channel_id=1, source_target_pairs={{192,0},{7,1},{194,2},{1,3},{196,4},{3,5},{198,6},{5,7},{200,8},{1... | collective-permute-start | bytes 2359304 | tf_op jit(solution)/shard_map/ppermute | solution.py:21
  38.8 1.2 %collective-permute-start.12 = (bf16[64,6144]{1,0:T(8,128)(2,1)S(1)}, bf16[64,6144]{1,0:T(8,128)(2,1)S(1)}, u32[]{:S(2)}, u32[]{:S(2)}) collective-permute-start(bf16[64,6144]{1,0:T(8,128)(2,1)S(1)} %constant_dynamic-update-slice_fusion.4.refs_7_), channel_id=1, source_target_pairs={{64,0},{3,1},{66,2},{5,3},{68,4},{7,5},{70,6},{1,7},{72,8},{11,9},... | collective-permute-start | bytes 2359304 | tf_op jit(solution)/shard_map/ppermute | solution.py:21
  40.0 6.6 %collective-permute-done.11.refs_14_.refs_6_ = bf16[64,6144]{1,0:T(8,128)(2,1)S(1)} collective-permute-done((bf16[64,6144]{1,0:T(8,128)(2,1)S(1)}, bf16[64,6144]{1,0:T(8,128)(2,1)S(1)}, u32[]{:S(2)}, u32[]{:S(2)}) %collective-permute-start.11) | collective-permute-done | bytes 786464 | tf_op jit(solution)/shard_map/ppermute | solution.py:30
  46.6 1.6 %collective-permute-start.13 = (bf16[64,6144]{1,0:T(8,128)(2,1)S(1)}, bf16[64,6144]{1,0:T(8,128)(2,1)S(1)}, u32[]{:S(2)}, u32[]{:S(2)}) collective-permute-start(bf16[64,6144]{1,0:T(8,128)(2,1)S(1)} %constant_dynamic-update-slice_fusion.2.refs_6_), channel_id=1, source_target_pairs={{192,0},{7,1},{194,2},{1,3},{196,4},{3,5},{198,6},{5,7},{200,8},{1... | collective-permute-start | bytes 2359304 | tf_op jit(solution)/shard_map/ppermute | solution.py:21
  48.3 0.1 collective-permute-start.17
  48.3 0.4 collective-permute-done.9.refs_0_
  48.8 0.9 collective-permute-start.15
  49.6 0.3 collective-permute-done.10.refs_1_
  50.0 0.4 collective-permute-start.16
  50.4 7.0 %collective-permute-done.17.refs_16_.refs_8_ = bf16[32,6144]{1,0:T(8,128)(2,1)S(1)} collective-permute-done((bf16[32,6144]{1,0:T(8,128)(2,1)S(1)}, bf16[32,6144]{1,0:T(8,128)(2,1)S(1)}, u32[]{:S(2)}, u32[]{:S(2)}) %collective-permute-start.17) | collective-permute-done | bytes 393248 | tf_op jit(solution)/shard_map/ppermute | solution.py:30
  57.3 2.5 %collective-permute-done.13.refs_4_ = bf16[64,6144]{1,0:T(8,128)(2,1)S(1)} collective-permute-done((bf16[64,6144]{1,0:T(8,128)(2,1)S(1)}, bf16[64,6144]{1,0:T(8,128)(2,1)S(1)}, u32[]{:S(2)}, u32[]{:S(2)}) %collective-permute-start.13) | collective-permute-done | bytes 786464 | tf_op jit(solution)/shard_map/ppermute | solution.py:21
  59.9 4.6 %shard_map.42 = (f32[144,2048]{1,0:T(8,128)S(1)}, f32[144,2048]{1,0:T(8,128)S(1)}, f32[144,2048]{1,0:T(8,128)S(1)}, bf16[128,512]{1,0:T(8,128)(2,1)S(1)}, f32[8,128]{1,0:T(8,128)S(1)}) custom-call(bf16[64,6144]{1,0:T(8,128)(2,1)S(1)} %collective-permute-done.9.refs_0_, bf16[64,6144]{1,0:T(8,128)(2,1)S(1)} %collective-permute-done.10.refs_1_, ...), custom_call_target="tpu_custom_call" | custom-call | flops 4294967296 | bytes 12582912 | tf_op jit(solution)/shard_map/pallas_call | solution.py:103
  64.5 0.1 convert_element_type.29
  64.6 1.9 %collective-permute-start.24 = (f16[144,2048]{1,0:T(8,128)(2,1)S(1)}, f16[144,2048]{1,0:T(8,128)(2,1)}, u32[]{:S(2)}, u32[]{:S(2)}) collective-permute-start(f16[144,2048]{1,0:T(8,128)(2,1)S(1)} %convert_element_type.29), channel_id=1, source_target_pairs={{64,0},{3,1},{66,2},{5,3},{68,4},{7,5},{70,6},{1,7},{72,8},{11,9},... | collective-permute-start | bytes 1769480 | tf_op jit(solution)/shard_map/ppermute | solution.py:21
  66.5 0.3 collective-permute-start.23
  66.9 2.2 %collective-permute-start.22 = (f16[144,2048]{1,0:T(8,128)(2,1)S(1)}, f16[144,2048]{1,0:T(8,128)(2,1)}, u32[]{:S(2)}, u32[]{:S(2)}) collective-permute-start(f16[144,2048]{1,0:T(8,128)(2,1)S(1)} %convert_element_type.27), channel_id=1, source_target_pairs={{128,0},{5,1},{130,2},{7,3},{132,4},{1,5},{134,6},{3,7},{136,8},{1... | collective-permute-start | bytes 1769480 | tf_op jit(solution)/shard_map/ppermute | solution.py:21
  69.1 1.0 shard_map.43
  70.1 8.2 %all-to-all-start = ((f32[64,8,128]{2,1,0:T(8,128)}), f32[64,8,128]{2,1,0:T(8,128)S(1)}, u32[]{:S(2)}, u32[]{:S(2)}) async-start(f32[64,8,128]{2,1,0:T(8,128)} %get-tuple-element.48), calls=%async_computation | async-start | bytes 524288 | tf_op jit(solution)/shard_map/all_to_all | solution.py:194
  78.3 2.1 %collective-permute-done.24 = f16[144,2048]{1,0:T(8,128)(2,1)} collective-permute-done((f16[144,2048]{1,0:T(8,128)(2,1)S(1)}, f16[144,2048]{1,0:T(8,128)(2,1)}, u32[]{:S(2)}, u32[]{:S(2)}) %collective-permute-start.24) | collective-permute-done | bytes 589856 | tf_op jit(solution)/shard_map/ppermute | solution.py:21
  80.4 0.8 fusion.4
  81.2 3.3 %collective-permute-done.23 = f16[144,2048]{1,0:T(8,128)(2,1)} collective-permute-done((f16[144,2048]{1,0:T(8,128)(2,1)S(1)}, f16[144,2048]{1,0:T(8,128)(2,1)}, u32[]{:S(2)}, u32[]{:S(2)}) %collective-permute-start.23) | collective-permute-done | bytes 589856 | tf_op jit(solution)/shard_map/ppermute | solution.py:21
  84.5 0.8 fusion.3
  85.3 0.8 fusion.2
  86.1 1.7 %multiply_add_fusion = f32[128,2048]{1,0:T(8,128)S(1)} fusion(f32[128,2048]{1,0:T(8,128)S(1)} %get-tuple-element.49, f16[144,2048]{1,0:T(8,128)(2,1)} %collective-permute-done.24, f16[144,2048]{1,0:T(8,128)(2,1)} %collective-permute-done.23, f16[144,2048]{1,0:T(8,128)(2,1)} %collective-permute-done.22, f32[2048]{0:T(1024)S(1)} %bitcast.4, f32[2048]{0:T(1024)S(1)} %bitcast.5, ...), kind=kLoop, calls=%fused_computation | loop fusion | flops 2359296 | bytes 3694592 | tf_op jit(solution)/shard_map/add | solution.py:188
  87.8 1.6 %collective-permute-start.25 = (f32[32,2048]{1,0:T(8,128)S(1)}, f32[32,2048]{1,0:T(8,128)S(1)}, u32[]{:S(2)}, u32[]{:S(2)}) collective-permute-start(f32[32,2048]{1,0:T(8,128)S(1)} %get-tuple-element.50), channel_id=1, source_target_pairs={{4,0},{129,1},{6,2},{131,3},{0,4},{133,5},{2,6},{135,7},{12,8},{13... | collective-permute-start | bytes 786440 | tf_op jit(solution)/shard_map/ppermute | solution.py:21
  89.4 1.3 %collective-permute-start.27 = (f32[32,2048]{1,0:T(8,128)S(1)}, f32[32,2048]{1,0:T(8,128)S(1)}, u32[]{:S(2)}, u32[]{:S(2)}) collective-permute-start(f32[32,2048]{1,0:T(8,128)S(1)} %get-tuple-element.51), channel_id=1, source_target_pairs={{2,0},{65,1},{4,2},{67,3},{6,4},{69,5},{0,6},{71,7},{10,8},{73,9},... | collective-permute-start | bytes 786440 | tf_op jit(solution)/shard_map/ppermute | solution.py:21
  90.7 1.4 %collective-permute-start.26 = (f32[32,2048]{1,0:T(8,128)S(1)}, f32[32,2048]{1,0:T(8,128)S(1)}, u32[]{:S(2)}, u32[]{:S(2)}) collective-permute-start(f32[32,2048]{1,0:T(8,128)S(1)} %get-tuple-element.52), channel_id=1, source_target_pairs={{6,0},{193,1},{0,2},{195,3},{2,4},{197,5},{4,6},{199,7},{14,8},{20... | collective-permute-start | bytes 786440 | tf_op jit(solution)/shard_map/ppermute | solution.py:21
  92.1 2.1 %collective-permute-start.21 = (f32[8,128]{1,0:T(8,128)S(1)}, f32[8,128]{1,0:T(8,128)S(1)}, u32[]{:S(2)}, u32[]{:S(2)}) collective-permute-start(f32[8,128]{1,0:T(8,128)S(1)} %reduce_sum.9), channel_id=1, source_target_pairs={{6,0},{7,1},{0,2},{1,3},{2,4},{3,5},{4,6},{5,7},{14,8},{15,9},{8,1... | collective-permute-start | bytes 12296 | tf_op jit(solution)/shard_map/ppermute | solution.py:21
  94.2 3.6 %collective-permute-done.21 = f32[8,128]{1,0:T(8,128)S(1)} collective-permute-done((f32[8,128]{1,0:T(8,128)S(1)}, f32[8,128]{1,0:T(8,128)S(1)}, u32[]{:S(2)}, u32[]{:S(2)}) %collective-permute-start.21) | collective-permute-done | bytes 4128 | tf_op jit(solution)/shard_map/ppermute | solution.py:21
  97.9 2.9 %collective-permute-start.19 = (f32[8,128]{1,0:T(8,128)S(1)}, f32[8,128]{1,0:T(8,128)S(1)}, u32[]{:S(2)}, u32[]{:S(2)}) collective-permute-start(f32[8,128]{1,0:T(8,128)S(1)} %reduce_sum.9), channel_id=1, source_target_pairs={{4,0},{5,1},{6,2},{7,3},{0,4},{1,5},{2,6},{3,7},{12,8},{13,9},{14,... | collective-permute-start | bytes 12296 | tf_op jit(solution)/shard_map/ppermute | solution.py:21
  100.7 2.2 %collective-permute-done.19 = f32[8,128]{1,0:T(8,128)S(1)} collective-permute-done((f32[8,128]{1,0:T(8,128)S(1)}, f32[8,128]{1,0:T(8,128)S(1)}, u32[]{:S(2)}, u32[]{:S(2)}) %collective-permute-start.19) | collective-permute-done | bytes 4128 | tf_op jit(solution)/shard_map/ppermute | solution.py:21
  103.0 0.5 slice.41
  104.2 0.8 fusion.1
  (34 shorter events, 0.5 us)
Async XLA Ops:
  2.4 1.9 %collective-permute-start.1 = (bf16[32,6144]{1,0:T(8,128)(2,1)}, bf16[32,6144]{1,0:T(8,128)(2,1)S(1)}, u32[]{:S(2)}, u32[]{:S(2)}) collective-permute-start(bf16[32,6144]{1,0:T(8,128)(2,1)} %shard_map.41.refs_8_.refs_0_), channel_id=1, source_target_pairs={{0,1},{1,0},{2,3},{3,2},{4,5},{5,4},{6,7},{7,6},{8,9},{9,8},{10,11... | collective-permute-start | bytes 1179656 | tf_op jit(solution)/shard_map/ppermute | solution.py:34
  2.4 11.8 %collective-permute-start = (bf16[32,6144]{1,0:T(8,128)(2,1)}, bf16[32,6144]{1,0:T(8,128)(2,1)S(1)}, u32[]{:S(2)}, u32[]{:S(2)}) collective-permute-start(bf16[32,6144]{1,0:T(8,128)(2,1)} %shard_map.41.refs_8_.refs_0_), channel_id=1, source_target_pairs={{56,0},{17,1},{58,2},{19,3},{60,4},{21,5},{62,6},{23,7},{48,8},{25... | collective-permute-start | bytes 1179656 | tf_op jit(solution)/shard_map/ppermute | solution.py:30
  4.4 15.9 %collective-permute-start.6 = (bf16[32,6144]{1,0:T(8,128)(2,1)}, bf16[32,6144]{1,0:T(8,128)(2,1)S(1)}, u32[]{:S(2)}, u32[]{:S(2)}) collective-permute-start(bf16[32,6144]{1,0:T(8,128)(2,1)} %shard_map.41.refs_8_.refs_0_), channel_id=1, source_target_pairs={{4,0},{129,1},{6,2},{131,3},{0,4},{133,5},{2,6},{135,7},{12,8},{13... | collective-permute-start | bytes 1179656 | tf_op jit(solution)/shard_map/ppermute | solution.py:21
  6.5 13.8 %collective-permute-start.5 = (bf16[32,6144]{1,0:T(8,128)(2,1)}, bf16[32,6144]{1,0:T(8,128)(2,1)S(1)}, u32[]{:S(2)}, u32[]{:S(2)}) collective-permute-start(bf16[32,6144]{1,0:T(8,128)(2,1)} %shard_map.41.refs_8_.refs_0_), channel_id=1, source_target_pairs={{6,0},{193,1},{0,2},{195,3},{2,4},{197,5},{4,6},{199,7},{14,8},{20... | collective-permute-start | bytes 1179656 | tf_op jit(solution)/shard_map/ppermute | solution.py:21
  8.1 12.2 %collective-permute-start.4 = (bf16[32,6144]{1,0:T(8,128)(2,1)}, bf16[32,6144]{1,0:T(8,128)(2,1)S(1)}, u32[]{:S(2)}, u32[]{:S(2)}) collective-permute-start(bf16[32,6144]{1,0:T(8,128)(2,1)} %shard_map.41.refs_8_.refs_0_), channel_id=1, source_target_pairs={{2,0},{65,1},{4,2},{67,3},{6,4},{69,5},{0,6},{71,7},{10,8},{73,9},... | collective-permute-start | bytes 1179656 | tf_op jit(solution)/shard_map/ppermute | solution.py:21
  8.5 11.6 %collective-permute-start.2 = (bf16[32,6144]{1,0:T(8,128)(2,1)S(1)}, bf16[32,6144]{1,0:T(8,128)(2,1)S(1)}, u32[]{:S(2)}, u32[]{:S(2)}) collective-permute-start(bf16[32,6144]{1,0:T(8,128)(2,1)S(1)} %collective-permute-done.1.refs_9_.refs_1_), channel_id=1, source_target_pairs={{56,0},{17,1},{58,2},{19,3},{60,4},{21,5},{62,6},{23,7},{48,8},{25... | collective-permute-start | bytes 1179656 | tf_op jit(solution)/shard_map/ppermute | solution.py:30
  20.2 13.3 %collective-permute-start.3 = (bf16[64,6144]{1,0:T(8,128)(2,1)S(1)}, bf16[64,6144]{1,0:T(8,128)(2,1)S(1)}, u32[]{:S(2)}, u32[]{:S(2)}) collective-permute-start(bf16[64,6144]{1,0:T(8,128)(2,1)S(1)} %constant_dynamic-update-slice_fusion.refs_10_.refs_2_), channel_id=1, source_target_pairs={{56,0},{17,1},{58,2},{19,3},{60,4},{21,5},{62,6},{23,7},{48,8},{25... | collective-permute-start | bytes 2359304 | tf_op jit(solution)/shard_map/ppermute | solution.py:30
  20.3 39.5 %copy-start = (bf16[32,6144]{1,0:T(8,128)(2,1)S(1)}, bf16[32,6144]{1,0:T(8,128)(2,1)}, u32[]{:S(2)}) copy-start(bf16[32,6144]{1,0:T(8,128)(2,1)} %shard_map.41.refs_8_.refs_0_) | copy-start | bytes 1179652
  20.4 15.6 %collective-permute-start.7 = (bf16[64,6144]{1,0:T(8,128)(2,1)S(1)}, bf16[64,6144]{1,0:T(8,128)(2,1)S(1)}, u32[]{:S(2)}, u32[]{:S(2)}) collective-permute-start(bf16[64,6144]{1,0:T(8,128)(2,1)S(1)} %constant_dynamic-update-slice_fusion.2.refs_6_), channel_id=1, source_target_pairs={{64,0},{3,1},{66,2},{5,3},{68,4},{7,5},{70,6},{1,7},{72,8},{11,9},... | collective-permute-start | bytes 2359304 | tf_op jit(solution)/shard_map/ppermute | solution.py:21
  23.5 13.3 %collective-permute-start.8 = (bf16[64,6144]{1,0:T(8,128)(2,1)S(1)}, bf16[64,6144]{1,0:T(8,128)(2,1)S(1)}, u32[]{:S(2)}, u32[]{:S(2)}) collective-permute-start(bf16[64,6144]{1,0:T(8,128)(2,1)S(1)} %constant_dynamic-update-slice_fusion.4.refs_7_), channel_id=1, source_target_pairs={{192,0},{7,1},{194,2},{1,3},{196,4},{3,5},{198,6},{5,7},{200,8},{1... | collective-permute-start | bytes 2359304 | tf_op jit(solution)/shard_map/ppermute | solution.py:21
  33.4 13.2 %collective-permute-start.11 = (bf16[64,6144]{1,0:T(8,128)(2,1)S(1)}, bf16[64,6144]{1,0:T(8,128)(2,1)S(1)}, u32[]{:S(2)}, u32[]{:S(2)}) collective-permute-start(bf16[64,6144]{1,0:T(8,128)(2,1)S(1)} %collective-permute-done.3.refs_12_.refs_4_), channel_id=1, source_target_pairs={{56,0},{17,1},{58,2},{19,3},{60,4},{21,5},{62,6},{23,7},{48,8},{25... | collective-permute-start | bytes 2359304 | tf_op jit(solution)/shard_map/ppermute | solution.py:30
  33.4 14.8 %collective-permute-start.14 = (bf16[64,6144]{1,0:T(8,128)(2,1)S(1)}, bf16[64,6144]{1,0:T(8,128)(2,1)S(1)}, u32[]{:S(2)}, u32[]{:S(2)}) collective-permute-start(bf16[64,6144]{1,0:T(8,128)(2,1)S(1)} %constant_dynamic-update-slice_fusion.refs_10_.refs_2_), channel_id=1, source_target_pairs={{0,1},{1,0},{2,3},{3,2},{4,5},{5,4},{6,7},{7,6},{8,9},{9,8},{10,11... | collective-permute-start | bytes 2359304 | tf_op jit(solution)/shard_map/ppermute | solution.py:34
  36.8 12.0 %collective-permute-start.9 = (bf16[64,6144]{1,0:T(8,128)(2,1)S(1)}, bf16[64,6144]{1,0:T(8,128)(2,1)S(1)}, u32[]{:S(2)}, u32[]{:S(2)}) collective-permute-start(bf16[64,6144]{1,0:T(8,128)(2,1)S(1)} %collective-permute-done.7.refs_2_), channel_id=1, source_target_pairs={{64,0},{3,1},{66,2},{5,3},{68,4},{7,5},{70,6},{1,7},{72,8},{11,9},... | collective-permute-start | bytes 2359304 | tf_op jit(solution)/shard_map/ppermute | solution.py:21
  36.8 13.2 %collective-permute-start.10 = (bf16[64,6144]{1,0:T(8,128)(2,1)S(1)}, bf16[64,6144]{1,0:T(8,128)(2,1)S(1)}, u32[]{:S(2)}, u32[]{:S(2)}) collective-permute-start(bf16[64,6144]{1,0:T(8,128)(2,1)S(1)} %collective-permute-done.8.refs_5_), channel_id=1, source_target_pairs={{192,0},{7,1},{194,2},{1,3},{196,4},{3,5},{198,6},{5,7},{200,8},{1... | collective-permute-start | bytes 2359304 | tf_op jit(solution)/shard_map/ppermute | solution.py:21
  38.8 18.5 %collective-permute-start.12 = (bf16[64,6144]{1,0:T(8,128)(2,1)S(1)}, bf16[64,6144]{1,0:T(8,128)(2,1)S(1)}, u32[]{:S(2)}, u32[]{:S(2)}) collective-permute-start(bf16[64,6144]{1,0:T(8,128)(2,1)S(1)} %constant_dynamic-update-slice_fusion.4.refs_7_), channel_id=1, source_target_pairs={{64,0},{3,1},{66,2},{5,3},{68,4},{7,5},{70,6},{1,7},{72,8},{11,9},... | collective-permute-start | bytes 2359304 | tf_op jit(solution)/shard_map/ppermute | solution.py:21
  46.6 13.2 %collective-permute-start.13 = (bf16[64,6144]{1,0:T(8,128)(2,1)S(1)}, bf16[64,6144]{1,0:T(8,128)(2,1)S(1)}, u32[]{:S(2)}, u32[]{:S(2)}) collective-permute-start(bf16[64,6144]{1,0:T(8,128)(2,1)S(1)} %constant_dynamic-update-slice_fusion.2.refs_6_), channel_id=1, source_target_pairs={{192,0},{7,1},{194,2},{1,3},{196,4},{3,5},{198,6},{5,7},{200,8},{1... | collective-permute-start | bytes 2359304 | tf_op jit(solution)/shard_map/ppermute | solution.py:21
  48.3 9.1 %collective-permute-start.17 = (bf16[32,6144]{1,0:T(8,128)(2,1)S(1)}, bf16[32,6144]{1,0:T(8,128)(2,1)S(1)}, u32[]{:S(2)}, u32[]{:S(2)}) collective-permute-start(bf16[32,6144]{1,0:T(8,128)(2,1)S(1)} %slice.40), channel_id=1, source_target_pairs={{56,0},{17,1},{58,2},{19,3},{60,4},{21,5},{62,6},{23,7},{48,8},{25... | collective-permute-start | bytes 1179656 | tf_op jit(solution)/shard_map/ppermute | solution.py:30
  48.8 11.1 %collective-permute-start.15 = (bf16[64,6144]{1,0:T(8,128)(2,1)S(1)}, bf16[64,6144]{1,0:T(8,128)(2,1)S(1)}, u32[]{:S(2)}, u32[]{:S(2)}) collective-permute-start(bf16[64,6144]{1,0:T(8,128)(2,1)S(1)} %collective-permute-done.3.refs_12_.refs_4_), channel_id=1, source_target_pairs={{0,1},{1,0},{2,3},{3,2},{4,5},{5,4},{6,7},{7,6},{8,9},{9,8},{10,11... | collective-permute-start | bytes 2359304 | tf_op jit(solution)/shard_map/ppermute | solution.py:34
  50.0 9.9 %collective-permute-start.16 = (bf16[64,6144]{1,0:T(8,128)(2,1)S(1)}, bf16[64,6144]{1,0:T(8,128)(2,1)S(1)}, u32[]{:S(2)}, u32[]{:S(2)}) collective-permute-start(bf16[64,6144]{1,0:T(8,128)(2,1)S(1)} %collective-permute-done.11.refs_14_.refs_6_), channel_id=1, source_target_pairs={{0,1},{1,0},{2,3},{3,2},{4,5},{5,4},{6,7},{7,6},{8,9},{9,8},{10,11... | collective-permute-start | bytes 2359304 | tf_op jit(solution)/shard_map/ppermute | solution.py:34
  57.3 2.5 %collective-permute-start.18 = (bf16[32,6144]{1,0:T(8,128)(2,1)S(1)}, bf16[32,6144]{1,0:T(8,128)(2,1)S(1)}, u32[]{:S(2)}, u32[]{:S(2)}) collective-permute-start(bf16[32,6144]{1,0:T(8,128)(2,1)S(1)} %collective-permute-done.17.refs_16_.refs_8_), channel_id=1, source_target_pairs={{0,1},{1,0},{2,3},{3,2},{4,5},{5,4},{6,7},{7,6},{8,9},{9,8},{10,11... | collective-permute-start | bytes 1179656 | tf_op jit(solution)/shard_map/ppermute | solution.py:34
  64.6 15.8 %collective-permute-start.24 = (f16[144,2048]{1,0:T(8,128)(2,1)S(1)}, f16[144,2048]{1,0:T(8,128)(2,1)}, u32[]{:S(2)}, u32[]{:S(2)}) collective-permute-start(f16[144,2048]{1,0:T(8,128)(2,1)S(1)} %convert_element_type.29), channel_id=1, source_target_pairs={{64,0},{3,1},{66,2},{5,3},{68,4},{7,5},{70,6},{1,7},{72,8},{11,9},... | collective-permute-start | bytes 1769480 | tf_op jit(solution)/shard_map/ppermute | solution.py:21
  66.5 17.9 %collective-permute-start.23 = (f16[144,2048]{1,0:T(8,128)(2,1)S(1)}, f16[144,2048]{1,0:T(8,128)(2,1)}, u32[]{:S(2)}, u32[]{:S(2)}) collective-permute-start(f16[144,2048]{1,0:T(8,128)(2,1)S(1)} %convert_element_type.28), channel_id=1, source_target_pairs={{192,0},{7,1},{194,2},{1,3},{196,4},{3,5},{198,6},{5,7},{200,8},{1... | collective-permute-start | bytes 1769480 | tf_op jit(solution)/shard_map/ppermute | solution.py:21
  66.9 18.3 %collective-permute-start.22 = (f16[144,2048]{1,0:T(8,128)(2,1)S(1)}, f16[144,2048]{1,0:T(8,128)(2,1)}, u32[]{:S(2)}, u32[]{:S(2)}) collective-permute-start(f16[144,2048]{1,0:T(8,128)(2,1)S(1)} %convert_element_type.27), channel_id=1, source_target_pairs={{128,0},{5,1},{130,2},{7,3},{132,4},{1,5},{134,6},{3,7},{136,8},{1... | collective-permute-start | bytes 1769480 | tf_op jit(solution)/shard_map/ppermute | solution.py:21
  70.1 21.9 %all-to-all-start = ((f32[64,8,128]{2,1,0:T(8,128)}), f32[64,8,128]{2,1,0:T(8,128)S(1)}, u32[]{:S(2)}, u32[]{:S(2)}) async-start(f32[64,8,128]{2,1,0:T(8,128)} %get-tuple-element.48), calls=%async_computation | async-start | bytes 524288 | tf_op jit(solution)/shard_map/all_to_all | solution.py:194
  87.8 16.3 %collective-permute-start.25 = (f32[32,2048]{1,0:T(8,128)S(1)}, f32[32,2048]{1,0:T(8,128)S(1)}, u32[]{:S(2)}, u32[]{:S(2)}) collective-permute-start(f32[32,2048]{1,0:T(8,128)S(1)} %get-tuple-element.50), channel_id=1, source_target_pairs={{4,0},{129,1},{6,2},{131,3},{0,4},{133,5},{2,6},{135,7},{12,8},{13... | collective-permute-start | bytes 786440 | tf_op jit(solution)/shard_map/ppermute | solution.py:21
  89.4 14.8 %collective-permute-start.27 = (f32[32,2048]{1,0:T(8,128)S(1)}, f32[32,2048]{1,0:T(8,128)S(1)}, u32[]{:S(2)}, u32[]{:S(2)}) collective-permute-start(f32[32,2048]{1,0:T(8,128)S(1)} %get-tuple-element.51), channel_id=1, source_target_pairs={{2,0},{65,1},{4,2},{67,3},{6,4},{69,5},{0,6},{71,7},{10,8},{73,9},... | collective-permute-start | bytes 786440 | tf_op jit(solution)/shard_map/ppermute | solution.py:21
  90.7 13.5 %collective-permute-start.26 = (f32[32,2048]{1,0:T(8,128)S(1)}, f32[32,2048]{1,0:T(8,128)S(1)}, u32[]{:S(2)}, u32[]{:S(2)}) collective-permute-start(f32[32,2048]{1,0:T(8,128)S(1)} %get-tuple-element.52), channel_id=1, source_target_pairs={{6,0},{193,1},{0,2},{195,3},{2,4},{197,5},{4,6},{199,7},{14,8},{20... | collective-permute-start | bytes 786440 | tf_op jit(solution)/shard_map/ppermute | solution.py:21
  92.1 5.7 %collective-permute-start.21 = (f32[8,128]{1,0:T(8,128)S(1)}, f32[8,128]{1,0:T(8,128)S(1)}, u32[]{:S(2)}, u32[]{:S(2)}) collective-permute-start(f32[8,128]{1,0:T(8,128)S(1)} %reduce_sum.9), channel_id=1, source_target_pairs={{6,0},{7,1},{0,2},{1,3},{2,4},{3,5},{4,6},{5,7},{14,8},{15,9},{8,1... | collective-permute-start | bytes 12296 | tf_op jit(solution)/shard_map/ppermute | solution.py:21
  94.2 6.5 %collective-permute-start.20 = (f32[8,128]{1,0:T(8,128)S(1)}, f32[8,128]{1,0:T(8,128)S(1)}, u32[]{:S(2)}, u32[]{:S(2)}) collective-permute-start(f32[8,128]{1,0:T(8,128)S(1)} %reduce_sum.9), channel_id=1, source_target_pairs={{2,0},{3,1},{4,2},{5,3},{6,4},{7,5},{0,6},{1,7},{10,8},{11,9},{12,... | collective-permute-start | bytes 12296 | tf_op jit(solution)/shard_map/ppermute | solution.py:21
  97.9 5.1 %collective-permute-start.19 = (f32[8,128]{1,0:T(8,128)S(1)}, f32[8,128]{1,0:T(8,128)S(1)}, u32[]{:S(2)}, u32[]{:S(2)}) collective-permute-start(f32[8,128]{1,0:T(8,128)S(1)} %reduce_sum.9), channel_id=1, source_target_pairs={{4,0},{5,1},{6,2},{7,3},{0,4},{1,5},{2,6},{3,7},{12,8},{13,9},{14,... | collective-permute-start | bytes 12296 | tf_op jit(solution)/shard_map/ppermute | solution.py:21

commit v8 on v7

--- a/solution.py
+++ b/solution.py
@@ -107,7 +107,7 @@
         out_shape=(scaled,) * 3
         + (
             jax.ShapeDtypeStruct((count, texts), jnp.bfloat16),
-            jax.ShapeDtypeStruct((8, 128), jnp.float32),
+            jax.ShapeDtypeStruct((1, 128), jnp.float32),
         ),
         scratch_shapes=[
             pltpu.VMEM((student_width // DEPTH, texts, DEPTH), jnp.bfloat16),

time: 108 us -> 106 us (0.981); the launches traced: 106 us -> 105 us
  waiting for transfers between devices: 47.4 us -> 50.1 us
  starting transfers between devices: 41.7 us -> 40.4 us
    ppermute x18, waiting for transfers between devices: 15.3 us -> 18 us  [shift(): return lax.ppermute(value, AXES, pairs)]
    ppermute x18, starting transfers between devices: 25.7 us -> 24.4 us  [shift(): return lax.ppermute(value, AXES, pairs)]
  transfers between devices with their start and end apart: 29 -> 29, of which waited for: 13 -> 13; matrix products, arithmetic and copies ran while one was open for 6% -> 4% of each run, Pallas kernels for 1% -> 1%
where the time goes in v8:
time: 106 us; the launch traced here: 105 us
  waiting for transfers between devices  50.1 us (47%)
  starting transfers between devices  40.4 us (38%)
  Pallas kernels  7.38 us (7%)
  other arithmetic  4.17 us (4%)
  between operations  2.03 us (2%)
  local copies, waits for them, and re-layouts  1.24 us (1%)
    ppermute x5, waiting for transfers between devices, round_z(): return lax.ppermute(value, AXES, pairs)  32.1 us
    ppermute x18, starting transfers between devices, shift(): return lax.ppermute(value, AXES, pairs)  24.4 us
    ppermute x18, waiting for transfers between devices, shift(): return lax.ppermute(value, AXES, pairs)  18 us
    all_to_all x1, starting transfers between devices, shards(): lax.all_to_all(squares, ('y', 'zh', 'zl', 'core'), 0, 0)  8.18 us
    pallas_call x1, Pallas kernels, pulls(): pl.pallas_call(excess_kernel, in_specs=[inside] * (len(pieces) + len(line...  4.63 us
    ppermute x5, starting transfers between devices, round_z(): return lax.ppermute(value, AXES, pairs)  4 us
    ppermute x5, starting transfers between devices, other_core(): return lax.ppermute(value, 'core', [(0, 1), (1, 0)])  3.81 us
  transfers between devices with their start and end apart: 29, of which 13 were waited for; matrix products, arithmetic and copies ran while one was open for 4% of the time, Pallas kernels for 1%

profile of v8, /device:TPU:2, one launch (start us, length us, event | category | flops | bytes accessed | tf_op | source)
XLA Modules:
  0.0 105.3 jit_solution(9214766753313657797)
XLA Ops:
  0.6 1.8 %shard_map.41.refs_8_.refs_0_ = bf16[32,6144]{1,0:T(8,128)(2,1)} custom-call(bf16[32,2048]{1,0:T(8,128)(2,1)} %student_ref.1, bf16[32,4096]{1,0:T(8,128)(2,1)} %teacher_ref.1), custom_call_target="tpu_custom_call" | custom-call | tf_op jit(solution)/shard_map/pallas_call | solution.py:45
  2.4 1.9 %collective-permute-start = (bf16[32,6144]{1,0:T(8,128)(2,1)}, bf16[32,6144]{1,0:T(8,128)(2,1)S(1)}, u32[]{:S(2)}, u32[]{:S(2)}) collective-permute-start(bf16[32,6144]{1,0:T(8,128)(2,1)} %shard_map.41.refs_8_.refs_0_), channel_id=1, source_target_pairs={{56,0},{17,1},{58,2},{19,3},{60,4},{21,5},{62,6},{23,7},{48,8},{25... | collective-permute-start | bytes 1179656 | tf_op jit(solution)/shard_map/ppermute | solution.py:30
  4.4 2.1 %collective-permute-start.6 = (bf16[32,6144]{1,0:T(8,128)(2,1)}, bf16[32,6144]{1,0:T(8,128)(2,1)S(1)}, u32[]{:S(2)}, u32[]{:S(2)}) collective-permute-start(bf16[32,6144]{1,0:T(8,128)(2,1)} %shard_map.41.refs_8_.refs_0_), channel_id=1, source_target_pairs={{4,0},{129,1},{6,2},{131,3},{0,4},{133,5},{2,6},{135,7},{12,8},{13... | collective-permute-start | bytes 1179656 | tf_op jit(solution)/shard_map/ppermute | solution.py:21
  6.5 1.6 %collective-permute-start.5 = (bf16[32,6144]{1,0:T(8,128)(2,1)}, bf16[32,6144]{1,0:T(8,128)(2,1)S(1)}, u32[]{:S(2)}, u32[]{:S(2)}) collective-permute-start(bf16[32,6144]{1,0:T(8,128)(2,1)} %shard_map.41.refs_8_.refs_0_), channel_id=1, source_target_pairs={{6,0},{193,1},{0,2},{195,3},{2,4},{197,5},{4,6},{199,7},{14,8},{20... | collective-permute-start | bytes 1179656 | tf_op jit(solution)/shard_map/ppermute | solution.py:21
  8.1 0.4 collective-permute-start.4
  8.5 1.9 %collective-permute-start.2 = (bf16[32,6144]{1,0:T(8,128)(2,1)S(1)}, bf16[32,6144]{1,0:T(8,128)(2,1)S(1)}, u32[]{:S(2)}, u32[]{:S(2)}) collective-permute-start(bf16[32,6144]{1,0:T(8,128)(2,1)S(1)} %collective-permute-done.1.refs_9_.refs_1_), channel_id=1, source_target_pairs={{56,0},{17,1},{58,2},{19,3},{60,4},{21,5},{62,6},{23,7},{48,8},{25... | collective-permute-start | bytes 1179656 | tf_op jit(solution)/shard_map/ppermute | solution.py:30
  10.4 1.0 constant_dynamic-update-slice_fusion.3
  11.5 2.8 %collective-permute-done = bf16[32,6144]{1,0:T(8,128)(2,1)S(1)} collective-permute-done((bf16[32,6144]{1,0:T(8,128)(2,1)}, bf16[32,6144]{1,0:T(8,128)(2,1)S(1)}, u32[]{:S(2)}, u32[]{:S(2)}) %collective-permute-start) | collective-permute-done | bytes 393248 | tf_op jit(solution)/shard_map/ppermute | solution.py:30
  14.3 5.8 %collective-permute-done.2 = bf16[32,6144]{1,0:T(8,128)(2,1)S(1)} collective-permute-done((bf16[32,6144]{1,0:T(8,128)(2,1)S(1)}, bf16[32,6144]{1,0:T(8,128)(2,1)S(1)}, u32[]{:S(2)}, u32[]{:S(2)}) %collective-permute-start.2) | collective-permute-done | bytes 393248 | tf_op jit(solution)/shard_map/ppermute | solution.py:30
  20.2 0.1 collective-permute-start.3
  20.4 3.1 %collective-permute-start.7 = (bf16[64,6144]{1,0:T(8,128)(2,1)S(1)}, bf16[64,6144]{1,0:T(8,128)(2,1)S(1)}, u32[]{:S(2)}, u32[]{:S(2)}) collective-permute-start(bf16[64,6144]{1,0:T(8,128)(2,1)S(1)} %constant_dynamic-update-slice_fusion.2.refs_6_), channel_id=1, source_target_pairs={{64,0},{3,1},{66,2},{5,3},{68,4},{7,5},{70,6},{1,7},{72,8},{11,9},... | collective-permute-start | bytes 2359304 | tf_op jit(solution)/shard_map/ppermute | solution.py:21
  23.5 0.1 collective-permute-start.8
  23.6 9.9 %collective-permute-done.3.refs_12_.refs_4_ = bf16[64,6144]{1,0:T(8,128)(2,1)S(1)} collective-permute-done((bf16[64,6144]{1,0:T(8,128)(2,1)S(1)}, bf16[64,6144]{1,0:T(8,128)(2,1)S(1)}, u32[]{:S(2)}, u32[]{:S(2)}) %collective-permute-start.3) | collective-permute-done | bytes 786464 | tf_op jit(solution)/shard_map/ppermute | solution.py:30
  33.4 2.5 %collective-permute-start.14 = (bf16[64,6144]{1,0:T(8,128)(2,1)S(1)}, bf16[64,6144]{1,0:T(8,128)(2,1)S(1)}, u32[]{:S(2)}, u32[]{:S(2)}) collective-permute-start(bf16[64,6144]{1,0:T(8,128)(2,1)S(1)} %constant_dynamic-update-slice_fusion.refs_10_.refs_2_), channel_id=1, source_target_pairs={{0,1},{1,0},{2,3},{3,2},{4,5},{5,4},{6,7},{7,6},{8,9},{9,8},{10,11... | collective-permute-start | bytes 2359304 | tf_op jit(solution)/shard_map/ppermute | solution.py:34
  36.0 0.8 collective-permute-done.8.refs_5_
  36.8 2.0 %collective-permute-start.10 = (bf16[64,6144]{1,0:T(8,128)(2,1)S(1)}, bf16[64,6144]{1,0:T(8,128)(2,1)S(1)}, u32[]{:S(2)}, u32[]{:S(2)}) collective-permute-start(bf16[64,6144]{1,0:T(8,128)(2,1)S(1)} %collective-permute-done.8.refs_5_), channel_id=1, source_target_pairs={{192,0},{7,1},{194,2},{1,3},{196,4},{3,5},{198,6},{5,7},{200,8},{1... | collective-permute-start | bytes 2359304 | tf_op jit(solution)/shard_map/ppermute | solution.py:21
  38.8 1.2 %collective-permute-start.12 = (bf16[64,6144]{1,0:T(8,128)(2,1)S(1)}, bf16[64,6144]{1,0:T(8,128)(2,1)S(1)}, u32[]{:S(2)}, u32[]{:S(2)}) collective-permute-start(bf16[64,6144]{1,0:T(8,128)(2,1)S(1)} %constant_dynamic-update-slice_fusion.4.refs_7_), channel_id=1, source_target_pairs={{64,0},{3,1},{66,2},{5,3},{68,4},{7,5},{70,6},{1,7},{72,8},{11,9},... | collective-permute-start | bytes 2359304 | tf_op jit(solution)/shard_map/ppermute | solution.py:21
  40.0 6.6 %collective-permute-done.11.refs_14_.refs_6_ = bf16[64,6144]{1,0:T(8,128)(2,1)S(1)} collective-permute-done((bf16[64,6144]{1,0:T(8,128)(2,1)S(1)}, bf16[64,6144]{1,0:T(8,128)(2,1)S(1)}, u32[]{:S(2)}, u32[]{:S(2)}) %collective-permute-start.11) | collective-permute-done | bytes 786464 | tf_op jit(solution)/shard_map/ppermute | solution.py:30
  46.6 1.6 %collective-permute-start.13 = (bf16[64,6144]{1,0:T(8,128)(2,1)S(1)}, bf16[64,6144]{1,0:T(8,128)(2,1)S(1)}, u32[]{:S(2)}, u32[]{:S(2)}) collective-permute-start(bf16[64,6144]{1,0:T(8,128)(2,1)S(1)} %constant_dynamic-update-slice_fusion.2.refs_6_), channel_id=1, source_target_pairs={{192,0},{7,1},{194,2},{1,3},{196,4},{3,5},{198,6},{5,7},{200,8},{1... | collective-permute-start | bytes 2359304 | tf_op jit(solution)/shard_map/ppermute | solution.py:21
  48.3 0.1 collective-permute-start.17
  48.3 0.4 collective-permute-done.9.refs_0_
  48.8 0.9 collective-permute-start.15
  49.6 0.3 collective-permute-done.10.refs_1_
  50.0 0.4 collective-permute-start.16
  50.4 7.0 %collective-permute-done.17.refs_16_.refs_8_ = bf16[32,6144]{1,0:T(8,128)(2,1)S(1)} collective-permute-done((bf16[32,6144]{1,0:T(8,128)(2,1)S(1)}, bf16[32,6144]{1,0:T(8,128)(2,1)S(1)}, u32[]{:S(2)}, u32[]{:S(2)}) %collective-permute-start.17) | collective-permute-done | bytes 393248 | tf_op jit(solution)/shard_map/ppermute | solution.py:30
  57.3 2.5 %collective-permute-done.13.refs_4_ = bf16[64,6144]{1,0:T(8,128)(2,1)S(1)} collective-permute-done((bf16[64,6144]{1,0:T(8,128)(2,1)S(1)}, bf16[64,6144]{1,0:T(8,128)(2,1)S(1)}, u32[]{:S(2)}, u32[]{:S(2)}) %collective-permute-start.13) | collective-permute-done | bytes 786464 | tf_op jit(solution)/shard_map/ppermute | solution.py:21
  59.9 4.6 %shard_map.42 = (f32[144,2048]{1,0:T(8,128)S(1)}, f32[144,2048]{1,0:T(8,128)S(1)}, f32[144,2048]{1,0:T(8,128)S(1)}, bf16[128,512]{1,0:T(8,128)(2,1)S(1)}, f32[1,128]{1,0:T(1,128)S(1)}) custom-call(bf16[64,6144]{1,0:T(8,128)(2,1)S(1)} %collective-permute-done.9.refs_0_, bf16[64,6144]{1,0:T(8,128)(2,1)S(1)} %collective-permute-done.10.refs_1_, ...), custom_call_target="tpu_custom_call" | custom-call | flops 4294967296 | bytes 12582912 | tf_op jit(solution)/shard_map/pallas_call | solution.py:103
  64.5 0.1 convert_element_type.29
  64.6 1.9 %collective-permute-start.24 = (f16[144,2048]{1,0:T(8,128)(2,1)S(1)}, f16[144,2048]{1,0:T(8,128)(2,1)S(1)}, u32[]{:S(2)}, u32[]{:S(2)}) collective-permute-start(f16[144,2048]{1,0:T(8,128)(2,1)S(1)} %convert_element_type.29), channel_id=1, source_target_pairs={{64,0},{3,1},{66,2},{5,3},{68,4},{7,5},{70,6},{1,7},{72,8},{11,9},... | collective-permute-start | bytes 1769480 | tf_op jit(solution)/shard_map/ppermute | solution.py:21
  66.5 0.3 collective-permute-start.23
  66.9 2.2 %collective-permute-start.22 = (f16[144,2048]{1,0:T(8,128)(2,1)S(1)}, f16[144,2048]{1,0:T(8,128)(2,1)}, u32[]{:S(2)}, u32[]{:S(2)}) collective-permute-start(f16[144,2048]{1,0:T(8,128)(2,1)S(1)} %convert_element_type.27), channel_id=1, source_target_pairs={{128,0},{5,1},{130,2},{7,3},{132,4},{1,5},{134,6},{3,7},{136,8},{1... | collective-permute-start | bytes 1769480 | tf_op jit(solution)/shard_map/ppermute | solution.py:21
  69.1 0.9 shard_map.43
  70.0 8.2 %all-to-all-start = ((f32[64,1,128]{2,1,0:T(1,128)}), f32[64,1,128]{2,1,0:T(1,128)S(1)}, u32[]{:S(2)}, u32[]{:S(2)}) async-start(f32[64,1,128]{2,1,0:T(1,128)} %get-tuple-element.48), calls=%async_computation | async-start | bytes 65536 | tf_op jit(solution)/shard_map/all_to_all | solution.py:194
  78.2 2.0 %collective-permute-done.24 = f16[144,2048]{1,0:T(8,128)(2,1)S(1)} collective-permute-done((f16[144,2048]{1,0:T(8,128)(2,1)S(1)}, f16[144,2048]{1,0:T(8,128)(2,1)S(1)}, u32[]{:S(2)}, u32[]{:S(2)}) %collective-permute-start.24) | collective-permute-done | bytes 589856 | tf_op jit(solution)/shard_map/ppermute | solution.py:21
  80.3 4.0 %collective-permute-done.23 = f16[144,2048]{1,0:T(8,128)(2,1)} collective-permute-done((f16[144,2048]{1,0:T(8,128)(2,1)S(1)}, f16[144,2048]{1,0:T(8,128)(2,1)}, u32[]{:S(2)}, u32[]{:S(2)}) %collective-permute-start.23) | collective-permute-done | bytes 589856 | tf_op jit(solution)/shard_map/ppermute | solution.py:21
  84.2 0.8 fusion.3
  85.0 0.8 fusion.2
  85.8 1.6 %multiply_add_fusion = f32[128,2048]{1,0:T(8,128)S(1)} fusion(f32[128,2048]{1,0:T(8,128)S(1)} %get-tuple-element.49, f16[144,2048]{1,0:T(8,128)(2,1)S(1)} %collective-permute-done.24, f16[144,2048]{1,0:T(8,128)(2,1)} %collective-permute-done.23, f16[144,2048]{1,0:T(8,128)(2,1)} %collective-permute-done.22, f32[2048]{0:T(1024)S(1)} %bitcast.7, ...), kind=kLoop, calls=%fused_computation | loop fusion | flops 2359296 | bytes 3694592 | tf_op jit(solution)/shard_map/add | solution.py:188
  87.4 1.6 %collective-permute-start.25 = (f32[32,2048]{1,0:T(8,128)S(1)}, f32[32,2048]{1,0:T(8,128)S(1)}, u32[]{:S(2)}, u32[]{:S(2)}) collective-permute-start(f32[32,2048]{1,0:T(8,128)S(1)} %get-tuple-element.50), channel_id=1, source_target_pairs={{4,0},{129,1},{6,2},{131,3},{0,4},{133,5},{2,6},{135,7},{12,8},{13... | collective-permute-start | bytes 786440 | tf_op jit(solution)/shard_map/ppermute | solution.py:21
  89.0 1.3 %collective-permute-start.27 = (f32[32,2048]{1,0:T(8,128)S(1)}, f32[32,2048]{1,0:T(8,128)S(1)}, u32[]{:S(2)}, u32[]{:S(2)}) collective-permute-start(f32[32,2048]{1,0:T(8,128)S(1)} %get-tuple-element.51), channel_id=1, source_target_pairs={{2,0},{65,1},{4,2},{67,3},{6,4},{69,5},{0,6},{71,7},{10,8},{73,9},... | collective-permute-start | bytes 786440 | tf_op jit(solution)/shard_map/ppermute | solution.py:21
  90.2 1.4 %collective-permute-start.26 = (f32[32,2048]{1,0:T(8,128)S(1)}, f32[32,2048]{1,0:T(8,128)S(1)}, u32[]{:S(2)}, u32[]{:S(2)}) collective-permute-start(f32[32,2048]{1,0:T(8,128)S(1)} %get-tuple-element.52), channel_id=1, source_target_pairs={{6,0},{193,1},{0,2},{195,3},{2,4},{197,5},{4,6},{199,7},{14,8},{20... | collective-permute-start | bytes 786440 | tf_op jit(solution)/shard_map/ppermute | solution.py:21
  91.6 0.1 reduce_sum.11
  91.7 0.7 collective-permute-start.20
  92.4 1.5 %collective-permute-start.21 = (f32[1,128]{1,0:T(1,128)S(1)}, f32[1,128]{1,0:T(1,128)S(1)}, u32[]{:S(2)}, u32[]{:S(2)}) collective-permute-start(f32[1,128]{1,0:T(1,128)S(1)} %bitcast.11), channel_id=1, source_target_pairs={{6,0},{7,1},{0,2},{1,3},{2,4},{3,5},{4,6},{5,7},{14,8},{15,9},{8,1... | collective-permute-start | bytes 1544 | tf_op jit(solution)/shard_map/ppermute | solution.py:21
  93.9 4.4 %collective-permute-done.20 = f32[1,128]{1,0:T(1,128)S(1)} collective-permute-done((f32[1,128]{1,0:T(1,128)S(1)}, f32[1,128]{1,0:T(1,128)S(1)}, u32[]{:S(2)}, u32[]{:S(2)}) %collective-permute-start.20) | collective-permute-done | bytes 544 | tf_op jit(solution)/shard_map/ppermute | solution.py:21
  98.2 1.5 %collective-permute-start.19 = (f32[1,128]{1,0:T(1,128)S(1)}, f32[1,128]{1,0:T(1,128)S(1)}, u32[]{:S(2)}, u32[]{:S(2)}) collective-permute-start(f32[1,128]{1,0:T(1,128)S(1)} %bitcast.12), channel_id=1, source_target_pairs={{4,0},{5,1},{6,2},{7,3},{0,4},{1,5},{2,6},{3,7},{12,8},{13,9},{14,... | collective-permute-start | bytes 1544 | tf_op jit(solution)/shard_map/ppermute | solution.py:21
  99.7 3.6 %collective-permute-done.19 = f32[1,128]{1,0:T(1,128)S(1)} collective-permute-done((f32[1,128]{1,0:T(1,128)S(1)}, f32[1,128]{1,0:T(1,128)S(1)}, u32[]{:S(2)}, u32[]{:S(2)}) %collective-permute-start.19) | collective-permute-done | bytes 544 | tf_op jit(solution)/shard_map/ppermute | solution.py:21
  103.4 0.8 fusion.1
  (33 shorter events, 0.4 us)
Async XLA Ops:
  2.4 1.9 %collective-permute-start.1 = (bf16[32,6144]{1,0:T(8,128)(2,1)}, bf16[32,6144]{1,0:T(8,128)(2,1)S(1)}, u32[]{:S(2)}, u32[]{:S(2)}) collective-permute-start(bf16[32,6144]{1,0:T(8,128)(2,1)} %shard_map.41.refs_8_.refs_0_), channel_id=1, source_target_pairs={{0,1},{1,0},{2,3},{3,2},{4,5},{5,4},{6,7},{7,6},{8,9},{9,8},{10,11... | collective-permute-start | bytes 1179656 | tf_op jit(solution)/shard_map/ppermute | solution.py:34
  2.4 11.8 %collective-permute-start = (bf16[32,6144]{1,0:T(8,128)(2,1)}, bf16[32,6144]{1,0:T(8,128)(2,1)S(1)}, u32[]{:S(2)}, u32[]{:S(2)}) collective-permute-start(bf16[32,6144]{1,0:T(8,128)(2,1)} %shard_map.41.refs_8_.refs_0_), channel_id=1, source_target_pairs={{56,0},{17,1},{58,2},{19,3},{60,4},{21,5},{62,6},{23,7},{48,8},{25... | collective-permute-start | bytes 1179656 | tf_op jit(solution)/shard_map/ppermute | solution.py:30
  4.4 15.9 %collective-permute-start.6 = (bf16[32,6144]{1,0:T(8,128)(2,1)}, bf16[32,6144]{1,0:T(8,128)(2,1)S(1)}, u32[]{:S(2)}, u32[]{:S(2)}) collective-permute-start(bf16[32,6144]{1,0:T(8,128)(2,1)} %shard_map.41.refs_8_.refs_0_), channel_id=1, source_target_pairs={{4,0},{129,1},{6,2},{131,3},{0,4},{133,5},{2,6},{135,7},{12,8},{13... | collective-permute-start | bytes 1179656 | tf_op jit(solution)/shard_map/ppermute | solution.py:21
  6.5 13.8 %collective-permute-start.5 = (bf16[32,6144]{1,0:T(8,128)(2,1)}, bf16[32,6144]{1,0:T(8,128)(2,1)S(1)}, u32[]{:S(2)}, u32[]{:S(2)}) collective-permute-start(bf16[32,6144]{1,0:T(8,128)(2,1)} %shard_map.41.refs_8_.refs_0_), channel_id=1, source_target_pairs={{6,0},{193,1},{0,2},{195,3},{2,4},{197,5},{4,6},{199,7},{14,8},{20... | collective-permute-start | bytes 1179656 | tf_op jit(solution)/shard_map/ppermute | solution.py:21
  8.1 12.2 %collective-permute-start.4 = (bf16[32,6144]{1,0:T(8,128)(2,1)}, bf16[32,6144]{1,0:T(8,128)(2,1)S(1)}, u32[]{:S(2)}, u32[]{:S(2)}) collective-permute-start(bf16[32,6144]{1,0:T(8,128)(2,1)} %shard_map.41.refs_8_.refs_0_), channel_id=1, source_target_pairs={{2,0},{65,1},{4,2},{67,3},{6,4},{69,5},{0,6},{71,7},{10,8},{73,9},... | collective-permute-start | bytes 1179656 | tf_op jit(solution)/shard_map/ppermute | solution.py:21
  8.5 11.6 %collective-permute-start.2 = (bf16[32,6144]{1,0:T(8,128)(2,1)S(1)}, bf16[32,6144]{1,0:T(8,128)(2,1)S(1)}, u32[]{:S(2)}, u32[]{:S(2)}) collective-permute-start(bf16[32,6144]{1,0:T(8,128)(2,1)S(1)} %collective-permute-done.1.refs_9_.refs_1_), channel_id=1, source_target_pairs={{56,0},{17,1},{58,2},{19,3},{60,4},{21,5},{62,6},{23,7},{48,8},{25... | collective-permute-start | bytes 1179656 | tf_op jit(solution)/shard_map/ppermute | solution.py:30
  20.2 13.3 %collective-permute-start.3 = (bf16[64,6144]{1,0:T(8,128)(2,1)S(1)}, bf16[64,6144]{1,0:T(8,128)(2,1)S(1)}, u32[]{:S(2)}, u32[]{:S(2)}) collective-permute-start(bf16[64,6144]{1,0:T(8,128)(2,1)S(1)} %constant_dynamic-update-slice_fusion.refs_10_.refs_2_), channel_id=1, source_target_pairs={{56,0},{17,1},{58,2},{19,3},{60,4},{21,5},{62,6},{23,7},{48,8},{25... | collective-permute-start | bytes 2359304 | tf_op jit(solution)/shard_map/ppermute | solution.py:30
  20.3 39.5 %copy-start = (bf16[32,6144]{1,0:T(8,128)(2,1)S(1)}, bf16[32,6144]{1,0:T(8,128)(2,1)}, u32[]{:S(2)}) copy-start(bf16[32,6144]{1,0:T(8,128)(2,1)} %shard_map.41.refs_8_.refs_0_) | copy-start | bytes 1179652
  20.4 15.6 %collective-permute-start.7 = (bf16[64,6144]{1,0:T(8,128)(2,1)S(1)}, bf16[64,6144]{1,0:T(8,128)(2,1)S(1)}, u32[]{:S(2)}, u32[]{:S(2)}) collective-permute-start(bf16[64,6144]{1,0:T(8,128)(2,1)S(1)} %constant_dynamic-update-slice_fusion.2.refs_6_), channel_id=1, source_target_pairs={{64,0},{3,1},{66,2},{5,3},{68,4},{7,5},{70,6},{1,7},{72,8},{11,9},... | collective-permute-start | bytes 2359304 | tf_op jit(solution)/shard_map/ppermute | solution.py:21
  23.5 13.3 %collective-permute-start.8 = (bf16[64,6144]{1,0:T(8,128)(2,1)S(1)}, bf16[64,6144]{1,0:T(8,128)(2,1)S(1)}, u32[]{:S(2)}, u32[]{:S(2)}) collective-permute-start(bf16[64,6144]{1,0:T(8,128)(2,1)S(1)} %constant_dynamic-update-slice_fusion.4.refs_7_), channel_id=1, source_target_pairs={{192,0},{7,1},{194,2},{1,3},{196,4},{3,5},{198,6},{5,7},{200,8},{1... | collective-permute-start | bytes 2359304 | tf_op jit(solution)/shard_map/ppermute | solution.py:21
  33.4 13.2 %collective-permute-start.11 = (bf16[64,6144]{1,0:T(8,128)(2,1)S(1)}, bf16[64,6144]{1,0:T(8,128)(2,1)S(1)}, u32[]{:S(2)}, u32[]{:S(2)}) collective-permute-start(bf16[64,6144]{1,0:T(8,128)(2,1)S(1)} %collective-permute-done.3.refs_12_.refs_4_), channel_id=1, source_target_pairs={{56,0},{17,1},{58,2},{19,3},{60,4},{21,5},{62,6},{23,7},{48,8},{25... | collective-permute-start | bytes 2359304 | tf_op jit(solution)/shard_map/ppermute | solution.py:30
  33.4 14.8 %collective-permute-start.14 = (bf16[64,6144]{1,0:T(8,128)(2,1)S(1)}, bf16[64,6144]{1,0:T(8,128)(2,1)S(1)}, u32[]{:S(2)}, u32[]{:S(2)}) collective-permute-start(bf16[64,6144]{1,0:T(8,128)(2,1)S(1)} %constant_dynamic-update-slice_fusion.refs_10_.refs_2_), channel_id=1, source_target_pairs={{0,1},{1,0},{2,3},{3,2},{4,5},{5,4},{6,7},{7,6},{8,9},{9,8},{10,11... | collective-permute-start | bytes 2359304 | tf_op jit(solution)/shard_map/ppermute | solution.py:34
  36.8 12.0 %collective-permute-start.9 = (bf16[64,6144]{1,0:T(8,128)(2,1)S(1)}, bf16[64,6144]{1,0:T(8,128)(2,1)S(1)}, u32[]{:S(2)}, u32[]{:S(2)}) collective-permute-start(bf16[64,6144]{1,0:T(8,128)(2,1)S(1)} %collective-permute-done.7.refs_2_), channel_id=1, source_target_pairs={{64,0},{3,1},{66,2},{5,3},{68,4},{7,5},{70,6},{1,7},{72,8},{11,9},... | collective-permute-start | bytes 2359304 | tf_op jit(solution)/shard_map/ppermute | solution.py:21
  36.8 13.2 %collective-permute-start.10 = (bf16[64,6144]{1,0:T(8,128)(2,1)S(1)}, bf16[64,6144]{1,0:T(8,128)(2,1)S(1)}, u32[]{:S(2)}, u32[]{:S(2)}) collective-permute-start(bf16[64,6144]{1,0:T(8,128)(2,1)S(1)} %collective-permute-done.8.refs_5_), channel_id=1, source_target_pairs={{192,0},{7,1},{194,2},{1,3},{196,4},{3,5},{198,6},{5,7},{200,8},{1... | collective-permute-start | bytes 2359304 | tf_op jit(solution)/shard_map/ppermute | solution.py:21
  38.8 18.5 %collective-permute-start.12 = (bf16[64,6144]{1,0:T(8,128)(2,1)S(1)}, bf16[64,6144]{1,0:T(8,128)(2,1)S(1)}, u32[]{:S(2)}, u32[]{:S(2)}) collective-permute-start(bf16[64,6144]{1,0:T(8,128)(2,1)S(1)} %constant_dynamic-update-slice_fusion.4.refs_7_), channel_id=1, source_target_pairs={{64,0},{3,1},{66,2},{5,3},{68,4},{7,5},{70,6},{1,7},{72,8},{11,9},... | collective-permute-start | bytes 2359304 | tf_op jit(solution)/shard_map/ppermute | solution.py:21
  46.6 13.2 %collective-permute-start.13 = (bf16[64,6144]{1,0:T(8,128)(2,1)S(1)}, bf16[64,6144]{1,0:T(8,128)(2,1)S(1)}, u32[]{:S(2)}, u32[]{:S(2)}) collective-permute-start(bf16[64,6144]{1,0:T(8,128)(2,1)S(1)} %constant_dynamic-update-slice_fusion.2.refs_6_), channel_id=1, source_target_pairs={{192,0},{7,1},{194,2},{1,3},{196,4},{3,5},{198,6},{5,7},{200,8},{1... | collective-permute-start | bytes 2359304 | tf_op jit(solution)/shard_map/ppermute | solution.py:21
  48.3 9.1 %collective-permute-start.17 = (bf16[32,6144]{1,0:T(8,128)(2,1)S(1)}, bf16[32,6144]{1,0:T(8,128)(2,1)S(1)}, u32[]{:S(2)}, u32[]{:S(2)}) collective-permute-start(bf16[32,6144]{1,0:T(8,128)(2,1)S(1)} %slice.40), channel_id=1, source_target_pairs={{56,0},{17,1},{58,2},{19,3},{60,4},{21,5},{62,6},{23,7},{48,8},{25... | collective-permute-start | bytes 1179656 | tf_op jit(solution)/shard_map/ppermute | solution.py:30
  48.8 11.1 %collective-permute-start.15 = (bf16[64,6144]{1,0:T(8,128)(2,1)S(1)}, bf16[64,6144]{1,0:T(8,128)(2,1)S(1)}, u32[]{:S(2)}, u32[]{:S(2)}) collective-permute-start(bf16[64,6144]{1,0:T(8,128)(2,1)S(1)} %collective-permute-done.3.refs_12_.refs_4_), channel_id=1, source_target_pairs={{0,1},{1,0},{2,3},{3,2},{4,5},{5,4},{6,7},{7,6},{8,9},{9,8},{10,11... | collective-permute-start | bytes 2359304 | tf_op jit(solution)/shard_map/ppermute | solution.py:34
  50.0 9.9 %collective-permute-start.16 = (bf16[64,6144]{1,0:T(8,128)(2,1)S(1)}, bf16[64,6144]{1,0:T(8,128)(2,1)S(1)}, u32[]{:S(2)}, u32[]{:S(2)}) collective-permute-start(bf16[64,6144]{1,0:T(8,128)(2,1)S(1)} %collective-permute-done.11.refs_14_.refs_6_), channel_id=1, source_target_pairs={{0,1},{1,0},{2,3},{3,2},{4,5},{5,4},{6,7},{7,6},{8,9},{9,8},{10,11... | collective-permute-start | bytes 2359304 | tf_op jit(solution)/shard_map/ppermute | solution.py:34
  57.3 2.5 %collective-permute-start.18 = (bf16[32,6144]{1,0:T(8,128)(2,1)S(1)}, bf16[32,6144]{1,0:T(8,128)(2,1)S(1)}, u32[]{:S(2)}, u32[]{:S(2)}) collective-permute-start(bf16[32,6144]{1,0:T(8,128)(2,1)S(1)} %collective-permute-done.17.refs_16_.refs_8_), channel_id=1, source_target_pairs={{0,1},{1,0},{2,3},{3,2},{4,5},{5,4},{6,7},{7,6},{8,9},{9,8},{10,11... | collective-permute-start | bytes 1179656 | tf_op jit(solution)/shard_map/ppermute | solution.py:34
  64.6 15.7 %collective-permute-start.24 = (f16[144,2048]{1,0:T(8,128)(2,1)S(1)}, f16[144,2048]{1,0:T(8,128)(2,1)S(1)}, u32[]{:S(2)}, u32[]{:S(2)}) collective-permute-start(f16[144,2048]{1,0:T(8,128)(2,1)S(1)} %convert_element_type.29), channel_id=1, source_target_pairs={{64,0},{3,1},{66,2},{5,3},{68,4},{7,5},{70,6},{1,7},{72,8},{11,9},... | collective-permute-start | bytes 1769480 | tf_op jit(solution)/shard_map/ppermute | solution.py:21
  66.5 17.7 %collective-permute-start.23 = (f16[144,2048]{1,0:T(8,128)(2,1)S(1)}, f16[144,2048]{1,0:T(8,128)(2,1)}, u32[]{:S(2)}, u32[]{:S(2)}) collective-permute-start(f16[144,2048]{1,0:T(8,128)(2,1)S(1)} %convert_element_type.28), channel_id=1, source_target_pairs={{192,0},{7,1},{194,2},{1,3},{196,4},{3,5},{198,6},{5,7},{200,8},{1... | collective-permute-start | bytes 1769480 | tf_op jit(solution)/shard_map/ppermute | solution.py:21
  66.9 18.1 %collective-permute-start.22 = (f16[144,2048]{1,0:T(8,128)(2,1)S(1)}, f16[144,2048]{1,0:T(8,128)(2,1)}, u32[]{:S(2)}, u32[]{:S(2)}) collective-permute-start(f16[144,2048]{1,0:T(8,128)(2,1)S(1)} %convert_element_type.27), channel_id=1, source_target_pairs={{128,0},{5,1},{130,2},{7,3},{132,4},{1,5},{134,6},{3,7},{136,8},{1... | collective-permute-start | bytes 1769480 | tf_op jit(solution)/shard_map/ppermute | solution.py:21
  70.0 21.6 %all-to-all-start = ((f32[64,1,128]{2,1,0:T(1,128)}), f32[64,1,128]{2,1,0:T(1,128)S(1)}, u32[]{:S(2)}, u32[]{:S(2)}) async-start(f32[64,1,128]{2,1,0:T(1,128)} %get-tuple-element.48), calls=%async_computation | async-start | bytes 65536 | tf_op jit(solution)/shard_map/all_to_all | solution.py:194
  87.4 15.9 %collective-permute-start.25 = (f32[32,2048]{1,0:T(8,128)S(1)}, f32[32,2048]{1,0:T(8,128)S(1)}, u32[]{:S(2)}, u32[]{:S(2)}) collective-permute-start(f32[32,2048]{1,0:T(8,128)S(1)} %get-tuple-element.50), channel_id=1, source_target_pairs={{4,0},{129,1},{6,2},{131,3},{0,4},{133,5},{2,6},{135,7},{12,8},{13... | collective-permute-start | bytes 786440 | tf_op jit(solution)/shard_map/ppermute | solution.py:21
  89.0 14.4 %collective-permute-start.27 = (f32[32,2048]{1,0:T(8,128)S(1)}, f32[32,2048]{1,0:T(8,128)S(1)}, u32[]{:S(2)}, u32[]{:S(2)}) collective-permute-start(f32[32,2048]{1,0:T(8,128)S(1)} %get-tuple-element.51), channel_id=1, source_target_pairs={{2,0},{65,1},{4,2},{67,3},{6,4},{69,5},{0,6},{71,7},{10,8},{73,9},... | collective-permute-start | bytes 786440 | tf_op jit(solution)/shard_map/ppermute | solution.py:21
  90.2 13.1 %collective-permute-start.26 = (f32[32,2048]{1,0:T(8,128)S(1)}, f32[32,2048]{1,0:T(8,128)S(1)}, u32[]{:S(2)}, u32[]{:S(2)}) collective-permute-start(f32[32,2048]{1,0:T(8,128)S(1)} %get-tuple-element.52), channel_id=1, source_target_pairs={{6,0},{193,1},{0,2},{195,3},{2,4},{197,5},{4,6},{199,7},{14,8},{20... | collective-permute-start | bytes 786440 | tf_op jit(solution)/shard_map/ppermute | solution.py:21
  91.7 6.5 %collective-permute-start.20 = (f32[1,128]{1,0:T(1,128)S(1)}, f32[1,128]{1,0:T(1,128)S(1)}, u32[]{:S(2)}, u32[]{:S(2)}) collective-permute-start(f32[1,128]{1,0:T(1,128)S(1)} %bitcast.10), channel_id=1, source_target_pairs={{2,0},{3,1},{4,2},{5,3},{6,4},{7,5},{0,6},{1,7},{10,8},{11,9},{12,... | collective-permute-start | bytes 1544 | tf_op jit(solution)/shard_map/ppermute | solution.py:21
  92.4 7.3 %collective-permute-start.21 = (f32[1,128]{1,0:T(1,128)S(1)}, f32[1,128]{1,0:T(1,128)S(1)}, u32[]{:S(2)}, u32[]{:S(2)}) collective-permute-start(f32[1,128]{1,0:T(1,128)S(1)} %bitcast.11), channel_id=1, source_target_pairs={{6,0},{7,1},{0,2},{1,3},{2,4},{3,5},{4,6},{5,7},{14,8},{15,9},{8,1... | collective-permute-start | bytes 1544 | tf_op jit(solution)/shard_map/ppermute | solution.py:21
  98.2 5.0 %collective-permute-start.19 = (f32[1,128]{1,0:T(1,128)S(1)}, f32[1,128]{1,0:T(1,128)S(1)}, u32[]{:S(2)}, u32[]{:S(2)}) collective-permute-start(f32[1,128]{1,0:T(1,128)S(1)} %bitcast.12), channel_id=1, source_target_pairs={{4,0},{5,1},{6,2},{7,3},{0,4},{1,5},{2,6},{3,7},{12,8},{13,9},{14,... | collective-permute-start | bytes 1544 | tf_op jit(solution)/shard_map/ppermute | solution.py:21

commit v9 on v8

--- a/solution.py
+++ b/solution.py
@@ -174,11 +174,11 @@
     lines += [ring, other_core(ring)]
     ring = round_z(ring[:texts])
     lines += [ring, other_core(ring)]
-    pieces = (first_across, second_across)
-    pieces += (first_up, second_up, first_down, second_down, first, second)
+    pieces = (first_up, second_up, first_down, second_down)
+    pieces += (first_across, second_across, first, second)
     *scaled, own, squares = pulls(pieces, lines, width)
     sent = [term.astype(jnp.float16) for term in scaled]
-    returned = [shift(term, far, -k) for term, k in zip(sent, (2, 1, 3))]
+    returned = [shift(term, far, -k) for term, k in zip(sent, (1, 3, 2))]
     own, squares = lax.optimization_barrier((own, squares, *sent))[:2]
     partial_term, squares = own_pull(own, squares, lines, width)
     count = own.shape[0]

time: 106 us -> 103 us (0.972)
  waiting for transfers between devices: 50.1 us -> 46.9 us
    ppermute x18, waiting for transfers between devices: 18 us -> 14.8 us  [shift(): return lax.ppermute(value, AXES, pairs)]
  transfers between devices with their start and end apart: 29 -> 29, of which waited for: 13 -> 12; matrix products, arithmetic and copies ran while one was open for 4% -> 4% of each run, Pallas kernels for 1% -> 1%
where the time goes in v9:
time: 103 us
  waiting for transfers between devices  46.9 us (46%)
  starting transfers between devices  41 us (40%)
  Pallas kernels  7.38 us (7%)
  other arithmetic  4.17 us (4%)
  between operations  2.04 us (2%)
  local copies, waits for them, and re-layouts  1.24 us (1%)
    ppermute x5, waiting for transfers between devices, round_z(): return lax.ppermute(value, AXES, pairs)  32.1 us
    ppermute x18, starting transfers between devices, shift(): return lax.ppermute(value, AXES, pairs)  24.3 us
    ppermute x18, waiting for transfers between devices, shift(): return lax.ppermute(value, AXES, pairs)  14.8 us
    all_to_all x1, starting transfers between devices, shards(): lax.all_to_all(squares, ('y', 'zh', 'zl', 'core'), 0, 0)  8.85 us
    pallas_call x1, Pallas kernels, pulls(): pl.pallas_call(excess_kernel, in_specs=[inside] * (len(pieces) + len(line...  4.63 us
    ppermute x5, starting transfers between devices, round_z(): return lax.ppermute(value, AXES, pairs)  4 us
    ppermute x5, starting transfers between devices, other_core(): return lax.ppermute(value, 'core', [(0, 1), (1, 0)])  3.81 us
  transfers between devices with their start and end apart: 29, of which 12 were waited for; matrix products, arithmetic and copies ran while one was open for 4% of the time, Pallas kernels for 1%

profile of v9, /device:TPU:2, one launch (start us, length us, event | category | flops | bytes accessed | tf_op | source)
XLA Modules:
  0.0 102.7 jit_solution(18239381300525518935)
XLA Ops:
  0.6 1.8 %shard_map.41.refs_8_.refs_0_ = bf16[32,6144]{1,0:T(8,128)(2,1)} custom-call(bf16[32,2048]{1,0:T(8,128)(2,1)} %student_ref.1, bf16[32,4096]{1,0:T(8,128)(2,1)} %teacher_ref.1), custom_call_target="tpu_custom_call" | custom-call | tf_op jit(solution)/shard_map/pallas_call | solution.py:45
  2.4 1.9 %collective-permute-start = (bf16[32,6144]{1,0:T(8,128)(2,1)}, bf16[32,6144]{1,0:T(8,128)(2,1)S(1)}, u32[]{:S(2)}, u32[]{:S(2)}) collective-permute-start(bf16[32,6144]{1,0:T(8,128)(2,1)} %shard_map.41.refs_8_.refs_0_), channel_id=1, source_target_pairs={{56,0},{17,1},{58,2},{19,3},{60,4},{21,5},{62,6},{23,7},{48,8},{25... | collective-permute-start | bytes 1179656 | tf_op jit(solution)/shard_map/ppermute | solution.py:30
  4.4 2.1 %collective-permute-start.6 = (bf16[32,6144]{1,0:T(8,128)(2,1)}, bf16[32,6144]{1,0:T(8,128)(2,1)S(1)}, u32[]{:S(2)}, u32[]{:S(2)}) collective-permute-start(bf16[32,6144]{1,0:T(8,128)(2,1)} %shard_map.41.refs_8_.refs_0_), channel_id=1, source_target_pairs={{4,0},{129,1},{6,2},{131,3},{0,4},{133,5},{2,6},{135,7},{12,8},{13... | collective-permute-start | bytes 1179656 | tf_op jit(solution)/shard_map/ppermute | solution.py:21
  6.5 1.6 %collective-permute-start.5 = (bf16[32,6144]{1,0:T(8,128)(2,1)}, bf16[32,6144]{1,0:T(8,128)(2,1)S(1)}, u32[]{:S(2)}, u32[]{:S(2)}) collective-permute-start(bf16[32,6144]{1,0:T(8,128)(2,1)} %shard_map.41.refs_8_.refs_0_), channel_id=1, source_target_pairs={{6,0},{193,1},{0,2},{195,3},{2,4},{197,5},{4,6},{199,7},{14,8},{20... | collective-permute-start | bytes 1179656 | tf_op jit(solution)/shard_map/ppermute | solution.py:21
  8.1 0.4 collective-permute-start.4
  8.5 1.9 %collective-permute-start.2 = (bf16[32,6144]{1,0:T(8,128)(2,1)S(1)}, bf16[32,6144]{1,0:T(8,128)(2,1)S(1)}, u32[]{:S(2)}, u32[]{:S(2)}) collective-permute-start(bf16[32,6144]{1,0:T(8,128)(2,1)S(1)} %collective-permute-done.1.refs_9_.refs_1_), channel_id=1, source_target_pairs={{56,0},{17,1},{58,2},{19,3},{60,4},{21,5},{62,6},{23,7},{48,8},{25... | collective-permute-start | bytes 1179656 | tf_op jit(solution)/shard_map/ppermute | solution.py:30
  10.4 1.0 constant_dynamic-update-slice_fusion.3
  11.5 2.8 %collective-permute-done = bf16[32,6144]{1,0:T(8,128)(2,1)S(1)} collective-permute-done((bf16[32,6144]{1,0:T(8,128)(2,1)}, bf16[32,6144]{1,0:T(8,128)(2,1)S(1)}, u32[]{:S(2)}, u32[]{:S(2)}) %collective-permute-start) | collective-permute-done | bytes 393248 | tf_op jit(solution)/shard_map/ppermute | solution.py:30
  14.3 5.8 %collective-permute-done.2 = bf16[32,6144]{1,0:T(8,128)(2,1)S(1)} collective-permute-done((bf16[32,6144]{1,0:T(8,128)(2,1)S(1)}, bf16[32,6144]{1,0:T(8,128)(2,1)S(1)}, u32[]{:S(2)}, u32[]{:S(2)}) %collective-permute-start.2) | collective-permute-done | bytes 393248 | tf_op jit(solution)/shard_map/ppermute | solution.py:30
  20.2 0.1 collective-permute-start.3
  20.4 3.1 %collective-permute-start.8 = (bf16[64,6144]{1,0:T(8,128)(2,1)S(1)}, bf16[64,6144]{1,0:T(8,128)(2,1)S(1)}, u32[]{:S(2)}, u32[]{:S(2)}) collective-permute-start(bf16[64,6144]{1,0:T(8,128)(2,1)S(1)} %constant_dynamic-update-slice_fusion.2.refs_6_), channel_id=1, source_target_pairs={{64,0},{3,1},{66,2},{5,3},{68,4},{7,5},{70,6},{1,7},{72,8},{11,9},... | collective-permute-start | bytes 2359304 | tf_op jit(solution)/shard_map/ppermute | solution.py:21
  23.5 0.1 collective-permute-start.9
  23.6 9.9 %collective-permute-done.3.refs_12_.refs_4_ = bf16[64,6144]{1,0:T(8,128)(2,1)S(1)} collective-permute-done((bf16[64,6144]{1,0:T(8,128)(2,1)S(1)}, bf16[64,6144]{1,0:T(8,128)(2,1)S(1)}, u32[]{:S(2)}, u32[]{:S(2)}) %collective-permute-start.3) | collective-permute-done | bytes 786464 | tf_op jit(solution)/shard_map/ppermute | solution.py:30
  33.4 2.5 %collective-permute-start.14 = (bf16[64,6144]{1,0:T(8,128)(2,1)S(1)}, bf16[64,6144]{1,0:T(8,128)(2,1)S(1)}, u32[]{:S(2)}, u32[]{:S(2)}) collective-permute-start(bf16[64,6144]{1,0:T(8,128)(2,1)S(1)} %constant_dynamic-update-slice_fusion.refs_10_.refs_2_), channel_id=1, source_target_pairs={{0,1},{1,0},{2,3},{3,2},{4,5},{5,4},{6,7},{7,6},{8,9},{9,8},{10,11... | collective-permute-start | bytes 2359304 | tf_op jit(solution)/shard_map/ppermute | solution.py:34
  36.0 0.8 collective-permute-done.9.refs_3_
  36.8 2.0 %collective-permute-start.13 = (bf16[64,6144]{1,0:T(8,128)(2,1)S(1)}, bf16[64,6144]{1,0:T(8,128)(2,1)S(1)}, u32[]{:S(2)}, u32[]{:S(2)}) collective-permute-start(bf16[64,6144]{1,0:T(8,128)(2,1)S(1)} %collective-permute-done.9.refs_3_), channel_id=1, source_target_pairs={{192,0},{7,1},{194,2},{1,3},{196,4},{3,5},{198,6},{5,7},{200,8},{1... | collective-permute-start | bytes 2359304 | tf_op jit(solution)/shard_map/ppermute | solution.py:21
  38.8 1.2 %collective-permute-start.10 = (bf16[64,6144]{1,0:T(8,128)(2,1)S(1)}, bf16[64,6144]{1,0:T(8,128)(2,1)S(1)}, u32[]{:S(2)}, u32[]{:S(2)}) collective-permute-start(bf16[64,6144]{1,0:T(8,128)(2,1)S(1)} %constant_dynamic-update-slice_fusion.4.refs_7_), channel_id=1, source_target_pairs={{64,0},{3,1},{66,2},{5,3},{68,4},{7,5},{70,6},{1,7},{72,8},{11,9},... | collective-permute-start | bytes 2359304 | tf_op jit(solution)/shard_map/ppermute | solution.py:21
  40.0 6.6 %collective-permute-done.7.refs_14_.refs_6_ = bf16[64,6144]{1,0:T(8,128)(2,1)S(1)} collective-permute-done((bf16[64,6144]{1,0:T(8,128)(2,1)S(1)}, bf16[64,6144]{1,0:T(8,128)(2,1)S(1)}, u32[]{:S(2)}, u32[]{:S(2)}) %collective-permute-start.7) | collective-permute-done | bytes 786464 | tf_op jit(solution)/shard_map/ppermute | solution.py:30
  46.6 1.6 %collective-permute-start.11 = (bf16[64,6144]{1,0:T(8,128)(2,1)S(1)}, bf16[64,6144]{1,0:T(8,128)(2,1)S(1)}, u32[]{:S(2)}, u32[]{:S(2)}) collective-permute-start(bf16[64,6144]{1,0:T(8,128)(2,1)S(1)} %constant_dynamic-update-slice_fusion.2.refs_6_), channel_id=1, source_target_pairs={{192,0},{7,1},{194,2},{1,3},{196,4},{3,5},{198,6},{5,7},{200,8},{1... | collective-permute-start | bytes 2359304 | tf_op jit(solution)/shard_map/ppermute | solution.py:21
  48.3 0.1 collective-permute-start.17
  48.3 0.4 collective-permute-done.12.refs_4_
  48.8 0.9 collective-permute-start.15
  49.6 0.3 collective-permute-done.13.refs_5_
  50.0 0.4 collective-permute-start.16
  50.4 7.0 %collective-permute-done.17.refs_16_.refs_8_ = bf16[32,6144]{1,0:T(8,128)(2,1)S(1)} collective-permute-done((bf16[32,6144]{1,0:T(8,128)(2,1)S(1)}, bf16[32,6144]{1,0:T(8,128)(2,1)S(1)}, u32[]{:S(2)}, u32[]{:S(2)}) %collective-permute-start.17) | collective-permute-done | bytes 393248 | tf_op jit(solution)/shard_map/ppermute | solution.py:30
  57.3 2.5 %collective-permute-done.11.refs_2_ = bf16[64,6144]{1,0:T(8,128)(2,1)S(1)} collective-permute-done((bf16[64,6144]{1,0:T(8,128)(2,1)S(1)}, bf16[64,6144]{1,0:T(8,128)(2,1)S(1)}, u32[]{:S(2)}, u32[]{:S(2)}) %collective-permute-start.11) | collective-permute-done | bytes 786464 | tf_op jit(solution)/shard_map/ppermute | solution.py:21
  59.9 4.6 %shard_map.42 = (f32[144,2048]{1,0:T(8,128)S(1)}, f32[144,2048]{1,0:T(8,128)S(1)}, f32[144,2048]{1,0:T(8,128)S(1)}, bf16[128,512]{1,0:T(8,128)(2,1)S(1)}, f32[1,128]{1,0:T(1,128)S(1)}) custom-call(bf16[64,6144]{1,0:T(8,128)(2,1)S(1)} %collective-permute-done.8.refs_0_, bf16[64,6144]{1,0:T(8,128)(2,1)S(1)} %collective-permute-done.10.refs_1_, ...), custom_call_target="tpu_custom_call" | custom-call | flops 4294967296 | bytes 12582912 | tf_op jit(solution)/shard_map/pallas_call | solution.py:103
  64.5 0.1 convert_element_type.29
  64.6 2.2 %collective-permute-start.24 = (f16[144,2048]{1,0:T(8,128)(2,1)S(1)}, f16[144,2048]{1,0:T(8,128)(2,1)S(1)}, u32[]{:S(2)}, u32[]{:S(2)}) collective-permute-start(f16[144,2048]{1,0:T(8,128)(2,1)S(1)} %convert_element_type.29), channel_id=1, source_target_pairs={{128,0},{5,1},{130,2},{7,3},{132,4},{1,5},{134,6},{3,7},{136,8},{1... | collective-permute-start | bytes 1769480 | tf_op jit(solution)/shard_map/ppermute | solution.py:21
  66.8 1.4 %collective-permute-start.23 = (f16[144,2048]{1,0:T(8,128)(2,1)S(1)}, f16[144,2048]{1,0:T(8,128)(2,1)}, u32[]{:S(2)}, u32[]{:S(2)}) collective-permute-start(f16[144,2048]{1,0:T(8,128)(2,1)S(1)} %convert_element_type.28), channel_id=1, source_target_pairs={{64,0},{3,1},{66,2},{5,3},{68,4},{7,5},{70,6},{1,7},{72,8},{11,9},... | collective-permute-start | bytes 1769480 | tf_op jit(solution)/shard_map/ppermute | solution.py:21
  68.3 0.1 convert_element_type.27
  68.3 0.8 collective-permute-start.22
  69.1 0.9 shard_map.43
  70.0 8.8 %all-to-all-start = ((f32[64,1,128]{2,1,0:T(1,128)}), f32[64,1,128]{2,1,0:T(1,128)S(1)}, u32[]{:S(2)}, u32[]{:S(2)}) async-start(f32[64,1,128]{2,1,0:T(1,128)} %get-tuple-element.48), calls=%async_computation | async-start | bytes 65536 | tf_op jit(solution)/shard_map/all_to_all | solution.py:194
  78.9 2.7 %collective-permute-done.23 = f16[144,2048]{1,0:T(8,128)(2,1)} collective-permute-done((f16[144,2048]{1,0:T(8,128)(2,1)S(1)}, f16[144,2048]{1,0:T(8,128)(2,1)}, u32[]{:S(2)}, u32[]{:S(2)}) %collective-permute-start.23) | collective-permute-done | bytes 589856 | tf_op jit(solution)/shard_map/ppermute | solution.py:21
  81.7 0.8 fusion.3
  82.5 0.8 fusion.2
  83.3 1.6 %multiply_add_fusion = f32[128,2048]{1,0:T(8,128)S(1)} fusion(f32[128,2048]{1,0:T(8,128)S(1)} %get-tuple-element.49, f16[144,2048]{1,0:T(8,128)(2,1)S(1)} %collective-permute-done.24, f16[144,2048]{1,0:T(8,128)(2,1)} %collective-permute-done.23, f16[144,2048]{1,0:T(8,128)(2,1)} %collective-permute-done.22, f32[2048]{0:T(1024)S(1)} %bitcast.7, ...), kind=kLoop, calls=%fused_computation | loop fusion | flops 2359296 | bytes 3694592 | tf_op jit(solution)/shard_map/add | solution.py:188
  84.9 1.6 %collective-permute-start.25 = (f32[32,2048]{1,0:T(8,128)S(1)}, f32[32,2048]{1,0:T(8,128)S(1)}, u32[]{:S(2)}, u32[]{:S(2)}) collective-permute-start(f32[32,2048]{1,0:T(8,128)S(1)} %get-tuple-element.50), channel_id=1, source_target_pairs={{4,0},{129,1},{6,2},{131,3},{0,4},{133,5},{2,6},{135,7},{12,8},{13... | collective-permute-start | bytes 786440 | tf_op jit(solution)/shard_map/ppermute | solution.py:21
  86.4 1.3 %collective-permute-start.27 = (f32[32,2048]{1,0:T(8,128)S(1)}, f32[32,2048]{1,0:T(8,128)S(1)}, u32[]{:S(2)}, u32[]{:S(2)}) collective-permute-start(f32[32,2048]{1,0:T(8,128)S(1)} %get-tuple-element.51), channel_id=1, source_target_pairs={{2,0},{65,1},{4,2},{67,3},{6,4},{69,5},{0,6},{71,7},{10,8},{73,9},... | collective-permute-start | bytes 786440 | tf_op jit(solution)/shard_map/ppermute | solution.py:21
  87.7 1.4 %collective-permute-start.26 = (f32[32,2048]{1,0:T(8,128)S(1)}, f32[32,2048]{1,0:T(8,128)S(1)}, u32[]{:S(2)}, u32[]{:S(2)}) collective-permute-start(f32[32,2048]{1,0:T(8,128)S(1)} %get-tuple-element.52), channel_id=1, source_target_pairs={{6,0},{193,1},{0,2},{195,3},{2,4},{197,5},{4,6},{199,7},{14,8},{20... | collective-permute-start | bytes 786440 | tf_op jit(solution)/shard_map/ppermute | solution.py:21
  89.1 0.1 reduce_sum.11
  89.2 2.0 %collective-permute-start.20 = (f32[1,128]{1,0:T(1,128)S(1)}, f32[1,128]{1,0:T(1,128)S(1)}, u32[]{:S(2)}, u32[]{:S(2)}) collective-permute-start(f32[1,128]{1,0:T(1,128)S(1)} %bitcast.10), channel_id=1, source_target_pairs={{2,0},{3,1},{4,2},{5,3},{6,4},{7,5},{0,6},{1,7},{10,8},{11,9},{12,... | collective-permute-start | bytes 1544 | tf_op jit(solution)/shard_map/ppermute | solution.py:21
  91.1 0.2 collective-permute-start.21
  91.3 4.4 %collective-permute-done.20 = f32[1,128]{1,0:T(1,128)S(1)} collective-permute-done((f32[1,128]{1,0:T(1,128)S(1)}, f32[1,128]{1,0:T(1,128)S(1)}, u32[]{:S(2)}, u32[]{:S(2)}) %collective-permute-start.20) | collective-permute-done | bytes 544 | tf_op jit(solution)/shard_map/ppermute | solution.py:21
  95.7 1.5 %collective-permute-start.19 = (f32[1,128]{1,0:T(1,128)S(1)}, f32[1,128]{1,0:T(1,128)S(1)}, u32[]{:S(2)}, u32[]{:S(2)}) collective-permute-start(f32[1,128]{1,0:T(1,128)S(1)} %bitcast.12), channel_id=1, source_target_pairs={{4,0},{5,1},{6,2},{7,3},{0,4},{1,5},{2,6},{3,7},{12,8},{13,9},{14,... | collective-permute-start | bytes 1544 | tf_op jit(solution)/shard_map/ppermute | solution.py:21
  97.2 3.6 %collective-permute-done.19 = f32[1,128]{1,0:T(1,128)S(1)} collective-permute-done((f32[1,128]{1,0:T(1,128)S(1)}, f32[1,128]{1,0:T(1,128)S(1)}, u32[]{:S(2)}, u32[]{:S(2)}) %collective-permute-start.19) | collective-permute-done | bytes 544 | tf_op jit(solution)/shard_map/ppermute | solution.py:21
  100.8 0.8 fusion.1
  (33 shorter events, 0.4 us)
Async XLA Ops:
  2.4 1.9 %collective-permute-start.1 = (bf16[32,6144]{1,0:T(8,128)(2,1)}, bf16[32,6144]{1,0:T(8,128)(2,1)S(1)}, u32[]{:S(2)}, u32[]{:S(2)}) collective-permute-start(bf16[32,6144]{1,0:T(8,128)(2,1)} %shard_map.41.refs_8_.refs_0_), channel_id=1, source_target_pairs={{0,1},{1,0},{2,3},{3,2},{4,5},{5,4},{6,7},{7,6},{8,9},{9,8},{10,11... | collective-permute-start | bytes 1179656 | tf_op jit(solution)/shard_map/ppermute | solution.py:34
  2.4 11.8 %collective-permute-start = (bf16[32,6144]{1,0:T(8,128)(2,1)}, bf16[32,6144]{1,0:T(8,128)(2,1)S(1)}, u32[]{:S(2)}, u32[]{:S(2)}) collective-permute-start(bf16[32,6144]{1,0:T(8,128)(2,1)} %shard_map.41.refs_8_.refs_0_), channel_id=1, source_target_pairs={{56,0},{17,1},{58,2},{19,3},{60,4},{21,5},{62,6},{23,7},{48,8},{25... | collective-permute-start | bytes 1179656 | tf_op jit(solution)/shard_map/ppermute | solution.py:30
  4.4 15.9 %collective-permute-start.6 = (bf16[32,6144]{1,0:T(8,128)(2,1)}, bf16[32,6144]{1,0:T(8,128)(2,1)S(1)}, u32[]{:S(2)}, u32[]{:S(2)}) collective-permute-start(bf16[32,6144]{1,0:T(8,128)(2,1)} %shard_map.41.refs_8_.refs_0_), channel_id=1, source_target_pairs={{4,0},{129,1},{6,2},{131,3},{0,4},{133,5},{2,6},{135,7},{12,8},{13... | collective-permute-start | bytes 1179656 | tf_op jit(solution)/shard_map/ppermute | solution.py:21
  6.5 13.8 %collective-permute-start.5 = (bf16[32,6144]{1,0:T(8,128)(2,1)}, bf16[32,6144]{1,0:T(8,128)(2,1)S(1)}, u32[]{:S(2)}, u32[]{:S(2)}) collective-permute-start(bf16[32,6144]{1,0:T(8,128)(2,1)} %shard_map.41.refs_8_.refs_0_), channel_id=1, source_target_pairs={{6,0},{193,1},{0,2},{195,3},{2,4},{197,5},{4,6},{199,7},{14,8},{20... | collective-permute-start | bytes 1179656 | tf_op jit(solution)/shard_map/ppermute | solution.py:21
  8.1 12.2 %collective-permute-start.4 = (bf16[32,6144]{1,0:T(8,128)(2,1)}, bf16[32,6144]{1,0:T(8,128)(2,1)S(1)}, u32[]{:S(2)}, u32[]{:S(2)}) collective-permute-start(bf16[32,6144]{1,0:T(8,128)(2,1)} %shard_map.41.refs_8_.refs_0_), channel_id=1, source_target_pairs={{2,0},{65,1},{4,2},{67,3},{6,4},{69,5},{0,6},{71,7},{10,8},{73,9},... | collective-permute-start | bytes 1179656 | tf_op jit(solution)/shard_map/ppermute | solution.py:21
  8.5 11.6 %collective-permute-start.2 = (bf16[32,6144]{1,0:T(8,128)(2,1)S(1)}, bf16[32,6144]{1,0:T(8,128)(2,1)S(1)}, u32[]{:S(2)}, u32[]{:S(2)}) collective-permute-start(bf16[32,6144]{1,0:T(8,128)(2,1)S(1)} %collective-permute-done.1.refs_9_.refs_1_), channel_id=1, source_target_pairs={{56,0},{17,1},{58,2},{19,3},{60,4},{21,5},{62,6},{23,7},{48,8},{25... | collective-permute-start | bytes 1179656 | tf_op jit(solution)/shard_map/ppermute | solution.py:30
  20.2 13.3 %collective-permute-start.3 = (bf16[64,6144]{1,0:T(8,128)(2,1)S(1)}, bf16[64,6144]{1,0:T(8,128)(2,1)S(1)}, u32[]{:S(2)}, u32[]{:S(2)}) collective-permute-start(bf16[64,6144]{1,0:T(8,128)(2,1)S(1)} %constant_dynamic-update-slice_fusion.refs_10_.refs_2_), channel_id=1, source_target_pairs={{56,0},{17,1},{58,2},{19,3},{60,4},{21,5},{62,6},{23,7},{48,8},{25... | collective-permute-start | bytes 2359304 | tf_op jit(solution)/shard_map/ppermute | solution.py:30
  20.3 39.5 %copy-start = (bf16[32,6144]{1,0:T(8,128)(2,1)S(1)}, bf16[32,6144]{1,0:T(8,128)(2,1)}, u32[]{:S(2)}) copy-start(bf16[32,6144]{1,0:T(8,128)(2,1)} %shard_map.41.refs_8_.refs_0_) | copy-start | bytes 1179652
  20.4 15.6 %collective-permute-start.8 = (bf16[64,6144]{1,0:T(8,128)(2,1)S(1)}, bf16[64,6144]{1,0:T(8,128)(2,1)S(1)}, u32[]{:S(2)}, u32[]{:S(2)}) collective-permute-start(bf16[64,6144]{1,0:T(8,128)(2,1)S(1)} %constant_dynamic-update-slice_fusion.2.refs_6_), channel_id=1, source_target_pairs={{64,0},{3,1},{66,2},{5,3},{68,4},{7,5},{70,6},{1,7},{72,8},{11,9},... | collective-permute-start | bytes 2359304 | tf_op jit(solution)/shard_map/ppermute | solution.py:21
  23.5 13.3 %collective-permute-start.9 = (bf16[64,6144]{1,0:T(8,128)(2,1)S(1)}, bf16[64,6144]{1,0:T(8,128)(2,1)S(1)}, u32[]{:S(2)}, u32[]{:S(2)}) collective-permute-start(bf16[64,6144]{1,0:T(8,128)(2,1)S(1)} %constant_dynamic-update-slice_fusion.4.refs_7_), channel_id=1, source_target_pairs={{192,0},{7,1},{194,2},{1,3},{196,4},{3,5},{198,6},{5,7},{200,8},{1... | collective-permute-start | bytes 2359304 | tf_op jit(solution)/shard_map/ppermute | solution.py:21
  33.4 13.2 %collective-permute-start.7 = (bf16[64,6144]{1,0:T(8,128)(2,1)S(1)}, bf16[64,6144]{1,0:T(8,128)(2,1)S(1)}, u32[]{:S(2)}, u32[]{:S(2)}) collective-permute-start(bf16[64,6144]{1,0:T(8,128)(2,1)S(1)} %collective-permute-done.3.refs_12_.refs_4_), channel_id=1, source_target_pairs={{56,0},{17,1},{58,2},{19,3},{60,4},{21,5},{62,6},{23,7},{48,8},{25... | collective-permute-start | bytes 2359304 | tf_op jit(solution)/shard_map/ppermute | solution.py:30
  33.4 14.8 %collective-permute-start.14 = (bf16[64,6144]{1,0:T(8,128)(2,1)S(1)}, bf16[64,6144]{1,0:T(8,128)(2,1)S(1)}, u32[]{:S(2)}, u32[]{:S(2)}) collective-permute-start(bf16[64,6144]{1,0:T(8,128)(2,1)S(1)} %constant_dynamic-update-slice_fusion.refs_10_.refs_2_), channel_id=1, source_target_pairs={{0,1},{1,0},{2,3},{3,2},{4,5},{5,4},{6,7},{7,6},{8,9},{9,8},{10,11... | collective-permute-start | bytes 2359304 | tf_op jit(solution)/shard_map/ppermute | solution.py:34
  36.8 12.0 %collective-permute-start.12 = (bf16[64,6144]{1,0:T(8,128)(2,1)S(1)}, bf16[64,6144]{1,0:T(8,128)(2,1)S(1)}, u32[]{:S(2)}, u32[]{:S(2)}) collective-permute-start(bf16[64,6144]{1,0:T(8,128)(2,1)S(1)} %collective-permute-done.8.refs_0_), channel_id=1, source_target_pairs={{64,0},{3,1},{66,2},{5,3},{68,4},{7,5},{70,6},{1,7},{72,8},{11,9},... | collective-permute-start | bytes 2359304 | tf_op jit(solution)/shard_map/ppermute | solution.py:21
  36.8 13.2 %collective-permute-start.13 = (bf16[64,6144]{1,0:T(8,128)(2,1)S(1)}, bf16[64,6144]{1,0:T(8,128)(2,1)S(1)}, u32[]{:S(2)}, u32[]{:S(2)}) collective-permute-start(bf16[64,6144]{1,0:T(8,128)(2,1)S(1)} %collective-permute-done.9.refs_3_), channel_id=1, source_target_pairs={{192,0},{7,1},{194,2},{1,3},{196,4},{3,5},{198,6},{5,7},{200,8},{1... | collective-permute-start | bytes 2359304 | tf_op jit(solution)/shard_map/ppermute | solution.py:21
  38.8 18.5 %collective-permute-start.10 = (bf16[64,6144]{1,0:T(8,128)(2,1)S(1)}, bf16[64,6144]{1,0:T(8,128)(2,1)S(1)}, u32[]{:S(2)}, u32[]{:S(2)}) collective-permute-start(bf16[64,6144]{1,0:T(8,128)(2,1)S(1)} %constant_dynamic-update-slice_fusion.4.refs_7_), channel_id=1, source_target_pairs={{64,0},{3,1},{66,2},{5,3},{68,4},{7,5},{70,6},{1,7},{72,8},{11,9},... | collective-permute-start | bytes 2359304 | tf_op jit(solution)/shard_map/ppermute | solution.py:21
  46.6 13.2 %collective-permute-start.11 = (bf16[64,6144]{1,0:T(8,128)(2,1)S(1)}, bf16[64,6144]{1,0:T(8,128)(2,1)S(1)}, u32[]{:S(2)}, u32[]{:S(2)}) collective-permute-start(bf16[64,6144]{1,0:T(8,128)(2,1)S(1)} %constant_dynamic-update-slice_fusion.2.refs_6_), channel_id=1, source_target_pairs={{192,0},{7,1},{194,2},{1,3},{196,4},{3,5},{198,6},{5,7},{200,8},{1... | collective-permute-start | bytes 2359304 | tf_op jit(solution)/shard_map/ppermute | solution.py:21
  48.3 9.1 %collective-permute-start.17 = (bf16[32,6144]{1,0:T(8,128)(2,1)S(1)}, bf16[32,6144]{1,0:T(8,128)(2,1)S(1)}, u32[]{:S(2)}, u32[]{:S(2)}) collective-permute-start(bf16[32,6144]{1,0:T(8,128)(2,1)S(1)} %slice.40), channel_id=1, source_target_pairs={{56,0},{17,1},{58,2},{19,3},{60,4},{21,5},{62,6},{23,7},{48,8},{25... | collective-permute-start | bytes 1179656 | tf_op jit(solution)/shard_map/ppermute | solution.py:30
  48.8 11.1 %collective-permute-start.15 = (bf16[64,6144]{1,0:T(8,128)(2,1)S(1)}, bf16[64,6144]{1,0:T(8,128)(2,1)S(1)}, u32[]{:S(2)}, u32[]{:S(2)}) collective-permute-start(bf16[64,6144]{1,0:T(8,128)(2,1)S(1)} %collective-permute-done.3.refs_12_.refs_4_), channel_id=1, source_target_pairs={{0,1},{1,0},{2,3},{3,2},{4,5},{5,4},{6,7},{7,6},{8,9},{9,8},{10,11... | collective-permute-start | bytes 2359304 | tf_op jit(solution)/shard_map/ppermute | solution.py:34
  50.0 9.9 %collective-permute-start.16 = (bf16[64,6144]{1,0:T(8,128)(2,1)S(1)}, bf16[64,6144]{1,0:T(8,128)(2,1)S(1)}, u32[]{:S(2)}, u32[]{:S(2)}) collective-permute-start(bf16[64,6144]{1,0:T(8,128)(2,1)S(1)} %collective-permute-done.7.refs_14_.refs_6_), channel_id=1, source_target_pairs={{0,1},{1,0},{2,3},{3,2},{4,5},{5,4},{6,7},{7,6},{8,9},{9,8},{10,11... | collective-permute-start | bytes 2359304 | tf_op jit(solution)/shard_map/ppermute | solution.py:34
  57.3 2.5 %collective-permute-start.18 = (bf16[32,6144]{1,0:T(8,128)(2,1)S(1)}, bf16[32,6144]{1,0:T(8,128)(2,1)S(1)}, u32[]{:S(2)}, u32[]{:S(2)}) collective-permute-start(bf16[32,6144]{1,0:T(8,128)(2,1)S(1)} %collective-permute-done.17.refs_16_.refs_8_), channel_id=1, source_target_pairs={{0,1},{1,0},{2,3},{3,2},{4,5},{5,4},{6,7},{7,6},{8,9},{9,8},{10,11... | collective-permute-start | bytes 1179656 | tf_op jit(solution)/shard_map/ppermute | solution.py:34
  64.6 14.3 %collective-permute-start.24 = (f16[144,2048]{1,0:T(8,128)(2,1)S(1)}, f16[144,2048]{1,0:T(8,128)(2,1)S(1)}, u32[]{:S(2)}, u32[]{:S(2)}) collective-permute-start(f16[144,2048]{1,0:T(8,128)(2,1)S(1)} %convert_element_type.29), channel_id=1, source_target_pairs={{128,0},{5,1},{130,2},{7,3},{132,4},{1,5},{134,6},{3,7},{136,8},{1... | collective-permute-start | bytes 1769480 | tf_op jit(solution)/shard_map/ppermute | solution.py:21
  66.8 14.8 %collective-permute-start.23 = (f16[144,2048]{1,0:T(8,128)(2,1)S(1)}, f16[144,2048]{1,0:T(8,128)(2,1)}, u32[]{:S(2)}, u32[]{:S(2)}) collective-permute-start(f16[144,2048]{1,0:T(8,128)(2,1)S(1)} %convert_element_type.28), channel_id=1, source_target_pairs={{64,0},{3,1},{66,2},{5,3},{68,4},{7,5},{70,6},{1,7},{72,8},{11,9},... | collective-permute-start | bytes 1769480 | tf_op jit(solution)/shard_map/ppermute | solution.py:21
  68.3 14.1 %collective-permute-start.22 = (f16[144,2048]{1,0:T(8,128)(2,1)S(1)}, f16[144,2048]{1,0:T(8,128)(2,1)}, u32[]{:S(2)}, u32[]{:S(2)}) collective-permute-start(f16[144,2048]{1,0:T(8,128)(2,1)S(1)} %convert_element_type.27), channel_id=1, source_target_pairs={{192,0},{7,1},{194,2},{1,3},{196,4},{3,5},{198,6},{5,7},{200,8},{1... | collective-permute-start | bytes 1769480 | tf_op jit(solution)/shard_map/ppermute | solution.py:21
  70.0 19.0 %all-to-all-start = ((f32[64,1,128]{2,1,0:T(1,128)}), f32[64,1,128]{2,1,0:T(1,128)S(1)}, u32[]{:S(2)}, u32[]{:S(2)}) async-start(f32[64,1,128]{2,1,0:T(1,128)} %get-tuple-element.48), calls=%async_computation | async-start | bytes 65536 | tf_op jit(solution)/shard_map/all_to_all | solution.py:194
  84.9 15.9 %collective-permute-start.25 = (f32[32,2048]{1,0:T(8,128)S(1)}, f32[32,2048]{1,0:T(8,128)S(1)}, u32[]{:S(2)}, u32[]{:S(2)}) collective-permute-start(f32[32,2048]{1,0:T(8,128)S(1)} %get-tuple-element.50), channel_id=1, source_target_pairs={{4,0},{129,1},{6,2},{131,3},{0,4},{133,5},{2,6},{135,7},{12,8},{13... | collective-permute-start | bytes 786440 | tf_op jit(solution)/shard_map/ppermute | solution.py:21
  86.4 14.4 %collective-permute-start.27 = (f32[32,2048]{1,0:T(8,128)S(1)}, f32[32,2048]{1,0:T(8,128)S(1)}, u32[]{:S(2)}, u32[]{:S(2)}) collective-permute-start(f32[32,2048]{1,0:T(8,128)S(1)} %get-tuple-element.51), channel_id=1, source_target_pairs={{2,0},{65,1},{4,2},{67,3},{6,4},{69,5},{0,6},{71,7},{10,8},{73,9},... | collective-permute-start | bytes 786440 | tf_op jit(solution)/shard_map/ppermute | solution.py:21
  87.7 13.1 %collective-permute-start.26 = (f32[32,2048]{1,0:T(8,128)S(1)}, f32[32,2048]{1,0:T(8,128)S(1)}, u32[]{:S(2)}, u32[]{:S(2)}) collective-permute-start(f32[32,2048]{1,0:T(8,128)S(1)} %get-tuple-element.52), channel_id=1, source_target_pairs={{6,0},{193,1},{0,2},{195,3},{2,4},{197,5},{4,6},{199,7},{14,8},{20... | collective-permute-start | bytes 786440 | tf_op jit(solution)/shard_map/ppermute | solution.py:21
  89.2 6.6 %collective-permute-start.20 = (f32[1,128]{1,0:T(1,128)S(1)}, f32[1,128]{1,0:T(1,128)S(1)}, u32[]{:S(2)}, u32[]{:S(2)}) collective-permute-start(f32[1,128]{1,0:T(1,128)S(1)} %bitcast.10), channel_id=1, source_target_pairs={{2,0},{3,1},{4,2},{5,3},{6,4},{7,5},{0,6},{1,7},{10,8},{11,9},{12,... | collective-permute-start | bytes 1544 | tf_op jit(solution)/shard_map/ppermute | solution.py:21
  91.1 6.1 %collective-permute-start.21 = (f32[1,128]{1,0:T(1,128)S(1)}, f32[1,128]{1,0:T(1,128)S(1)}, u32[]{:S(2)}, u32[]{:S(2)}) collective-permute-start(f32[1,128]{1,0:T(1,128)S(1)} %bitcast.11), channel_id=1, source_target_pairs={{6,0},{7,1},{0,2},{1,3},{2,4},{3,5},{4,6},{5,7},{14,8},{15,9},{8,1... | collective-permute-start | bytes 1544 | tf_op jit(solution)/shard_map/ppermute | solution.py:21
  95.7 5.0 %collective-permute-start.19 = (f32[1,128]{1,0:T(1,128)S(1)}, f32[1,128]{1,0:T(1,128)S(1)}, u32[]{:S(2)}, u32[]{:S(2)}) collective-permute-start(f32[1,128]{1,0:T(1,128)S(1)} %bitcast.12), channel_id=1, source_target_pairs={{4,0},{5,1},{6,2},{7,3},{0,4},{1,5},{2,6},{3,7},{12,8},{13,9},{14,... | collective-permute-start | bytes 1544 | tf_op jit(solution)/shard_map/ppermute | solution.py:21

commit v10 on v9

--- a/solution.py
+++ b/solution.py
@@ -191,8 +191,8 @@
     for i, k in ((3, 2), (1, 1), (2, 3)):
         pulled += shift(blocks[i], near, -k)
 
-    total = jnp.sum(lax.all_to_all(squares, ("y", "zh", "zl", "core"), 0, 0), axis=0)
-    ring = [shift(total, ("x", "x"), k) for k in (1, 2, 3)]
+    total = jnp.sum(lax.all_to_all(squares, ("zh", "zl", "x", "core"), 0, 0), axis=0)
+    ring = [shift(total, ("y", "y"), k) for k in (1, 2, 3)]
     total = (total + ring[1]) + (ring[0] + ring[2])
     return total[0, 0] / jnp.float32(texts * 256), pulled
 

time: 103 us -> 102 us (level); the launches traced: 103 us -> 100 us
  waiting for transfers between devices: 46.9 us -> 43.2 us
  starting transfers between devices: 41 us -> 42.1 us
    ppermute x18, waiting for transfers between devices: 14.8 us -> 11.1 us  [shift(): return lax.ppermute(value, AXES, pairs)]
  transfers between devices with their start and end apart: 29 -> 29, of which waited for: 12 -> 14; matrix products, arithmetic and copies ran while one was open for 4% -> 5% of each run, Pallas kernels for 1% -> 1%
where the time goes in v10:
time: 102 us; the launch traced here: 100 us
  waiting for transfers between devices  43.2 us (42%)
  starting transfers between devices  42.1 us (41%)
  Pallas kernels  7.38 us (7%)
  other arithmetic  4.17 us (4%)
  between operations  2.04 us (2%)
  local copies, waits for them, and re-layouts  1.24 us (1%)
    ppermute x5, waiting for transfers between devices, round_z(): return lax.ppermute(value, AXES, pairs)  32.1 us
    ppermute x18, starting transfers between devices, shift(): return lax.ppermute(value, AXES, pairs)  25.2 us
    ppermute x18, waiting for transfers between devices, shift(): return lax.ppermute(value, AXES, pairs)  11.1 us
    all_to_all x1, starting transfers between devices, shards(): lax.all_to_all(squares, ('zh', 'zl', 'x', 'core'), 0, 0)  9.04 us
    pallas_call x1, Pallas kernels, pulls(): pl.pallas_call(excess_kernel, in_specs=[inside] * (len(pieces) + len(line...  4.63 us
    ppermute x5, starting transfers between devices, round_z(): return lax.ppermute(value, AXES, pairs)  4 us
    ppermute x5, starting transfers between devices, other_core(): return lax.ppermute(value, 'core', [(0, 1), (1, 0)])  3.81 us
  transfers between devices with their start and end apart: 29, of which 14 were waited for; matrix products, arithmetic and copies ran while one was open for 5% of the time, Pallas kernels for 1%

profile of v10, /device:TPU:2, one launch (start us, length us, event | category | flops | bytes accessed | tf_op | source)
XLA Modules:
  0.0 100.1 jit_solution(9881469686522976642)
XLA Ops:
  0.6 1.8 %shard_map.41.refs_8_.refs_0_ = bf16[32,6144]{1,0:T(8,128)(2,1)} custom-call(bf16[32,2048]{1,0:T(8,128)(2,1)} %student_ref.1, bf16[32,4096]{1,0:T(8,128)(2,1)} %teacher_ref.1), custom_call_target="tpu_custom_call" | custom-call | tf_op jit(solution)/shard_map/pallas_call | solution.py:45
  2.4 1.9 %collective-permute-start = (bf16[32,6144]{1,0:T(8,128)(2,1)}, bf16[32,6144]{1,0:T(8,128)(2,1)S(1)}, u32[]{:S(2)}, u32[]{:S(2)}) collective-permute-start(bf16[32,6144]{1,0:T(8,128)(2,1)} %shard_map.41.refs_8_.refs_0_), channel_id=1, source_target_pairs={{56,0},{17,1},{58,2},{19,3},{60,4},{21,5},{62,6},{23,7},{48,8},{25... | collective-permute-start | bytes 1179656 | tf_op jit(solution)/shard_map/ppermute | solution.py:30
  4.4 2.1 %collective-permute-start.6 = (bf16[32,6144]{1,0:T(8,128)(2,1)}, bf16[32,6144]{1,0:T(8,128)(2,1)S(1)}, u32[]{:S(2)}, u32[]{:S(2)}) collective-permute-start(bf16[32,6144]{1,0:T(8,128)(2,1)} %shard_map.41.refs_8_.refs_0_), channel_id=1, source_target_pairs={{4,0},{129,1},{6,2},{131,3},{0,4},{133,5},{2,6},{135,7},{12,8},{13... | collective-permute-start | bytes 1179656 | tf_op jit(solution)/shard_map/ppermute | solution.py:21
  6.5 1.6 %collective-permute-start.5 = (bf16[32,6144]{1,0:T(8,128)(2,1)}, bf16[32,6144]{1,0:T(8,128)(2,1)S(1)}, u32[]{:S(2)}, u32[]{:S(2)}) collective-permute-start(bf16[32,6144]{1,0:T(8,128)(2,1)} %shard_map.41.refs_8_.refs_0_), channel_id=1, source_target_pairs={{6,0},{193,1},{0,2},{195,3},{2,4},{197,5},{4,6},{199,7},{14,8},{20... | collective-permute-start | bytes 1179656 | tf_op jit(solution)/shard_map/ppermute | solution.py:21
  8.1 0.4 collective-permute-start.4
  8.5 1.9 %collective-permute-start.2 = (bf16[32,6144]{1,0:T(8,128)(2,1)S(1)}, bf16[32,6144]{1,0:T(8,128)(2,1)S(1)}, u32[]{:S(2)}, u32[]{:S(2)}) collective-permute-start(bf16[32,6144]{1,0:T(8,128)(2,1)S(1)} %collective-permute-done.1.refs_9_.refs_1_), channel_id=1, source_target_pairs={{56,0},{17,1},{58,2},{19,3},{60,4},{21,5},{62,6},{23,7},{48,8},{25... | collective-permute-start | bytes 1179656 | tf_op jit(solution)/shard_map/ppermute | solution.py:30
  10.4 1.0 %constant_dynamic-update-slice_fusion.3 = bf16[64,6144]{1,0:T(8,128)(2,1)S(1)} fusion(bf16[32,6144]{1,0:T(8,128)(2,1)} %shard_map.41.refs_8_.refs_0_), kind=kLoop, calls=%fused_computation.7 | loop fusion | bytes 786432
  11.5 2.8 %collective-permute-done = bf16[32,6144]{1,0:T(8,128)(2,1)S(1)} collective-permute-done((bf16[32,6144]{1,0:T(8,128)(2,1)}, bf16[32,6144]{1,0:T(8,128)(2,1)S(1)}, u32[]{:S(2)}, u32[]{:S(2)}) %collective-permute-start) | collective-permute-done | bytes 393248 | tf_op jit(solution)/shard_map/ppermute | solution.py:30
  14.3 5.8 %collective-permute-done.2 = bf16[32,6144]{1,0:T(8,128)(2,1)S(1)} collective-permute-done((bf16[32,6144]{1,0:T(8,128)(2,1)S(1)}, bf16[32,6144]{1,0:T(8,128)(2,1)S(1)}, u32[]{:S(2)}, u32[]{:S(2)}) %collective-permute-start.2) | collective-permute-done | bytes 393248 | tf_op jit(solution)/shard_map/ppermute | solution.py:30
  20.2 0.1 collective-permute-start.3
  20.4 3.1 %collective-permute-start.8 = (bf16[64,6144]{1,0:T(8,128)(2,1)S(1)}, bf16[64,6144]{1,0:T(8,128)(2,1)S(1)}, u32[]{:S(2)}, u32[]{:S(2)}) collective-permute-start(bf16[64,6144]{1,0:T(8,128)(2,1)S(1)} %constant_dynamic-update-slice_fusion.2.refs_6_), channel_id=1, source_target_pairs={{64,0},{3,1},{66,2},{5,3},{68,4},{7,5},{70,6},{1,7},{72,8},{11,9},... | collective-permute-start | bytes 2359304 | tf_op jit(solution)/shard_map/ppermute | solution.py:21
  23.5 0.1 collective-permute-start.9
  23.6 9.9 %collective-permute-done.3.refs_12_.refs_4_ = bf16[64,6144]{1,0:T(8,128)(2,1)S(1)} collective-permute-done((bf16[64,6144]{1,0:T(8,128)(2,1)S(1)}, bf16[64,6144]{1,0:T(8,128)(2,1)S(1)}, u32[]{:S(2)}, u32[]{:S(2)}) %collective-permute-start.3) | collective-permute-done | bytes 786464 | tf_op jit(solution)/shard_map/ppermute | solution.py:30
  33.4 2.5 %collective-permute-start.14 = (bf16[64,6144]{1,0:T(8,128)(2,1)S(1)}, bf16[64,6144]{1,0:T(8,128)(2,1)S(1)}, u32[]{:S(2)}, u32[]{:S(2)}) collective-permute-start(bf16[64,6144]{1,0:T(8,128)(2,1)S(1)} %constant_dynamic-update-slice_fusion.refs_10_.refs_2_), channel_id=1, source_target_pairs={{0,1},{1,0},{2,3},{3,2},{4,5},{5,4},{6,7},{7,6},{8,9},{9,8},{10,11... | collective-permute-start | bytes 2359304 | tf_op jit(solution)/shard_map/ppermute | solution.py:34
  36.0 0.8 collective-permute-done.9.refs_3_
  36.8 2.0 %collective-permute-start.13 = (bf16[64,6144]{1,0:T(8,128)(2,1)S(1)}, bf16[64,6144]{1,0:T(8,128)(2,1)S(1)}, u32[]{:S(2)}, u32[]{:S(2)}) collective-permute-start(bf16[64,6144]{1,0:T(8,128)(2,1)S(1)} %collective-permute-done.9.refs_3_), channel_id=1, source_target_pairs={{192,0},{7,1},{194,2},{1,3},{196,4},{3,5},{198,6},{5,7},{200,8},{1... | collective-permute-start | bytes 2359304 | tf_op jit(solution)/shard_map/ppermute | solution.py:21
  38.8 1.2 %collective-permute-start.10 = (bf16[64,6144]{1,0:T(8,128)(2,1)S(1)}, bf16[64,6144]{1,0:T(8,128)(2,1)S(1)}, u32[]{:S(2)}, u32[]{:S(2)}) collective-permute-start(bf16[64,6144]{1,0:T(8,128)(2,1)S(1)} %constant_dynamic-update-slice_fusion.4.refs_7_), channel_id=1, source_target_pairs={{64,0},{3,1},{66,2},{5,3},{68,4},{7,5},{70,6},{1,7},{72,8},{11,9},... | collective-permute-start | bytes 2359304 | tf_op jit(solution)/shard_map/ppermute | solution.py:21
  40.0 6.6 %collective-permute-done.7.refs_14_.refs_6_ = bf16[64,6144]{1,0:T(8,128)(2,1)S(1)} collective-permute-done((bf16[64,6144]{1,0:T(8,128)(2,1)S(1)}, bf16[64,6144]{1,0:T(8,128)(2,1)S(1)}, u32[]{:S(2)}, u32[]{:S(2)}) %collective-permute-start.7) | collective-permute-done | bytes 786464 | tf_op jit(solution)/shard_map/ppermute | solution.py:30
  46.6 1.6 %collective-permute-start.11 = (bf16[64,6144]{1,0:T(8,128)(2,1)S(1)}, bf16[64,6144]{1,0:T(8,128)(2,1)S(1)}, u32[]{:S(2)}, u32[]{:S(2)}) collective-permute-start(bf16[64,6144]{1,0:T(8,128)(2,1)S(1)} %constant_dynamic-update-slice_fusion.2.refs_6_), channel_id=1, source_target_pairs={{192,0},{7,1},{194,2},{1,3},{196,4},{3,5},{198,6},{5,7},{200,8},{1... | collective-permute-start | bytes 2359304 | tf_op jit(solution)/shard_map/ppermute | solution.py:21
  48.3 0.1 collective-permute-start.17
  48.3 0.4 collective-permute-done.12.refs_4_
  48.8 0.9 collective-permute-start.15
  49.6 0.3 collective-permute-done.13.refs_5_
  50.0 0.4 collective-permute-start.16
  50.4 7.0 %collective-permute-done.17.refs_16_.refs_8_ = bf16[32,6144]{1,0:T(8,128)(2,1)S(1)} collective-permute-done((bf16[32,6144]{1,0:T(8,128)(2,1)S(1)}, bf16[32,6144]{1,0:T(8,128)(2,1)S(1)}, u32[]{:S(2)}, u32[]{:S(2)}) %collective-permute-start.17) | collective-permute-done | bytes 393248 | tf_op jit(solution)/shard_map/ppermute | solution.py:30
  57.3 2.5 %collective-permute-done.11.refs_2_ = bf16[64,6144]{1,0:T(8,128)(2,1)S(1)} collective-permute-done((bf16[64,6144]{1,0:T(8,128)(2,1)S(1)}, bf16[64,6144]{1,0:T(8,128)(2,1)S(1)}, u32[]{:S(2)}, u32[]{:S(2)}) %collective-permute-start.11) | collective-permute-done | bytes 786464 | tf_op jit(solution)/shard_map/ppermute | solution.py:21
  59.9 4.6 %shard_map.42 = (f32[144,2048]{1,0:T(8,128)S(1)}, f32[144,2048]{1,0:T(8,128)S(1)}, f32[144,2048]{1,0:T(8,128)S(1)}, bf16[128,512]{1,0:T(8,128)(2,1)S(1)}, f32[1,128]{1,0:T(1,128)S(1)}) custom-call(bf16[64,6144]{1,0:T(8,128)(2,1)S(1)} %collective-permute-done.8.refs_0_, bf16[64,6144]{1,0:T(8,128)(2,1)S(1)} %collective-permute-done.10.refs_1_, ...), custom_call_target="tpu_custom_call" | custom-call | flops 4294967296 | bytes 12582912 | tf_op jit(solution)/shard_map/pallas_call | solution.py:103
  64.5 0.1 convert_element_type.29
  64.6 2.2 %collective-permute-start.24 = (f16[144,2048]{1,0:T(8,128)(2,1)S(1)}, f16[144,2048]{1,0:T(8,128)(2,1)S(1)}, u32[]{:S(2)}, u32[]{:S(2)}) collective-permute-start(f16[144,2048]{1,0:T(8,128)(2,1)S(1)} %convert_element_type.29), channel_id=1, source_target_pairs={{128,0},{5,1},{130,2},{7,3},{132,4},{1,5},{134,6},{3,7},{136,8},{1... | collective-permute-start | bytes 1769480 | tf_op jit(solution)/shard_map/ppermute | solution.py:21
  66.7 0.1 convert_element_type.28
  66.8 1.4 %collective-permute-start.23 = (f16[144,2048]{1,0:T(8,128)(2,1)S(1)}, f16[144,2048]{1,0:T(8,128)(2,1)}, u32[]{:S(2)}, u32[]{:S(2)}) collective-permute-start(f16[144,2048]{1,0:T(8,128)(2,1)S(1)} %convert_element_type.28), channel_id=1, source_target_pairs={{64,0},{3,1},{66,2},{5,3},{68,4},{7,5},{70,6},{1,7},{72,8},{11,9},... | collective-permute-start | bytes 1769480 | tf_op jit(solution)/shard_map/ppermute | solution.py:21
  68.3 0.8 collective-permute-start.22
  69.1 0.9 shard_map.43
  70.0 9.0 %all-to-all-start = ((f32[64,1,128]{2,1,0:T(1,128)}), f32[64,1,128]{2,1,0:T(1,128)S(1)}, u32[]{:S(2)}, u32[]{:S(2)}) async-start(f32[64,1,128]{2,1,0:T(1,128)} %get-tuple-element.48), calls=%async_computation | async-start | bytes 65536 | tf_op jit(solution)/shard_map/all_to_all | solution.py:194
  79.1 2.5 %collective-permute-done.23 = f16[144,2048]{1,0:T(8,128)(2,1)} collective-permute-done((f16[144,2048]{1,0:T(8,128)(2,1)S(1)}, f16[144,2048]{1,0:T(8,128)(2,1)}, u32[]{:S(2)}, u32[]{:S(2)}) %collective-permute-start.23) | collective-permute-done | bytes 589856 | tf_op jit(solution)/shard_map/ppermute | solution.py:21
  81.7 0.8 fusion.3
  82.5 0.8 fusion.2
  83.3 1.6 %multiply_add_fusion = f32[128,2048]{1,0:T(8,128)S(1)} fusion(f32[128,2048]{1,0:T(8,128)S(1)} %get-tuple-element.49, f16[144,2048]{1,0:T(8,128)(2,1)S(1)} %collective-permute-done.24, f16[144,2048]{1,0:T(8,128)(2,1)} %collective-permute-done.23, f16[144,2048]{1,0:T(8,128)(2,1)} %collective-permute-done.22, f32[2048]{0:T(1024)S(1)} %bitcast.7, ...), kind=kLoop, calls=%fused_computation | loop fusion | flops 2359296 | bytes 3694592 | tf_op jit(solution)/shard_map/add | solution.py:188
  84.9 1.6 %collective-permute-start.25 = (f32[32,2048]{1,0:T(8,128)S(1)}, f32[32,2048]{1,0:T(8,128)S(1)}, u32[]{:S(2)}, u32[]{:S(2)}) collective-permute-start(f32[32,2048]{1,0:T(8,128)S(1)} %get-tuple-element.50), channel_id=1, source_target_pairs={{4,0},{129,1},{6,2},{131,3},{0,4},{133,5},{2,6},{135,7},{12,8},{13... | collective-permute-start | bytes 786440 | tf_op jit(solution)/shard_map/ppermute | solution.py:21
  86.4 1.3 %collective-permute-start.27 = (f32[32,2048]{1,0:T(8,128)S(1)}, f32[32,2048]{1,0:T(8,128)S(1)}, u32[]{:S(2)}, u32[]{:S(2)}) collective-permute-start(f32[32,2048]{1,0:T(8,128)S(1)} %get-tuple-element.51), channel_id=1, source_target_pairs={{2,0},{65,1},{4,2},{67,3},{6,4},{69,5},{0,6},{71,7},{10,8},{73,9},... | collective-permute-start | bytes 786440 | tf_op jit(solution)/shard_map/ppermute | solution.py:21
  87.7 1.4 %collective-permute-start.26 = (f32[32,2048]{1,0:T(8,128)S(1)}, f32[32,2048]{1,0:T(8,128)S(1)}, u32[]{:S(2)}, u32[]{:S(2)}) collective-permute-start(f32[32,2048]{1,0:T(8,128)S(1)} %get-tuple-element.52), channel_id=1, source_target_pairs={{6,0},{193,1},{0,2},{195,3},{2,4},{197,5},{4,6},{199,7},{14,8},{20... | collective-permute-start | bytes 786440 | tf_op jit(solution)/shard_map/ppermute | solution.py:21
  89.1 0.1 reduce_sum.11
  89.2 2.7 %collective-permute-start.20 = (f32[1,128]{1,0:T(1,128)S(1)}, f32[1,128]{1,0:T(1,128)S(1)}, u32[]{:S(2)}, u32[]{:S(2)}) collective-permute-start(f32[1,128]{1,0:T(1,128)S(1)} %bitcast.10), channel_id=1, source_target_pairs={{64,0},{65,1},{66,2},{67,3},{68,4},{69,5},{70,6},{71,7},{72,8},{73... | collective-permute-start | bytes 1544 | tf_op jit(solution)/shard_map/ppermute | solution.py:21
  91.8 1.3 %collective-permute-done.20 = f32[1,128]{1,0:T(1,128)S(1)} collective-permute-done((f32[1,128]{1,0:T(1,128)S(1)}, f32[1,128]{1,0:T(1,128)S(1)}, u32[]{:S(2)}, u32[]{:S(2)}) %collective-permute-start.20) | collective-permute-done | bytes 544 | tf_op jit(solution)/shard_map/ppermute | solution.py:21
  93.1 1.9 %collective-permute-start.19 = (f32[1,128]{1,0:T(1,128)S(1)}, f32[1,128]{1,0:T(1,128)S(1)}, u32[]{:S(2)}, u32[]{:S(2)}) collective-permute-start(f32[1,128]{1,0:T(1,128)S(1)} %bitcast.12), channel_id=1, source_target_pairs={{128,0},{129,1},{130,2},{131,3},{132,4},{133,5},{134,6},{135,7},{1... | collective-permute-start | bytes 1544 | tf_op jit(solution)/shard_map/ppermute | solution.py:21
  95.0 1.5 %collective-permute-done.21 = f32[1,128]{1,0:T(1,128)S(1)} collective-permute-done((f32[1,128]{1,0:T(1,128)S(1)}, f32[1,128]{1,0:T(1,128)S(1)}, u32[]{:S(2)}, u32[]{:S(2)}) %collective-permute-start.21) | collective-permute-done | bytes 544 | tf_op jit(solution)/shard_map/ppermute | solution.py:21
  96.6 1.6 %collective-permute-done.19 = f32[1,128]{1,0:T(1,128)S(1)} collective-permute-done((f32[1,128]{1,0:T(1,128)S(1)}, f32[1,128]{1,0:T(1,128)S(1)}, u32[]{:S(2)}, u32[]{:S(2)}) %collective-permute-start.19) | collective-permute-done | bytes 544 | tf_op jit(solution)/shard_map/ppermute | solution.py:21
  98.2 0.8 fusion.1
  (33 shorter events, 0.4 us)
Async XLA Ops:
  2.4 1.9 %collective-permute-start.1 = (bf16[32,6144]{1,0:T(8,128)(2,1)}, bf16[32,6144]{1,0:T(8,128)(2,1)S(1)}, u32[]{:S(2)}, u32[]{:S(2)}) collective-permute-start(bf16[32,6144]{1,0:T(8,128)(2,1)} %shard_map.41.refs_8_.refs_0_), channel_id=1, source_target_pairs={{0,1},{1,0},{2,3},{3,2},{4,5},{5,4},{6,7},{7,6},{8,9},{9,8},{10,11... | collective-permute-start | bytes 1179656 | tf_op jit(solution)/shard_map/ppermute | solution.py:34
  2.4 11.8 %collective-permute-start = (bf16[32,6144]{1,0:T(8,128)(2,1)}, bf16[32,6144]{1,0:T(8,128)(2,1)S(1)}, u32[]{:S(2)}, u32[]{:S(2)}) collective-permute-start(bf16[32,6144]{1,0:T(8,128)(2,1)} %shard_map.41.refs_8_.refs_0_), channel_id=1, source_target_pairs={{56,0},{17,1},{58,2},{19,3},{60,4},{21,5},{62,6},{23,7},{48,8},{25... | collective-permute-start | bytes 1179656 | tf_op jit(solution)/shard_map/ppermute | solution.py:30
  4.4 15.9 %collective-permute-start.6 = (bf16[32,6144]{1,0:T(8,128)(2,1)}, bf16[32,6144]{1,0:T(8,128)(2,1)S(1)}, u32[]{:S(2)}, u32[]{:S(2)}) collective-permute-start(bf16[32,6144]{1,0:T(8,128)(2,1)} %shard_map.41.refs_8_.refs_0_), channel_id=1, source_target_pairs={{4,0},{129,1},{6,2},{131,3},{0,4},{133,5},{2,6},{135,7},{12,8},{13... | collective-permute-start | bytes 1179656 | tf_op jit(solution)/shard_map/ppermute | solution.py:21
  6.5 13.8 %collective-permute-start.5 = (bf16[32,6144]{1,0:T(8,128)(2,1)}, bf16[32,6144]{1,0:T(8,128)(2,1)S(1)}, u32[]{:S(2)}, u32[]{:S(2)}) collective-permute-start(bf16[32,6144]{1,0:T(8,128)(2,1)} %shard_map.41.refs_8_.refs_0_), channel_id=1, source_target_pairs={{6,0},{193,1},{0,2},{195,3},{2,4},{197,5},{4,6},{199,7},{14,8},{20... | collective-permute-start | bytes 1179656 | tf_op jit(solution)/shard_map/ppermute | solution.py:21
  8.1 12.2 %collective-permute-start.4 = (bf16[32,6144]{1,0:T(8,128)(2,1)}, bf16[32,6144]{1,0:T(8,128)(2,1)S(1)}, u32[]{:S(2)}, u32[]{:S(2)}) collective-permute-start(bf16[32,6144]{1,0:T(8,128)(2,1)} %shard_map.41.refs_8_.refs_0_), channel_id=1, source_target_pairs={{2,0},{65,1},{4,2},{67,3},{6,4},{69,5},{0,6},{71,7},{10,8},{73,9},... | collective-permute-start | bytes 1179656 | tf_op jit(solution)/shard_map/ppermute | solution.py:21
  8.5 11.6 %collective-permute-start.2 = (bf16[32,6144]{1,0:T(8,128)(2,1)S(1)}, bf16[32,6144]{1,0:T(8,128)(2,1)S(1)}, u32[]{:S(2)}, u32[]{:S(2)}) collective-permute-start(bf16[32,6144]{1,0:T(8,128)(2,1)S(1)} %collective-permute-done.1.refs_9_.refs_1_), channel_id=1, source_target_pairs={{56,0},{17,1},{58,2},{19,3},{60,4},{21,5},{62,6},{23,7},{48,8},{25... | collective-permute-start | bytes 1179656 | tf_op jit(solution)/shard_map/ppermute | solution.py:30
  20.2 13.3 %collective-permute-start.3 = (bf16[64,6144]{1,0:T(8,128)(2,1)S(1)}, bf16[64,6144]{1,0:T(8,128)(2,1)S(1)}, u32[]{:S(2)}, u32[]{:S(2)}) collective-permute-start(bf16[64,6144]{1,0:T(8,128)(2,1)S(1)} %constant_dynamic-update-slice_fusion.refs_10_.refs_2_), channel_id=1, source_target_pairs={{56,0},{17,1},{58,2},{19,3},{60,4},{21,5},{62,6},{23,7},{48,8},{25... | collective-permute-start | bytes 2359304 | tf_op jit(solution)/shard_map/ppermute | solution.py:30
  20.3 39.5 %copy-start = (bf16[32,6144]{1,0:T(8,128)(2,1)S(1)}, bf16[32,6144]{1,0:T(8,128)(2,1)}, u32[]{:S(2)}) copy-start(bf16[32,6144]{1,0:T(8,128)(2,1)} %shard_map.41.refs_8_.refs_0_) | copy-start | bytes 1179652
  20.4 15.6 %collective-permute-start.8 = (bf16[64,6144]{1,0:T(8,128)(2,1)S(1)}, bf16[64,6144]{1,0:T(8,128)(2,1)S(1)}, u32[]{:S(2)}, u32[]{:S(2)}) collective-permute-start(bf16[64,6144]{1,0:T(8,128)(2,1)S(1)} %constant_dynamic-update-slice_fusion.2.refs_6_), channel_id=1, source_target_pairs={{64,0},{3,1},{66,2},{5,3},{68,4},{7,5},{70,6},{1,7},{72,8},{11,9},... | collective-permute-start | bytes 2359304 | tf_op jit(solution)/shard_map/ppermute | solution.py:21
  23.5 13.3 %collective-permute-start.9 = (bf16[64,6144]{1,0:T(8,128)(2,1)S(1)}, bf16[64,6144]{1,0:T(8,128)(2,1)S(1)}, u32[]{:S(2)}, u32[]{:S(2)}) collective-permute-start(bf16[64,6144]{1,0:T(8,128)(2,1)S(1)} %constant_dynamic-update-slice_fusion.4.refs_7_), channel_id=1, source_target_pairs={{192,0},{7,1},{194,2},{1,3},{196,4},{3,5},{198,6},{5,7},{200,8},{1... | collective-permute-start | bytes 2359304 | tf_op jit(solution)/shard_map/ppermute | solution.py:21
  33.4 13.2 %collective-permute-start.7 = (bf16[64,6144]{1,0:T(8,128)(2,1)S(1)}, bf16[64,6144]{1,0:T(8,128)(2,1)S(1)}, u32[]{:S(2)}, u32[]{:S(2)}) collective-permute-start(bf16[64,6144]{1,0:T(8,128)(2,1)S(1)} %collective-permute-done.3.refs_12_.refs_4_), channel_id=1, source_target_pairs={{56,0},{17,1},{58,2},{19,3},{60,4},{21,5},{62,6},{23,7},{48,8},{25... | collective-permute-start | bytes 2359304 | tf_op jit(solution)/shard_map/ppermute | solution.py:30
  33.4 14.8 %collective-permute-start.14 = (bf16[64,6144]{1,0:T(8,128)(2,1)S(1)}, bf16[64,6144]{1,0:T(8,128)(2,1)S(1)}, u32[]{:S(2)}, u32[]{:S(2)}) collective-permute-start(bf16[64,6144]{1,0:T(8,128)(2,1)S(1)} %constant_dynamic-update-slice_fusion.refs_10_.refs_2_), channel_id=1, source_target_pairs={{0,1},{1,0},{2,3},{3,2},{4,5},{5,4},{6,7},{7,6},{8,9},{9,8},{10,11... | collective-permute-start | bytes 2359304 | tf_op jit(solution)/shard_map/ppermute | solution.py:34
  36.8 12.0 %collective-permute-start.12 = (bf16[64,6144]{1,0:T(8,128)(2,1)S(1)}, bf16[64,6144]{1,0:T(8,128)(2,1)S(1)}, u32[]{:S(2)}, u32[]{:S(2)}) collective-permute-start(bf16[64,6144]{1,0:T(8,128)(2,1)S(1)} %collective-permute-done.8.refs_0_), channel_id=1, source_target_pairs={{64,0},{3,1},{66,2},{5,3},{68,4},{7,5},{70,6},{1,7},{72,8},{11,9},... | collective-permute-start | bytes 2359304 | tf_op jit(solution)/shard_map/ppermute | solution.py:21
  36.8 13.2 %collective-permute-start.13 = (bf16[64,6144]{1,0:T(8,128)(2,1)S(1)}, bf16[64,6144]{1,0:T(8,128)(2,1)S(1)}, u32[]{:S(2)}, u32[]{:S(2)}) collective-permute-start(bf16[64,6144]{1,0:T(8,128)(2,1)S(1)} %collective-permute-done.9.refs_3_), channel_id=1, source_target_pairs={{192,0},{7,1},{194,2},{1,3},{196,4},{3,5},{198,6},{5,7},{200,8},{1... | collective-permute-start | bytes 2359304 | tf_op jit(solution)/shard_map/ppermute | solution.py:21
  38.8 18.5 %collective-permute-start.10 = (bf16[64,6144]{1,0:T(8,128)(2,1)S(1)}, bf16[64,6144]{1,0:T(8,128)(2,1)S(1)}, u32[]{:S(2)}, u32[]{:S(2)}) collective-permute-start(bf16[64,6144]{1,0:T(8,128)(2,1)S(1)} %constant_dynamic-update-slice_fusion.4.refs_7_), channel_id=1, source_target_pairs={{64,0},{3,1},{66,2},{5,3},{68,4},{7,5},{70,6},{1,7},{72,8},{11,9},... | collective-permute-start | bytes 2359304 | tf_op jit(solution)/shard_map/ppermute | solution.py:21
  46.6 13.2 %collective-permute-start.11 = (bf16[64,6144]{1,0:T(8,128)(2,1)S(1)}, bf16[64,6144]{1,0:T(8,128)(2,1)S(1)}, u32[]{:S(2)}, u32[]{:S(2)}) collective-permute-start(bf16[64,6144]{1,0:T(8,128)(2,1)S(1)} %constant_dynamic-update-slice_fusion.2.refs_6_), channel_id=1, source_target_pairs={{192,0},{7,1},{194,2},{1,3},{196,4},{3,5},{198,6},{5,7},{200,8},{1... | collective-permute-start | bytes 2359304 | tf_op jit(solution)/shard_map/ppermute | solution.py:21
  48.3 9.1 %collective-permute-start.17 = (bf16[32,6144]{1,0:T(8,128)(2,1)S(1)}, bf16[32,6144]{1,0:T(8,128)(2,1)S(1)}, u32[]{:S(2)}, u32[]{:S(2)}) collective-permute-start(bf16[32,6144]{1,0:T(8,128)(2,1)S(1)} %slice.40), channel_id=1, source_target_pairs={{56,0},{17,1},{58,2},{19,3},{60,4},{21,5},{62,6},{23,7},{48,8},{25... | collective-permute-start | bytes 1179656 | tf_op jit(solution)/shard_map/ppermute | solution.py:30
  48.8 11.1 %collective-permute-start.15 = (bf16[64,6144]{1,0:T(8,128)(2,1)S(1)}, bf16[64,6144]{1,0:T(8,128)(2,1)S(1)}, u32[]{:S(2)}, u32[]{:S(2)}) collective-permute-start(bf16[64,6144]{1,0:T(8,128)(2,1)S(1)} %collective-permute-done.3.refs_12_.refs_4_), channel_id=1, source_target_pairs={{0,1},{1,0},{2,3},{3,2},{4,5},{5,4},{6,7},{7,6},{8,9},{9,8},{10,11... | collective-permute-start | bytes 2359304 | tf_op jit(solution)/shard_map/ppermute | solution.py:34
  50.0 9.9 %collective-permute-start.16 = (bf16[64,6144]{1,0:T(8,128)(2,1)S(1)}, bf16[64,6144]{1,0:T(8,128)(2,1)S(1)}, u32[]{:S(2)}, u32[]{:S(2)}) collective-permute-start(bf16[64,6144]{1,0:T(8,128)(2,1)S(1)} %collective-permute-done.7.refs_14_.refs_6_), channel_id=1, source_target_pairs={{0,1},{1,0},{2,3},{3,2},{4,5},{5,4},{6,7},{7,6},{8,9},{9,8},{10,11... | collective-permute-start | bytes 2359304 | tf_op jit(solution)/shard_map/ppermute | solution.py:34
  57.3 2.5 %collective-permute-start.18 = (bf16[32,6144]{1,0:T(8,128)(2,1)S(1)}, bf16[32,6144]{1,0:T(8,128)(2,1)S(1)}, u32[]{:S(2)}, u32[]{:S(2)}) collective-permute-start(bf16[32,6144]{1,0:T(8,128)(2,1)S(1)} %collective-permute-done.17.refs_16_.refs_8_), channel_id=1, source_target_pairs={{0,1},{1,0},{2,3},{3,2},{4,5},{5,4},{6,7},{7,6},{8,9},{9,8},{10,11... | collective-permute-start | bytes 1179656 | tf_op jit(solution)/shard_map/ppermute | solution.py:34
  64.6 14.5 %collective-permute-start.24 = (f16[144,2048]{1,0:T(8,128)(2,1)S(1)}, f16[144,2048]{1,0:T(8,128)(2,1)S(1)}, u32[]{:S(2)}, u32[]{:S(2)}) collective-permute-start(f16[144,2048]{1,0:T(8,128)(2,1)S(1)} %convert_element_type.29), channel_id=1, source_target_pairs={{128,0},{5,1},{130,2},{7,3},{132,4},{1,5},{134,6},{3,7},{136,8},{1... | collective-permute-start | bytes 1769480 | tf_op jit(solution)/shard_map/ppermute | solution.py:21
  66.8 14.8 %collective-permute-start.23 = (f16[144,2048]{1,0:T(8,128)(2,1)S(1)}, f16[144,2048]{1,0:T(8,128)(2,1)}, u32[]{:S(2)}, u32[]{:S(2)}) collective-permute-start(f16[144,2048]{1,0:T(8,128)(2,1)S(1)} %convert_element_type.28), channel_id=1, source_target_pairs={{64,0},{3,1},{66,2},{5,3},{68,4},{7,5},{70,6},{1,7},{72,8},{11,9},... | collective-permute-start | bytes 1769480 | tf_op jit(solution)/shard_map/ppermute | solution.py:21
  68.3 14.1 %collective-permute-start.22 = (f16[144,2048]{1,0:T(8,128)(2,1)S(1)}, f16[144,2048]{1,0:T(8,128)(2,1)}, u32[]{:S(2)}, u32[]{:S(2)}) collective-permute-start(f16[144,2048]{1,0:T(8,128)(2,1)S(1)} %convert_element_type.27), channel_id=1, source_target_pairs={{192,0},{7,1},{194,2},{1,3},{196,4},{3,5},{198,6},{5,7},{200,8},{1... | collective-permute-start | bytes 1769480 | tf_op jit(solution)/shard_map/ppermute | solution.py:21
  70.0 19.0 %all-to-all-start = ((f32[64,1,128]{2,1,0:T(1,128)}), f32[64,1,128]{2,1,0:T(1,128)S(1)}, u32[]{:S(2)}, u32[]{:S(2)}) async-start(f32[64,1,128]{2,1,0:T(1,128)} %get-tuple-element.48), calls=%async_computation | async-start | bytes 65536 | tf_op jit(solution)/shard_map/all_to_all | solution.py:194
  84.9 13.3 %collective-permute-start.25 = (f32[32,2048]{1,0:T(8,128)S(1)}, f32[32,2048]{1,0:T(8,128)S(1)}, u32[]{:S(2)}, u32[]{:S(2)}) collective-permute-start(f32[32,2048]{1,0:T(8,128)S(1)} %get-tuple-element.50), channel_id=1, source_target_pairs={{4,0},{129,1},{6,2},{131,3},{0,4},{133,5},{2,6},{135,7},{12,8},{13... | collective-permute-start | bytes 786440 | tf_op jit(solution)/shard_map/ppermute | solution.py:21
  86.4 11.8 %collective-permute-start.27 = (f32[32,2048]{1,0:T(8,128)S(1)}, f32[32,2048]{1,0:T(8,128)S(1)}, u32[]{:S(2)}, u32[]{:S(2)}) collective-permute-start(f32[32,2048]{1,0:T(8,128)S(1)} %get-tuple-element.51), channel_id=1, source_target_pairs={{2,0},{65,1},{4,2},{67,3},{6,4},{69,5},{0,6},{71,7},{10,8},{73,9},... | collective-permute-start | bytes 786440 | tf_op jit(solution)/shard_map/ppermute | solution.py:21
  87.7 10.5 %collective-permute-start.26 = (f32[32,2048]{1,0:T(8,128)S(1)}, f32[32,2048]{1,0:T(8,128)S(1)}, u32[]{:S(2)}, u32[]{:S(2)}) collective-permute-start(f32[32,2048]{1,0:T(8,128)S(1)} %get-tuple-element.52), channel_id=1, source_target_pairs={{6,0},{193,1},{0,2},{195,3},{2,4},{197,5},{4,6},{199,7},{14,8},{20... | collective-permute-start | bytes 786440 | tf_op jit(solution)/shard_map/ppermute | solution.py:21
  89.2 4.0 %collective-permute-start.20 = (f32[1,128]{1,0:T(1,128)S(1)}, f32[1,128]{1,0:T(1,128)S(1)}, u32[]{:S(2)}, u32[]{:S(2)}) collective-permute-start(f32[1,128]{1,0:T(1,128)S(1)} %bitcast.10), channel_id=1, source_target_pairs={{64,0},{65,1},{66,2},{67,3},{68,4},{69,5},{70,6},{71,7},{72,8},{73... | collective-permute-start | bytes 1544 | tf_op jit(solution)/shard_map/ppermute | solution.py:21
  91.8 4.8 %collective-permute-start.21 = (f32[1,128]{1,0:T(1,128)S(1)}, f32[1,128]{1,0:T(1,128)S(1)}, u32[]{:S(2)}, u32[]{:S(2)}) collective-permute-start(f32[1,128]{1,0:T(1,128)S(1)} %bitcast.11), channel_id=1, source_target_pairs={{192,0},{193,1},{194,2},{195,3},{196,4},{197,5},{198,6},{199,7},{2... | collective-permute-start | bytes 1544 | tf_op jit(solution)/shard_map/ppermute | solution.py:21
  93.1 5.0 %collective-permute-start.19 = (f32[1,128]{1,0:T(1,128)S(1)}, f32[1,128]{1,0:T(1,128)S(1)}, u32[]{:S(2)}, u32[]{:S(2)}) collective-permute-start(f32[1,128]{1,0:T(1,128)S(1)} %bitcast.12), channel_id=1, source_target_pairs={{128,0},{129,1},{130,2},{131,3},{132,4},{133,5},{134,6},{135,7},{1... | collective-permute-start | bytes 1544 | tf_op jit(solution)/shard_map/ppermute | solution.py:21

commit v11 on v10

--- a/solution.py
+++ b/solution.py
@@ -152,7 +152,7 @@
     texts, width = student.shape
     both = join(student, teacher)
     tie = lax.optimization_barrier
-    near, far = ("x", "y"), ("y", "x")
+    near, far = ("y", "x"), ("x", "y")
     other = other_core(both)
     ring = [round_z(both)]
     both, other = tie((both, other))

time: 102 us -> 103 us (level); the launches traced: 100 us -> 102 us
  waiting for transfers between devices: 43.2 us -> 45.8 us
    ppermute x5, starting transfers between devices: 3.81 us -> 0.3 us  [other_core(): return lax.ppermute(value, 'core', [(0, 1), (1, 0)])]
    ppermute x5, waiting for transfers between devices: 32.1 us -> 35.3 us  [round_z(): return lax.ppermute(value, AXES, pairs)]
    ppermute x18, starting transfers between devices: 25.2 us -> 27.4 us  [shift(): return lax.ppermute(value, AXES, pairs)]
    ppermute x18, waiting for transfers between devices: 11.1 us -> 9.79 us  [shift(): return lax.ppermute(value, AXES, pairs)]
  transfers between devices with their start and end apart: 29 -> 29, of which waited for: 14 -> 13; matrix products, arithmetic and copies ran while one was open for 5% -> 4% of each run, Pallas kernels for 1% -> 1%
where the time goes in v11:
time: 103 us; the launch traced here: 102 us
  waiting for transfers between devices  45.8 us (44%)
  starting transfers between devices  41.6 us (40%)
  Pallas kernels  7.37 us (7%)
  other arithmetic  4.17 us (4%)
  between operations  2.05 us (2%)
  local copies, waits for them, and re-layouts  1.24 us (1%)
    ppermute x5, waiting for transfers between devices, round_z(): return lax.ppermute(value, AXES, pairs)  35.3 us
    ppermute x18, starting transfers between devices, shift(): return lax.ppermute(value, AXES, pairs)  27.4 us
    all_to_all x1, starting transfers between devices, shards(): lax.all_to_all(squares, ('zh', 'zl', 'x', 'core'), 0, 0)  9.94 us
    ppermute x18, waiting for transfers between devices, shift(): return lax.ppermute(value, AXES, pairs)  9.79 us
    pallas_call x1, Pallas kernels, pulls(): pl.pallas_call(excess_kernel, in_specs=[inside] * (len(pieces) + len(line...  4.62 us
    ppermute x5, starting transfers between devices, round_z(): return lax.ppermute(value, AXES, pairs)  4 us
  transfers between devices with their start and end apart: 29, of which 13 were waited for; matrix products, arithmetic and copies ran while one was open for 4% of the time, Pallas kernels for 1%

profile of v11, /device:TPU:2, one launch (start us, length us, event | category | flops | bytes accessed | tf_op | source)
XLA Modules:
  0.0 102.2 jit_solution(774185798847430055)
XLA Ops:
  0.6 1.8 %shard_map.41.refs_8_.refs_0_ = bf16[32,6144]{1,0:T(8,128)(2,1)} custom-call(bf16[32,2048]{1,0:T(8,128)(2,1)} %student_ref.1, bf16[32,4096]{1,0:T(8,128)(2,1)} %teacher_ref.1), custom_call_target="tpu_custom_call" | custom-call | tf_op jit(solution)/shard_map/pallas_call | solution.py:45
  2.4 1.9 %collective-permute-start = (bf16[32,6144]{1,0:T(8,128)(2,1)}, bf16[32,6144]{1,0:T(8,128)(2,1)S(1)}, u32[]{:S(2)}, u32[]{:S(2)}) collective-permute-start(bf16[32,6144]{1,0:T(8,128)(2,1)} %shard_map.41.refs_8_.refs_0_), channel_id=1, source_target_pairs={{56,0},{17,1},{58,2},{19,3},{60,4},{21,5},{62,6},{23,7},{48,8},{25... | collective-permute-start | bytes 1179656 | tf_op jit(solution)/shard_map/ppermute | solution.py:30
  4.4 3.2 %collective-permute-start.6 = (bf16[32,6144]{1,0:T(8,128)(2,1)}, bf16[32,6144]{1,0:T(8,128)(2,1)S(1)}, u32[]{:S(2)}, u32[]{:S(2)}) collective-permute-start(bf16[32,6144]{1,0:T(8,128)(2,1)} %shard_map.41.refs_8_.refs_0_), channel_id=1, source_target_pairs={{128,0},{5,1},{130,2},{7,3},{132,4},{1,5},{134,6},{3,7},{136,8},{1... | collective-permute-start | bytes 1179656 | tf_op jit(solution)/shard_map/ppermute | solution.py:21
  7.6 0.7 collective-permute-start.5
  8.2 2.6 %collective-permute-start.4 = (bf16[32,6144]{1,0:T(8,128)(2,1)}, bf16[32,6144]{1,0:T(8,128)(2,1)S(1)}, u32[]{:S(2)}, u32[]{:S(2)}) collective-permute-start(bf16[32,6144]{1,0:T(8,128)(2,1)} %shard_map.41.refs_8_.refs_0_), channel_id=1, source_target_pairs={{64,0},{3,1},{66,2},{5,3},{68,4},{7,5},{70,6},{1,7},{72,8},{11,9},... | collective-permute-start | bytes 1179656 | tf_op jit(solution)/shard_map/ppermute | solution.py:21
  10.8 1.9 %collective-permute-start.2 = (bf16[32,6144]{1,0:T(8,128)(2,1)S(1)}, bf16[32,6144]{1,0:T(8,128)(2,1)S(1)}, u32[]{:S(2)}, u32[]{:S(2)}) collective-permute-start(bf16[32,6144]{1,0:T(8,128)(2,1)S(1)} %collective-permute-done.1.refs_9_.refs_1_), channel_id=1, source_target_pairs={{56,0},{17,1},{58,2},{19,3},{60,4},{21,5},{62,6},{23,7},{48,8},{25... | collective-permute-start | bytes 1179656 | tf_op jit(solution)/shard_map/ppermute | solution.py:30
  12.7 1.0 constant_dynamic-update-slice_fusion.3
  13.7 0.5 collective-permute-done
  14.3 8.1 %collective-permute-done.2 = bf16[32,6144]{1,0:T(8,128)(2,1)S(1)} collective-permute-done((bf16[32,6144]{1,0:T(8,128)(2,1)S(1)}, bf16[32,6144]{1,0:T(8,128)(2,1)S(1)}, u32[]{:S(2)}, u32[]{:S(2)}) %collective-permute-start.2) | collective-permute-done | bytes 393248 | tf_op jit(solution)/shard_map/ppermute | solution.py:30
  22.4 0.1 collective-permute-start.3
  22.6 0.6 collective-permute-start.8
  23.3 1.6 %collective-permute-start.9 = (bf16[64,6144]{1,0:T(8,128)(2,1)S(1)}, bf16[64,6144]{1,0:T(8,128)(2,1)S(1)}, u32[]{:S(2)}, u32[]{:S(2)}) collective-permute-start(bf16[64,6144]{1,0:T(8,128)(2,1)S(1)} %constant_dynamic-update-slice_fusion.4.refs_7_), channel_id=1, source_target_pairs={{6,0},{193,1},{0,2},{195,3},{2,4},{197,5},{4,6},{199,7},{14,8},{20... | collective-permute-start | bytes 2359304 | tf_op jit(solution)/shard_map/ppermute | solution.py:21
  24.9 10.9 %collective-permute-done.3.refs_12_.refs_4_ = bf16[64,6144]{1,0:T(8,128)(2,1)S(1)} collective-permute-done((bf16[64,6144]{1,0:T(8,128)(2,1)S(1)}, bf16[64,6144]{1,0:T(8,128)(2,1)S(1)}, u32[]{:S(2)}, u32[]{:S(2)}) %collective-permute-start.3) | collective-permute-done | bytes 786464 | tf_op jit(solution)/shard_map/ppermute | solution.py:30
  35.7 0.4 collective-permute-done.9.refs_3_
  36.1 3.2 %collective-permute-start.12 = (bf16[64,6144]{1,0:T(8,128)(2,1)S(1)}, bf16[64,6144]{1,0:T(8,128)(2,1)S(1)}, u32[]{:S(2)}, u32[]{:S(2)}) collective-permute-start(bf16[64,6144]{1,0:T(8,128)(2,1)S(1)} %collective-permute-done.8.refs_0_), channel_id=1, source_target_pairs={{2,0},{65,1},{4,2},{67,3},{6,4},{69,5},{0,6},{71,7},{10,8},{73,9},... | collective-permute-start | bytes 2359304 | tf_op jit(solution)/shard_map/ppermute | solution.py:21
  39.3 2.0 %collective-permute-start.10 = (bf16[64,6144]{1,0:T(8,128)(2,1)S(1)}, bf16[64,6144]{1,0:T(8,128)(2,1)S(1)}, u32[]{:S(2)}, u32[]{:S(2)}) collective-permute-start(bf16[64,6144]{1,0:T(8,128)(2,1)S(1)} %constant_dynamic-update-slice_fusion.4.refs_7_), channel_id=1, source_target_pairs={{2,0},{65,1},{4,2},{67,3},{6,4},{69,5},{0,6},{71,7},{10,8},{73,9},... | collective-permute-start | bytes 2359304 | tf_op jit(solution)/shard_map/ppermute | solution.py:21
  41.4 7.6 %collective-permute-done.7.refs_14_.refs_6_ = bf16[64,6144]{1,0:T(8,128)(2,1)S(1)} collective-permute-done((bf16[64,6144]{1,0:T(8,128)(2,1)S(1)}, bf16[64,6144]{1,0:T(8,128)(2,1)S(1)}, u32[]{:S(2)}, u32[]{:S(2)}) %collective-permute-start.7) | collective-permute-done | bytes 786464 | tf_op jit(solution)/shard_map/ppermute | solution.py:30
  48.9 1.5 %collective-permute-start.11 = (bf16[64,6144]{1,0:T(8,128)(2,1)S(1)}, bf16[64,6144]{1,0:T(8,128)(2,1)S(1)}, u32[]{:S(2)}, u32[]{:S(2)}) collective-permute-start(bf16[64,6144]{1,0:T(8,128)(2,1)S(1)} %constant_dynamic-update-slice_fusion.2.refs_6_), channel_id=1, source_target_pairs={{6,0},{193,1},{0,2},{195,3},{2,4},{197,5},{4,6},{199,7},{14,8},{20... | collective-permute-start | bytes 2359304 | tf_op jit(solution)/shard_map/ppermute | solution.py:21
  50.5 0.1 collective-permute-start.17
  50.6 0.3 collective-permute-start.15
  50.8 0.5 collective-permute-done.13.refs_5_
  51.3 0.0 collective-permute-start.16
  51.3 8.2 %collective-permute-done.17.refs_16_.refs_8_ = bf16[32,6144]{1,0:T(8,128)(2,1)S(1)} collective-permute-done((bf16[32,6144]{1,0:T(8,128)(2,1)S(1)}, bf16[32,6144]{1,0:T(8,128)(2,1)S(1)}, u32[]{:S(2)}, u32[]{:S(2)}) %collective-permute-start.17) | collective-permute-done | bytes 393248 | tf_op jit(solution)/shard_map/ppermute | solution.py:30
  59.5 1.4 %collective-permute-done.11.refs_2_ = bf16[64,6144]{1,0:T(8,128)(2,1)S(1)} collective-permute-done((bf16[64,6144]{1,0:T(8,128)(2,1)S(1)}, bf16[64,6144]{1,0:T(8,128)(2,1)S(1)}, u32[]{:S(2)}, u32[]{:S(2)}) %collective-permute-start.11) | collective-permute-done | bytes 786464 | tf_op jit(solution)/shard_map/ppermute | solution.py:21
  60.9 0.3 collective-permute-done.18.refs_17_.refs_9_
  61.2 4.6 %shard_map.42 = (f32[144,2048]{1,0:T(8,128)S(1)}, f32[144,2048]{1,0:T(8,128)S(1)}, f32[144,2048]{1,0:T(8,128)S(1)}, bf16[128,512]{1,0:T(8,128)(2,1)S(1)}, f32[1,128]{1,0:T(1,128)S(1)}) custom-call(bf16[64,6144]{1,0:T(8,128)(2,1)S(1)} %collective-permute-done.8.refs_0_, bf16[64,6144]{1,0:T(8,128)(2,1)S(1)} %collective-permute-done.10.refs_1_, ...), custom_call_target="tpu_custom_call" | custom-call | flops 4294967296 | bytes 12582912 | tf_op jit(solution)/shard_map/pallas_call | solution.py:103
  65.9 0.1 convert_element_type.29
  66.0 1.9 %collective-permute-start.24 = (f16[144,2048]{1,0:T(8,128)(2,1)S(1)}, f16[144,2048]{1,0:T(8,128)(2,1)S(1)}, u32[]{:S(2)}, u32[]{:S(2)}) collective-permute-start(f16[144,2048]{1,0:T(8,128)(2,1)S(1)} %convert_element_type.29), channel_id=1, source_target_pairs={{4,0},{129,1},{6,2},{131,3},{0,4},{133,5},{2,6},{135,7},{12,8},{13... | collective-permute-start | bytes 1769480 | tf_op jit(solution)/shard_map/ppermute | solution.py:21
  67.9 0.1 convert_element_type.28
  67.9 1.5 %collective-permute-start.23 = (f16[144,2048]{1,0:T(8,128)(2,1)S(1)}, f16[144,2048]{1,0:T(8,128)(2,1)}, u32[]{:S(2)}, u32[]{:S(2)}) collective-permute-start(f16[144,2048]{1,0:T(8,128)(2,1)S(1)} %convert_element_type.28), channel_id=1, source_target_pairs={{2,0},{65,1},{4,2},{67,3},{6,4},{69,5},{0,6},{71,7},{10,8},{73,9},... | collective-permute-start | bytes 1769480 | tf_op jit(solution)/shard_map/ppermute | solution.py:21
  69.5 0.1 convert_element_type.27
  69.5 0.7 collective-permute-start.22
  70.2 0.9 shard_map.43
  71.2 9.9 %all-to-all-start = ((f32[64,1,128]{2,1,0:T(1,128)}), f32[64,1,128]{2,1,0:T(1,128)S(1)}, u32[]{:S(2)}, u32[]{:S(2)}) async-start(f32[64,1,128]{2,1,0:T(1,128)} %get-tuple-element.48), calls=%async_computation | async-start | bytes 65536 | tf_op jit(solution)/shard_map/all_to_all | solution.py:194
  81.1 2.7 %collective-permute-done.23 = f16[144,2048]{1,0:T(8,128)(2,1)} collective-permute-done((f16[144,2048]{1,0:T(8,128)(2,1)S(1)}, f16[144,2048]{1,0:T(8,128)(2,1)}, u32[]{:S(2)}, u32[]{:S(2)}) %collective-permute-start.23) | collective-permute-done | bytes 589856 | tf_op jit(solution)/shard_map/ppermute | solution.py:21
  83.9 0.8 fusion.3
  84.7 0.8 fusion.2
  85.4 1.6 %multiply_add_fusion = f32[128,2048]{1,0:T(8,128)S(1)} fusion(f32[128,2048]{1,0:T(8,128)S(1)} %get-tuple-element.49, f16[144,2048]{1,0:T(8,128)(2,1)S(1)} %collective-permute-done.24, f16[144,2048]{1,0:T(8,128)(2,1)} %collective-permute-done.23, f16[144,2048]{1,0:T(8,128)(2,1)} %collective-permute-done.22, f32[2048]{0:T(1024)S(1)} %bitcast.7, ...), kind=kLoop, calls=%fused_computation | loop fusion | flops 2359296 | bytes 3694592 | tf_op jit(solution)/shard_map/add | solution.py:188
  87.0 0.1 fusion.5
  87.0 0.1 collective-permute-start.25
  87.1 2.1 %collective-permute-start.27 = (f32[32,2048]{1,0:T(8,128)S(1)}, f32[32,2048]{1,0:T(8,128)S(1)}, u32[]{:S(2)}, u32[]{:S(2)}) collective-permute-start(f32[32,2048]{1,0:T(8,128)S(1)} %get-tuple-element.51), channel_id=1, source_target_pairs={{64,0},{3,1},{66,2},{5,3},{68,4},{7,5},{70,6},{1,7},{72,8},{11,9},... | collective-permute-start | bytes 786440 | tf_op jit(solution)/shard_map/ppermute | solution.py:21
  89.3 0.4 all-to-all-done
  89.6 0.1 reduce_sum.11
  89.7 2.9 %collective-permute-start.20 = (f32[1,128]{1,0:T(1,128)S(1)}, f32[1,128]{1,0:T(1,128)S(1)}, u32[]{:S(2)}, u32[]{:S(2)}) collective-permute-start(f32[1,128]{1,0:T(1,128)S(1)} %bitcast.10), channel_id=1, source_target_pairs={{64,0},{65,1},{66,2},{67,3},{68,4},{69,5},{70,6},{71,7},{72,8},{73... | collective-permute-start | bytes 1544 | tf_op jit(solution)/shard_map/ppermute | solution.py:21
  92.7 2.5 %collective-permute-done.20 = f32[1,128]{1,0:T(1,128)S(1)} collective-permute-done((f32[1,128]{1,0:T(1,128)S(1)}, f32[1,128]{1,0:T(1,128)S(1)}, u32[]{:S(2)}, u32[]{:S(2)}) %collective-permute-start.20) | collective-permute-done | bytes 544 | tf_op jit(solution)/shard_map/ppermute | solution.py:21
  95.2 2.8 %collective-permute-start.19 = (f32[1,128]{1,0:T(1,128)S(1)}, f32[1,128]{1,0:T(1,128)S(1)}, u32[]{:S(2)}, u32[]{:S(2)}) collective-permute-start(f32[1,128]{1,0:T(1,128)S(1)} %bitcast.12), channel_id=1, source_target_pairs={{128,0},{129,1},{130,2},{131,3},{132,4},{133,5},{134,6},{135,7},{1... | collective-permute-start | bytes 1544 | tf_op jit(solution)/shard_map/ppermute | solution.py:21
  98.0 2.3 %collective-permute-done.19 = f32[1,128]{1,0:T(1,128)S(1)} collective-permute-done((f32[1,128]{1,0:T(1,128)S(1)}, f32[1,128]{1,0:T(1,128)S(1)}, u32[]{:S(2)}, u32[]{:S(2)}) %collective-permute-start.19) | collective-permute-done | bytes 544 | tf_op jit(solution)/shard_map/ppermute | solution.py:21
  100.3 0.8 fusion.1
  (33 shorter events, 0.3 us)
Async XLA Ops:
  2.4 1.9 %collective-permute-start.1 = (bf16[32,6144]{1,0:T(8,128)(2,1)}, bf16[32,6144]{1,0:T(8,128)(2,1)S(1)}, u32[]{:S(2)}, u32[]{:S(2)}) collective-permute-start(bf16[32,6144]{1,0:T(8,128)(2,1)} %shard_map.41.refs_8_.refs_0_), channel_id=1, source_target_pairs={{0,1},{1,0},{2,3},{3,2},{4,5},{5,4},{6,7},{7,6},{8,9},{9,8},{10,11... | collective-permute-start | bytes 1179656 | tf_op jit(solution)/shard_map/ppermute | solution.py:34
  2.4 11.8 %collective-permute-start = (bf16[32,6144]{1,0:T(8,128)(2,1)}, bf16[32,6144]{1,0:T(8,128)(2,1)S(1)}, u32[]{:S(2)}, u32[]{:S(2)}) collective-permute-start(bf16[32,6144]{1,0:T(8,128)(2,1)} %shard_map.41.refs_8_.refs_0_), channel_id=1, source_target_pairs={{56,0},{17,1},{58,2},{19,3},{60,4},{21,5},{62,6},{23,7},{48,8},{25... | collective-permute-start | bytes 1179656 | tf_op jit(solution)/shard_map/ppermute | solution.py:30
  4.4 18.2 %collective-permute-start.6 = (bf16[32,6144]{1,0:T(8,128)(2,1)}, bf16[32,6144]{1,0:T(8,128)(2,1)S(1)}, u32[]{:S(2)}, u32[]{:S(2)}) collective-permute-start(bf16[32,6144]{1,0:T(8,128)(2,1)} %shard_map.41.refs_8_.refs_0_), channel_id=1, source_target_pairs={{128,0},{5,1},{130,2},{7,3},{132,4},{1,5},{134,6},{3,7},{136,8},{1... | collective-permute-start | bytes 1179656 | tf_op jit(solution)/shard_map/ppermute | solution.py:21
  7.6 15.0 %collective-permute-start.5 = (bf16[32,6144]{1,0:T(8,128)(2,1)}, bf16[32,6144]{1,0:T(8,128)(2,1)S(1)}, u32[]{:S(2)}, u32[]{:S(2)}) collective-permute-start(bf16[32,6144]{1,0:T(8,128)(2,1)} %shard_map.41.refs_8_.refs_0_), channel_id=1, source_target_pairs={{192,0},{7,1},{194,2},{1,3},{196,4},{3,5},{198,6},{5,7},{200,8},{1... | collective-permute-start | bytes 1179656 | tf_op jit(solution)/shard_map/ppermute | solution.py:21
  8.2 14.3 %collective-permute-start.4 = (bf16[32,6144]{1,0:T(8,128)(2,1)}, bf16[32,6144]{1,0:T(8,128)(2,1)S(1)}, u32[]{:S(2)}, u32[]{:S(2)}) collective-permute-start(bf16[32,6144]{1,0:T(8,128)(2,1)} %shard_map.41.refs_8_.refs_0_), channel_id=1, source_target_pairs={{64,0},{3,1},{66,2},{5,3},{68,4},{7,5},{70,6},{1,7},{72,8},{11,9},... | collective-permute-start | bytes 1179656 | tf_op jit(solution)/shard_map/ppermute | solution.py:21
  10.8 11.6 %collective-permute-start.2 = (bf16[32,6144]{1,0:T(8,128)(2,1)S(1)}, bf16[32,6144]{1,0:T(8,128)(2,1)S(1)}, u32[]{:S(2)}, u32[]{:S(2)}) collective-permute-start(bf16[32,6144]{1,0:T(8,128)(2,1)S(1)} %collective-permute-done.1.refs_9_.refs_1_), channel_id=1, source_target_pairs={{56,0},{17,1},{58,2},{19,3},{60,4},{21,5},{62,6},{23,7},{48,8},{25... | collective-permute-start | bytes 1179656 | tf_op jit(solution)/shard_map/ppermute | solution.py:30
  22.4 13.3 %collective-permute-start.3 = (bf16[64,6144]{1,0:T(8,128)(2,1)S(1)}, bf16[64,6144]{1,0:T(8,128)(2,1)S(1)}, u32[]{:S(2)}, u32[]{:S(2)}) collective-permute-start(bf16[64,6144]{1,0:T(8,128)(2,1)S(1)} %constant_dynamic-update-slice_fusion.refs_10_.refs_2_), channel_id=1, source_target_pairs={{56,0},{17,1},{58,2},{19,3},{60,4},{21,5},{62,6},{23,7},{48,8},{25... | collective-permute-start | bytes 2359304 | tf_op jit(solution)/shard_map/ppermute | solution.py:30
  22.6 38.6 %copy-start = (bf16[32,6144]{1,0:T(8,128)(2,1)S(1)}, bf16[32,6144]{1,0:T(8,128)(2,1)}, u32[]{:S(2)}) copy-start(bf16[32,6144]{1,0:T(8,128)(2,1)} %shard_map.41.refs_8_.refs_0_) | copy-start | bytes 1179652
  22.6 13.1 %collective-permute-start.8 = (bf16[64,6144]{1,0:T(8,128)(2,1)S(1)}, bf16[64,6144]{1,0:T(8,128)(2,1)S(1)}, u32[]{:S(2)}, u32[]{:S(2)}) collective-permute-start(bf16[64,6144]{1,0:T(8,128)(2,1)S(1)} %constant_dynamic-update-slice_fusion.2.refs_6_), channel_id=1, source_target_pairs={{2,0},{65,1},{4,2},{67,3},{6,4},{69,5},{0,6},{71,7},{10,8},{73,9},... | collective-permute-start | bytes 2359304 | tf_op jit(solution)/shard_map/ppermute | solution.py:21
  23.3 12.8 %collective-permute-start.9 = (bf16[64,6144]{1,0:T(8,128)(2,1)S(1)}, bf16[64,6144]{1,0:T(8,128)(2,1)S(1)}, u32[]{:S(2)}, u32[]{:S(2)}) collective-permute-start(bf16[64,6144]{1,0:T(8,128)(2,1)S(1)} %constant_dynamic-update-slice_fusion.4.refs_7_), channel_id=1, source_target_pairs={{6,0},{193,1},{0,2},{195,3},{2,4},{197,5},{4,6},{199,7},{14,8},{20... | collective-permute-start | bytes 2359304 | tf_op jit(solution)/shard_map/ppermute | solution.py:21
  35.7 13.2 %collective-permute-start.7 = (bf16[64,6144]{1,0:T(8,128)(2,1)S(1)}, bf16[64,6144]{1,0:T(8,128)(2,1)S(1)}, u32[]{:S(2)}, u32[]{:S(2)}) collective-permute-start(bf16[64,6144]{1,0:T(8,128)(2,1)S(1)} %collective-permute-done.3.refs_12_.refs_4_), channel_id=1, source_target_pairs={{56,0},{17,1},{58,2},{19,3},{60,4},{21,5},{62,6},{23,7},{48,8},{25... | collective-permute-start | bytes 2359304 | tf_op jit(solution)/shard_map/ppermute | solution.py:30
  35.7 14.7 %collective-permute-start.14 = (bf16[64,6144]{1,0:T(8,128)(2,1)S(1)}, bf16[64,6144]{1,0:T(8,128)(2,1)S(1)}, u32[]{:S(2)}, u32[]{:S(2)}) collective-permute-start(bf16[64,6144]{1,0:T(8,128)(2,1)S(1)} %constant_dynamic-update-slice_fusion.refs_10_.refs_2_), channel_id=1, source_target_pairs={{0,1},{1,0},{2,3},{3,2},{4,5},{5,4},{6,7},{7,6},{8,9},{9,8},{10,11... | collective-permute-start | bytes 2359304 | tf_op jit(solution)/shard_map/ppermute | solution.py:34
  36.1 14.5 %collective-permute-start.12 = (bf16[64,6144]{1,0:T(8,128)(2,1)S(1)}, bf16[64,6144]{1,0:T(8,128)(2,1)S(1)}, u32[]{:S(2)}, u32[]{:S(2)}) collective-permute-start(bf16[64,6144]{1,0:T(8,128)(2,1)S(1)} %collective-permute-done.8.refs_0_), channel_id=1, source_target_pairs={{2,0},{65,1},{4,2},{67,3},{6,4},{69,5},{0,6},{71,7},{10,8},{73,9},... | collective-permute-start | bytes 2359304 | tf_op jit(solution)/shard_map/ppermute | solution.py:21
  39.3 12.0 %collective-permute-start.13 = (bf16[64,6144]{1,0:T(8,128)(2,1)S(1)}, bf16[64,6144]{1,0:T(8,128)(2,1)S(1)}, u32[]{:S(2)}, u32[]{:S(2)}) collective-permute-start(bf16[64,6144]{1,0:T(8,128)(2,1)S(1)} %collective-permute-done.9.refs_3_), channel_id=1, source_target_pairs={{6,0},{193,1},{0,2},{195,3},{2,4},{197,5},{4,6},{199,7},{14,8},{20... | collective-permute-start | bytes 2359304 | tf_op jit(solution)/shard_map/ppermute | solution.py:21
  39.3 20.2 %collective-permute-start.10 = (bf16[64,6144]{1,0:T(8,128)(2,1)S(1)}, bf16[64,6144]{1,0:T(8,128)(2,1)S(1)}, u32[]{:S(2)}, u32[]{:S(2)}) collective-permute-start(bf16[64,6144]{1,0:T(8,128)(2,1)S(1)} %constant_dynamic-update-slice_fusion.4.refs_7_), channel_id=1, source_target_pairs={{2,0},{65,1},{4,2},{67,3},{6,4},{69,5},{0,6},{71,7},{10,8},{73,9},... | collective-permute-start | bytes 2359304 | tf_op jit(solution)/shard_map/ppermute | solution.py:21
  48.9 12.0 %collective-permute-start.11 = (bf16[64,6144]{1,0:T(8,128)(2,1)S(1)}, bf16[64,6144]{1,0:T(8,128)(2,1)S(1)}, u32[]{:S(2)}, u32[]{:S(2)}) collective-permute-start(bf16[64,6144]{1,0:T(8,128)(2,1)S(1)} %constant_dynamic-update-slice_fusion.2.refs_6_), channel_id=1, source_target_pairs={{6,0},{193,1},{0,2},{195,3},{2,4},{197,5},{4,6},{199,7},{14,8},{20... | collective-permute-start | bytes 2359304 | tf_op jit(solution)/shard_map/ppermute | solution.py:21
  50.5 9.1 %collective-permute-start.17 = (bf16[32,6144]{1,0:T(8,128)(2,1)S(1)}, bf16[32,6144]{1,0:T(8,128)(2,1)S(1)}, u32[]{:S(2)}, u32[]{:S(2)}) collective-permute-start(bf16[32,6144]{1,0:T(8,128)(2,1)S(1)} %slice.40), channel_id=1, source_target_pairs={{56,0},{17,1},{58,2},{19,3},{60,4},{21,5},{62,6},{23,7},{48,8},{25... | collective-permute-start | bytes 1179656 | tf_op jit(solution)/shard_map/ppermute | solution.py:30
  50.6 10.4 %collective-permute-start.15 = (bf16[64,6144]{1,0:T(8,128)(2,1)S(1)}, bf16[64,6144]{1,0:T(8,128)(2,1)S(1)}, u32[]{:S(2)}, u32[]{:S(2)}) collective-permute-start(bf16[64,6144]{1,0:T(8,128)(2,1)S(1)} %collective-permute-done.3.refs_12_.refs_4_), channel_id=1, source_target_pairs={{0,1},{1,0},{2,3},{3,2},{4,5},{5,4},{6,7},{7,6},{8,9},{9,8},{10,11... | collective-permute-start | bytes 2359304 | tf_op jit(solution)/shard_map/ppermute | solution.py:34
  51.3 9.9 %collective-permute-start.16 = (bf16[64,6144]{1,0:T(8,128)(2,1)S(1)}, bf16[64,6144]{1,0:T(8,128)(2,1)S(1)}, u32[]{:S(2)}, u32[]{:S(2)}) collective-permute-start(bf16[64,6144]{1,0:T(8,128)(2,1)S(1)} %collective-permute-done.7.refs_14_.refs_6_), channel_id=1, source_target_pairs={{0,1},{1,0},{2,3},{3,2},{4,5},{5,4},{6,7},{7,6},{8,9},{9,8},{10,11... | collective-permute-start | bytes 2359304 | tf_op jit(solution)/shard_map/ppermute | solution.py:34
  59.5 1.7 %collective-permute-start.18 = (bf16[32,6144]{1,0:T(8,128)(2,1)S(1)}, bf16[32,6144]{1,0:T(8,128)(2,1)S(1)}, u32[]{:S(2)}, u32[]{:S(2)}) collective-permute-start(bf16[32,6144]{1,0:T(8,128)(2,1)S(1)} %collective-permute-done.17.refs_16_.refs_8_), channel_id=1, source_target_pairs={{0,1},{1,0},{2,3},{3,2},{4,5},{5,4},{6,7},{7,6},{8,9},{9,8},{10,11... | collective-permute-start | bytes 1179656 | tf_op jit(solution)/shard_map/ppermute | solution.py:34
  66.0 15.1 %collective-permute-start.24 = (f16[144,2048]{1,0:T(8,128)(2,1)S(1)}, f16[144,2048]{1,0:T(8,128)(2,1)S(1)}, u32[]{:S(2)}, u32[]{:S(2)}) collective-permute-start(f16[144,2048]{1,0:T(8,128)(2,1)S(1)} %convert_element_type.29), channel_id=1, source_target_pairs={{4,0},{129,1},{6,2},{131,3},{0,4},{133,5},{2,6},{135,7},{12,8},{13... | collective-permute-start | bytes 1769480 | tf_op jit(solution)/shard_map/ppermute | solution.py:21
  67.9 15.9 %collective-permute-start.23 = (f16[144,2048]{1,0:T(8,128)(2,1)S(1)}, f16[144,2048]{1,0:T(8,128)(2,1)}, u32[]{:S(2)}, u32[]{:S(2)}) collective-permute-start(f16[144,2048]{1,0:T(8,128)(2,1)S(1)} %convert_element_type.28), channel_id=1, source_target_pairs={{2,0},{65,1},{4,2},{67,3},{6,4},{69,5},{0,6},{71,7},{10,8},{73,9},... | collective-permute-start | bytes 1769480 | tf_op jit(solution)/shard_map/ppermute | solution.py:21
  69.5 15.1 %collective-permute-start.22 = (f16[144,2048]{1,0:T(8,128)(2,1)S(1)}, f16[144,2048]{1,0:T(8,128)(2,1)}, u32[]{:S(2)}, u32[]{:S(2)}) collective-permute-start(f16[144,2048]{1,0:T(8,128)(2,1)S(1)} %convert_element_type.27), channel_id=1, source_target_pairs={{6,0},{193,1},{0,2},{195,3},{2,4},{197,5},{4,6},{199,7},{14,8},{20... | collective-permute-start | bytes 1769480 | tf_op jit(solution)/shard_map/ppermute | solution.py:21
  71.2 18.5 %all-to-all-start = ((f32[64,1,128]{2,1,0:T(1,128)}), f32[64,1,128]{2,1,0:T(1,128)S(1)}, u32[]{:S(2)}, u32[]{:S(2)}) async-start(f32[64,1,128]{2,1,0:T(1,128)} %get-tuple-element.48), calls=%async_computation | async-start | bytes 65536 | tf_op jit(solution)/shard_map/all_to_all | solution.py:194
  87.0 13.3 %collective-permute-start.25 = (f32[32,2048]{1,0:T(8,128)S(1)}, f32[32,2048]{1,0:T(8,128)S(1)}, u32[]{:S(2)}, u32[]{:S(2)}) collective-permute-start(f32[32,2048]{1,0:T(8,128)S(1)} %get-tuple-element.50), channel_id=1, source_target_pairs={{128,0},{5,1},{130,2},{7,3},{132,4},{1,5},{134,6},{3,7},{136,8},{1... | collective-permute-start | bytes 786440 | tf_op jit(solution)/shard_map/ppermute | solution.py:21
  87.1 13.2 %collective-permute-start.27 = (f32[32,2048]{1,0:T(8,128)S(1)}, f32[32,2048]{1,0:T(8,128)S(1)}, u32[]{:S(2)}, u32[]{:S(2)}) collective-permute-start(f32[32,2048]{1,0:T(8,128)S(1)} %get-tuple-element.51), channel_id=1, source_target_pairs={{64,0},{3,1},{66,2},{5,3},{68,4},{7,5},{70,6},{1,7},{72,8},{11,9},... | collective-permute-start | bytes 786440 | tf_op jit(solution)/shard_map/ppermute | solution.py:21
  89.3 11.1 %collective-permute-start.26 = (f32[32,2048]{1,0:T(8,128)S(1)}, f32[32,2048]{1,0:T(8,128)S(1)}, u32[]{:S(2)}, u32[]{:S(2)}) collective-permute-start(f32[32,2048]{1,0:T(8,128)S(1)} %get-tuple-element.52), channel_id=1, source_target_pairs={{192,0},{7,1},{194,2},{1,3},{196,4},{3,5},{198,6},{5,7},{200,8},{1... | collective-permute-start | bytes 786440 | tf_op jit(solution)/shard_map/ppermute | solution.py:21
  89.7 5.5 %collective-permute-start.20 = (f32[1,128]{1,0:T(1,128)S(1)}, f32[1,128]{1,0:T(1,128)S(1)}, u32[]{:S(2)}, u32[]{:S(2)}) collective-permute-start(f32[1,128]{1,0:T(1,128)S(1)} %bitcast.10), channel_id=1, source_target_pairs={{64,0},{65,1},{66,2},{67,3},{68,4},{69,5},{70,6},{71,7},{72,8},{73... | collective-permute-start | bytes 1544 | tf_op jit(solution)/shard_map/ppermute | solution.py:21
  92.7 5.3 %collective-permute-start.21 = (f32[1,128]{1,0:T(1,128)S(1)}, f32[1,128]{1,0:T(1,128)S(1)}, u32[]{:S(2)}, u32[]{:S(2)}) collective-permute-start(f32[1,128]{1,0:T(1,128)S(1)} %bitcast.11), channel_id=1, source_target_pairs={{192,0},{193,1},{194,2},{195,3},{196,4},{197,5},{198,6},{199,7},{2... | collective-permute-start | bytes 1544 | tf_op jit(solution)/shard_map/ppermute | solution.py:21
  95.2 5.0 %collective-permute-start.19 = (f32[1,128]{1,0:T(1,128)S(1)}, f32[1,128]{1,0:T(1,128)S(1)}, u32[]{:S(2)}, u32[]{:S(2)}) collective-permute-start(f32[1,128]{1,0:T(1,128)S(1)} %bitcast.12), channel_id=1, source_target_pairs={{128,0},{129,1},{130,2},{131,3},{132,4},{133,5},{134,6},{135,7},{1... | collective-permute-start | bytes 1544 | tf_op jit(solution)/shard_map/ppermute | solution.py:21
